TPU v7x, 32 devices: a whole 2x2x4 slice. The times are simulated.
32 devices in a mesh: gx: 4 (over z), gy: 4 (over y, core), band: 2 (over x).
Axes of the slice: x: 2, y: 2, z: 4, core: 2. Of those that a mesh axis runs over, the one named last changes fastest.
Arguments:
- orbitals: float32 [4, 128, 32, 256], P('band', 'gx', 'gy'), may hold values from -600 to 600
- potential: float32 [128, 32, 256], P('gx', 'gy'), may hold values from -0.5 to 0.5
- order: int32 [4], replicated, may hold values from 0 to 3, as said below
Outputs:
- basis: float32 [4, 128, 32, 256], P('band', 'gx', 'gy')
Inputs may be any that keep to these rules, and one draw needn't show every extreme that they name: `order`: each orbital appears once; position p names the orbital orthonormalized p-th.
All inputs are finite; a program needn't handle non-finite values.
Results may differ from a plain program's by a relative error of at most 0.00026.
Values sent between devices are 32-bit elements; how exact they have to be, the bound alone decides.
No kernel may reach another device: no remote copies, remote signals or barrier semaphores. Data moves between devices by JAX's collectives and lax.ppermute only.
A program may use at most 64 MiB of HBM per device.

v0:
```python
import jax
import jax.numpy as jnp
from jax import lax
from jax.sharding import PartitionSpec as P

DEGREE = 8


def extended_2(cells, sides, width):
    for axis, dim in sides:
        count = lax.axis_size(axis)
        ends = count - 1
        head = lax.slice_in_dim(cells, 0, width, axis=dim)
        tail = lax.slice_in_dim(cells, cells.shape[dim] - width, cells.shape[dim], axis=dim)
        cells = jnp.concatenate(
            [
                lax.ppermute(tail, axis, [(i, (i + 1) % count) for i in range(ends)]),
                cells,
                lax.ppermute(head, axis, [((i + 1) % count, i) for i in range(ends)]),
            ],
            axis=dim,
        )
    return cells


def apply_operator(extended, potential):
    middle = extended[:, 2:-2, 2:-2, :]
    padded_z = jnp.pad(middle, ((0, 0), (0, 0), (0, 0), (2, 2)))
    nearest = extended[:, 1:-3, 2:-2] + extended[:, 3:-1, 2:-2]
    nearest = nearest + extended[:, 2:-2, 1:-3] + extended[:, 2:-2, 3:-1]
    nearest = nearest + padded_z[..., 1:-3] + padded_z[..., 3:-1]
    distant = extended[:, :-4, 2:-2] + extended[:, 4:, 2:-2]
    distant = distant + extended[:, 2:-2, :-4] + extended[:, 2:-2, 4:]
    distant = distant + padded_z[..., :-4] + padded_z[..., 4:]
    applied = (3.75 + potential) * middle - nearest * (2.0 / 3.0) + distant / 24.0
    return (applied - 4.25 * middle) / 4.25


def mixing_matrix(correlation, order):
    orbital_count = correlation.shape[0]
    positions = jnp.arange(orbital_count, dtype=jnp.int32)
    arrange = (order[:, None] == positions[None, :]).astype(jnp.float32)
    highest = lax.Precision.HIGHEST
    ordered = jnp.dot(
        jnp.dot(arrange, correlation, precision=highest), arrange.T, precision=highest
    )
    lower_factor = jnp.linalg.cholesky(ordered)
    inverse = jax.scipy.linalg.solve_triangular(
        lower_factor, jnp.eye(orbital_count, dtype=jnp.float32), lower=True
    )
    return jnp.dot(jnp.dot(arrange.T, inverse, precision=highest), arrange, precision=highest)


def shallow_step(field, potential):
    extended = extended_2(field, (("gx", 1), ("gy", 2)), 2)
    return apply_operator(extended, potential)


def per_device(orbitals, potential, order):
    group, width_x, width_y, depth_z = orbitals.shape
    previous = orbitals
    current = shallow_step(orbitals, potential)
    for repeat in range(DEGREE - 1):
        following = 2.0 * shallow_step(current, potential) - previous
        previous, current = (current, following)
    gathered = lax.all_gather(current, "band", axis=0, tiled=True)
    flattened = gathered.reshape(gathered.shape[0], -1)
    cell_total = float(width_x * lax.axis_size("gx") * width_y * lax.axis_size("gy") * depth_z)
    band_pos = lax.axis_index("band")
    partial_value = jnp.dot(
        flattened, flattened.T, precision=lax.Precision.HIGHEST, preferred_element_type=jnp.float32
    )
    correlation = lax.psum(partial_value, ("gx", "gy")) / cell_total
    mixing = mixing_matrix(correlation, order)
    own_mixing = lax.dynamic_slice_in_dim(mixing, band_pos * group, group, 0)
    basis = jnp.dot(
        own_mixing, flattened, precision=lax.Precision.HIGHEST, preferred_element_type=jnp.float32
    )
    return basis.reshape(orbitals.shape)


def solution(mesh):
    in_specs = (P("band", "gx", "gy", None), P("gx", "gy", None), P())
    out_specs = P("band", "gx", "gy", None)
    return jax.shard_map(
        per_device, mesh=mesh, in_specs=in_specs, out_specs=out_specs, check_vma=False
    )
```

profile of v0, /device:TPU:0, one launch (start us, length us, event | category | flops | bytes accessed | tf_op | source)
XLA Modules:
  0.0 226.0 jit_solution(12946494789410168071)
XLA Ops:
  7.8 4.9 %collective-permute-start = (f32[2,2,8,256]{3,1,2,0:T(2,128)S(1)}, f32[2,2,8,256]{3,1,2,0:T(2,128)S(1)}, u32[]{:S(2)}, u32[]{:S(2)}) collective-permute-start(f32[2,2,8,256]{3,1,2,0:T(2,128)S(1)} %get-tuple-element.55), channel_id=1, source_target_pairs={{0,8},{8,16},{16,24},{1,9},{9,17},{17,25},{2,10},{10,18},{18,26},{... | collective-permute-start | bytes 98312 | tf_op jit(solution)/shard_map/ppermute | solution.py:17
  14.3 4.4 %collective-permute-done.1 = f32[2,2,8,256]{3,1,2,0:T(2,128)S(1)} collective-permute-done((f32[2,2,8,256]{3,1,2,0:T(2,128)S(1)}, f32[2,2,8,256]{3,1,2,0:T(2,128)S(1)}, u32[]{:S(2)}, u32[]{:S(2)}) %collective-permute-start.1) | collective-permute-done | bytes 32800 | tf_op jit(solution)/shard_map/ppermute | solution.py:19
  21.5 3.5 %collective-permute-done.3 = f32[2,36,2,256]{3,1,2,0:T(8,128)S(1)} collective-permute-done((f32[2,36,2,256]{3,1,2,0:T(8,128)S(1)}, f32[2,36,2,256]{3,1,2,0:T(8,128)S(1)}, u32[]{:S(2)}, u32[]{:S(2)}) %collective-permute-start.3) | collective-permute-done | bytes 147488 | tf_op jit(solution)/shard_map/ppermute | solution.py:19
  26.0 3.5 %collective-permute-start.4 = (f32[2,2,8,256]{3,1,2,0:T(2,128)S(1)}, f32[2,2,8,256]{3,1,2,0:T(2,128)S(1)}, u32[]{:S(2)}, u32[]{:S(2)}) collective-permute-start(f32[2,2,8,256]{3,1,2,0:T(2,128)S(1)} %get-tuple-element.51), channel_id=1, source_target_pairs={{0,8},{8,16},{16,24},{1,9},{9,17},{17,25},{2,10},{10,18},{18,26},{... | collective-permute-start | bytes 98312 | tf_op jit(solution)/shard_map/ppermute | solution.py:17
  31.1 4.2 %collective-permute-done.5 = f32[2,2,8,256]{3,1,2,0:T(2,128)S(1)} collective-permute-done((f32[2,2,8,256]{3,1,2,0:T(2,128)S(1)}, f32[2,2,8,256]{3,1,2,0:T(2,128)S(1)}, u32[]{:S(2)}, u32[]{:S(2)}) %collective-permute-start.5) | collective-permute-done | bytes 32800 | tf_op jit(solution)/shard_map/ppermute | solution.py:19
  35.3 4.3 %collective-permute-start.6 = (f32[2,36,2,256]{3,1,2,0:T(8,128)S(1)}, f32[2,36,2,256]{3,1,2,0:T(8,128)S(1)}, u32[]{:S(2)}, u32[]{:S(2)}) collective-permute-start(f32[2,36,2,256]{3,1,2,0:T(8,128)S(1)} %get-tuple-element.33), channel_id=1, source_target_pairs={{0,2},{2,4},{4,6},{1,3},{3,5},{5,7},{8,10},{10,12},{12,14},{9,11},... | collective-permute-start | bytes 442376 | tf_op jit(solution)/shard_map/ppermute | solution.py:17
  44.7 3.5 %collective-permute-start.8 = (f32[2,2,8,256]{3,1,2,0:T(2,128)S(1)}, f32[2,2,8,256]{3,1,2,0:T(2,128)S(1)}, u32[]{:S(2)}, u32[]{:S(2)}) collective-permute-start(f32[2,2,8,256]{3,1,2,0:T(2,128)S(1)} %get-tuple-element.49), channel_id=1, source_target_pairs={{0,8},{8,16},{16,24},{1,9},{9,17},{17,25},{2,10},{10,18},{18,26},{... | collective-permute-start | bytes 98312 | tf_op jit(solution)/shard_map/ppermute | solution.py:17
  49.8 4.2 %collective-permute-done.9 = f32[2,2,8,256]{3,1,2,0:T(2,128)S(1)} collective-permute-done((f32[2,2,8,256]{3,1,2,0:T(2,128)S(1)}, f32[2,2,8,256]{3,1,2,0:T(2,128)S(1)}, u32[]{:S(2)}, u32[]{:S(2)}) %collective-permute-start.9) | collective-permute-done | bytes 32800 | tf_op jit(solution)/shard_map/ppermute | solution.py:19
  54.1 4.3 %collective-permute-start.10 = (f32[2,36,2,256]{3,1,2,0:T(8,128)S(1)}, f32[2,36,2,256]{3,1,2,0:T(8,128)S(1)}, u32[]{:S(2)}, u32[]{:S(2)}) collective-permute-start(f32[2,36,2,256]{3,1,2,0:T(8,128)S(1)} %get-tuple-element.29), channel_id=1, source_target_pairs={{0,2},{2,4},{4,6},{1,3},{3,5},{5,7},{8,10},{10,12},{12,14},{9,11},... | collective-permute-start | bytes 442376 | tf_op jit(solution)/shard_map/ppermute | solution.py:17
  59.7 2.7 %collective-permute-done.11 = f32[2,36,2,256]{3,1,2,0:T(8,128)S(1)} collective-permute-done((f32[2,36,2,256]{3,1,2,0:T(8,128)S(1)}, f32[2,36,2,256]{3,1,2,0:T(8,128)S(1)}, u32[]{:S(2)}, u32[]{:S(2)}) %collective-permute-start.11) | collective-permute-done | bytes 147488 | tf_op jit(solution)/shard_map/ppermute | solution.py:19
  66.9 4.2 %collective-permute-done.13 = f32[2,2,8,256]{3,1,2,0:T(2,128)S(1)} collective-permute-done((f32[2,2,8,256]{3,1,2,0:T(2,128)S(1)}, f32[2,2,8,256]{3,1,2,0:T(2,128)S(1)}, u32[]{:S(2)}, u32[]{:S(2)}) %collective-permute-start.13) | collective-permute-done | bytes 32800 | tf_op jit(solution)/shard_map/ppermute | solution.py:19
  71.2 4.3 %collective-permute-start.14 = (f32[2,36,2,256]{3,1,2,0:T(8,128)S(1)}, f32[2,36,2,256]{3,1,2,0:T(8,128)S(1)}, u32[]{:S(2)}, u32[]{:S(2)}) collective-permute-start(f32[2,36,2,256]{3,1,2,0:T(8,128)S(1)} %get-tuple-element.25), channel_id=1, source_target_pairs={{0,2},{2,4},{4,6},{1,3},{3,5},{5,7},{8,10},{10,12},{12,14},{9,11},... | collective-permute-start | bytes 442376 | tf_op jit(solution)/shard_map/ppermute | solution.py:17
  76.9 2.7 %collective-permute-done.15 = f32[2,36,2,256]{3,1,2,0:T(8,128)S(1)} collective-permute-done((f32[2,36,2,256]{3,1,2,0:T(8,128)S(1)}, f32[2,36,2,256]{3,1,2,0:T(8,128)S(1)}, u32[]{:S(2)}, u32[]{:S(2)}) %collective-permute-start.15) | collective-permute-done | bytes 147488 | tf_op jit(solution)/shard_map/ppermute | solution.py:19
  84.1 4.2 %collective-permute-done.17 = f32[2,2,8,256]{3,1,2,0:T(2,128)S(1)} collective-permute-done((f32[2,2,8,256]{3,1,2,0:T(2,128)S(1)}, f32[2,2,8,256]{3,1,2,0:T(2,128)S(1)}, u32[]{:S(2)}, u32[]{:S(2)}) %collective-permute-start.17) | collective-permute-done | bytes 32800 | tf_op jit(solution)/shard_map/ppermute | solution.py:19
  88.3 4.3 %collective-permute-start.18 = (f32[2,36,2,256]{3,1,2,0:T(8,128)S(1)}, f32[2,36,2,256]{3,1,2,0:T(8,128)S(1)}, u32[]{:S(2)}, u32[]{:S(2)}) collective-permute-start(f32[2,36,2,256]{3,1,2,0:T(8,128)S(1)} %get-tuple-element.21), channel_id=1, source_target_pairs={{0,2},{2,4},{4,6},{1,3},{3,5},{5,7},{8,10},{10,12},{12,14},{9,11},... | collective-permute-start | bytes 442376 | tf_op jit(solution)/shard_map/ppermute | solution.py:17
  101.2 4.2 %collective-permute-done.21 = f32[2,2,8,256]{3,1,2,0:T(2,128)S(1)} collective-permute-done((f32[2,2,8,256]{3,1,2,0:T(2,128)S(1)}, f32[2,2,8,256]{3,1,2,0:T(2,128)S(1)}, u32[]{:S(2)}, u32[]{:S(2)}) %collective-permute-start.21) | collective-permute-done | bytes 32800 | tf_op jit(solution)/shard_map/ppermute | solution.py:19
  105.4 4.3 %collective-permute-start.22 = (f32[2,36,2,256]{3,1,2,0:T(8,128)S(1)}, f32[2,36,2,256]{3,1,2,0:T(8,128)S(1)}, u32[]{:S(2)}, u32[]{:S(2)}) collective-permute-start(f32[2,36,2,256]{3,1,2,0:T(8,128)S(1)} %get-tuple-element.17), channel_id=1, source_target_pairs={{0,2},{2,4},{4,6},{1,3},{3,5},{5,7},{8,10},{10,12},{12,14},{9,11},... | collective-permute-start | bytes 442376 | tf_op jit(solution)/shard_map/ppermute | solution.py:17
  118.3 4.2 %collective-permute-done.25 = f32[2,2,8,256]{3,1,2,0:T(2,128)S(1)} collective-permute-done((f32[2,2,8,256]{3,1,2,0:T(2,128)S(1)}, f32[2,2,8,256]{3,1,2,0:T(2,128)S(1)}, u32[]{:S(2)}, u32[]{:S(2)}) %collective-permute-start.25) | collective-permute-done | bytes 32800 | tf_op jit(solution)/shard_map/ppermute | solution.py:19
  122.5 4.3 %collective-permute-start.26 = (f32[2,36,2,256]{3,1,2,0:T(8,128)S(1)}, f32[2,36,2,256]{3,1,2,0:T(8,128)S(1)}, u32[]{:S(2)}, u32[]{:S(2)}) collective-permute-start(f32[2,36,2,256]{3,1,2,0:T(8,128)S(1)} %get-tuple-element.13), channel_id=1, source_target_pairs={{0,2},{2,4},{4,6},{1,3},{3,5},{5,7},{8,10},{10,12},{12,14},{9,11},... | collective-permute-start | bytes 442376 | tf_op jit(solution)/shard_map/ppermute | solution.py:17
  135.4 4.2 %collective-permute-done.29 = f32[2,2,8,256]{3,1,2,0:T(2,128)S(1)} collective-permute-done((f32[2,2,8,256]{3,1,2,0:T(2,128)S(1)}, f32[2,2,8,256]{3,1,2,0:T(2,128)S(1)}, u32[]{:S(2)}, u32[]{:S(2)}) %collective-permute-start.29) | collective-permute-done | bytes 32800 | tf_op jit(solution)/shard_map/ppermute | solution.py:19
  139.6 4.3 %collective-permute-start.30 = (f32[2,36,2,256]{3,1,2,0:T(8,128)S(1)}, f32[2,36,2,256]{3,1,2,0:T(8,128)S(1)}, u32[]{:S(2)}, u32[]{:S(2)}) collective-permute-start(f32[2,36,2,256]{3,1,2,0:T(8,128)S(1)} %get-tuple-element.9), channel_id=1, source_target_pairs={{0,2},{2,4},{4,6},{1,3},{3,5},{5,7},{8,10},{10,12},{12,14},{9,11},... | collective-permute-start | bytes 442376 | tf_op jit(solution)/shard_map/ppermute | solution.py:17
  150.1 22.2 %all-gather.2.cloned.1.call-done = f32[4,32,8,256]{3,2,1,0:T(8,128)} async-done(((f32[2,32,8,256]{3,2,1,0:T(8,128)}), f32[4,32,8,256]{3,2,1,0:T(8,128)}) %all-gather.2.cloned.1.call-update) | async-done | bytes 1048592 | tf_op jit(solution)/shard_map/all_gather | solution.py:66
  172.3 7.2 %convolution_bitcast_fusion = f32[4,4]{1,0:T(4,128)S(1)} fusion(f32[4,32,8,256]{3,2,1,0:T(8,128)} %all-gather.2.cloned.1.call-done), kind=kOutput, calls=%fused_computation | convolution fusion | flops 12582912 | bytes 1048640 | tf_op jit(solution)/shard_map/dot_general | solution.py:70
  179.4 33.2 %psum.7 = f32[4,4]{1,0:T(4,128)S(1)} all-reduce(f32[4,4]{1,0:T(4,128)S(1)} %convolution_bitcast_fusion), channel_id=1, replica_groups=mesh['gx'=4,'gy'=4,'band'=2] {'gx','gy'}, use_global_device_ids=true, to_apply=%region_0.1 | all-reduce | flops 16 | bytes 128 | tf_op jit(solution)/shard_map/psum | solution.py:73
  (106 shorter events, 64.2 us)
Async XLA Ops:
  6.5 165.7 %all-gather.2.cloned.1.call-start = ((), (), s32[]{:S(2)}) async-start(), calls=%async_computation | async-start | bytes 1572864 | tf_op jit(solution)/shard_map/all_gather | solution.py:66
  7.8 6.5 %collective-permute-start = (f32[2,2,8,256]{3,1,2,0:T(2,128)S(1)}, f32[2,2,8,256]{3,1,2,0:T(2,128)S(1)}, u32[]{:S(2)}, u32[]{:S(2)}) collective-permute-start(f32[2,2,8,256]{3,1,2,0:T(2,128)S(1)} %get-tuple-element.55), channel_id=1, source_target_pairs={{0,8},{8,16},{16,24},{1,9},{9,17},{17,25},{2,10},{10,18},{18,26},{... | collective-permute-start | bytes 98312 | tf_op jit(solution)/shard_map/ppermute | solution.py:17
  12.7 5.9 %collective-permute-start.1 = (f32[2,2,8,256]{3,1,2,0:T(2,128)S(1)}, f32[2,2,8,256]{3,1,2,0:T(2,128)S(1)}, u32[]{:S(2)}, u32[]{:S(2)}) collective-permute-start(f32[2,2,8,256]{3,1,2,0:T(2,128)S(1)} %get-tuple-element.56), channel_id=1, source_target_pairs={{8,0},{16,8},{24,16},{9,1},{17,9},{25,17},{10,2},{18,10},{26,18},{... | collective-permute-start | bytes 98312 | tf_op jit(solution)/shard_map/ppermute | solution.py:19
  20.0 5.0 %collective-permute-start.3 = (f32[2,36,2,256]{3,1,2,0:T(8,128)S(1)}, f32[2,36,2,256]{3,1,2,0:T(8,128)S(1)}, u32[]{:S(2)}, u32[]{:S(2)}) collective-permute-start(f32[2,36,2,256]{3,1,2,0:T(8,128)S(1)} %get-tuple-element.38), channel_id=1, source_target_pairs={{2,0},{4,2},{6,4},{3,1},{5,3},{7,5},{10,8},{12,10},{14,12},{11,9},... | collective-permute-start | bytes 442376 | tf_op jit(solution)/shard_map/ppermute | solution.py:19
  26.0 5.1 %collective-permute-start.4 = (f32[2,2,8,256]{3,1,2,0:T(2,128)S(1)}, f32[2,2,8,256]{3,1,2,0:T(2,128)S(1)}, u32[]{:S(2)}, u32[]{:S(2)}) collective-permute-start(f32[2,2,8,256]{3,1,2,0:T(2,128)S(1)} %get-tuple-element.51), channel_id=1, source_target_pairs={{0,8},{8,16},{16,24},{1,9},{9,17},{17,25},{2,10},{10,18},{18,26},{... | collective-permute-start | bytes 98312 | tf_op jit(solution)/shard_map/ppermute | solution.py:17
  29.5 5.8 %collective-permute-start.5 = (f32[2,2,8,256]{3,1,2,0:T(2,128)S(1)}, f32[2,2,8,256]{3,1,2,0:T(2,128)S(1)}, u32[]{:S(2)}, u32[]{:S(2)}) collective-permute-start(f32[2,2,8,256]{3,1,2,0:T(2,128)S(1)} %get-tuple-element.52), channel_id=1, source_target_pairs={{8,0},{16,8},{24,16},{9,1},{17,9},{25,17},{10,2},{18,10},{26,18},{... | collective-permute-start | bytes 98312 | tf_op jit(solution)/shard_map/ppermute | solution.py:19
  35.3 5.7 %collective-permute-start.6 = (f32[2,36,2,256]{3,1,2,0:T(8,128)S(1)}, f32[2,36,2,256]{3,1,2,0:T(8,128)S(1)}, u32[]{:S(2)}, u32[]{:S(2)}) collective-permute-start(f32[2,36,2,256]{3,1,2,0:T(8,128)S(1)} %get-tuple-element.33), channel_id=1, source_target_pairs={{0,2},{2,4},{4,6},{1,3},{3,5},{5,7},{8,10},{10,12},{12,14},{9,11},... | collective-permute-start | bytes 442376 | tf_op jit(solution)/shard_map/ppermute | solution.py:17
  39.7 4.1 %collective-permute-start.7 = (f32[2,36,2,256]{3,1,2,0:T(8,128)S(1)}, f32[2,36,2,256]{3,1,2,0:T(8,128)S(1)}, u32[]{:S(2)}, u32[]{:S(2)}) collective-permute-start(f32[2,36,2,256]{3,1,2,0:T(8,128)S(1)} %get-tuple-element.34), channel_id=1, source_target_pairs={{2,0},{4,2},{6,4},{3,1},{5,3},{7,5},{10,8},{12,10},{14,12},{11,9},... | collective-permute-start | bytes 442376 | tf_op jit(solution)/shard_map/ppermute | solution.py:19
  44.7 5.1 %collective-permute-start.8 = (f32[2,2,8,256]{3,1,2,0:T(2,128)S(1)}, f32[2,2,8,256]{3,1,2,0:T(2,128)S(1)}, u32[]{:S(2)}, u32[]{:S(2)}) collective-permute-start(f32[2,2,8,256]{3,1,2,0:T(2,128)S(1)} %get-tuple-element.49), channel_id=1, source_target_pairs={{0,8},{8,16},{16,24},{1,9},{9,17},{17,25},{2,10},{10,18},{18,26},{... | collective-permute-start | bytes 98312 | tf_op jit(solution)/shard_map/ppermute | solution.py:17
  48.2 5.8 %collective-permute-start.9 = (f32[2,2,8,256]{3,1,2,0:T(2,128)S(1)}, f32[2,2,8,256]{3,1,2,0:T(2,128)S(1)}, u32[]{:S(2)}, u32[]{:S(2)}) collective-permute-start(f32[2,2,8,256]{3,1,2,0:T(2,128)S(1)} %get-tuple-element.50), channel_id=1, source_target_pairs={{8,0},{16,8},{24,16},{9,1},{17,9},{25,17},{10,2},{18,10},{26,18},{... | collective-permute-start | bytes 98312 | tf_op jit(solution)/shard_map/ppermute | solution.py:19
  54.1 5.6 %collective-permute-start.10 = (f32[2,36,2,256]{3,1,2,0:T(8,128)S(1)}, f32[2,36,2,256]{3,1,2,0:T(8,128)S(1)}, u32[]{:S(2)}, u32[]{:S(2)}) collective-permute-start(f32[2,36,2,256]{3,1,2,0:T(8,128)S(1)} %get-tuple-element.29), channel_id=1, source_target_pairs={{0,2},{2,4},{4,6},{1,3},{3,5},{5,7},{8,10},{10,12},{12,14},{9,11},... | collective-permute-start | bytes 442376 | tf_op jit(solution)/shard_map/ppermute | solution.py:17
  58.4 4.1 %collective-permute-start.11 = (f32[2,36,2,256]{3,1,2,0:T(8,128)S(1)}, f32[2,36,2,256]{3,1,2,0:T(8,128)S(1)}, u32[]{:S(2)}, u32[]{:S(2)}) collective-permute-start(f32[2,36,2,256]{3,1,2,0:T(8,128)S(1)} %get-tuple-element.30), channel_id=1, source_target_pairs={{2,0},{4,2},{6,4},{3,1},{5,3},{7,5},{10,8},{12,10},{14,12},{11,9},... | collective-permute-start | bytes 442376 | tf_op jit(solution)/shard_map/ppermute | solution.py:19
  65.4 5.8 %collective-permute-start.13 = (f32[2,2,8,256]{3,1,2,0:T(2,128)S(1)}, f32[2,2,8,256]{3,1,2,0:T(2,128)S(1)}, u32[]{:S(2)}, u32[]{:S(2)}) collective-permute-start(f32[2,2,8,256]{3,1,2,0:T(2,128)S(1)} %get-tuple-element.48), channel_id=1, source_target_pairs={{8,0},{16,8},{24,16},{9,1},{17,9},{25,17},{10,2},{18,10},{26,18},{... | collective-permute-start | bytes 98312 | tf_op jit(solution)/shard_map/ppermute | solution.py:19
  71.2 5.6 %collective-permute-start.14 = (f32[2,36,2,256]{3,1,2,0:T(8,128)S(1)}, f32[2,36,2,256]{3,1,2,0:T(8,128)S(1)}, u32[]{:S(2)}, u32[]{:S(2)}) collective-permute-start(f32[2,36,2,256]{3,1,2,0:T(8,128)S(1)} %get-tuple-element.25), channel_id=1, source_target_pairs={{0,2},{2,4},{4,6},{1,3},{3,5},{5,7},{8,10},{10,12},{12,14},{9,11},... | collective-permute-start | bytes 442376 | tf_op jit(solution)/shard_map/ppermute | solution.py:17
  75.6 4.1 %collective-permute-start.15 = (f32[2,36,2,256]{3,1,2,0:T(8,128)S(1)}, f32[2,36,2,256]{3,1,2,0:T(8,128)S(1)}, u32[]{:S(2)}, u32[]{:S(2)}) collective-permute-start(f32[2,36,2,256]{3,1,2,0:T(8,128)S(1)} %get-tuple-element.26), channel_id=1, source_target_pairs={{2,0},{4,2},{6,4},{3,1},{5,3},{7,5},{10,8},{12,10},{14,12},{11,9},... | collective-permute-start | bytes 442376 | tf_op jit(solution)/shard_map/ppermute | solution.py:19
  82.5 5.8 %collective-permute-start.17 = (f32[2,2,8,256]{3,1,2,0:T(2,128)S(1)}, f32[2,2,8,256]{3,1,2,0:T(2,128)S(1)}, u32[]{:S(2)}, u32[]{:S(2)}) collective-permute-start(f32[2,2,8,256]{3,1,2,0:T(2,128)S(1)} %get-tuple-element.46), channel_id=1, source_target_pairs={{8,0},{16,8},{24,16},{9,1},{17,9},{25,17},{10,2},{18,10},{26,18},{... | collective-permute-start | bytes 98312 | tf_op jit(solution)/shard_map/ppermute | solution.py:19
  88.3 5.6 %collective-permute-start.18 = (f32[2,36,2,256]{3,1,2,0:T(8,128)S(1)}, f32[2,36,2,256]{3,1,2,0:T(8,128)S(1)}, u32[]{:S(2)}, u32[]{:S(2)}) collective-permute-start(f32[2,36,2,256]{3,1,2,0:T(8,128)S(1)} %get-tuple-element.21), channel_id=1, source_target_pairs={{0,2},{2,4},{4,6},{1,3},{3,5},{5,7},{8,10},{10,12},{12,14},{9,11},... | collective-permute-start | bytes 442376 | tf_op jit(solution)/shard_map/ppermute | solution.py:17
  99.6 5.8 %collective-permute-start.21 = (f32[2,2,8,256]{3,1,2,0:T(2,128)S(1)}, f32[2,2,8,256]{3,1,2,0:T(2,128)S(1)}, u32[]{:S(2)}, u32[]{:S(2)}) collective-permute-start(f32[2,2,8,256]{3,1,2,0:T(2,128)S(1)} %get-tuple-element.44), channel_id=1, source_target_pairs={{8,0},{16,8},{24,16},{9,1},{17,9},{25,17},{10,2},{18,10},{26,18},{... | collective-permute-start | bytes 98312 | tf_op jit(solution)/shard_map/ppermute | solution.py:19
  105.4 5.6 %collective-permute-start.22 = (f32[2,36,2,256]{3,1,2,0:T(8,128)S(1)}, f32[2,36,2,256]{3,1,2,0:T(8,128)S(1)}, u32[]{:S(2)}, u32[]{:S(2)}) collective-permute-start(f32[2,36,2,256]{3,1,2,0:T(8,128)S(1)} %get-tuple-element.17), channel_id=1, source_target_pairs={{0,2},{2,4},{4,6},{1,3},{3,5},{5,7},{8,10},{10,12},{12,14},{9,11},... | collective-permute-start | bytes 442376 | tf_op jit(solution)/shard_map/ppermute | solution.py:17
  109.8 4.1 %collective-permute-start.23 = (f32[2,36,2,256]{3,1,2,0:T(8,128)S(1)}, f32[2,36,2,256]{3,1,2,0:T(8,128)S(1)}, u32[]{:S(2)}, u32[]{:S(2)}) collective-permute-start(f32[2,36,2,256]{3,1,2,0:T(8,128)S(1)} %get-tuple-element.18), channel_id=1, source_target_pairs={{2,0},{4,2},{6,4},{3,1},{5,3},{7,5},{10,8},{12,10},{14,12},{11,9},... | collective-permute-start | bytes 442376 | tf_op jit(solution)/shard_map/ppermute | solution.py:19
  116.7 5.8 %collective-permute-start.25 = (f32[2,2,8,256]{3,1,2,0:T(2,128)S(1)}, f32[2,2,8,256]{3,1,2,0:T(2,128)S(1)}, u32[]{:S(2)}, u32[]{:S(2)}) collective-permute-start(f32[2,2,8,256]{3,1,2,0:T(2,128)S(1)} %get-tuple-element.42), channel_id=1, source_target_pairs={{8,0},{16,8},{24,16},{9,1},{17,9},{25,17},{10,2},{18,10},{26,18},{... | collective-permute-start | bytes 98312 | tf_op jit(solution)/shard_map/ppermute | solution.py:19
  122.5 5.6 %collective-permute-start.26 = (f32[2,36,2,256]{3,1,2,0:T(8,128)S(1)}, f32[2,36,2,256]{3,1,2,0:T(8,128)S(1)}, u32[]{:S(2)}, u32[]{:S(2)}) collective-permute-start(f32[2,36,2,256]{3,1,2,0:T(8,128)S(1)} %get-tuple-element.13), channel_id=1, source_target_pairs={{0,2},{2,4},{4,6},{1,3},{3,5},{5,7},{8,10},{10,12},{12,14},{9,11},... | collective-permute-start | bytes 442376 | tf_op jit(solution)/shard_map/ppermute | solution.py:17
  133.8 5.8 %collective-permute-start.29 = (f32[2,2,8,256]{3,1,2,0:T(2,128)S(1)}, f32[2,2,8,256]{3,1,2,0:T(2,128)S(1)}, u32[]{:S(2)}, u32[]{:S(2)}) collective-permute-start(f32[2,2,8,256]{3,1,2,0:T(2,128)S(1)} %get-tuple-element.40), channel_id=1, source_target_pairs={{8,0},{16,8},{24,16},{9,1},{17,9},{25,17},{10,2},{18,10},{26,18},{... | collective-permute-start | bytes 98312 | tf_op jit(solution)/shard_map/ppermute | solution.py:19
  139.6 5.8 %collective-permute-start.30 = (f32[2,36,2,256]{3,1,2,0:T(8,128)S(1)}, f32[2,36,2,256]{3,1,2,0:T(8,128)S(1)}, u32[]{:S(2)}, u32[]{:S(2)}) collective-permute-start(f32[2,36,2,256]{3,1,2,0:T(8,128)S(1)} %get-tuple-element.9), channel_id=1, source_target_pairs={{0,2},{2,4},{4,6},{1,3},{3,5},{5,7},{8,10},{10,12},{12,14},{9,11},... | collective-permute-start | bytes 442376 | tf_op jit(solution)/shard_map/ppermute | solution.py:17
  (13 other events, 120.6 us)
Sparse Core Ops, SparseCore 0:
  150.2 22.0 all-gather.1
where the time goes:
time: 227 us; the launch traced here: 226 us
  waiting for transfers between devices  80.8 us (36%)
  starting transfers between devices  74.1 us (33%)
  blocking collectives  33.2 us (15%)
  between operations  14 us (6%)
  matrix products  9.98 us (4%)
  other arithmetic  9.58 us (4%)
  local copies, waits for them, and re-layouts  4.35 us (2%)
    ppermute x16, waiting for transfers between devices, extended_2(): lax.ppermute(head, axis, [((i + 1) % count, i) for i in range(ends)])  56.4 us
    ppermute x16, starting transfers between devices, extended_2(): lax.ppermute(tail, axis, [(i, (i + 1) % count) for i in range(ends)])  53.1 us
    psum x1, blocking collectives, per_device(): correlation = lax.psum(partial_value, ('gx', 'gy')) / cell_total  33.2 us
    all_gather x1, waiting for transfers between devices, per_device(): gathered = lax.all_gather(current, 'band', axis=0, tiled=True)  22.2 us
    ppermute x16, starting transfers between devices, extended_2(): lax.ppermute(head, axis, [((i + 1) % count, i) for i in range(ends)])  21 us
    dot_general x1, matrix products, per_device(): jnp.dot(flattened, flattened.T, precision=lax.Precision.HIGHEST, preferre...  7.16 us
    sub x7, other arithmetic, per_device(): following = 2.0 * shallow_step(current, potential) - previous  5.28 us
  transfers between devices with their start and end apart: 33, of which 25 were waited for; matrix products, arithmetic and copies ran while one was open for 0% of the time, Pallas kernels for 0%

commit v1 on v0

v1 whole, which is shorter than its diff:
```python
import functools

import jax
import jax.numpy as jnp
from jax import lax
from jax.experimental import pallas as pl
from jax.experimental.pallas import tpu as pltpu
from jax.sharding import PartitionSpec as P

STEPS = 4
HALO = 2 * STEPS
PAD = 8
LANES = 128
PLANES = 4
NEAR = -(2.0 / 3.0) / 4.25
FAR = (1.0 / 24.0) / 4.25
VMEM = pl.BlockSpec(memory_space=pltpu.VMEM)
SMEM = pl.BlockSpec(memory_space=pltpu.SMEM)
PARAMS = pltpu.CompilerParams(vmem_limit_bytes=40 * 1024 * 1024)


def struct(*shape):
    return jax.ShapeDtypeStruct(shape, jnp.float32)


def place():
    along_y = lax.axis_index("gy")
    return along_y % 2, along_y // 2, lax.axis_index("gx")


def one_sided():
    return lax.axis_size("gy") == 4


def tile_count():
    return 3 if one_sided() else 4


def own_slots(core, chip):
    first = chip if one_sided() else 1
    return first + core, first + 1 - core


def halo_slots(chip):
    return [2 - 2 * chip] if one_sided() else [0, 3]


def rows_of(slot):
    return pl.ds(pl.multiple_of(PAD + 8 * slot, 8), 8)


def fill(window, tiles, x_left, x_right, y_halos, corners, core, chip, change=lambda a: a):
    width = tiles[0].shape[0]
    for half in range(2):
        lanes = slice(half * LANES, (half + 1) * LANES)
        for index, slot in enumerate(own_slots(core, chip)):
            rows = rows_of(slot)
            window[half, HALO : HALO + width, rows, :] = change(tiles[index][:, :, lanes])
            window[half, :HALO, rows, :] = change(x_left[index, :, :, lanes])
            window[half, HALO + width :, rows, :] = change(x_right[index, :, :, lanes])
        for slot, middle, (left, right) in zip(halo_slots(chip), y_halos, corners):
            rows = rows_of(slot)
            window[half, HALO : HALO + width, rows, :] = change(middle[:, :, lanes])
            window[half, :HALO, rows, :] = change(left[:, :, lanes])
            window[half, HALO + width :, rows, :] = change(right[:, :, lanes])


def z_matrix(depth):
    gap = jnp.abs(
        lax.broadcasted_iota(jnp.int32, (depth, depth), 0)
        - lax.broadcasted_iota(jnp.int32, (depth, depth), 1)
    )
    return jnp.where(gap == 1, -16.0, jnp.where(gap == 2, 1.0, 0.0)).astype(jnp.bfloat16)


def stencil(source, target, local, x, along_z, first):
    height = source.shape[2] - 2 * PAD
    body = slice(PAD, PAD + height)
    now = pl.ds(x, PLANES)
    values = [source[half, now, body, :] for half in range(2)]
    high = [v.astype(jnp.bfloat16) for v in values]
    low = [(v - h.astype(jnp.float32)).astype(jnp.bfloat16) for v, h in zip(values, high)]

    def joined(parts):
        return jnp.concatenate([p.reshape(PLANES * height, LANES) for p in parts], axis=1)

    z_sum = jnp.dot(joined(high), along_z, preferred_element_type=jnp.float32)
    z_sum = z_sum + jnp.dot(joined(low), along_z, preferred_element_type=jnp.float32)
    scale = 1.0 if first else 2.0
    for half in range(2):
        near = source[half, pl.ds(x - 1, PLANES), body, :] + source[half, pl.ds(x + 1, PLANES), body, :]
        near = near + source[half, now, PAD - 1 : PAD - 1 + height, :]
        near = near + source[half, now, PAD + 1 : PAD + 1 + height, :]
        far = source[half, pl.ds(x - 2, PLANES), body, :] + source[half, pl.ds(x + 2, PLANES), body, :]
        far = far + source[half, now, PAD - 2 : PAD - 2 + height, :]
        far = far + source[half, now, PAD + 2 : PAD + 2 + height, :]
        far = far + z_sum[:, half * LANES : (half + 1) * LANES].reshape(PLANES, height, LANES)
        result = local[half, now, body, :] * values[half] * scale
        result = result + near * (NEAR * scale) + far * (FAR * scale)
        if not first:
            result = result - target[half, now, body, :]
        target[half, now, body, :] = result


def four_steps(a, b, local, along_z, chip, along_x):
    extent = a.shape[1]
    height = a.shape[2] - 2 * PAD
    for buffer in (a, b):
        for rows in (slice(0, PAD), slice(PAD + height, PAD + height + PAD)):
            buffer[:, :, rows, :] = jnp.zeros((2, extent, PAD, LANES), jnp.float32)
    buffers = (a, b)
    for step in range(STEPS):
        source, target = buffers[step % 2], buffers[(step + 1) % 2]
        low = 2 * (step + 1)
        blocks = (extent - 2 * low) // PLANES

        def block(index, carry, source=source, target=target, low=low, step=step):
            stencil(source, target, local, low + index * PLANES, along_z, step == 0)
            return carry

        lax.fori_loop(0, blocks, block, 0, unroll=2)
        if step < STEPS - 1:
            @pl.when(along_x == 0)
            def _():
                target[:, :HALO] = jnp.zeros((2, HALO) + target.shape[2:], jnp.float32)

            @pl.when(along_x == lax.axis_size("gx") - 1)
            def _():
                target[:, extent - HALO :] = jnp.zeros((2, HALO) + target.shape[2:], jnp.float32)

            if not one_sided():
                zero = jnp.zeros((2, extent, 8, LANES), jnp.float32)

                @pl.when(chip == 0)
                def _():
                    target[:, :, PAD : PAD + 8, :] = zero

                @pl.when(chip == lax.axis_size("gy") // 2 - 1)
                def _():
                    target[:, :, PAD + 24 : PAD + 32, :] = zero


def edge_flags(core, chip):
    if one_sided():
        return [core == 1 - chip]
    return [core == 1, core == 0]


def pack_kernel(orbitals, received, potential, received_potential, y_out, left_out, right_out, *d_out):
    core, chip, _ = place()
    width = potential.shape[0]
    fields = ((orbitals.at[core], received), (potential, received_potential))
    for f, (own, other) in enumerate(fields):
        for t, tile in enumerate((own, other)):
            left_out[f, t] = tile[:HALO]
            right_out[f, t] = tile[width - HALO :]
        for k, flag in enumerate(edge_flags(core, chip)):
            for chosen, tile in ((flag, own), (jnp.logical_not(flag), other)):

                @pl.when(chosen)
                def _(tile=tile, k=k, f=f):
                    y_out[k, f] = tile[...]
                    d_out[2 * k][f] = tile[:HALO]
                    d_out[2 * k + 1][f] = tile[width - HALO :]


def first_kernel(count, *refs):
    orbitals, received, potential, received_potential, x_left, x_right = refs[:6]
    y_halos = refs[6 : 6 + count]
    corners = refs[6 + count : 6 + 3 * count]
    own_out, other_out, y_out, left_out, right_out = refs[6 + 3 * count : 11 + 3 * count]
    d_out = refs[11 + 3 * count : 11 + 5 * count]
    a, b, local = refs[11 + 5 * count :]
    core, chip, along_x = place()
    width, depth = potential.shape[0], potential.shape[2]

    def pieces(f):
        return (
            x_left.at[f],
            x_right.at[f],
            [y.at[f] for y in y_halos],
            [(corners[2 * k].at[f], corners[2 * k + 1].at[f]) for k in range(count)],
        )

    fill(a, (orbitals.at[core], received), *pieces(0), core, chip)
    fill(local, (potential, received_potential), *pieces(1), core, chip, lambda v: (v - 0.5) / 4.25)
    four_steps(a, b, local, z_matrix(depth), chip, along_x)
    outs = (own_out, other_out)
    for t, slot in enumerate(own_slots(core, chip)):
        for half in range(2):
            lanes = slice(half * LANES, (half + 1) * LANES)
            tile = a[half, HALO : HALO + width, rows_of(slot), :]
            outs[t][:, :, lanes] = tile
            left_out[t, :, :, lanes] = tile[:HALO]
            right_out[t, :, :, lanes] = tile[width - HALO :]
    for k, flag in enumerate(edge_flags(core, chip)):
        own_slot, other_slot = own_slots(core, chip)
        slot = jnp.where(flag, own_slot, other_slot)
        for half in range(2):
            lanes = slice(half * LANES, (half + 1) * LANES)
            tile = a[half, HALO : HALO + width, rows_of(slot), :]
            y_out[k, :, :, lanes] = tile
            d_out[2 * k][:, :, lanes] = tile[:HALO]
            d_out[2 * k + 1][:, :, lanes] = tile[width - HALO :]


def second_kernel(count, *refs):
    orbitals, received, potential, received_potential = refs[:4]
    own, other, x_left, x_right = refs[4:8]
    y_halos = refs[8 : 8 + count]
    corners = refs[8 + count : 8 + 3 * count]
    rest = refs[8 + 3 * count :]
    p_left, p_right = rest[:2]
    p_halos = rest[2 : 2 + count]
    p_corners = rest[2 + count : 2 + 3 * count]
    keep, give, a, b, local = rest[2 + 3 * count :]
    core, chip, along_x = place()
    width, depth = potential.shape[0], potential.shape[2]
    fill(
        a,
        (own, other),
        x_left,
        x_right,
        y_halos,
        [(corners[2 * k], corners[2 * k + 1]) for k in range(count)],
        core,
        chip,
    )
    fill(
        local,
        (potential, received_potential),
        p_left.at[1],
        p_right.at[1],
        [y.at[1] for y in p_halos],
        [(p_corners[2 * k].at[1], p_corners[2 * k + 1].at[1]) for k in range(count)],
        core,
        chip,
        lambda v: (v - 0.5) / 4.25,
    )
    four_steps(a, b, local, z_matrix(depth), chip, along_x)
    start = (orbitals.at[core], received)
    outs = (keep, give)
    for t, slot in enumerate(own_slots(core, chip)):
        for half in range(2):
            lanes = slice(half * LANES, (half + 1) * LANES)
            tile = a[half, HALO : HALO + width, rows_of(slot), :]
            outs[t][:, :, lanes] = 2.0 * tile - start[t][:, :, lanes]


def slot_orbitals(bands):
    core, _, _ = place()
    band = lax.axis_index("band")
    names = []
    for d in range(bands):
        group = lax.rem(band + bands - d, bands)
        names += [2 * group + core, 2 * group + 1 - core]
    return names


def correlation_kernel(bands, *refs):
    slots, out = refs[:-1], refs[-1]
    names = slot_orbitals(bands)
    row = lax.broadcasted_iota(jnp.int32, (8, LANES), 0)
    column = lax.broadcasted_iota(jnp.int32, (8, LANES), 1)
    count = len(slots)
    pairs = [(i, j) for i in range(count) for j in range(i, count)]
    width, height, depth = slots[0].shape

    def body(index, totals):
        planes = [s[pl.ds(index * PLANES, PLANES)] for s in slots]
        found = []
        for (i, j), total in zip(pairs, totals):
            product = jnp.sum(planes[i] * planes[j], axis=0)
            for half in range(depth // LANES):
                total = total + product[:, half * LANES : (half + 1) * LANES]
            found.append(total)
        return tuple(found)

    zero = jnp.zeros((height, LANES), jnp.float32)
    totals = lax.fori_loop(0, width // PLANES, body, (zero,) * len(pairs))
    result = jnp.zeros((8, LANES), jnp.float32)
    for (i, j), total in zip(pairs, totals):
        here = ((row == names[i]) & (column == names[j])) | ((row == names[j]) & (column == names[i]))
        result = jnp.where(here, jnp.sum(total), result)
    out[...] = result


def basis_kernel(bands, cells, *refs):
    correlation, order = refs[:2]
    slots = refs[2 : 2 + 2 * bands]
    out, mixing = refs[2 + 2 * bands :]
    names = slot_orbitals(bands)
    count = 2 * bands
    band = lax.axis_index("band")

    def splat(value):
        return jnp.full((8, LANES), value, jnp.float32)

    at = [order[p] for p in range(count)]
    mixing[...] = jnp.zeros_like(mixing)
    lower = {}
    inverse_diagonal = []
    for j in range(count):
        for i in range(j, count):
            total = splat(correlation[at[i], at[j]]) * (1.0 / cells)
            for k in range(j):
                total = total - lower[i, k] * lower[j, k]
            if i == j:
                diagonal = jnp.sqrt(total)
                inverse_diagonal.append(1.0 / diagonal)
            else:
                lower[i, j] = total * inverse_diagonal[j]
    inverse = {}
    for j in range(count):
        inverse[j, j] = inverse_diagonal[j]
        for i in range(j + 1, count):
            total = lower[i, j] * inverse[j, j]
            for k in range(j + 1, i):
                total = total + lower[i, k] * inverse[k, j]
            inverse[i, j] = -total * inverse_diagonal[i]
    for (i, j), value in inverse.items():
        mixing[at[i], at[j]] = value
    width, _, depth = slots[0].shape
    for r in range(2):
        factors = [mixing[2 * band + r, name] for name in names]

        def body(x, carry, r=r, factors=factors):
            for half in range(depth // LANES):
                lanes = slice(half * LANES, (half + 1) * LANES)
                total = factors[0] * slots[0][x, :, lanes]
                for factor, slot in zip(factors[1:], slots[1:]):
                    total = total + factor * slot[x, :, lanes]
                out[r, x, :, lanes] = total
            return carry

        lax.fori_loop(0, width, body, 0, unroll=4)


def moves(dx, dy_chip, swap=False):
    nx, ny = lax.axis_size("gx"), lax.axis_size("gy")
    pairs = []
    for x in range(nx):
        for y in range(ny):
            chip, core = y // 2, y % 2
            to_x = x + dx
            to_chip = 1 - chip if dy_chip == "flip" else chip + dy_chip
            to_core = 1 - core if swap else core
            if 0 <= to_x < nx and 0 <= to_chip < ny // 2:
                pairs.append((x * ny + y, to_x * ny + to_chip * 2 + to_core))
    return pairs


def send(value, dx, dy_chip, swap=False):
    return lax.ppermute(value, ("gx", "gy"), moves(dx, dy_chip, swap))


def y_steps():
    return ["flip"] if one_sided() else [1, -1]


def exchange(y_out, left_out, right_out, d_out):
    y_halos = [send(y_out[k], 0, step) for k, step in enumerate(y_steps())]
    corners = []
    for k, step in enumerate(y_steps()):
        corners += [send(d_out[2 * k + 1], 1, step), send(d_out[2 * k], -1, step)]
    x_left = send(right_out, 1, 0)
    x_right = send(left_out, -1, 0)
    return x_left, x_right, *y_halos, *corners


def summed(value, axis):
    count = lax.axis_size(axis)
    if count & (count - 1):
        return lax.psum(value, axis)
    step = 1
    while step < count:
        value = value + lax.ppermute(value, axis, [(i, i ^ step) for i in range(count)])
        step *= 2
    return value


def per_device(orbitals, potential, order):
    group, width, height, depth = orbitals.shape
    bands = lax.axis_size("band")
    cells = float(width * lax.axis_size("gx") * height * lax.axis_size("gy") * depth)
    count = len(y_steps())
    core, chip, _ = place()
    extent = width + 2 * HALO
    window = (2, extent, 8 * tile_count() + 2 * PAD, LANES)
    scratch = [pltpu.VMEM(window, jnp.float32)] * 3

    other = lax.dynamic_index_in_dim(orbitals, 1 - core, 0, keepdims=False)
    received = send(other, 0, 0, True)
    received_potential = send(potential, 0, 0, True)
    tile = (width, height, depth)
    ends = (2, HALO, height, depth)
    corner = (HALO, height, depth)
    packed = pl.pallas_call(
        pack_kernel,
        out_shape=[struct(count, 2, *tile), struct(2, *ends), struct(2, *ends)]
        + [struct(2, *corner)] * (2 * count),
        in_specs=[VMEM] * 4,
        out_specs=[VMEM] * (3 + 2 * count),
        compiler_params=PARAMS,
        name="pack",
    )(orbitals, received, potential, received_potential)
    halos = exchange(*packed[:3], packed[3:])
    first = pl.pallas_call(
        functools.partial(first_kernel, count),
        out_shape=[struct(*tile)] * 2
        + [struct(count, *tile), struct(*ends), struct(*ends)]
        + [struct(*corner)] * (2 * count),
        in_specs=[VMEM] * (6 + 3 * count),
        out_specs=[VMEM] * (5 + 2 * count),
        scratch_shapes=scratch,
        compiler_params=PARAMS,
        name="first_round",
    )(orbitals, received, potential, received_potential, *halos)
    own, sibling = first[:2]
    second_halos = exchange(*first[2:5], first[5:])
    keep, give = pl.pallas_call(
        functools.partial(second_kernel, count),
        out_shape=[struct(*tile)] * 2,
        in_specs=[VMEM] * (10 + 6 * count),
        out_specs=[VMEM] * 2,
        scratch_shapes=scratch,
        compiler_params=PARAMS,
        name="second_round",
    )(orbitals, received, potential, received_potential, own, sibling, *second_halos, *halos)

    slots = [keep, send(give, 0, 0, True)]
    for d in range(1, bands):
        same, crossed = [], []
        for y in range(lax.axis_size("gy")):
            for b in range(bands):
                to = (b + d) % bands
                same.append((y * bands + b, y * bands + to))
                crossed.append((y * bands + b, (y ^ 1) * bands + to))
        slots.append(lax.ppermute(keep, ("gy", "band"), same))
        slots.append(lax.ppermute(give, ("gy", "band"), crossed))
    partial_value = pl.pallas_call(
        functools.partial(correlation_kernel, bands),
        out_shape=struct(8, LANES),
        in_specs=[VMEM] * len(slots),
        out_specs=VMEM,
        compiler_params=PARAMS,
        name="correlation",
    )(*slots)
    correlation = summed(summed(partial_value, "gy"), "gx")
    return pl.pallas_call(
        functools.partial(basis_kernel, bands, cells),
        out_shape=struct(*orbitals.shape),
        in_specs=[SMEM, SMEM] + [VMEM] * len(slots),
        out_specs=VMEM,
        scratch_shapes=[pltpu.VMEM((2 * bands, 2 * bands, 8, LANES), jnp.float32)],
        compiler_params=PARAMS,
        name="basis",
    )(correlation, order, *slots)


def solution(mesh):
    in_specs = (P("band", "gx", "gy", None), P("gx", "gy", None), P())
    out_specs = P("band", "gx", "gy", None)
    return jax.shard_map(
        per_device, mesh=mesh, in_specs=in_specs, out_specs=out_specs, check_vma=False
    )
```

time: 227 us -> 82.9 us (0.37)
  waiting for transfers between devices: 80.8 us -> 34.7 us
  starting transfers between devices: 74.1 us -> 33.6 us
  blocking collectives: 33.2 us -> 0 us
  between operations: 14 us -> 0.13 us
  Pallas kernels: 0 us -> 12.2 us
  matrix products: 9.98 us -> 0 us
  other arithmetic: 9.58 us -> 0.01 us
  local copies, waits for them, and re-layouts: 4.35 us -> 2 us
    ppermute x32 -> x19, starting transfers between devices: 74.1 us -> 33.6 us  [the longest x13 28.8 us: send(): return lax.ppermute(value, ('gx', 'gy'), moves(dx, dy_chip, swap))]
    psum x1 -> x0, blocking collectives: 33.2 us -> none  [per_device(): correlation = lax.psum(partial_value, ('gx', 'gy')) / cell_total]
    ppermute x32 -> x19, waiting for transfers between devices: 58.6 us -> 34.7 us  [the longest x13 13.9 us: send(): return lax.ppermute(value, ('gx', 'gy'), moves(dx, dy_chip, swap))]
    all_gather x1 -> x0, waiting for transfers between devices: 22.2 us -> none  [per_device(): gathered = lax.all_gather(current, 'band', axis=0, tiled=True)]
    pallas_call x0 -> x5, Pallas kernels: none -> 12.2 us  [the longest x1 5.03 us: per_device(): pl.pallas_call(functools.partial(first_kernel, count), out_shape=[struct(...]
    dot_general x6 -> x0, matrix products: 9.8 us -> none  [the longest x1 7.16 us: per_device(): jnp.dot(flattened, flattened.T, precision=lax.Precision.HIGHEST, preferre...]
    sub x7 -> x0, other arithmetic: 5.28 us -> none  [per_device(): following = 2.0 * shallow_step(current, potential) - previous]
  transfers between devices with their start and end apart: 33 -> 19, of which waited for: 25 -> 12; matrix products, arithmetic and copies ran while one was open for 0% -> 0% of each run, Pallas kernels for 0% -> 0%
where the time goes in v1:
time: 82.9 us; the launch traced here: 82.6 us
  waiting for transfers between devices  34.7 us (42%)
  starting transfers between devices  33.6 us (41%)
  Pallas kernels  12.2 us (15%)
  local copies, waits for them, and re-layouts  2 us (2%)
    ppermute x13, starting transfers between devices, send(): return lax.ppermute(value, ('gx', 'gy'), moves(dx, dy_chip, swap))  28.8 us
    ppermute x13, waiting for transfers between devices, send(): return lax.ppermute(value, ('gx', 'gy'), moves(dx, dy_chip, swap))  13.9 us
    ppermute x4, waiting for transfers between devices, summed(): lax.ppermute(value, axis, [(i, i ^ step) for i in range(count)])  8.74 us
    ppermute x1, waiting for transfers between devices, per_device(): slots.append(lax.ppermute(give, ('gy', 'band'), crossed))  6.41 us
    ppermute x1, waiting for transfers between devices, per_device(): slots.append(lax.ppermute(keep, ('gy', 'band'), same))  5.67 us
    pallas_call x1, Pallas kernels, per_device(): pl.pallas_call(functools.partial(first_kernel, count), out_shape=[struct(...  5.03 us
    pallas_call x1, Pallas kernels, per_device(): pl.pallas_call(functools.partial(second_kernel, count), out_shape=[struct...  5.02 us
    ppermute x4, starting transfers between devices, summed(): lax.ppermute(value, axis, [(i, i ^ step) for i in range(count)])  4.21 us
  transfers between devices with their start and end apart: 19, of which 12 were waited for; matrix products, arithmetic and copies ran while one was open for 0% of the time, Pallas kernels for 0%

profile of v1, /device:TPU:0, one launch (start us, length us, event | category | flops | bytes accessed | tf_op | source)
XLA Modules:
  0.0 82.6 jit_solution(2809759980050379919)
XLA Ops:
  4.4 3.0 %collective-permute-start.4 = (f32[2,32,8,256]{3,2,1,0:T(8,128)S(1)}, f32[2,32,8,256]{3,2,1,0:T(8,128)S(1)}, u32[]{:S(2)}, u32[]{:S(2)}) collective-permute-start(f32[2,32,8,256]{3,2,1,0:T(8,128)S(1)} %bitcast.4), channel_id=1, source_target_pairs={{0,4},{2,6},{4,0},{6,2},{8,12},{10,14},{12,8},{14,10},{16,20},{18,... | collective-permute-start | bytes 1572872 | tf_op jit(solution)/shard_map/ppermute | solution.py:354
  7.3 3.5 %collective-permute-start.2 = (f32[2,2,8,8,256]{4,3,2,1,0:T(8,128)S(1)}, f32[2,2,8,8,256]{4,3,2,1,0:T(8,128)S(1)}, u32[]{:S(2)}, u32[]{:S(2)}) collective-permute-start(f32[2,2,8,8,256]{4,3,2,1,0:T(8,128)S(1)} %get-tuple-element.19), channel_id=1, source_target_pairs={{0,8},{2,10},{4,12},{6,14},{8,16},{10,18},{12,20},{14,22},{16,24},... | collective-permute-start | bytes 786440 | tf_op jit(solution)/shard_map/ppermute | solution.py:354
  10.8 1.3 %collective-permute-start.3 = (f32[2,2,8,8,256]{4,3,2,1,0:T(8,128)S(1)}, f32[2,2,8,8,256]{4,3,2,1,0:T(8,128)S(1)}, u32[]{:S(2)}, u32[]{:S(2)}) collective-permute-start(f32[2,2,8,8,256]{4,3,2,1,0:T(8,128)S(1)} %get-tuple-element.20), channel_id=1, source_target_pairs={{8,0},{10,2},{12,4},{14,6},{16,8},{18,10},{20,12},{22,14},{24,16},... | collective-permute-start | bytes 786440 | tf_op jit(solution)/shard_map/ppermute | solution.py:354
  12.1 4.5 %collective-permute-start.5 = (f32[2,8,8,256]{3,2,1,0:T(8,128)S(1)}, f32[2,8,8,256]{3,2,1,0:T(8,128)S(1)}, u32[]{:S(2)}, u32[]{:S(2)}) collective-permute-start(f32[2,8,8,256]{3,2,1,0:T(8,128)S(1)} %get-tuple-element.22), channel_id=1, source_target_pairs={{0,12},{2,14},{4,8},{6,10},{8,20},{10,22},{12,16},{14,18},{16,28},... | collective-permute-start | bytes 393224 | tf_op jit(solution)/shard_map/ppermute | solution.py:354
  16.6 1.3 %collective-permute-start.6 = (f32[2,8,8,256]{3,2,1,0:T(8,128)S(1)}, f32[2,8,8,256]{3,2,1,0:T(8,128)S(1)}, u32[]{:S(2)}, u32[]{:S(2)}) collective-permute-start(f32[2,8,8,256]{3,2,1,0:T(8,128)S(1)} %get-tuple-element.23), channel_id=1, source_target_pairs={{8,4},{10,6},{12,0},{14,2},{16,12},{18,14},{20,8},{22,10},{24,20},... | collective-permute-start | bytes 393224 | tf_op jit(solution)/shard_map/ppermute | solution.py:354
  17.9 1.3 %collective-permute-done.5.refs_7_.refs_14_ = f32[2,8,8,256]{3,2,1,0:T(8,128)S(1)} collective-permute-done((f32[2,8,8,256]{3,2,1,0:T(8,128)S(1)}, f32[2,8,8,256]{3,2,1,0:T(8,128)S(1)}, u32[]{:S(2)}, u32[]{:S(2)}) %collective-permute-start.5) | collective-permute-done | bytes 131104 | tf_op jit(solution)/shard_map/ppermute | solution.py:354
  19.2 5.2 %collective-permute-done.6.refs_8_.refs_15_ = f32[2,8,8,256]{3,2,1,0:T(8,128)S(1)} collective-permute-done((f32[2,8,8,256]{3,2,1,0:T(8,128)S(1)}, f32[2,8,8,256]{3,2,1,0:T(8,128)S(1)}, u32[]{:S(2)}, u32[]{:S(2)}) %collective-permute-start.6) | collective-permute-done | bytes 131104 | tf_op jit(solution)/shard_map/ppermute | solution.py:354
  24.4 5.0 %first_round.1 = (f32[32,8,256]{2,1,0:T(8,128)S(1)}, f32[32,8,256]{2,1,0:T(8,128)S(1)}, f32[1,32,8,256]{3,2,1,0:T(8,128)S(1)}, f32[2,8,8,256]{3,2,1,0:T(8,128)S(...) custom-call(f32[2,32,8,256]{3,2,1,0:T(8,128)S(1)} %copy-done, ...), custom_call_target="tpu_custom_call" | custom-call | tf_op jit(solution)/shard_map/first_round/pallas_call | solution.py:408
  29.4 1.6 %collective-permute-start.9 = (f32[32,8,256]{2,1,0:T(8,128)S(1)}, f32[32,8,256]{2,1,0:T(8,128)S(1)}, u32[]{:S(2)}, u32[]{:S(2)}) collective-permute-start(f32[32,8,256]{2,1,0:T(8,128)S(1)} %bitcast.5), channel_id=1, source_target_pairs={{0,4},{2,6},{4,0},{6,2},{8,12},{10,14},{12,8},{14,10},{16,20},{18,... | collective-permute-start | bytes 786440 | tf_op jit(solution)/shard_map/ppermute | solution.py:354
  31.0 4.4 %collective-permute-start.7 = (f32[2,8,8,256]{3,2,1,0:T(8,128)S(1)}, f32[2,8,8,256]{3,2,1,0:T(8,128)S(1)}, u32[]{:S(2)}, u32[]{:S(2)}) collective-permute-start(f32[2,8,8,256]{3,2,1,0:T(8,128)S(1)} %get-tuple-element.26), channel_id=1, source_target_pairs={{0,8},{2,10},{4,12},{6,14},{8,16},{10,18},{12,20},{14,22},{16,24},... | collective-permute-start | bytes 393224 | tf_op jit(solution)/shard_map/ppermute | solution.py:354
  35.4 1.3 %collective-permute-start.8 = (f32[2,8,8,256]{3,2,1,0:T(8,128)S(1)}, f32[2,8,8,256]{3,2,1,0:T(8,128)S(1)}, u32[]{:S(2)}, u32[]{:S(2)}) collective-permute-start(f32[2,8,8,256]{3,2,1,0:T(8,128)S(1)} %get-tuple-element.27), channel_id=1, source_target_pairs={{8,0},{10,2},{12,4},{14,6},{16,8},{18,10},{20,12},{22,14},{24,16},... | collective-permute-start | bytes 393224 | tf_op jit(solution)/shard_map/ppermute | solution.py:354
  36.7 4.5 %collective-permute-start.10 = (f32[8,8,256]{2,1,0:T(8,128)S(1)}, f32[8,8,256]{2,1,0:T(8,128)S(1)}, u32[]{:S(2)}, u32[]{:S(2)}) collective-permute-start(f32[8,8,256]{2,1,0:T(8,128)S(1)} %get-tuple-element.29), channel_id=1, source_target_pairs={{0,12},{2,14},{4,8},{6,10},{8,20},{10,22},{12,16},{14,18},{16,28},... | collective-permute-start | bytes 196616 | tf_op jit(solution)/shard_map/ppermute | solution.py:354
  41.2 1.3 %collective-permute-start.11 = (f32[8,8,256]{2,1,0:T(8,128)S(1)}, f32[8,8,256]{2,1,0:T(8,128)S(1)}, u32[]{:S(2)}, u32[]{:S(2)}) collective-permute-start(f32[8,8,256]{2,1,0:T(8,128)S(1)} %get-tuple-element.30), channel_id=1, source_target_pairs={{8,4},{10,6},{12,0},{14,2},{16,12},{18,14},{20,8},{22,10},{24,20},... | collective-permute-start | bytes 196616 | tf_op jit(solution)/shard_map/ppermute | solution.py:354
  43.1 5.2 %collective-permute-done.11.refs_10_ = f32[8,8,256]{2,1,0:T(8,128)S(1)} collective-permute-done((f32[8,8,256]{2,1,0:T(8,128)S(1)}, f32[8,8,256]{2,1,0:T(8,128)S(1)}, u32[]{:S(2)}, u32[]{:S(2)}) %collective-permute-start.11) | collective-permute-done | bytes 65568 | tf_op jit(solution)/shard_map/ppermute | solution.py:354
  48.3 5.0 %second_round.1 = (f32[32,8,256]{2,1,0:T(8,128)S(1)}, f32[32,8,256]{2,1,0:T(8,128)S(1)}) custom-call(f32[2,32,8,256]{3,2,1,0:T(8,128)S(1)} %copy-done, f32[32,8,256]{2,1,0:T(8,128)S(1)} %collective-permute-done.received.refs_1_, f32[32,8,256]{2,1,0:T(8,128)S(1)} %copy-done.1, f32[32,8,256]{2,1,0:T(8,128)S(1)} %collective-permute-done.1.received_potential.refs_3_, ...), custom_call_target="tpu_custom_call" | custom-call | tf_op jit(solution)/shard_map/second_round/pallas_call | solution.py:421
  53.4 1.6 %collective-permute-start.12 = (f32[32,8,256]{2,1,0:T(8,128)S(1)}, f32[32,8,256]{2,1,0:T(8,128)S(1)}, u32[]{:S(2)}, u32[]{:S(2)}) collective-permute-start(f32[32,8,256]{2,1,0:T(8,128)S(1)} %get-tuple-element.32), channel_id=1, source_target_pairs={{0,2},{2,0},{4,6},{6,4},{8,10},{10,8},{12,14},{14,12},{16,18},{18,... | collective-permute-start | bytes 786440 | tf_op jit(solution)/shard_map/ppermute | solution.py:354
  55.5 6.4 %collective-permute-done.14.refs_3_.refs_5_ = f32[32,8,256]{2,1,0:T(8,128)S(1)} collective-permute-done((f32[32,8,256]{2,1,0:T(8,128)S(1)}, f32[32,8,256]{2,1,0:T(8,128)S(1)}, u32[]{:S(2)}, u32[]{:S(2)}) %collective-permute-start.14) | collective-permute-done | bytes 262176 | tf_op jit(solution)/shard_map/ppermute | solution.py:440
  62.0 5.7 %collective-permute-done.13.refs_2_.refs_4_ = f32[32,8,256]{2,1,0:T(8,128)S(1)} collective-permute-done((f32[32,8,256]{2,1,0:T(8,128)S(1)}, f32[32,8,256]{2,1,0:T(8,128)S(1)}, u32[]{:S(2)}, u32[]{:S(2)}) %collective-permute-start.13) | collective-permute-done | bytes 262176 | tf_op jit(solution)/shard_map/ppermute | solution.py:439
  69.2 1.5 %collective-permute-start.16 = (f32[8,128]{1,0:T(8,128)S(1)}, f32[8,128]{1,0:T(8,128)S(1)}, u32[]{:S(2)}, u32[]{:S(2)}) collective-permute-start(f32[8,128]{1,0:T(8,128)S(1)} %add.23), channel_id=1, source_target_pairs={{0,4},{2,6},{4,0},{6,2},{1,5},{3,7},{5,1},{7,3},{8,12},{10,14},{12... | collective-permute-start | bytes 12296 | tf_op jit(solution)/shard_map/ppermute | solution.py:377
  70.7 2.1 %collective-permute-done.16 = f32[8,128]{1,0:T(8,128)S(1)} collective-permute-done((f32[8,128]{1,0:T(8,128)S(1)}, f32[8,128]{1,0:T(8,128)S(1)}, u32[]{:S(2)}, u32[]{:S(2)}) %collective-permute-start.16) | collective-permute-done | bytes 4128 | tf_op jit(solution)/shard_map/ppermute | solution.py:377
  72.8 1.5 %collective-permute-start.17 = (f32[8,128]{1,0:T(8,128)S(1)}, f32[8,128]{1,0:T(8,128)S(1)}, u32[]{:S(2)}, u32[]{:S(2)}) collective-permute-start(f32[8,128]{1,0:T(8,128)S(1)} %add.24), channel_id=1, source_target_pairs={{0,8},{8,0},{16,24},{24,16},{1,9},{9,1},{17,25},{25,17},{2,10},{10... | collective-permute-start | bytes 12296 | tf_op jit(solution)/shard_map/ppermute | solution.py:377
  74.3 2.1 %collective-permute-done.17 = f32[8,128]{1,0:T(8,128)S(1)} collective-permute-done((f32[8,128]{1,0:T(8,128)S(1)}, f32[8,128]{1,0:T(8,128)S(1)}, u32[]{:S(2)}, u32[]{:S(2)}) %collective-permute-start.17) | collective-permute-done | bytes 4128 | tf_op jit(solution)/shard_map/ppermute | solution.py:377
  77.5 3.5 %collective-permute-done.18 = f32[8,128]{1,0:T(8,128)S(1)} collective-permute-done((f32[8,128]{1,0:T(8,128)S(1)}, f32[8,128]{1,0:T(8,128)S(1)}, u32[]{:S(2)}, u32[]{:S(2)}) %collective-permute-start.18) | collective-permute-done | bytes 4128 | tf_op jit(solution)/shard_map/ppermute | solution.py:377
  80.9 1.7 %basis.1 = f32[2,32,8,256]{3,2,1,0:T(8,128)} custom-call(f32[8,128]{1,0:T(8,128)S(1)} %add.26.refs_0_, s32[4]{0:T(128)S(1)} %copy-done.2, f32[32,8,256]{2,1,0:T(8,128)S(1)} %get-tuple-element.31.refs_0_.refs_2_, f32[32,8,256]{2,1,0:T(8,128)S(1)} %collective-permute-done.12.refs_1_.refs_3_, f32[32,8,256]{2,1,0:T(8,128)S(1)} %collective-permute-done.13.refs_2_.refs_4_, ...), custom_call_target="tpu_custom_call" | custom-call | tf_op jit(solution)/shard_map/basis/pallas_call | solution.py:450
  (30 shorter events, 8.2 us)
Async XLA Ops:
  0.0 3.3 %copy-start = (f32[2,32,8,256]{3,2,1,0:T(8,128)S(1)}, f32[2,32,8,256]{3,2,1,0:T(8,128)}, u32[]{:S(2)}) copy-start(f32[2,32,8,256]{3,2,1,0:T(8,128)} %refs_0_.3) | copy-start | bytes 1572868
  1.0 1.7 %collective-permute-start = (f32[32,8,256]{2,1,0:T(8,128)S(1)}, f32[32,8,256]{2,1,0:T(8,128)S(1)}, u32[]{:S(2)}, u32[]{:S(2)}) collective-permute-start(f32[32,8,256]{2,1,0:T(8,128)S(1)} %dynamic-slice_bitcast_fusion), channel_id=1, source_target_pairs={{0,2},{2,0},{4,6},{6,4},{8,10},{10,8},{12,14},{14,12},{16,18},{18,... | collective-permute-start | bytes 786440 | tf_op jit(solution)/shard_map/ppermute | solution.py:354
  1.6 1.7 %collective-permute-start.1 = (f32[32,8,256]{2,1,0:T(8,128)}, f32[32,8,256]{2,1,0:T(8,128)S(1)}, u32[]{:S(2)}, u32[]{:S(2)}) collective-permute-start(f32[32,8,256]{2,1,0:T(8,128)} %refs_2_.3), channel_id=1, source_target_pairs={{0,2},{2,0},{4,6},{6,4},{8,10},{10,8},{12,14},{14,12},{16,18},{18,... | collective-permute-start | bytes 786440 | tf_op jit(solution)/shard_map/ppermute | solution.py:354
  3.3 1.0 %copy-start.1 = (f32[32,8,256]{2,1,0:T(8,128)S(1)}, f32[32,8,256]{2,1,0:T(8,128)}, u32[]{:S(2)}) copy-start(f32[32,8,256]{2,1,0:T(8,128)} %refs_2_.3) | copy-start | bytes 786436
  4.4 20.0 %collective-permute-start.4 = (f32[2,32,8,256]{3,2,1,0:T(8,128)S(1)}, f32[2,32,8,256]{3,2,1,0:T(8,128)S(1)}, u32[]{:S(2)}, u32[]{:S(2)}) collective-permute-start(f32[2,32,8,256]{3,2,1,0:T(8,128)S(1)} %bitcast.4), channel_id=1, source_target_pairs={{0,4},{2,6},{4,0},{6,2},{8,12},{10,14},{12,8},{14,10},{16,20},{18,... | collective-permute-start | bytes 1572872 | tf_op jit(solution)/shard_map/ppermute | solution.py:354
  7.3 17.1 %collective-permute-start.2 = (f32[2,2,8,8,256]{4,3,2,1,0:T(8,128)S(1)}, f32[2,2,8,8,256]{4,3,2,1,0:T(8,128)S(1)}, u32[]{:S(2)}, u32[]{:S(2)}) collective-permute-start(f32[2,2,8,8,256]{4,3,2,1,0:T(8,128)S(1)} %get-tuple-element.19), channel_id=1, source_target_pairs={{0,8},{2,10},{4,12},{6,14},{8,16},{10,18},{12,20},{14,22},{16,24},... | collective-permute-start | bytes 786440 | tf_op jit(solution)/shard_map/ppermute | solution.py:354
  10.8 13.6 %collective-permute-start.3 = (f32[2,2,8,8,256]{4,3,2,1,0:T(8,128)S(1)}, f32[2,2,8,8,256]{4,3,2,1,0:T(8,128)S(1)}, u32[]{:S(2)}, u32[]{:S(2)}) collective-permute-start(f32[2,2,8,8,256]{4,3,2,1,0:T(8,128)S(1)} %get-tuple-element.20), channel_id=1, source_target_pairs={{8,0},{10,2},{12,4},{14,6},{16,8},{18,10},{20,12},{22,14},{24,16},... | collective-permute-start | bytes 786440 | tf_op jit(solution)/shard_map/ppermute | solution.py:354
  12.1 7.1 %collective-permute-start.5 = (f32[2,8,8,256]{3,2,1,0:T(8,128)S(1)}, f32[2,8,8,256]{3,2,1,0:T(8,128)S(1)}, u32[]{:S(2)}, u32[]{:S(2)}) collective-permute-start(f32[2,8,8,256]{3,2,1,0:T(8,128)S(1)} %get-tuple-element.22), channel_id=1, source_target_pairs={{0,12},{2,14},{4,8},{6,10},{8,20},{10,22},{12,16},{14,18},{16,28},... | collective-permute-start | bytes 393224 | tf_op jit(solution)/shard_map/ppermute | solution.py:354
  16.6 7.8 %collective-permute-start.6 = (f32[2,8,8,256]{3,2,1,0:T(8,128)S(1)}, f32[2,8,8,256]{3,2,1,0:T(8,128)S(1)}, u32[]{:S(2)}, u32[]{:S(2)}) collective-permute-start(f32[2,8,8,256]{3,2,1,0:T(8,128)S(1)} %get-tuple-element.23), channel_id=1, source_target_pairs={{8,4},{10,6},{12,0},{14,2},{16,12},{18,14},{20,8},{22,10},{24,20},... | collective-permute-start | bytes 393224 | tf_op jit(solution)/shard_map/ppermute | solution.py:354
  29.4 18.9 %collective-permute-start.9 = (f32[32,8,256]{2,1,0:T(8,128)S(1)}, f32[32,8,256]{2,1,0:T(8,128)S(1)}, u32[]{:S(2)}, u32[]{:S(2)}) collective-permute-start(f32[32,8,256]{2,1,0:T(8,128)S(1)} %bitcast.5), channel_id=1, source_target_pairs={{0,4},{2,6},{4,0},{6,2},{8,12},{10,14},{12,8},{14,10},{16,20},{18,... | collective-permute-start | bytes 786440 | tf_op jit(solution)/shard_map/ppermute | solution.py:354
  31.0 17.3 %collective-permute-start.7 = (f32[2,8,8,256]{3,2,1,0:T(8,128)S(1)}, f32[2,8,8,256]{3,2,1,0:T(8,128)S(1)}, u32[]{:S(2)}, u32[]{:S(2)}) collective-permute-start(f32[2,8,8,256]{3,2,1,0:T(8,128)S(1)} %get-tuple-element.26), channel_id=1, source_target_pairs={{0,8},{2,10},{4,12},{6,14},{8,16},{10,18},{12,20},{14,22},{16,24},... | collective-permute-start | bytes 393224 | tf_op jit(solution)/shard_map/ppermute | solution.py:354
  35.4 12.9 %collective-permute-start.8 = (f32[2,8,8,256]{3,2,1,0:T(8,128)S(1)}, f32[2,8,8,256]{3,2,1,0:T(8,128)S(1)}, u32[]{:S(2)}, u32[]{:S(2)}) collective-permute-start(f32[2,8,8,256]{3,2,1,0:T(8,128)S(1)} %get-tuple-element.27), channel_id=1, source_target_pairs={{8,0},{10,2},{12,4},{14,6},{16,8},{18,10},{20,12},{22,14},{24,16},... | collective-permute-start | bytes 393224 | tf_op jit(solution)/shard_map/ppermute | solution.py:354
  36.7 6.4 %collective-permute-start.10 = (f32[8,8,256]{2,1,0:T(8,128)S(1)}, f32[8,8,256]{2,1,0:T(8,128)S(1)}, u32[]{:S(2)}, u32[]{:S(2)}) collective-permute-start(f32[8,8,256]{2,1,0:T(8,128)S(1)} %get-tuple-element.29), channel_id=1, source_target_pairs={{0,12},{2,14},{4,8},{6,10},{8,20},{10,22},{12,16},{14,18},{16,28},... | collective-permute-start | bytes 196616 | tf_op jit(solution)/shard_map/ppermute | solution.py:354
  41.2 7.1 %collective-permute-start.11 = (f32[8,8,256]{2,1,0:T(8,128)S(1)}, f32[8,8,256]{2,1,0:T(8,128)S(1)}, u32[]{:S(2)}, u32[]{:S(2)}) collective-permute-start(f32[8,8,256]{2,1,0:T(8,128)S(1)} %get-tuple-element.30), channel_id=1, source_target_pairs={{8,4},{10,6},{12,0},{14,2},{16,12},{18,14},{20,8},{22,10},{24,20},... | collective-permute-start | bytes 196616 | tf_op jit(solution)/shard_map/ppermute | solution.py:354
  53.3 8.6 %collective-permute-start.14 = (f32[32,8,256]{2,1,0:T(8,128)S(1)}, f32[32,8,256]{2,1,0:T(8,128)S(1)}, u32[]{:S(2)}, u32[]{:S(2)}) collective-permute-start(f32[32,8,256]{2,1,0:T(8,128)S(1)} %get-tuple-element.32), channel_id=1, source_target_pairs={{0,3},{1,2},{2,1},{3,0},{4,7},{5,6},{6,5},{7,4},{8,11},{9,10},{10,... | collective-permute-start | bytes 786440 | tf_op jit(solution)/shard_map/ppermute | solution.py:440
  53.4 8.5 %collective-permute-start.12 = (f32[32,8,256]{2,1,0:T(8,128)S(1)}, f32[32,8,256]{2,1,0:T(8,128)S(1)}, u32[]{:S(2)}, u32[]{:S(2)}) collective-permute-start(f32[32,8,256]{2,1,0:T(8,128)S(1)} %get-tuple-element.32), channel_id=1, source_target_pairs={{0,2},{2,0},{4,6},{6,4},{8,10},{10,8},{12,14},{14,12},{16,18},{18,... | collective-permute-start | bytes 786440 | tf_op jit(solution)/shard_map/ppermute | solution.py:354
  55.0 12.6 %collective-permute-start.13 = (f32[32,8,256]{2,1,0:T(8,128)S(1)}, f32[32,8,256]{2,1,0:T(8,128)S(1)}, u32[]{:S(2)}, u32[]{:S(2)}) collective-permute-start(f32[32,8,256]{2,1,0:T(8,128)S(1)} %get-tuple-element.31.refs_0_.refs_2_), channel_id=1, source_target_pairs={{0,1},{1,0},{2,3},{3,2},{4,5},{5,4},{6,7},{7,6},{8,9},{9,8},{10,11... | collective-permute-start | bytes 786440 | tf_op jit(solution)/shard_map/ppermute | solution.py:439
  68.0 1.2 %collective-permute-start.15 = (f32[8,128]{1,0:T(8,128)S(1)}, f32[8,128]{1,0:T(8,128)S(1)}, u32[]{:S(2)}, u32[]{:S(2)}) collective-permute-start(f32[8,128]{1,0:T(8,128)S(1)} %correlation.1), channel_id=1, source_target_pairs={{0,2},{2,0},{4,6},{6,4},{1,3},{3,1},{5,7},{7,5},{8,10},{10,8},{12,... | collective-permute-start | bytes 12296 | tf_op jit(solution)/shard_map/ppermute | solution.py:377
  69.2 3.6 %collective-permute-start.16 = (f32[8,128]{1,0:T(8,128)S(1)}, f32[8,128]{1,0:T(8,128)S(1)}, u32[]{:S(2)}, u32[]{:S(2)}) collective-permute-start(f32[8,128]{1,0:T(8,128)S(1)} %add.23), channel_id=1, source_target_pairs={{0,4},{2,6},{4,0},{6,2},{1,5},{3,7},{5,1},{7,3},{8,12},{10,14},{12... | collective-permute-start | bytes 12296 | tf_op jit(solution)/shard_map/ppermute | solution.py:377
  72.8 3.6 %collective-permute-start.17 = (f32[8,128]{1,0:T(8,128)S(1)}, f32[8,128]{1,0:T(8,128)S(1)}, u32[]{:S(2)}, u32[]{:S(2)}) collective-permute-start(f32[8,128]{1,0:T(8,128)S(1)} %add.24), channel_id=1, source_target_pairs={{0,8},{8,0},{16,24},{24,16},{1,9},{9,1},{17,25},{25,17},{2,10},{10... | collective-permute-start | bytes 12296 | tf_op jit(solution)/shard_map/ppermute | solution.py:377
  76.4 4.5 %copy-start.2 = (s32[4]{0:T(128)S(1)}, s32[4]{0:T(128)}, u32[]{:S(2)}) copy-start(s32[4]{0:T(128)} %refs_1_.1) | copy-start | bytes 52
  76.4 4.5 %collective-permute-start.18 = (f32[8,128]{1,0:T(8,128)S(1)}, f32[8,128]{1,0:T(8,128)S(1)}, u32[]{:S(2)}, u32[]{:S(2)}) collective-permute-start(f32[8,128]{1,0:T(8,128)S(1)} %add.25), channel_id=1, source_target_pairs={{0,16},{8,24},{16,0},{24,8},{1,17},{9,25},{17,1},{25,9},{2,18},{10... | collective-permute-start | bytes 12296 | tf_op jit(solution)/shard_map/ppermute | solution.py:377

commit v2 on v1

--- a/solution.py
+++ b/solution.py
@@ -36,33 +36,60 @@
     return 3 if one_sided() else 4
 
 
+def y_phases():
+    return range(1 if one_sided() else 2)
+
+
+def upward(position, phase):
+    return (position % 2) == phase
+
+
 def own_slots(core, chip):
     first = chip if one_sided() else 1
     return first + core, first + 1 - core
 
 
-def halo_slots(chip):
-    return [2 - 2 * chip] if one_sided() else [0, 3]
+def halo_slot(chip, up):
+    first = chip if one_sided() else 1
+    return jnp.where(up, first + 2, first - 1)
 
 
 def rows_of(slot):
     return pl.ds(pl.multiple_of(PAD + 8 * slot, 8), 8)
 
 
-def fill(window, tiles, x_left, x_right, y_halos, corners, core, chip, change=lambda a: a):
-    width = tiles[0].shape[0]
+def put(window, first_plane, rows, planes, change=lambda a: a):
+    count = planes.shape[0]
     for half in range(2):
         lanes = slice(half * LANES, (half + 1) * LANES)
-        for index, slot in enumerate(own_slots(core, chip)):
-            rows = rows_of(slot)
-            window[half, HALO : HALO + width, rows, :] = change(tiles[index][:, :, lanes])
-            window[half, :HALO, rows, :] = change(x_left[index, :, :, lanes])
-            window[half, HALO + width :, rows, :] = change(x_right[index, :, :, lanes])
-        for slot, middle, (left, right) in zip(halo_slots(chip), y_halos, corners):
-            rows = rows_of(slot)
-            window[half, HALO : HALO + width, rows, :] = change(middle[:, :, lanes])
-            window[half, :HALO, rows, :] = change(left[:, :, lanes])
-            window[half, HALO + width :, rows, :] = change(right[:, :, lanes])
+        window[half, pl.ds(first_plane, count), rows, :] = change(planes[:, :, lanes])
+
+
+def halo_start(right, width, count):
+    return jnp.where(right, HALO + width, HALO - count)
+
+
+def fill(window, tiles, x_halos, y_halos, corners, change=lambda a: a):
+    core, chip, along_x = place()
+    width = tiles[0].shape[0]
+    slots = own_slots(core, chip)
+    for index, slot in enumerate(slots):
+        put(window, HALO, rows_of(slot), tiles[index], change)
+        for phase in range(2):
+            halo = x_halos[phase].at[index]
+            start = halo_start(upward(along_x, phase), width, halo.shape[0])
+            put(window, start, rows_of(slot), halo, change)
+    for phase in y_phases():
+        rows = rows_of(halo_slot(chip, upward(chip, phase)))
+        put(window, HALO, rows, y_halos[phase], change)
+        for x_phase in range(2):
+            corner = corners[2 * phase + x_phase]
+            start = halo_start(upward(along_x, x_phase), width, corner.shape[0])
+            put(window, start, rows, corner, change)
+
+
+def near_planes(right, width, count):
+    return pl.ds(jnp.where(right, width - count, 0), count)
 
 
 def z_matrix(depth):
@@ -140,103 +167,109 @@
                     target[:, :, PAD + 24 : PAD + 32, :] = zero
 
 
-def edge_flags(core, chip):
-    if one_sided():
-        return [core == 1 - chip]
-    return [core == 1, core == 0]
-
-
-def pack_kernel(orbitals, received, potential, received_potential, y_out, left_out, right_out, *d_out):
+def edge_is_own(core, chip, phase):
+    return core == jnp.where(upward(chip, phase), 1, 0)
+
+
+def pack_kernel(orbitals, received, potential, received_potential, *outs):
+    core, chip, along_x = place()
+    width = potential.shape[0]
+    y_out = outs[: len(y_phases())]
+    x_out = outs[len(y_phases()) : len(y_phases()) + 2]
+    d_out = outs[len(y_phases()) + 2 :]
+    tiles = (orbitals.at[core], received)
+    local = (potential, received_potential)
+    for x_phase in range(2):
+        right = upward(along_x, x_phase)
+        for t in range(2):
+            x_out[x_phase][t, :HALO] = tiles[t][near_planes(right, width, HALO)]
+            x_out[x_phase][t, HALO:] = local[t][near_planes(right, width, HALO - 2)]
+    for phase in y_phases():
+        own = edge_is_own(core, chip, phase)
+        for t, chosen in enumerate((own, jnp.logical_not(own))):
+
+            @pl.when(chosen)
+            def _(t=t, phase=phase):
+                y_out[phase][...] = tiles[t][...]
+                for x_phase in range(2):
+                    right = upward(along_x, x_phase)
+                    out = d_out[2 * phase + x_phase]
+                    out[: HALO - 1] = tiles[t][near_planes(right, width, HALO - 1)]
+                    out[HALO - 1 :] = local[t][near_planes(right, width, HALO - 3)]
+
+
+def fill_local(window, potential, received_potential, edge, passed, x_halos, corners):
     core, chip, _ = place()
-    width = potential.shape[0]
-    fields = ((orbitals.at[core], received), (potential, received_potential))
-    for f, (own, other) in enumerate(fields):
-        for t, tile in enumerate((own, other)):
-            left_out[f, t] = tile[:HALO]
-            right_out[f, t] = tile[width - HALO :]
-        for k, flag in enumerate(edge_flags(core, chip)):
-            for chosen, tile in ((flag, own), (jnp.logical_not(flag), other)):
-
-                @pl.when(chosen)
-                def _(tile=tile, k=k, f=f):
-                    y_out[k, f] = tile[...]
-                    d_out[2 * k][f] = tile[:HALO]
-                    d_out[2 * k + 1][f] = tile[width - HALO :]
-
-
-def first_kernel(count, *refs):
-    orbitals, received, potential, received_potential, x_left, x_right = refs[:6]
-    y_halos = refs[6 : 6 + count]
-    corners = refs[6 + count : 6 + 3 * count]
-    own_out, other_out, y_out, left_out, right_out = refs[6 + 3 * count : 11 + 3 * count]
-    d_out = refs[11 + 3 * count : 11 + 5 * count]
-    a, b, local = refs[11 + 5 * count :]
-    core, chip, along_x = place()
-    width, depth = potential.shape[0], potential.shape[2]
-
-    def pieces(f):
-        return (
-            x_left.at[f],
-            x_right.at[f],
-            [y.at[f] for y in y_halos],
-            [(corners[2 * k].at[f], corners[2 * k + 1].at[f]) for k in range(count)],
-        )
-
-    fill(a, (orbitals.at[core], received), *pieces(0), core, chip)
-    fill(local, (potential, received_potential), *pieces(1), core, chip, lambda v: (v - 0.5) / 4.25)
-    four_steps(a, b, local, z_matrix(depth), chip, along_x)
-    outs = (own_out, other_out)
-    for t, slot in enumerate(own_slots(core, chip)):
-        for half in range(2):
-            lanes = slice(half * LANES, (half + 1) * LANES)
-            tile = a[half, HALO : HALO + width, rows_of(slot), :]
-            outs[t][:, :, lanes] = tile
-            left_out[t, :, :, lanes] = tile[:HALO]
-            right_out[t, :, :, lanes] = tile[width - HALO :]
-    for k, flag in enumerate(edge_flags(core, chip)):
-        own_slot, other_slot = own_slots(core, chip)
-        slot = jnp.where(flag, own_slot, other_slot)
-        for half in range(2):
-            lanes = slice(half * LANES, (half + 1) * LANES)
-            tile = a[half, HALO : HALO + width, rows_of(slot), :]
-            y_out[k, :, :, lanes] = tile
-            d_out[2 * k][:, :, lanes] = tile[:HALO]
-            d_out[2 * k + 1][:, :, lanes] = tile[width - HALO :]
-
-
-def second_kernel(count, *refs):
-    orbitals, received, potential, received_potential = refs[:4]
-    own, other, x_left, x_right = refs[4:8]
-    y_halos = refs[8 : 8 + count]
-    corners = refs[8 + count : 8 + 3 * count]
-    rest = refs[8 + 3 * count :]
-    p_left, p_right = rest[:2]
-    p_halos = rest[2 : 2 + count]
-    p_corners = rest[2 + count : 2 + 3 * count]
-    keep, give, a, b, local = rest[2 + 3 * count :]
+    fill(
+        window,
+        (potential, received_potential),
+        [x.at[:, HALO:] for x in x_halos],
+        [edge] * len(y_phases()),
+        [c.at[HALO - 1 :] for c in corners],
+        lambda v: (v - 0.5) / 4.25,
+    )
+    for phase in y_phases():
+        up = upward(chip, phase)
+
+        @pl.when(core != jnp.where(up, 1, 0))
+        def _(up=up):
+            put(window, HALO, rows_of(halo_slot(chip, up)), passed, lambda v: (v - 0.5) / 4.25)
+
+
+def first_kernel(*refs):
+    count = len(y_phases())
+    orbitals, received, potential, received_potential, edge, passed = refs[:6]
+    y_halos, x_halos, corners = refs[6 : 6 + count], refs[6 + count : 8 + count], refs[8 + count : 8 + 3 * count]
+    own_out, other_out = refs[8 + 3 * count : 10 + 3 * count]
+    outs = refs[10 + 3 * count : 12 + 6 * count]
+    a, b, local = refs[12 + 6 * count :]
     core, chip, along_x = place()
     width, depth = potential.shape[0], potential.shape[2]
     fill(
         a,
-        (own, other),
-        x_left,
-        x_right,
+        (orbitals.at[core], received),
+        [x.at[:, :HALO] for x in x_halos],
         y_halos,
-        [(corners[2 * k], corners[2 * k + 1]) for k in range(count)],
-        core,
-        chip,
+        [c.at[: HALO - 1] for c in corners],
     )
-    fill(
-        local,
-        (potential, received_potential),
-        p_left.at[1],
-        p_right.at[1],
-        [y.at[1] for y in p_halos],
-        [(p_corners[2 * k].at[1], p_corners[2 * k + 1].at[1]) for k in range(count)],
-        core,
-        chip,
-        lambda v: (v - 0.5) / 4.25,
-    )
+    fill_local(local, potential, received_potential, edge, passed, x_halos, corners)
+    four_steps(a, b, local, z_matrix(depth), chip, along_x)
+    y_out, x_out, d_out = outs[:count], outs[count : count + 2], outs[count + 2 :]
+    slots = own_slots(core, chip)
+    for half in range(2):
+        lanes = slice(half * LANES, (half + 1) * LANES)
+
+        def planes(slot, start, size, half=half):
+            return a[half, pl.ds(HALO + start, size), rows_of(slot), :]
+
+        def ends(right, size):
+            return jnp.where(right, width - size, 0)
+
+        for t, out in enumerate((own_out, other_out)):
+            out[:, :, lanes] = planes(slots[t], 0, width)
+            for x_phase in range(2):
+                start = ends(upward(along_x, x_phase), HALO)
+                x_out[x_phase][t, :, :, lanes] = planes(slots[t], start, HALO)
+        for phase in y_phases():
+            slot = jnp.where(edge_is_own(core, chip, phase), *slots)
+            y_out[phase][:, :, lanes] = planes(slot, 0, width)
+            for x_phase in range(2):
+                start = ends(upward(along_x, x_phase), HALO - 1)
+                d_out[2 * phase + x_phase][:, :, lanes] = planes(slot, start, HALO - 1)
+
+
+def second_kernel(*refs):
+    count = len(y_phases())
+    orbitals, received, potential, received_potential, edge, passed, own, other = refs[:8]
+    halos = refs[8 : 10 + 3 * count]
+    y_halos, x_halos, corners = halos[:count], halos[count : count + 2], halos[count + 2 :]
+    p_x_halos = refs[10 + 3 * count : 12 + 3 * count]
+    p_corners = refs[12 + 3 * count : 12 + 5 * count]
+    keep, give, a, b, local = refs[12 + 5 * count :]
+    core, chip, along_x = place()
+    width, depth = potential.shape[0], potential.shape[2]
+    fill(a, (own, other), x_halos, y_halos, corners)
+    fill_local(local, potential, received_potential, edge, passed, p_x_halos, p_corners)
     four_steps(a, b, local, z_matrix(depth), chip, along_x)
     start = (orbitals.at[core], received)
     outs = (keep, give)
@@ -336,45 +369,57 @@
         lax.fori_loop(0, width, body, 0, unroll=4)
 
 
-def moves(dx, dy_chip, swap=False):
+def partner(position, phase, count):
+    other = position + 1 if position % 2 == phase else position - 1
+    return other if 0 <= other < count else None
+
+
+def meet(value, x_phase=None, y_phase=None):
     nx, ny = lax.axis_size("gx"), lax.axis_size("gy")
     pairs = []
     for x in range(nx):
         for y in range(ny):
-            chip, core = y // 2, y % 2
-            to_x = x + dx
-            to_chip = 1 - chip if dy_chip == "flip" else chip + dy_chip
-            to_core = 1 - core if swap else core
-            if 0 <= to_x < nx and 0 <= to_chip < ny // 2:
-                pairs.append((x * ny + y, to_x * ny + to_chip * 2 + to_core))
-    return pairs
-
-
-def send(value, dx, dy_chip, swap=False):
-    return lax.ppermute(value, ("gx", "gy"), moves(dx, dy_chip, swap))
-
-
-def y_steps():
-    return ["flip"] if one_sided() else [1, -1]
-
-
-def exchange(y_out, left_out, right_out, d_out):
-    y_halos = [send(y_out[k], 0, step) for k, step in enumerate(y_steps())]
-    corners = []
-    for k, step in enumerate(y_steps()):
-        corners += [send(d_out[2 * k + 1], 1, step), send(d_out[2 * k], -1, step)]
-    x_left = send(right_out, 1, 0)
-    x_right = send(left_out, -1, 0)
-    return x_left, x_right, *y_halos, *corners
+            to_x = x if x_phase is None else partner(x, x_phase, nx)
+            chip = y // 2 if y_phase is None else partner(y // 2, y_phase, ny // 2)
+            if to_x is not None and chip is not None:
+                pairs.append((x * ny + y, to_x * ny + chip * 2 + y % 2))
+    return lax.ppermute(value, ("gx", "gy"), pairs)
+
+
+def swap(value):
+    count = lax.axis_size("gy")
+    return lax.ppermute(value, "gy", [(y, y ^ 1) for y in range(count)])
+
+
+def face(value):
+    count = lax.axis_size("gy")
+    pairs = [(y, partner(y, 1, count)) for y in range(count)]
+    return lax.ppermute(value, "gy", [p for p in pairs if p[1] is not None])
+
+
+def exchange(payloads):
+    count = len(y_phases())
+    halos = [meet(payloads[phase], y_phase=phase) for phase in y_phases()]
+    halos += [meet(payloads[count + phase], x_phase=phase) for phase in range(2)]
+    for y_phase in y_phases():
+        for x_phase in range(2):
+            halos.append(meet(payloads[count + 2 + 2 * y_phase + x_phase], x_phase, y_phase))
+    return halos
 
 
 def summed(value, axis):
     count = lax.axis_size(axis)
     if count & (count - 1):
         return lax.psum(value, axis)
+
+    def of(step):
+        return lax.ppermute(value, axis, [(i, i ^ step) for i in range(count)])
+
+    if count == 4:
+        return (value + of(1)) + (of(2) + of(3))
     step = 1
     while step < count:
-        value = value + lax.ppermute(value, axis, [(i, i ^ step) for i in range(count)])
+        value = value + of(step)
         step *= 2
     return value
 
@@ -383,52 +428,56 @@
     group, width, height, depth = orbitals.shape
     bands = lax.axis_size("band")
     cells = float(width * lax.axis_size("gx") * height * lax.axis_size("gy") * depth)
-    count = len(y_steps())
+    count = len(y_phases())
     core, chip, _ = place()
-    extent = width + 2 * HALO
-    window = (2, extent, 8 * tile_count() + 2 * PAD, LANES)
+    window = (2, width + 2 * HALO, 8 * tile_count() + 2 * PAD, LANES)
     scratch = [pltpu.VMEM(window, jnp.float32)] * 3
 
+    edge = face(potential)
     other = lax.dynamic_index_in_dim(orbitals, 1 - core, 0, keepdims=False)
-    received = send(other, 0, 0, True)
-    received_potential = send(potential, 0, 0, True)
+    received = swap(other)
+    received_potential = swap(potential)
     tile = (width, height, depth)
-    ends = (2, HALO, height, depth)
-    corner = (HALO, height, depth)
+
+    def payloads(in_x, in_corner):
+        return (
+            [struct(*tile)] * count
+            + [struct(2, in_x, height, depth)] * 2
+            + [struct(in_corner, height, depth)] * (2 * count)
+        )
+
     packed = pl.pallas_call(
         pack_kernel,
-        out_shape=[struct(count, 2, *tile), struct(2, *ends), struct(2, *ends)]
-        + [struct(2, *corner)] * (2 * count),
+        out_shape=payloads(2 * HALO - 2, 2 * HALO - 4),
         in_specs=[VMEM] * 4,
-        out_specs=[VMEM] * (3 + 2 * count),
+        out_specs=[VMEM] * (2 + 3 * count),
         compiler_params=PARAMS,
         name="pack",
     )(orbitals, received, potential, received_potential)
-    halos = exchange(*packed[:3], packed[3:])
-    first = pl.pallas_call(
-        functools.partial(first_kernel, count),
-        out_shape=[struct(*tile)] * 2
-        + [struct(count, *tile), struct(*ends), struct(*ends)]
-        + [struct(*corner)] * (2 * count),
-        in_specs=[VMEM] * (6 + 3 * count),
-        out_specs=[VMEM] * (5 + 2 * count),
+    halos = exchange(packed)
+    passed = swap(edge)
+    local = (potential, received_potential, edge, passed)
+    own, sibling, *packed = pl.pallas_call(
+        first_kernel,
+        out_shape=[struct(*tile)] * 2 + payloads(HALO, HALO - 1),
+        in_specs=[VMEM] * (8 + 3 * count),
+        out_specs=[VMEM] * (4 + 3 * count),
         scratch_shapes=scratch,
         compiler_params=PARAMS,
         name="first_round",
-    )(orbitals, received, potential, received_potential, *halos)
-    own, sibling = first[:2]
-    second_halos = exchange(*first[2:5], first[5:])
+    )(orbitals, received, *local, *halos)
+    second_halos = exchange(packed)
     keep, give = pl.pallas_call(
-        functools.partial(second_kernel, count),
+        second_kernel,
         out_shape=[struct(*tile)] * 2,
-        in_specs=[VMEM] * (10 + 6 * count),
+        in_specs=[VMEM] * (12 + 5 * count),
         out_specs=[VMEM] * 2,
         scratch_shapes=scratch,
         compiler_params=PARAMS,
         name="second_round",
-    )(orbitals, received, potential, received_potential, own, sibling, *second_halos, *halos)
-
-    slots = [keep, send(give, 0, 0, True)]
+    )(orbitals, received, *local, own, sibling, *second_halos, *halos[count:])
+
+    slots = [keep, swap(give)]
     for d in range(1, bands):
         same, crossed = [], []
         for y in range(lax.axis_size("gy")):

time: 82.9 us -> 78.7 us (0.949)
  waiting for transfers between devices: 34.7 us -> 23.3 us
  starting transfers between devices: 33.6 us -> 40.9 us
    ppermute x17 -> x21, waiting for transfers between devices: 22.6 us -> 11.2 us  [the longest x6 6.28 us: of(): return lax.ppermute(value, axis, [(i, i ^ step) for i in range(count)])]
    ppermute x17 -> x21, starting transfers between devices: 33 us -> 40.3 us  [the longest x10 22.8 us: meet(): return lax.ppermute(value, ('gx', 'gy'), pairs)]
  transfers between devices with their start and end apart: 19 -> 23, of which waited for: 12 -> 8; matrix products, arithmetic and copies ran while one was open for 0% -> 1% of each run, Pallas kernels for 0% -> 0%
where the time goes in v2:
time: 78.7 us; the launch traced here: 78.4 us
  starting transfers between devices  40.9 us (52%)
  waiting for transfers between devices  23.3 us (30%)
  Pallas kernels  12.2 us (16%)
  local copies, waits for them, and re-layouts  1.92 us (2%)
    ppermute x10, starting transfers between devices, meet(): return lax.ppermute(value, ('gx', 'gy'), pairs)  22.8 us
    ppermute x4, starting transfers between devices, swap(): return lax.ppermute(value, 'gy', [(y, y ^ 1) for y in range(count)])  9.17 us
    ppermute x6, starting transfers between devices, of(): return lax.ppermute(value, axis, [(i, i ^ step) for i in range(count)])  7.48 us
    ppermute x1, waiting for transfers between devices, per_device(): slots.append(lax.ppermute(give, ('gy', 'band'), crossed))  6.41 us
    ppermute x6, waiting for transfers between devices, of(): return lax.ppermute(value, axis, [(i, i ^ step) for i in range(count)])  6.28 us
    ppermute x1, waiting for transfers between devices, per_device(): slots.append(lax.ppermute(keep, ('gy', 'band'), same))  5.67 us
    pallas_call x1, Pallas kernels, per_device(): pl.pallas_call(first_kernel, out_shape=[struct(*tile)] * 2 + payloads(HAL...  5.07 us
    pallas_call x1, Pallas kernels, per_device(): pl.pallas_call(second_kernel, out_shape=[struct(*tile)] * 2, in_specs=[VM...  5.04 us
  transfers between devices with their start and end apart: 23, of which 8 were waited for; matrix products, arithmetic and copies ran while one was open for 1% of the time, Pallas kernels for 0%

profile of v2, /device:TPU:0, one launch (start us, length us, event | category | flops | bytes accessed | tf_op | source)
XLA Modules:
  0.0 78.4 jit_solution(16118245021157373105)
XLA Ops:
  0.8 1.0 %dynamic-slice_bitcast_fusion = f32[32,8,256]{2,1,0:T(8,128)S(1)} fusion(f32[2,32,8,256]{3,2,1,0:T(8,128)} %refs_0_.3, s32[]{:T(128)S(6)} %select_n.12), kind=kLoop, calls=%fused_computation | loop fusion | bytes 524292 | tf_op jit(solution)/shard_map/jit(dynamic_index_in_dim)/squeeze | solution.py:437
  1.8 4.4 %collective-permute-start = (f32[32,8,256]{2,1,0:T(8,128)S(1)}, f32[32,8,256]{2,1,0:T(8,128)S(1)}, u32[]{:S(2)}, u32[]{:S(2)}) collective-permute-start(f32[32,8,256]{2,1,0:T(8,128)S(1)} %dynamic-slice_bitcast_fusion), channel_id=1, source_target_pairs={{0,2},{2,0},{4,6},{6,4},{1,3},{3,1},{5,7},{7,5},{8,10},{10,8},{12,... | collective-permute-start | bytes 786440 | tf_op jit(solution)/shard_map/ppermute | solution.py:391
  6.3 3.1 %collective-permute-start.3 = (f32[32,8,256]{2,1,0:T(8,128)S(1)}, f32[32,8,256]{2,1,0:T(8,128)S(1)}, u32[]{:S(2)}, u32[]{:S(2)}) collective-permute-start(f32[32,8,256]{2,1,0:T(8,128)S(1)} %collective-permute-done.2.refs_4_), channel_id=1, source_target_pairs={{0,2},{2,0},{4,6},{6,4},{1,3},{3,1},{5,7},{7,5},{8,10},{10,8},{12,... | collective-permute-start | bytes 786440 | tf_op jit(solution)/shard_map/ppermute | solution.py:391
  10.4 1.7 %collective-permute-start.4 = (f32[32,8,256]{2,1,0:T(8,128)S(1)}, f32[32,8,256]{2,1,0:T(8,128)S(1)}, u32[]{:S(2)}, u32[]{:S(2)}) collective-permute-start(f32[32,8,256]{2,1,0:T(8,128)S(1)} %get-tuple-element.19), channel_id=1, source_target_pairs={{0,4},{2,6},{4,0},{6,2},{8,12},{10,14},{12,8},{14,10},{16,20},{18,... | collective-permute-start | bytes 786440 | tf_op jit(solution)/shard_map/ppermute | solution.py:386
  12.1 1.6 %collective-permute-start.5 = (f32[2,14,8,256]{3,2,1,0:T(8,128)S(1)}, f32[2,14,8,256]{3,2,1,0:T(8,128)S(1)}, u32[]{:S(2)}, u32[]{:S(2)}) collective-permute-start(f32[2,14,8,256]{3,2,1,0:T(8,128)S(1)} %get-tuple-element.20), channel_id=1, source_target_pairs={{0,8},{2,10},{4,12},{6,14},{8,0},{10,2},{12,4},{14,6},{16,24},{18,... | collective-permute-start | bytes 688136 | tf_op jit(solution)/shard_map/ppermute | solution.py:386
  14.3 4.3 %collective-permute-start.7 = (f32[12,8,256]{2,1,0:T(8,128)S(1)}, f32[12,8,256]{2,1,0:T(8,128)S(1)}, u32[]{:S(2)}, u32[]{:S(2)}) collective-permute-start(f32[12,8,256]{2,1,0:T(8,128)S(1)} %get-tuple-element.22), channel_id=1, source_target_pairs={{0,12},{2,14},{4,8},{6,10},{8,4},{10,6},{12,0},{14,2},{16,28},{18,... | collective-permute-start | bytes 294920 | tf_op jit(solution)/shard_map/ppermute | solution.py:386
  18.6 3.1 %collective-permute-done.7.refs_9_.refs_15_ = f32[12,8,256]{2,1,0:T(8,128)S(1)} collective-permute-done((f32[12,8,256]{2,1,0:T(8,128)S(1)}, f32[12,8,256]{2,1,0:T(8,128)S(1)}, u32[]{:S(2)}, u32[]{:S(2)}) %collective-permute-start.7) | collective-permute-done | bytes 98336 | tf_op jit(solution)/shard_map/ppermute | solution.py:386
  22.4 5.1 %first_round.1 = (f32[32,8,256]{2,1,0:T(8,128)S(1)}, f32[32,8,256]{2,1,0:T(8,128)S(1)}, f32[32,8,256]{2,1,0:T(8,128)S(1)}, f32[2,8,8,256]{3,2,1,0:T(8,128)S(1)},...) custom-call(f32[2,32,8,256]{3,2,1,0:T(8,128)S(1)} %copy-done, ...), custom_call_target="tpu_custom_call" | custom-call | tf_op jit(solution)/shard_map/first_round/pallas_call | solution.py:460
  27.5 1.7 %collective-permute-start.9 = (f32[32,8,256]{2,1,0:T(8,128)S(1)}, f32[32,8,256]{2,1,0:T(8,128)S(1)}, u32[]{:S(2)}, u32[]{:S(2)}) collective-permute-start(f32[32,8,256]{2,1,0:T(8,128)S(1)} %get-tuple-element.26), channel_id=1, source_target_pairs={{0,4},{2,6},{4,0},{6,2},{8,12},{10,14},{12,8},{14,10},{16,20},{18,... | collective-permute-start | bytes 786440 | tf_op jit(solution)/shard_map/ppermute | solution.py:386
  29.2 8.2 %collective-permute-start.10 = (f32[2,8,8,256]{3,2,1,0:T(8,128)S(1)}, f32[2,8,8,256]{3,2,1,0:T(8,128)S(1)}, u32[]{:S(2)}, u32[]{:S(2)}) collective-permute-start(f32[2,8,8,256]{3,2,1,0:T(8,128)S(1)} %get-tuple-element.27), channel_id=1, source_target_pairs={{0,8},{2,10},{4,12},{6,14},{8,0},{10,2},{12,4},{14,6},{16,24},{18,... | collective-permute-start | bytes 393224 | tf_op jit(solution)/shard_map/ppermute | solution.py:386
  38.1 2.7 %collective-permute-start.12 = (f32[7,8,256]{2,1,0:T(8,128)S(1)}, f32[7,8,256]{2,1,0:T(8,128)S(1)}, u32[]{:S(2)}, u32[]{:S(2)}) collective-permute-start(f32[7,8,256]{2,1,0:T(8,128)S(1)} %get-tuple-element.29), channel_id=1, source_target_pairs={{0,12},{2,14},{4,8},{6,10},{8,4},{10,6},{12,0},{14,2},{16,28},{18,... | collective-permute-start | bytes 172040 | tf_op jit(solution)/shard_map/ppermute | solution.py:386
  41.5 1.8 %collective-permute-done.12.refs_11_ = f32[7,8,256]{2,1,0:T(8,128)S(1)} collective-permute-done((f32[7,8,256]{2,1,0:T(8,128)S(1)}, f32[7,8,256]{2,1,0:T(8,128)S(1)}, u32[]{:S(2)}, u32[]{:S(2)}) %collective-permute-start.12) | collective-permute-done | bytes 57376 | tf_op jit(solution)/shard_map/ppermute | solution.py:386
  43.3 5.0 %second_round.1 = (f32[32,8,256]{2,1,0:T(8,128)S(1)}, f32[32,8,256]{2,1,0:T(8,128)S(1)}) custom-call(f32[2,32,8,256]{3,2,1,0:T(8,128)S(1)} %copy-done, f32[32,8,256]{2,1,0:T(8,128)S(1)} %collective-permute-done.received.refs_1_, f32[32,8,256]{2,1,0:T(8,128)S(1)} %copy-done.1, f32[32,8,256]{2,1,0:T(8,128)S(1)} %collective-permute-done.1.received_potential.refs_3_, ...), custom_call_target="tpu_custom_call" | custom-call | tf_op jit(solution)/shard_map/second_round/pallas_call | solution.py:470
  48.4 1.6 %collective-permute-start.14 = (f32[32,8,256]{2,1,0:T(8,128)S(1)}, f32[32,8,256]{2,1,0:T(8,128)S(1)}, u32[]{:S(2)}, u32[]{:S(2)}) collective-permute-start(f32[32,8,256]{2,1,0:T(8,128)S(1)} %get-tuple-element.32), channel_id=1, source_target_pairs={{0,2},{2,0},{4,6},{6,4},{1,3},{3,1},{5,7},{7,5},{8,10},{10,8},{12,... | collective-permute-start | bytes 786440 | tf_op jit(solution)/shard_map/ppermute | solution.py:391
  50.5 6.4 %collective-permute-done.16.refs_3_.refs_5_ = f32[32,8,256]{2,1,0:T(8,128)S(1)} collective-permute-done((f32[32,8,256]{2,1,0:T(8,128)S(1)}, f32[32,8,256]{2,1,0:T(8,128)S(1)}, u32[]{:S(2)}, u32[]{:S(2)}) %collective-permute-start.16) | collective-permute-done | bytes 262176 | tf_op jit(solution)/shard_map/ppermute | solution.py:489
  56.9 5.7 %collective-permute-done.15.refs_2_.refs_4_ = f32[32,8,256]{2,1,0:T(8,128)S(1)} collective-permute-done((f32[32,8,256]{2,1,0:T(8,128)S(1)}, f32[32,8,256]{2,1,0:T(8,128)S(1)}, u32[]{:S(2)}, u32[]{:S(2)}) %collective-permute-start.15) | collective-permute-done | bytes 262176 | tf_op jit(solution)/shard_map/ppermute | solution.py:488
  63.0 1.1 %collective-permute-start.19 = (f32[8,128]{1,0:T(8,128)S(1)}, f32[8,128]{1,0:T(8,128)S(1)}, u32[]{:S(2)}, u32[]{:S(2)}) collective-permute-start(f32[8,128]{1,0:T(8,128)S(1)} %correlation.1), channel_id=1, source_target_pairs={{0,6},{2,4},{4,2},{6,0},{1,7},{3,5},{5,3},{7,1},{8,14},{10,12},{12... | collective-permute-start | bytes 12296 | tf_op jit(solution)/shard_map/ppermute | solution.py:416
  64.9 1.2 %collective-permute-done.19 = f32[8,128]{1,0:T(8,128)S(1)} collective-permute-done((f32[8,128]{1,0:T(8,128)S(1)}, f32[8,128]{1,0:T(8,128)S(1)}, u32[]{:S(2)}, u32[]{:S(2)}) %collective-permute-start.19) | collective-permute-done | bytes 4128 | tf_op jit(solution)/shard_map/ppermute | solution.py:416
  66.1 1.6 %collective-permute-done.18 = f32[8,128]{1,0:T(8,128)S(1)} collective-permute-done((f32[8,128]{1,0:T(8,128)S(1)}, f32[8,128]{1,0:T(8,128)S(1)}, u32[]{:S(2)}, u32[]{:S(2)}) %collective-permute-start.18) | collective-permute-done | bytes 4128 | tf_op jit(solution)/shard_map/ppermute | solution.py:416
  67.7 1.6 %collective-permute-start.22 = (f32[8,128]{1,0:T(8,128)S(1)}, f32[8,128]{1,0:T(8,128)S(1)}, u32[]{:S(2)}, u32[]{:S(2)}) collective-permute-start(f32[8,128]{1,0:T(8,128)S(1)} %add_add_fusion.1), channel_id=1, source_target_pairs={{0,24},{8,16},{16,8},{24,0},{1,25},{9,17},{17,9},{25,1},{2,26},{10... | collective-permute-start | bytes 12296 | tf_op jit(solution)/shard_map/ppermute | solution.py:416
  69.3 3.9 %collective-permute-start.21 = (f32[8,128]{1,0:T(8,128)S(1)}, f32[8,128]{1,0:T(8,128)S(1)}, u32[]{:S(2)}, u32[]{:S(2)}) collective-permute-start(f32[8,128]{1,0:T(8,128)S(1)} %add_add_fusion.1), channel_id=1, source_target_pairs={{0,16},{8,24},{16,0},{24,8},{1,17},{9,25},{17,1},{25,9},{2,18},{10... | collective-permute-start | bytes 12296 | tf_op jit(solution)/shard_map/ppermute | solution.py:416
  73.3 1.5 %collective-permute-done.21 = f32[8,128]{1,0:T(8,128)S(1)} collective-permute-done((f32[8,128]{1,0:T(8,128)S(1)}, f32[8,128]{1,0:T(8,128)S(1)}, u32[]{:S(2)}, u32[]{:S(2)}) %collective-permute-start.21) | collective-permute-done | bytes 4128 | tf_op jit(solution)/shard_map/ppermute | solution.py:416
  74.8 2.0 %collective-permute-done.20 = f32[8,128]{1,0:T(8,128)S(1)} collective-permute-done((f32[8,128]{1,0:T(8,128)S(1)}, f32[8,128]{1,0:T(8,128)S(1)}, u32[]{:S(2)}, u32[]{:S(2)}) %collective-permute-start.20) | collective-permute-done | bytes 4128 | tf_op jit(solution)/shard_map/ppermute | solution.py:416
  76.8 1.7 %basis.1 = f32[2,32,8,256]{3,2,1,0:T(8,128)} custom-call(f32[8,128]{1,0:T(8,128)S(1)} %add_add_fusion.refs_0_, s32[4]{0:T(128)S(1)} %copy-done.2, f32[32,8,256]{2,1,0:T(8,128)S(1)} %get-tuple-element.31.refs_0_.refs_2_, f32[32,8,256]{2,1,0:T(8,128)S(1)} %collective-permute-done.14.refs_1_.refs_3_, f32[32,8,256]{2,1,0:T(8,128)S(1)} %collective-permute-done.15.refs_2_.refs_4_, ...), custom_call_target="tpu_custom_call" | custom-call | tf_op jit(solution)/shard_map/basis/pallas_call | solution.py:499
  (36 shorter events, 6.4 us)
Async XLA Ops:
  0.0 9.4 %copy-start = (f32[2,32,8,256]{3,2,1,0:T(8,128)S(1)}, f32[2,32,8,256]{3,2,1,0:T(8,128)}, u32[]{:S(2)}) copy-start(f32[2,32,8,256]{3,2,1,0:T(8,128)} %refs_0_.3) | copy-start | bytes 1572868
  0.0 6.3 %collective-permute-start.2 = (f32[32,8,256]{2,1,0:T(8,128)}, f32[32,8,256]{2,1,0:T(8,128)S(1)}, u32[]{:S(2)}, u32[]{:S(2)}) collective-permute-start(f32[32,8,256]{2,1,0:T(8,128)} %refs_2_.3), channel_id=1, source_target_pairs={{2,4},{4,2},{3,5},{5,3},{10,12},{12,10},{11,13},{13,11},{18,20},{2... | collective-permute-start | bytes 786440 | tf_op jit(solution)/shard_map/ppermute | solution.py:397
  1.8 7.6 %collective-permute-start = (f32[32,8,256]{2,1,0:T(8,128)S(1)}, f32[32,8,256]{2,1,0:T(8,128)S(1)}, u32[]{:S(2)}, u32[]{:S(2)}) collective-permute-start(f32[32,8,256]{2,1,0:T(8,128)S(1)} %dynamic-slice_bitcast_fusion), channel_id=1, source_target_pairs={{0,2},{2,0},{4,6},{6,4},{1,3},{3,1},{5,7},{7,5},{8,10},{10,8},{12,... | collective-permute-start | bytes 786440 | tf_op jit(solution)/shard_map/ppermute | solution.py:391
  6.2 3.2 %collective-permute-start.1 = (f32[32,8,256]{2,1,0:T(8,128)}, f32[32,8,256]{2,1,0:T(8,128)S(1)}, u32[]{:S(2)}, u32[]{:S(2)}) collective-permute-start(f32[32,8,256]{2,1,0:T(8,128)} %refs_2_.3), channel_id=1, source_target_pairs={{0,2},{2,0},{4,6},{6,4},{1,3},{3,1},{5,7},{7,5},{8,10},{10,8},{12,... | collective-permute-start | bytes 786440 | tf_op jit(solution)/shard_map/ppermute | solution.py:391
  6.3 16.2 %collective-permute-start.3 = (f32[32,8,256]{2,1,0:T(8,128)S(1)}, f32[32,8,256]{2,1,0:T(8,128)S(1)}, u32[]{:S(2)}, u32[]{:S(2)}) collective-permute-start(f32[32,8,256]{2,1,0:T(8,128)S(1)} %collective-permute-done.2.refs_4_), channel_id=1, source_target_pairs={{0,2},{2,0},{4,6},{6,4},{1,3},{3,1},{5,7},{7,5},{8,10},{10,8},{12,... | collective-permute-start | bytes 786440 | tf_op jit(solution)/shard_map/ppermute | solution.py:391
  10.4 12.0 %collective-permute-start.4 = (f32[32,8,256]{2,1,0:T(8,128)S(1)}, f32[32,8,256]{2,1,0:T(8,128)S(1)}, u32[]{:S(2)}, u32[]{:S(2)}) collective-permute-start(f32[32,8,256]{2,1,0:T(8,128)S(1)} %get-tuple-element.19), channel_id=1, source_target_pairs={{0,4},{2,6},{4,0},{6,2},{8,12},{10,14},{12,8},{14,10},{16,20},{18,... | collective-permute-start | bytes 786440 | tf_op jit(solution)/shard_map/ppermute | solution.py:386
  12.1 10.3 %collective-permute-start.5 = (f32[2,14,8,256]{3,2,1,0:T(8,128)S(1)}, f32[2,14,8,256]{3,2,1,0:T(8,128)S(1)}, u32[]{:S(2)}, u32[]{:S(2)}) collective-permute-start(f32[2,14,8,256]{3,2,1,0:T(8,128)S(1)} %get-tuple-element.20), channel_id=1, source_target_pairs={{0,8},{2,10},{4,12},{6,14},{8,0},{10,2},{12,4},{14,6},{16,24},{18,... | collective-permute-start | bytes 688136 | tf_op jit(solution)/shard_map/ppermute | solution.py:386
  13.7 8.7 %collective-permute-start.6 = (f32[2,14,8,256]{3,2,1,0:T(8,128)S(1)}, f32[2,14,8,256]{3,2,1,0:T(8,128)S(1)}, u32[]{:S(2)}, u32[]{:S(2)}) collective-permute-start(f32[2,14,8,256]{3,2,1,0:T(8,128)S(1)} %get-tuple-element.21), channel_id=1, source_target_pairs={{8,16},{10,18},{12,20},{14,22},{16,8},{18,10},{20,12},{22,14},{9,1... | collective-permute-start | bytes 688136 | tf_op jit(solution)/shard_map/ppermute | solution.py:386
  14.3 7.4 %collective-permute-start.7 = (f32[12,8,256]{2,1,0:T(8,128)S(1)}, f32[12,8,256]{2,1,0:T(8,128)S(1)}, u32[]{:S(2)}, u32[]{:S(2)}) collective-permute-start(f32[12,8,256]{2,1,0:T(8,128)S(1)} %get-tuple-element.22), channel_id=1, source_target_pairs={{0,12},{2,14},{4,8},{6,10},{8,4},{10,6},{12,0},{14,2},{16,28},{18,... | collective-permute-start | bytes 294920 | tf_op jit(solution)/shard_map/ppermute | solution.py:386
  21.7 0.7 collective-permute-start.8
  27.5 15.8 %collective-permute-start.9 = (f32[32,8,256]{2,1,0:T(8,128)S(1)}, f32[32,8,256]{2,1,0:T(8,128)S(1)}, u32[]{:S(2)}, u32[]{:S(2)}) collective-permute-start(f32[32,8,256]{2,1,0:T(8,128)S(1)} %get-tuple-element.26), channel_id=1, source_target_pairs={{0,4},{2,6},{4,0},{6,2},{8,12},{10,14},{12,8},{14,10},{16,20},{18,... | collective-permute-start | bytes 786440 | tf_op jit(solution)/shard_map/ppermute | solution.py:386
  29.2 14.0 %collective-permute-start.10 = (f32[2,8,8,256]{3,2,1,0:T(8,128)S(1)}, f32[2,8,8,256]{3,2,1,0:T(8,128)S(1)}, u32[]{:S(2)}, u32[]{:S(2)}) collective-permute-start(f32[2,8,8,256]{3,2,1,0:T(8,128)S(1)} %get-tuple-element.27), channel_id=1, source_target_pairs={{0,8},{2,10},{4,12},{6,14},{8,0},{10,2},{12,4},{14,6},{16,24},{18,... | collective-permute-start | bytes 393224 | tf_op jit(solution)/shard_map/ppermute | solution.py:386
  37.5 5.8 %collective-permute-start.11 = (f32[2,8,8,256]{3,2,1,0:T(8,128)S(1)}, f32[2,8,8,256]{3,2,1,0:T(8,128)S(1)}, u32[]{:S(2)}, u32[]{:S(2)}) collective-permute-start(f32[2,8,8,256]{3,2,1,0:T(8,128)S(1)} %get-tuple-element.28), channel_id=1, source_target_pairs={{8,16},{10,18},{12,20},{14,22},{16,8},{18,10},{20,12},{22,14},{9,1... | collective-permute-start | bytes 393224 | tf_op jit(solution)/shard_map/ppermute | solution.py:386
  38.1 5.1 %collective-permute-start.12 = (f32[7,8,256]{2,1,0:T(8,128)S(1)}, f32[7,8,256]{2,1,0:T(8,128)S(1)}, u32[]{:S(2)}, u32[]{:S(2)}) collective-permute-start(f32[7,8,256]{2,1,0:T(8,128)S(1)} %get-tuple-element.29), channel_id=1, source_target_pairs={{0,12},{2,14},{4,8},{6,10},{8,4},{10,6},{12,0},{14,2},{16,28},{18,... | collective-permute-start | bytes 172040 | tf_op jit(solution)/shard_map/ppermute | solution.py:386
  40.8 2.4 %collective-permute-start.13 = (f32[7,8,256]{2,1,0:T(8,128)S(1)}, f32[7,8,256]{2,1,0:T(8,128)S(1)}, u32[]{:S(2)}, u32[]{:S(2)}) collective-permute-start(f32[7,8,256]{2,1,0:T(8,128)S(1)} %get-tuple-element.30), channel_id=1, source_target_pairs={{8,20},{10,22},{12,16},{14,18},{16,12},{18,14},{20,8},{22,10},{9,2... | collective-permute-start | bytes 172040 | tf_op jit(solution)/shard_map/ppermute | solution.py:386
  48.3 8.6 %collective-permute-start.16 = (f32[32,8,256]{2,1,0:T(8,128)S(1)}, f32[32,8,256]{2,1,0:T(8,128)S(1)}, u32[]{:S(2)}, u32[]{:S(2)}) collective-permute-start(f32[32,8,256]{2,1,0:T(8,128)S(1)} %get-tuple-element.32), channel_id=1, source_target_pairs={{0,3},{1,2},{2,1},{3,0},{4,7},{5,6},{6,5},{7,4},{8,11},{9,10},{10,... | collective-permute-start | bytes 786440 | tf_op jit(solution)/shard_map/ppermute | solution.py:489
  48.4 8.5 %collective-permute-start.14 = (f32[32,8,256]{2,1,0:T(8,128)S(1)}, f32[32,8,256]{2,1,0:T(8,128)S(1)}, u32[]{:S(2)}, u32[]{:S(2)}) collective-permute-start(f32[32,8,256]{2,1,0:T(8,128)S(1)} %get-tuple-element.32), channel_id=1, source_target_pairs={{0,2},{2,0},{4,6},{6,4},{1,3},{3,1},{5,7},{7,5},{8,10},{10,8},{12,... | collective-permute-start | bytes 786440 | tf_op jit(solution)/shard_map/ppermute | solution.py:391
  50.0 12.6 %collective-permute-start.15 = (f32[32,8,256]{2,1,0:T(8,128)S(1)}, f32[32,8,256]{2,1,0:T(8,128)S(1)}, u32[]{:S(2)}, u32[]{:S(2)}) collective-permute-start(f32[32,8,256]{2,1,0:T(8,128)S(1)} %get-tuple-element.31.refs_0_.refs_2_), channel_id=1, source_target_pairs={{0,1},{1,0},{2,3},{3,2},{4,5},{5,4},{6,7},{7,6},{8,9},{9,8},{10,11... | collective-permute-start | bytes 786440 | tf_op jit(solution)/shard_map/ppermute | solution.py:488
  63.0 3.1 %collective-permute-start.19 = (f32[8,128]{1,0:T(8,128)S(1)}, f32[8,128]{1,0:T(8,128)S(1)}, u32[]{:S(2)}, u32[]{:S(2)}) collective-permute-start(f32[8,128]{1,0:T(8,128)S(1)} %correlation.1), channel_id=1, source_target_pairs={{0,6},{2,4},{4,2},{6,0},{1,7},{3,5},{5,3},{7,1},{8,14},{10,12},{12... | collective-permute-start | bytes 12296 | tf_op jit(solution)/shard_map/ppermute | solution.py:416
  64.1 3.6 %collective-permute-start.18 = (f32[8,128]{1,0:T(8,128)S(1)}, f32[8,128]{1,0:T(8,128)S(1)}, u32[]{:S(2)}, u32[]{:S(2)}) collective-permute-start(f32[8,128]{1,0:T(8,128)S(1)} %correlation.1), channel_id=1, source_target_pairs={{0,4},{2,6},{4,0},{6,2},{1,5},{3,7},{5,1},{7,3},{8,12},{10,14},{12... | collective-permute-start | bytes 12296 | tf_op jit(solution)/shard_map/ppermute | solution.py:416
  64.7 3.0 %collective-permute-start.17 = (f32[8,128]{1,0:T(8,128)S(1)}, f32[8,128]{1,0:T(8,128)S(1)}, u32[]{:S(2)}, u32[]{:S(2)}) collective-permute-start(f32[8,128]{1,0:T(8,128)S(1)} %correlation.1), channel_id=1, source_target_pairs={{0,2},{2,0},{4,6},{6,4},{1,3},{3,1},{5,7},{7,5},{8,10},{10,8},{12,... | collective-permute-start | bytes 12296 | tf_op jit(solution)/shard_map/ppermute | solution.py:416
  67.7 5.6 %collective-permute-start.22 = (f32[8,128]{1,0:T(8,128)S(1)}, f32[8,128]{1,0:T(8,128)S(1)}, u32[]{:S(2)}, u32[]{:S(2)}) collective-permute-start(f32[8,128]{1,0:T(8,128)S(1)} %add_add_fusion.1), channel_id=1, source_target_pairs={{0,24},{8,16},{16,8},{24,0},{1,25},{9,17},{17,9},{25,1},{2,26},{10... | collective-permute-start | bytes 12296 | tf_op jit(solution)/shard_map/ppermute | solution.py:416
  69.3 5.5 %collective-permute-start.21 = (f32[8,128]{1,0:T(8,128)S(1)}, f32[8,128]{1,0:T(8,128)S(1)}, u32[]{:S(2)}, u32[]{:S(2)}) collective-permute-start(f32[8,128]{1,0:T(8,128)S(1)} %add_add_fusion.1), channel_id=1, source_target_pairs={{0,16},{8,24},{16,0},{24,8},{1,17},{9,25},{17,1},{25,9},{2,18},{10... | collective-permute-start | bytes 12296 | tf_op jit(solution)/shard_map/ppermute | solution.py:416
  73.1 3.6 %collective-permute-start.20 = (f32[8,128]{1,0:T(8,128)S(1)}, f32[8,128]{1,0:T(8,128)S(1)}, u32[]{:S(2)}, u32[]{:S(2)}) collective-permute-start(f32[8,128]{1,0:T(8,128)S(1)} %add_add_fusion.1), channel_id=1, source_target_pairs={{0,8},{8,0},{16,24},{24,16},{1,9},{9,1},{17,25},{25,17},{2,10},{10... | collective-permute-start | bytes 12296 | tf_op jit(solution)/shard_map/ppermute | solution.py:416
  (2 other events, 10.0 us)

commit v3 on v2

--- a/solution.py
+++ b/solution.py
@@ -129,12 +129,13 @@
         target[half, now, body, :] = result
 
 
-def four_steps(a, b, local, along_z, chip, along_x):
+def four_steps(a, b, local, along_z):
     extent = a.shape[1]
     height = a.shape[2] - 2 * PAD
     for buffer in (a, b):
         for rows in (slice(0, PAD), slice(PAD + height, PAD + height + PAD)):
             buffer[:, :, rows, :] = jnp.zeros((2, extent, PAD, LANES), jnp.float32)
+    outside_is_zero(a)
     buffers = (a, b)
     for step in range(STEPS):
         source, target = buffers[step % 2], buffers[(step + 1) % 2]
@@ -147,24 +148,24 @@
 
         lax.fori_loop(0, blocks, block, 0, unroll=2)
         if step < STEPS - 1:
-            @pl.when(along_x == 0)
-            def _():
-                target[:, :HALO] = jnp.zeros((2, HALO) + target.shape[2:], jnp.float32)
-
-            @pl.when(along_x == lax.axis_size("gx") - 1)
-            def _():
-                target[:, extent - HALO :] = jnp.zeros((2, HALO) + target.shape[2:], jnp.float32)
-
-            if not one_sided():
-                zero = jnp.zeros((2, extent, 8, LANES), jnp.float32)
-
-                @pl.when(chip == 0)
-                def _():
-                    target[:, :, PAD : PAD + 8, :] = zero
-
-                @pl.when(chip == lax.axis_size("gy") // 2 - 1)
-                def _():
-                    target[:, :, PAD + 24 : PAD + 32, :] = zero
+            outside_is_zero(target)
+
+
+def outside_is_zero(window):
+    _, chip, along_x = place()
+    extent = window.shape[1]
+
+    def clear(where, planes, rows=slice(None)):
+        @pl.when(where)
+        def _():
+            region = window[:, planes, rows, :]
+            window[:, planes, rows, :] = jnp.zeros_like(region)
+
+    clear(along_x == 0, slice(0, HALO))
+    clear(along_x == lax.axis_size("gx") - 1, slice(extent - HALO, extent))
+    if not one_sided():
+        clear(chip == 0, slice(None), slice(PAD, PAD + 8))
+        clear(chip == lax.axis_size("gy") // 2 - 1, slice(None), slice(PAD + 24, PAD + 32))
 
 
 def edge_is_own(core, chip, phase):
@@ -233,7 +234,7 @@
         [c.at[: HALO - 1] for c in corners],
     )
     fill_local(local, potential, received_potential, edge, passed, x_halos, corners)
-    four_steps(a, b, local, z_matrix(depth), chip, along_x)
+    four_steps(a, b, local, z_matrix(depth))
     y_out, x_out, d_out = outs[:count], outs[count : count + 2], outs[count + 2 :]
     slots = own_slots(core, chip)
     for half in range(2):
@@ -270,7 +271,7 @@
     width, depth = potential.shape[0], potential.shape[2]
     fill(a, (own, other), x_halos, y_halos, corners)
     fill_local(local, potential, received_potential, edge, passed, p_x_halos, p_corners)
-    four_steps(a, b, local, z_matrix(depth), chip, along_x)
+    four_steps(a, b, local, z_matrix(depth))
     start = (orbitals.at[core], received)
     outs = (keep, give)
     for t, slot in enumerate(own_slots(core, chip)):
@@ -381,7 +382,9 @@
         for y in range(ny):
             to_x = x if x_phase is None else partner(x, x_phase, nx)
             chip = y // 2 if y_phase is None else partner(y // 2, y_phase, ny // 2)
-            if to_x is not None and chip is not None:
+            if to_x is None or chip is None:
+                pairs.append((x * ny + y, x * ny + (y ^ 1)))
+            else:
                 pairs.append((x * ny + y, to_x * ny + chip * 2 + y % 2))
     return lax.ppermute(value, ("gx", "gy"), pairs)
 
@@ -392,9 +395,16 @@
 
 
 def face(value):
-    count = lax.axis_size("gy")
-    pairs = [(y, partner(y, 1, count)) for y in range(count)]
-    return lax.ppermute(value, "gy", [p for p in pairs if p[1] is not None])
+    count, bands = lax.axis_size("gy"), lax.axis_size("band")
+    pairs = []
+    for y in range(count):
+        for band in range(bands):
+            to = partner(y, 1, count)
+            if to is not None:
+                pairs.append((y * bands + band, to * bands + band))
+            elif bands % 2 == 0:
+                pairs.append((y * bands + band, y * bands + (band ^ 1)))
+    return lax.ppermute(value, ("gy", "band"), pairs)
 
 
 def exchange(payloads):

time: 78.7 us -> 72.5 us (0.921)
  starting transfers between devices: 40.9 us -> 27.9 us
  waiting for transfers between devices: 23.3 us -> 30.2 us
    ppermute x4, starting transfers between devices: 9.17 us -> 1.51 us  [swap(): return lax.ppermute(value, 'gy', [(y, y ^ 1) for y in range(count)])]
    ppermute x10, starting transfers between devices: 22.8 us -> 15.7 us  [meet(): return lax.ppermute(value, ('gx', 'gy'), pairs)]
    ppermute x10, waiting for transfers between devices: 4.89 us -> 9.36 us  [meet(): return lax.ppermute(value, ('gx', 'gy'), pairs)]
    ppermute x1, waiting for transfers between devices: 0.01 us -> 3.01 us  [face(): return lax.ppermute(value, ('gy', 'band'), pairs)]
    ppermute x1, starting transfers between devices: 0.8 us -> 2.94 us  [face(): return lax.ppermute(value, ('gy', 'band'), pairs)]
    ppermute x6, starting transfers between devices: 7.48 us -> 6.38 us  [of(): return lax.ppermute(value, axis, [(i, i ^ step) for i in range(count)])]
  transfers between devices with their start and end apart: 23 -> 23, of which waited for: 8 -> 11; matrix products, arithmetic and copies ran while one was open for 1% -> 1% of each run, Pallas kernels for 0% -> 0%
where the time goes in v3:
time: 72.5 us; the launch traced here: 72.4 us
  waiting for transfers between devices  30.2 us (42%)
  starting transfers between devices  27.9 us (38%)
  Pallas kernels  12.2 us (17%)
  local copies, waits for them, and re-layouts  1.92 us (3%)
    ppermute x10, starting transfers between devices, meet(): return lax.ppermute(value, ('gx', 'gy'), pairs)  15.7 us
    ppermute x10, waiting for transfers between devices, meet(): return lax.ppermute(value, ('gx', 'gy'), pairs)  9.36 us
    ppermute x1, waiting for transfers between devices, per_device(): slots.append(lax.ppermute(give, ('gy', 'band'), crossed))  6.42 us
    ppermute x6, starting transfers between devices, of(): return lax.ppermute(value, axis, [(i, i ^ step) for i in range(count)])  6.38 us
    ppermute x6, waiting for transfers between devices, of(): return lax.ppermute(value, axis, [(i, i ^ step) for i in range(count)])  5.76 us
    ppermute x1, waiting for transfers between devices, per_device(): slots.append(lax.ppermute(keep, ('gy', 'band'), same))  5.66 us
    pallas_call x1, Pallas kernels, per_device(): pl.pallas_call(first_kernel, out_shape=[struct(*tile)] * 2 + payloads(HAL...  5.1 us
    pallas_call x1, Pallas kernels, per_device(): pl.pallas_call(second_kernel, out_shape=[struct(*tile)] * 2, in_specs=[VM...  5.07 us
  transfers between devices with their start and end apart: 23, of which 11 were waited for; matrix products, arithmetic and copies ran while one was open for 1% of the time, Pallas kernels for 0%

profile of v3, /device:TPU:0, one launch (start us, length us, event | category | flops | bytes accessed | tf_op | source)
XLA Modules:
  0.0 72.4 jit_solution(1737561315745359761)
XLA Ops:
  0.0 2.9 %collective-permute-start.2 = (f32[32,8,256]{2,1,0:T(8,128)}, f32[32,8,256]{2,1,0:T(8,128)S(1)}, u32[]{:S(2)}, u32[]{:S(2)}) collective-permute-start(f32[32,8,256]{2,1,0:T(8,128)} %refs_2_.3), channel_id=1, source_target_pairs={{0,1},{1,0},{2,4},{3,5},{4,2},{5,3},{6,7},{7,6},{8,9},{9,8},{10,12... | collective-permute-start | bytes 786440 | tf_op jit(solution)/shard_map/ppermute | solution.py:407
  2.9 1.0 %dynamic-slice_bitcast_fusion = f32[32,8,256]{2,1,0:T(8,128)S(1)} fusion(f32[2,32,8,256]{3,2,1,0:T(8,128)} %refs_0_.3, s32[]{:T(128)S(6)} %select_n.12), kind=kLoop, calls=%fused_computation | loop fusion | bytes 524292 | tf_op jit(solution)/shard_map/jit(dynamic_index_in_dim)/squeeze | solution.py:447
  4.5 3.0 %collective-permute-done.2.refs_4_ = f32[32,8,256]{2,1,0:T(8,128)S(1)} collective-permute-done((f32[32,8,256]{2,1,0:T(8,128)}, f32[32,8,256]{2,1,0:T(8,128)S(1)}, u32[]{:S(2)}, u32[]{:S(2)}) %collective-permute-start.2) | collective-permute-done | bytes 262176 | tf_op jit(solution)/shard_map/ppermute | solution.py:407
  7.6 0.9 %copy-done.1 = f32[32,8,256]{2,1,0:T(8,128)S(1)} copy-done((f32[32,8,256]{2,1,0:T(8,128)S(1)}, f32[32,8,256]{2,1,0:T(8,128)}, u32[]{:S(2)}) %copy-start.1) | copy-done | bytes 262168
  8.6 1.4 %collective-permute-start.4 = (f32[32,8,256]{2,1,0:T(8,128)S(1)}, f32[32,8,256]{2,1,0:T(8,128)S(1)}, u32[]{:S(2)}, u32[]{:S(2)}) collective-permute-start(f32[32,8,256]{2,1,0:T(8,128)S(1)} %get-tuple-element.19), channel_id=1, source_target_pairs={{0,4},{2,6},{4,0},{6,2},{8,12},{10,14},{12,8},{14,10},{16,20},{18,... | collective-permute-start | bytes 786440 | tf_op jit(solution)/shard_map/ppermute | solution.py:389
  10.1 1.6 %collective-permute-start.5 = (f32[2,14,8,256]{3,2,1,0:T(8,128)S(1)}, f32[2,14,8,256]{3,2,1,0:T(8,128)S(1)}, u32[]{:S(2)}, u32[]{:S(2)}) collective-permute-start(f32[2,14,8,256]{3,2,1,0:T(8,128)S(1)} %get-tuple-element.20), channel_id=1, source_target_pairs={{0,8},{2,10},{4,12},{6,14},{8,0},{10,2},{12,4},{14,6},{16,24},{18,... | collective-permute-start | bytes 688136 | tf_op jit(solution)/shard_map/ppermute | solution.py:389
  11.7 3.7 %collective-permute-start.7 = (f32[12,8,256]{2,1,0:T(8,128)S(1)}, f32[12,8,256]{2,1,0:T(8,128)S(1)}, u32[]{:S(2)}, u32[]{:S(2)}) collective-permute-start(f32[12,8,256]{2,1,0:T(8,128)S(1)} %get-tuple-element.22), channel_id=1, source_target_pairs={{0,12},{2,14},{4,8},{6,10},{8,4},{10,6},{12,0},{14,2},{16,28},{18,... | collective-permute-start | bytes 294920 | tf_op jit(solution)/shard_map/ppermute | solution.py:389
  15.3 4.9 %collective-permute-done.7.refs_9_.refs_15_ = f32[12,8,256]{2,1,0:T(8,128)S(1)} collective-permute-done((f32[12,8,256]{2,1,0:T(8,128)S(1)}, f32[12,8,256]{2,1,0:T(8,128)S(1)}, u32[]{:S(2)}, u32[]{:S(2)}) %collective-permute-start.7) | collective-permute-done | bytes 98336 | tf_op jit(solution)/shard_map/ppermute | solution.py:389
  20.3 1.3 %collective-permute-done.8.refs_10_.refs_16_ = f32[12,8,256]{2,1,0:T(8,128)S(1)} collective-permute-done((f32[12,8,256]{2,1,0:T(8,128)S(1)}, f32[12,8,256]{2,1,0:T(8,128)S(1)}, u32[]{:S(2)}, u32[]{:S(2)}) %collective-permute-start.8) | collective-permute-done | bytes 98336 | tf_op jit(solution)/shard_map/ppermute | solution.py:389
  21.6 5.1 %first_round.1 = (f32[32,8,256]{2,1,0:T(8,128)S(1)}, f32[32,8,256]{2,1,0:T(8,128)S(1)}, f32[32,8,256]{2,1,0:T(8,128)S(1)}, f32[2,8,8,256]{3,2,1,0:T(8,128)S(1)},...) custom-call(f32[2,32,8,256]{3,2,1,0:T(8,128)S(1)} %copy-done, ...), custom_call_target="tpu_custom_call" | custom-call | tf_op jit(solution)/shard_map/first_round/pallas_call | solution.py:470
  26.7 1.1 %collective-permute-start.9 = (f32[32,8,256]{2,1,0:T(8,128)S(1)}, f32[32,8,256]{2,1,0:T(8,128)S(1)}, u32[]{:S(2)}, u32[]{:S(2)}) collective-permute-start(f32[32,8,256]{2,1,0:T(8,128)S(1)} %get-tuple-element.26), channel_id=1, source_target_pairs={{0,4},{2,6},{4,0},{6,2},{8,12},{10,14},{12,8},{14,10},{16,20},{18,... | collective-permute-start | bytes 786440 | tf_op jit(solution)/shard_map/ppermute | solution.py:389
  27.8 5.7 %collective-permute-start.10 = (f32[2,8,8,256]{3,2,1,0:T(8,128)S(1)}, f32[2,8,8,256]{3,2,1,0:T(8,128)S(1)}, u32[]{:S(2)}, u32[]{:S(2)}) collective-permute-start(f32[2,8,8,256]{3,2,1,0:T(8,128)S(1)} %get-tuple-element.27), channel_id=1, source_target_pairs={{0,8},{2,10},{4,12},{6,14},{8,0},{10,2},{12,4},{14,6},{16,24},{18,... | collective-permute-start | bytes 393224 | tf_op jit(solution)/shard_map/ppermute | solution.py:389
  33.6 2.1 %collective-permute-start.12 = (f32[7,8,256]{2,1,0:T(8,128)S(1)}, f32[7,8,256]{2,1,0:T(8,128)S(1)}, u32[]{:S(2)}, u32[]{:S(2)}) collective-permute-start(f32[7,8,256]{2,1,0:T(8,128)S(1)} %get-tuple-element.29), channel_id=1, source_target_pairs={{0,12},{2,14},{4,8},{6,10},{8,4},{10,6},{12,0},{14,2},{16,28},{18,... | collective-permute-start | bytes 172040 | tf_op jit(solution)/shard_map/ppermute | solution.py:389
  35.7 3.1 %collective-permute-done.12.refs_11_ = f32[7,8,256]{2,1,0:T(8,128)S(1)} collective-permute-done((f32[7,8,256]{2,1,0:T(8,128)S(1)}, f32[7,8,256]{2,1,0:T(8,128)S(1)}, u32[]{:S(2)}, u32[]{:S(2)}) %collective-permute-start.12) | collective-permute-done | bytes 57376 | tf_op jit(solution)/shard_map/ppermute | solution.py:389
  38.8 5.1 %second_round.1 = (f32[32,8,256]{2,1,0:T(8,128)S(1)}, f32[32,8,256]{2,1,0:T(8,128)S(1)}) custom-call(f32[2,32,8,256]{3,2,1,0:T(8,128)S(1)} %copy-done, f32[32,8,256]{2,1,0:T(8,128)S(1)} %collective-permute-done.received.refs_1_, f32[32,8,256]{2,1,0:T(8,128)S(1)} %copy-done.1, f32[32,8,256]{2,1,0:T(8,128)S(1)} %collective-permute-done.1.received_potential.refs_3_, ...), custom_call_target="tpu_custom_call" | custom-call | tf_op jit(solution)/shard_map/second_round/pallas_call | solution.py:480
  46.1 6.4 %collective-permute-done.16.refs_3_.refs_5_ = f32[32,8,256]{2,1,0:T(8,128)S(1)} collective-permute-done((f32[32,8,256]{2,1,0:T(8,128)S(1)}, f32[32,8,256]{2,1,0:T(8,128)S(1)}, u32[]{:S(2)}, u32[]{:S(2)}) %collective-permute-start.16) | collective-permute-done | bytes 262176 | tf_op jit(solution)/shard_map/ppermute | solution.py:499
  52.5 5.7 %collective-permute-done.15.refs_2_.refs_4_ = f32[32,8,256]{2,1,0:T(8,128)S(1)} collective-permute-done((f32[32,8,256]{2,1,0:T(8,128)S(1)}, f32[32,8,256]{2,1,0:T(8,128)S(1)}, u32[]{:S(2)}, u32[]{:S(2)}) %collective-permute-start.15) | collective-permute-done | bytes 262176 | tf_op jit(solution)/shard_map/ppermute | solution.py:498
  60.4 1.2 %collective-permute-done.19 = f32[8,128]{1,0:T(8,128)S(1)} collective-permute-done((f32[8,128]{1,0:T(8,128)S(1)}, f32[8,128]{1,0:T(8,128)S(1)}, u32[]{:S(2)}, u32[]{:S(2)}) %collective-permute-start.19) | collective-permute-done | bytes 4128 | tf_op jit(solution)/shard_map/ppermute | solution.py:426
  61.6 1.3 %collective-permute-done.18 = f32[8,128]{1,0:T(8,128)S(1)} collective-permute-done((f32[8,128]{1,0:T(8,128)S(1)}, f32[8,128]{1,0:T(8,128)S(1)}, u32[]{:S(2)}, u32[]{:S(2)}) %collective-permute-start.18) | collective-permute-done | bytes 4128 | tf_op jit(solution)/shard_map/ppermute | solution.py:426
  63.0 2.5 %collective-permute-start.22 = (f32[8,128]{1,0:T(8,128)S(1)}, f32[8,128]{1,0:T(8,128)S(1)}, u32[]{:S(2)}, u32[]{:S(2)}) collective-permute-start(f32[8,128]{1,0:T(8,128)S(1)} %add_add_fusion.1), channel_id=1, source_target_pairs={{0,24},{8,16},{16,8},{24,0},{1,25},{9,17},{17,9},{25,1},{2,26},{10... | collective-permute-start | bytes 12296 | tf_op jit(solution)/shard_map/ppermute | solution.py:426
  65.5 1.5 %collective-permute-start.21 = (f32[8,128]{1,0:T(8,128)S(1)}, f32[8,128]{1,0:T(8,128)S(1)}, u32[]{:S(2)}, u32[]{:S(2)}) collective-permute-start(f32[8,128]{1,0:T(8,128)S(1)} %add_add_fusion.1), channel_id=1, source_target_pairs={{0,16},{8,24},{16,0},{24,8},{1,17},{9,25},{17,1},{25,9},{2,18},{10... | collective-permute-start | bytes 12296 | tf_op jit(solution)/shard_map/ppermute | solution.py:426
  67.4 1.1 %collective-permute-done.22 = f32[8,128]{1,0:T(8,128)S(1)} collective-permute-done((f32[8,128]{1,0:T(8,128)S(1)}, f32[8,128]{1,0:T(8,128)S(1)}, u32[]{:S(2)}, u32[]{:S(2)}) %collective-permute-start.22) | collective-permute-done | bytes 4128 | tf_op jit(solution)/shard_map/ppermute | solution.py:426
  68.5 1.5 %collective-permute-done.21 = f32[8,128]{1,0:T(8,128)S(1)} collective-permute-done((f32[8,128]{1,0:T(8,128)S(1)}, f32[8,128]{1,0:T(8,128)S(1)}, u32[]{:S(2)}, u32[]{:S(2)}) %collective-permute-start.21) | collective-permute-done | bytes 4128 | tf_op jit(solution)/shard_map/ppermute | solution.py:426
  70.7 1.7 %basis.1 = f32[2,32,8,256]{3,2,1,0:T(8,128)} custom-call(f32[8,128]{1,0:T(8,128)S(1)} %add_add_fusion.refs_0_, s32[4]{0:T(128)S(1)} %copy-done.2, f32[32,8,256]{2,1,0:T(8,128)S(1)} %get-tuple-element.31.refs_0_.refs_2_, f32[32,8,256]{2,1,0:T(8,128)S(1)} %collective-permute-done.14.refs_1_.refs_3_, f32[32,8,256]{2,1,0:T(8,128)S(1)} %collective-permute-done.15.refs_2_.refs_4_, ...), custom_call_target="tpu_custom_call" | custom-call | tf_op jit(solution)/shard_map/basis/pallas_call | solution.py:509
  (36 shorter events, 6.3 us)
Async XLA Ops:
  0.0 7.5 %collective-permute-start.2 = (f32[32,8,256]{2,1,0:T(8,128)}, f32[32,8,256]{2,1,0:T(8,128)S(1)}, u32[]{:S(2)}, u32[]{:S(2)}) collective-permute-start(f32[32,8,256]{2,1,0:T(8,128)} %refs_2_.3), channel_id=1, source_target_pairs={{0,1},{1,0},{2,4},{3,5},{4,2},{5,3},{6,7},{7,6},{8,9},{9,8},{10,12... | collective-permute-start | bytes 786440 | tf_op jit(solution)/shard_map/ppermute | solution.py:407
  3.9 3.7 %collective-permute-start = (f32[32,8,256]{2,1,0:T(8,128)S(1)}, f32[32,8,256]{2,1,0:T(8,128)S(1)}, u32[]{:S(2)}, u32[]{:S(2)}) collective-permute-start(f32[32,8,256]{2,1,0:T(8,128)S(1)} %dynamic-slice_bitcast_fusion), channel_id=1, source_target_pairs={{0,2},{2,0},{4,6},{6,4},{1,3},{3,1},{5,7},{7,5},{8,10},{10,8},{12,... | collective-permute-start | bytes 786440 | tf_op jit(solution)/shard_map/ppermute | solution.py:394
  4.1 3.5 %collective-permute-start.1 = (f32[32,8,256]{2,1,0:T(8,128)}, f32[32,8,256]{2,1,0:T(8,128)S(1)}, u32[]{:S(2)}, u32[]{:S(2)}) collective-permute-start(f32[32,8,256]{2,1,0:T(8,128)} %refs_2_.3), channel_id=1, source_target_pairs={{0,2},{2,0},{4,6},{6,4},{1,3},{3,1},{5,7},{7,5},{8,10},{10,8},{12,... | collective-permute-start | bytes 786440 | tf_op jit(solution)/shard_map/ppermute | solution.py:394
  7.5 14.1 %collective-permute-start.3 = (f32[32,8,256]{2,1,0:T(8,128)S(1)}, f32[32,8,256]{2,1,0:T(8,128)S(1)}, u32[]{:S(2)}, u32[]{:S(2)}) collective-permute-start(f32[32,8,256]{2,1,0:T(8,128)S(1)} %collective-permute-done.2.refs_4_), channel_id=1, source_target_pairs={{0,2},{2,0},{4,6},{6,4},{1,3},{3,1},{5,7},{7,5},{8,10},{10,8},{12,... | collective-permute-start | bytes 786440 | tf_op jit(solution)/shard_map/ppermute | solution.py:394
  8.6 12.9 %collective-permute-start.4 = (f32[32,8,256]{2,1,0:T(8,128)S(1)}, f32[32,8,256]{2,1,0:T(8,128)S(1)}, u32[]{:S(2)}, u32[]{:S(2)}) collective-permute-start(f32[32,8,256]{2,1,0:T(8,128)S(1)} %get-tuple-element.19), channel_id=1, source_target_pairs={{0,4},{2,6},{4,0},{6,2},{8,12},{10,14},{12,8},{14,10},{16,20},{18,... | collective-permute-start | bytes 786440 | tf_op jit(solution)/shard_map/ppermute | solution.py:389
  10.1 11.5 %collective-permute-start.5 = (f32[2,14,8,256]{3,2,1,0:T(8,128)S(1)}, f32[2,14,8,256]{3,2,1,0:T(8,128)S(1)}, u32[]{:S(2)}, u32[]{:S(2)}) collective-permute-start(f32[2,14,8,256]{3,2,1,0:T(8,128)S(1)} %get-tuple-element.20), channel_id=1, source_target_pairs={{0,8},{2,10},{4,12},{6,14},{8,0},{10,2},{12,4},{14,6},{16,24},{18,... | collective-permute-start | bytes 688136 | tf_op jit(solution)/shard_map/ppermute | solution.py:389
  11.7 9.9 %collective-permute-start.6 = (f32[2,14,8,256]{3,2,1,0:T(8,128)S(1)}, f32[2,14,8,256]{3,2,1,0:T(8,128)S(1)}, u32[]{:S(2)}, u32[]{:S(2)}) collective-permute-start(f32[2,14,8,256]{3,2,1,0:T(8,128)S(1)} %get-tuple-element.21), channel_id=1, source_target_pairs={{0,2},{2,0},{4,6},{6,4},{8,16},{10,18},{12,20},{14,22},{16,8},{18,... | collective-permute-start | bytes 688136 | tf_op jit(solution)/shard_map/ppermute | solution.py:389
  11.7 8.6 %collective-permute-start.7 = (f32[12,8,256]{2,1,0:T(8,128)S(1)}, f32[12,8,256]{2,1,0:T(8,128)S(1)}, u32[]{:S(2)}, u32[]{:S(2)}) collective-permute-start(f32[12,8,256]{2,1,0:T(8,128)S(1)} %get-tuple-element.22), channel_id=1, source_target_pairs={{0,12},{2,14},{4,8},{6,10},{8,4},{10,6},{12,0},{14,2},{16,28},{18,... | collective-permute-start | bytes 294920 | tf_op jit(solution)/shard_map/ppermute | solution.py:389
  20.3 1.3 %collective-permute-start.8 = (f32[12,8,256]{2,1,0:T(8,128)S(1)}, f32[12,8,256]{2,1,0:T(8,128)S(1)}, u32[]{:S(2)}, u32[]{:S(2)}) collective-permute-start(f32[12,8,256]{2,1,0:T(8,128)S(1)} %get-tuple-element.23), channel_id=1, source_target_pairs={{0,2},{2,0},{4,6},{6,4},{8,20},{10,22},{12,16},{14,18},{16,12},{18... | collective-permute-start | bytes 294920 | tf_op jit(solution)/shard_map/ppermute | solution.py:389
  26.7 12.1 %collective-permute-start.9 = (f32[32,8,256]{2,1,0:T(8,128)S(1)}, f32[32,8,256]{2,1,0:T(8,128)S(1)}, u32[]{:S(2)}, u32[]{:S(2)}) collective-permute-start(f32[32,8,256]{2,1,0:T(8,128)S(1)} %get-tuple-element.26), channel_id=1, source_target_pairs={{0,4},{2,6},{4,0},{6,2},{8,12},{10,14},{12,8},{14,10},{16,20},{18,... | collective-permute-start | bytes 786440 | tf_op jit(solution)/shard_map/ppermute | solution.py:389
  27.8 11.0 %collective-permute-start.10 = (f32[2,8,8,256]{3,2,1,0:T(8,128)S(1)}, f32[2,8,8,256]{3,2,1,0:T(8,128)S(1)}, u32[]{:S(2)}, u32[]{:S(2)}) collective-permute-start(f32[2,8,8,256]{3,2,1,0:T(8,128)S(1)} %get-tuple-element.27), channel_id=1, source_target_pairs={{0,8},{2,10},{4,12},{6,14},{8,0},{10,2},{12,4},{14,6},{16,24},{18,... | collective-permute-start | bytes 393224 | tf_op jit(solution)/shard_map/ppermute | solution.py:389
  33.6 5.2 %collective-permute-start.11 = (f32[2,8,8,256]{3,2,1,0:T(8,128)S(1)}, f32[2,8,8,256]{3,2,1,0:T(8,128)S(1)}, u32[]{:S(2)}, u32[]{:S(2)}) collective-permute-start(f32[2,8,8,256]{3,2,1,0:T(8,128)S(1)} %get-tuple-element.28), channel_id=1, source_target_pairs={{0,2},{2,0},{4,6},{6,4},{8,16},{10,18},{12,20},{14,22},{16,8},{18,... | collective-permute-start | bytes 393224 | tf_op jit(solution)/shard_map/ppermute | solution.py:389
  33.6 5.2 %collective-permute-start.12 = (f32[7,8,256]{2,1,0:T(8,128)S(1)}, f32[7,8,256]{2,1,0:T(8,128)S(1)}, u32[]{:S(2)}, u32[]{:S(2)}) collective-permute-start(f32[7,8,256]{2,1,0:T(8,128)S(1)} %get-tuple-element.29), channel_id=1, source_target_pairs={{0,12},{2,14},{4,8},{6,10},{8,4},{10,6},{12,0},{14,2},{16,28},{18,... | collective-permute-start | bytes 172040 | tf_op jit(solution)/shard_map/ppermute | solution.py:389
  35.7 3.1 %collective-permute-start.13 = (f32[7,8,256]{2,1,0:T(8,128)S(1)}, f32[7,8,256]{2,1,0:T(8,128)S(1)}, u32[]{:S(2)}, u32[]{:S(2)}) collective-permute-start(f32[7,8,256]{2,1,0:T(8,128)S(1)} %get-tuple-element.30), channel_id=1, source_target_pairs={{0,2},{2,0},{4,6},{6,4},{8,20},{10,22},{12,16},{14,18},{16,12},{18... | collective-permute-start | bytes 172040 | tf_op jit(solution)/shard_map/ppermute | solution.py:389
  43.9 8.6 %collective-permute-start.16 = (f32[32,8,256]{2,1,0:T(8,128)S(1)}, f32[32,8,256]{2,1,0:T(8,128)S(1)}, u32[]{:S(2)}, u32[]{:S(2)}) collective-permute-start(f32[32,8,256]{2,1,0:T(8,128)S(1)} %get-tuple-element.32), channel_id=1, source_target_pairs={{0,3},{1,2},{2,1},{3,0},{4,7},{5,6},{6,5},{7,4},{8,11},{9,10},{10,... | collective-permute-start | bytes 786440 | tf_op jit(solution)/shard_map/ppermute | solution.py:499
  44.7 7.8 %collective-permute-start.14 = (f32[32,8,256]{2,1,0:T(8,128)S(1)}, f32[32,8,256]{2,1,0:T(8,128)S(1)}, u32[]{:S(2)}, u32[]{:S(2)}) collective-permute-start(f32[32,8,256]{2,1,0:T(8,128)S(1)} %get-tuple-element.32), channel_id=1, source_target_pairs={{0,2},{2,0},{4,6},{6,4},{1,3},{3,1},{5,7},{7,5},{8,10},{10,8},{12,... | collective-permute-start | bytes 786440 | tf_op jit(solution)/shard_map/ppermute | solution.py:394
  45.6 12.6 %collective-permute-start.15 = (f32[32,8,256]{2,1,0:T(8,128)S(1)}, f32[32,8,256]{2,1,0:T(8,128)S(1)}, u32[]{:S(2)}, u32[]{:S(2)}) collective-permute-start(f32[32,8,256]{2,1,0:T(8,128)S(1)} %get-tuple-element.31.refs_0_.refs_2_), channel_id=1, source_target_pairs={{0,1},{1,0},{2,3},{3,2},{4,5},{5,4},{6,7},{7,6},{8,9},{9,8},{10,11... | collective-permute-start | bytes 786440 | tf_op jit(solution)/shard_map/ppermute | solution.py:498
  58.5 3.1 %collective-permute-start.19 = (f32[8,128]{1,0:T(8,128)S(1)}, f32[8,128]{1,0:T(8,128)S(1)}, u32[]{:S(2)}, u32[]{:S(2)}) collective-permute-start(f32[8,128]{1,0:T(8,128)S(1)} %correlation.1), channel_id=1, source_target_pairs={{0,6},{2,4},{4,2},{6,0},{1,7},{3,5},{5,3},{7,1},{8,14},{10,12},{12... | collective-permute-start | bytes 12296 | tf_op jit(solution)/shard_map/ppermute | solution.py:426
  59.4 3.6 %collective-permute-start.18 = (f32[8,128]{1,0:T(8,128)S(1)}, f32[8,128]{1,0:T(8,128)S(1)}, u32[]{:S(2)}, u32[]{:S(2)}) collective-permute-start(f32[8,128]{1,0:T(8,128)S(1)} %correlation.1), channel_id=1, source_target_pairs={{0,4},{2,6},{4,0},{6,2},{1,5},{3,7},{5,1},{7,3},{8,12},{10,14},{12... | collective-permute-start | bytes 12296 | tf_op jit(solution)/shard_map/ppermute | solution.py:426
  60.3 2.7 %collective-permute-start.17 = (f32[8,128]{1,0:T(8,128)S(1)}, f32[8,128]{1,0:T(8,128)S(1)}, u32[]{:S(2)}, u32[]{:S(2)}) collective-permute-start(f32[8,128]{1,0:T(8,128)S(1)} %correlation.1), channel_id=1, source_target_pairs={{0,2},{2,0},{4,6},{6,4},{1,3},{3,1},{5,7},{7,5},{8,10},{10,8},{12,... | collective-permute-start | bytes 12296 | tf_op jit(solution)/shard_map/ppermute | solution.py:426
  63.0 7.7 %copy-start.2 = (s32[4]{0:T(128)S(1)}, s32[4]{0:T(128)}, u32[]{:S(2)}) copy-start(s32[4]{0:T(128)} %refs_1_.1) | copy-start | bytes 52
  63.0 5.5 %collective-permute-start.22 = (f32[8,128]{1,0:T(8,128)S(1)}, f32[8,128]{1,0:T(8,128)S(1)}, u32[]{:S(2)}, u32[]{:S(2)}) collective-permute-start(f32[8,128]{1,0:T(8,128)S(1)} %add_add_fusion.1), channel_id=1, source_target_pairs={{0,24},{8,16},{16,8},{24,0},{1,25},{9,17},{17,9},{25,1},{2,26},{10... | collective-permute-start | bytes 12296 | tf_op jit(solution)/shard_map/ppermute | solution.py:426
  65.5 4.5 %collective-permute-start.21 = (f32[8,128]{1,0:T(8,128)S(1)}, f32[8,128]{1,0:T(8,128)S(1)}, u32[]{:S(2)}, u32[]{:S(2)}) collective-permute-start(f32[8,128]{1,0:T(8,128)S(1)} %add_add_fusion.1), channel_id=1, source_target_pairs={{0,16},{8,24},{16,0},{24,8},{1,17},{9,25},{17,1},{25,9},{2,18},{10... | collective-permute-start | bytes 12296 | tf_op jit(solution)/shard_map/ppermute | solution.py:426
  67.1 3.6 %collective-permute-start.20 = (f32[8,128]{1,0:T(8,128)S(1)}, f32[8,128]{1,0:T(8,128)S(1)}, u32[]{:S(2)}, u32[]{:S(2)}) collective-permute-start(f32[8,128]{1,0:T(8,128)S(1)} %add_add_fusion.1), channel_id=1, source_target_pairs={{0,8},{8,0},{16,24},{24,16},{1,9},{9,1},{17,25},{25,17},{2,10},{10... | collective-permute-start | bytes 12296 | tf_op jit(solution)/shard_map/ppermute | solution.py:426
  (2 other events, 8.6 us)

commit v4 on v3

--- a/solution.py
+++ b/solution.py
@@ -178,7 +178,7 @@
     y_out = outs[: len(y_phases())]
     x_out = outs[len(y_phases()) : len(y_phases()) + 2]
     d_out = outs[len(y_phases()) + 2 :]
-    tiles = (orbitals.at[core], received)
+    tiles = (orbitals.at[core], received.at[core])
     local = (potential, received_potential)
     for x_phase in range(2):
         right = upward(along_x, x_phase)
@@ -228,7 +228,7 @@
     width, depth = potential.shape[0], potential.shape[2]
     fill(
         a,
-        (orbitals.at[core], received),
+        (orbitals.at[core], received.at[core]),
         [x.at[:, :HALO] for x in x_halos],
         y_halos,
         [c.at[: HALO - 1] for c in corners],
@@ -272,7 +272,7 @@
     fill(a, (own, other), x_halos, y_halos, corners)
     fill_local(local, potential, received_potential, edge, passed, p_x_halos, p_corners)
     four_steps(a, b, local, z_matrix(depth))
-    start = (orbitals.at[core], received)
+    start = (orbitals.at[core], received.at[core])
     outs = (keep, give)
     for t, slot in enumerate(own_slots(core, chip)):
         for half in range(2):
@@ -439,13 +439,11 @@
     bands = lax.axis_size("band")
     cells = float(width * lax.axis_size("gx") * height * lax.axis_size("gy") * depth)
     count = len(y_phases())
-    core, chip, _ = place()
     window = (2, width + 2 * HALO, 8 * tile_count() + 2 * PAD, LANES)
     scratch = [pltpu.VMEM(window, jnp.float32)] * 3
 
     edge = face(potential)
-    other = lax.dynamic_index_in_dim(orbitals, 1 - core, 0, keepdims=False)
-    received = swap(other)
+    received = swap(orbitals)
     received_potential = swap(potential)
     tile = (width, height, depth)
 
@@ -465,6 +463,7 @@
         name="pack",
     )(orbitals, received, potential, received_potential)
     halos = exchange(packed)
+    edge, _ = lax.optimization_barrier((edge, halos[count]))
     passed = swap(edge)
     local = (potential, received_potential, edge, passed)
     own, sibling, *packed = pl.pallas_call(

time: 72.5 us -> 72.4 us (level)
  waiting for transfers between devices: 30.2 us -> 28.8 us
  starting transfers between devices: 27.9 us -> 29.1 us
    ppermute x1, waiting for transfers between devices: 3.01 us -> 0.01 us  [face(): return lax.ppermute(value, ('gy', 'band'), pairs)]
    unnamed x6, local copies, waits for them, and re-layouts: 0.95 us -> 2 us
    squeeze x1 -> x0, local copies, waits for them, and re-layouts: 0.97 us -> none  [per_device(): other = lax.dynamic_index_in_dim(orbitals, 1 - core, 0, keepdims=False)]
    ppermute x10, waiting for transfers between devices: 9.36 us -> 10.3 us  [meet(): return lax.ppermute(value, ('gx', 'gy'), pairs)]
    ppermute x6, starting transfers between devices: 6.38 us -> 7.11 us  [of(): return lax.ppermute(value, axis, [(i, i ^ step) for i in range(count)])]
  transfers between devices with their start and end apart: 23 -> 23, of which waited for: 11 -> 10; matrix products, arithmetic and copies ran while one was open for 1% -> 0% of each run, Pallas kernels for 0% -> 0%
where the time goes in v4:
time: 72.4 us; the launch traced here: 72.2 us
  starting transfers between devices  29.1 us (40%)
  waiting for transfers between devices  28.8 us (40%)
  Pallas kernels  12.2 us (17%)
  local copies, waits for them, and re-layouts  2 us (3%)
    ppermute x10, starting transfers between devices, meet(): return lax.ppermute(value, ('gx', 'gy'), pairs)  16.3 us
    ppermute x10, waiting for transfers between devices, meet(): return lax.ppermute(value, ('gx', 'gy'), pairs)  10.3 us
    ppermute x6, starting transfers between devices, of(): return lax.ppermute(value, axis, [(i, i ^ step) for i in range(count)])  7.11 us
    ppermute x1, waiting for transfers between devices, per_device(): slots.append(lax.ppermute(give, ('gy', 'band'), crossed))  6.41 us
    ppermute x6, waiting for transfers between devices, of(): return lax.ppermute(value, axis, [(i, i ^ step) for i in range(count)])  6.39 us
    ppermute x1, waiting for transfers between devices, per_device(): slots.append(lax.ppermute(keep, ('gy', 'band'), same))  5.67 us
    pallas_call x1, Pallas kernels, per_device(): pl.pallas_call(first_kernel, out_shape=[struct(*tile)] * 2 + payloads(HAL...  5.09 us
    pallas_call x1, Pallas kernels, per_device(): pl.pallas_call(second_kernel, out_shape=[struct(*tile)] * 2, in_specs=[VM...  5.06 us
  transfers between devices with their start and end apart: 23, of which 10 were waited for; matrix products, arithmetic and copies ran while one was open for 0% of the time, Pallas kernels for 0%

profile of v4, /device:TPU:0, one launch (start us, length us, event | category | flops | bytes accessed | tf_op | source)
XLA Modules:
  0.0 72.2 jit_solution(5790275115042357535)
XLA Ops:
  0.5 2.9 %collective-permute-start.2 = (f32[32,8,256]{2,1,0:T(8,128)}, f32[32,8,256]{2,1,0:T(8,128)S(1)}, u32[]{:S(2)}, u32[]{:S(2)}) collective-permute-start(f32[32,8,256]{2,1,0:T(8,128)} %refs_2_.3), channel_id=1, source_target_pairs={{0,1},{1,0},{2,4},{3,5},{4,2},{5,3},{6,7},{7,6},{8,9},{9,8},{10,12... | collective-permute-start | bytes 786440 | tf_op jit(solution)/shard_map/ppermute | solution.py:407
  3.5 1.0 %copy-done = f32[2,32,8,256]{3,2,1,0:T(8,128)S(1)} copy-done((f32[2,32,8,256]{3,2,1,0:T(8,128)S(1)}, f32[2,32,8,256]{3,2,1,0:T(8,128)}, u32[]{:S(2)}) %copy-start) | copy-done | bytes 524312
  4.5 0.9 %copy-done.1 = f32[32,8,256]{2,1,0:T(8,128)S(1)} copy-done((f32[32,8,256]{2,1,0:T(8,128)S(1)}, f32[32,8,256]{2,1,0:T(8,128)}, u32[]{:S(2)}) %copy-start.1) | copy-done | bytes 262168
  5.5 2.1 %collective-permute-start.3 = (f32[2,14,8,256]{3,2,1,0:T(8,128)S(1)}, f32[2,14,8,256]{3,2,1,0:T(8,128)S(1)}, u32[]{:S(2)}, u32[]{:S(2)}) collective-permute-start(f32[2,14,8,256]{3,2,1,0:T(8,128)S(1)} %get-tuple-element.20), channel_id=1, source_target_pairs={{0,8},{2,10},{4,12},{6,14},{8,0},{10,2},{12,4},{14,6},{16,24},{18,... | collective-permute-start | bytes 688136 | tf_op jit(solution)/shard_map/ppermute | solution.py:389
  7.6 1.5 %collective-permute-start.5 = (f32[32,8,256]{2,1,0:T(8,128)S(1)}, f32[32,8,256]{2,1,0:T(8,128)S(1)}, u32[]{:S(2)}, u32[]{:S(2)}) collective-permute-start(f32[32,8,256]{2,1,0:T(8,128)S(1)} %get-tuple-element.22), channel_id=1, source_target_pairs={{0,4},{2,6},{4,0},{6,2},{8,12},{10,14},{12,8},{14,10},{16,20},{18,... | collective-permute-start | bytes 786440 | tf_op jit(solution)/shard_map/ppermute | solution.py:389
  9.2 4.4 %collective-permute-done.3.refs_7_.refs_13_ = f32[2,14,8,256]{3,2,1,0:T(8,128)S(1)} collective-permute-done((f32[2,14,8,256]{3,2,1,0:T(8,128)S(1)}, f32[2,14,8,256]{3,2,1,0:T(8,128)S(1)}, u32[]{:S(2)}, u32[]{:S(2)}) %collective-permute-start.3) | collective-permute-done | bytes 229408 | tf_op jit(solution)/shard_map/ppermute | solution.py:389
  14.1 3.8 %collective-permute-start.7 = (f32[12,8,256]{2,1,0:T(8,128)S(1)}, f32[12,8,256]{2,1,0:T(8,128)S(1)}, u32[]{:S(2)}, u32[]{:S(2)}) collective-permute-start(f32[12,8,256]{2,1,0:T(8,128)S(1)} %get-tuple-element.24), channel_id=1, source_target_pairs={{0,12},{2,14},{4,8},{6,10},{8,4},{10,6},{12,0},{14,2},{16,28},{18,... | collective-permute-start | bytes 294920 | tf_op jit(solution)/shard_map/ppermute | solution.py:389
  17.8 3.2 %collective-permute-done.7.refs_9_.refs_15_ = f32[12,8,256]{2,1,0:T(8,128)S(1)} collective-permute-done((f32[12,8,256]{2,1,0:T(8,128)S(1)}, f32[12,8,256]{2,1,0:T(8,128)S(1)}, u32[]{:S(2)}, u32[]{:S(2)}) %collective-permute-start.7) | collective-permute-done | bytes 98336 | tf_op jit(solution)/shard_map/ppermute | solution.py:389
  21.0 5.1 %first_round.1 = (f32[32,8,256]{2,1,0:T(8,128)S(1)}, f32[32,8,256]{2,1,0:T(8,128)S(1)}, f32[32,8,256]{2,1,0:T(8,128)S(1)}, f32[2,8,8,256]{3,2,1,0:T(8,128)S(1)},...) custom-call(f32[2,32,8,256]{3,2,1,0:T(8,128)S(1)} %copy-done, ...), custom_call_target="tpu_custom_call" | custom-call | tf_op jit(solution)/shard_map/first_round/pallas_call | solution.py:469
  26.7 5.3 %collective-permute-start.10 = (f32[2,8,8,256]{3,2,1,0:T(8,128)S(1)}, f32[2,8,8,256]{3,2,1,0:T(8,128)S(1)}, u32[]{:S(2)}, u32[]{:S(2)}) collective-permute-start(f32[2,8,8,256]{3,2,1,0:T(8,128)S(1)} %get-tuple-element.29), channel_id=1, source_target_pairs={{0,8},{2,10},{4,12},{6,14},{8,0},{10,2},{12,4},{14,6},{16,24},{18,... | collective-permute-start | bytes 393224 | tf_op jit(solution)/shard_map/ppermute | solution.py:389
  32.0 2.6 %collective-permute-start.12 = (f32[7,8,256]{2,1,0:T(8,128)S(1)}, f32[7,8,256]{2,1,0:T(8,128)S(1)}, u32[]{:S(2)}, u32[]{:S(2)}) collective-permute-start(f32[7,8,256]{2,1,0:T(8,128)S(1)} %get-tuple-element.31), channel_id=1, source_target_pairs={{0,12},{2,14},{4,8},{6,10},{8,4},{10,6},{12,0},{14,2},{16,28},{18,... | collective-permute-start | bytes 172040 | tf_op jit(solution)/shard_map/ppermute | solution.py:389
  34.5 2.7 %collective-permute-done.12.refs_11_ = f32[7,8,256]{2,1,0:T(8,128)S(1)} collective-permute-done((f32[7,8,256]{2,1,0:T(8,128)S(1)}, f32[7,8,256]{2,1,0:T(8,128)S(1)}, u32[]{:S(2)}, u32[]{:S(2)}) %collective-permute-start.12) | collective-permute-done | bytes 57376 | tf_op jit(solution)/shard_map/ppermute | solution.py:389
  37.3 5.1 %second_round.1 = (f32[32,8,256]{2,1,0:T(8,128)S(1)}, f32[32,8,256]{2,1,0:T(8,128)S(1)}) custom-call(f32[2,32,8,256]{3,2,1,0:T(8,128)S(1)} %copy-done, f32[2,32,8,256]{3,2,1,0:T(8,128)S(1)} %collective-permute-done.received.refs_1_, f32[32,8,256]{2,1,0:T(8,128)S(1)} %copy-done.1, f32[32,8,256]{2,1,0:T(8,128)S(1)} %collective-permute-done.1.received_potential.refs_3_, ...), custom_call_target="tpu_custom_call" | custom-call | tf_op jit(solution)/shard_map/second_round/pallas_call | solution.py:479
  42.3 0.9 %collective-permute-start.16 = (f32[32,8,256]{2,1,0:T(8,128)S(1)}, f32[32,8,256]{2,1,0:T(8,128)S(1)}, u32[]{:S(2)}, u32[]{:S(2)}) collective-permute-start(f32[32,8,256]{2,1,0:T(8,128)S(1)} %get-tuple-element.34), channel_id=1, source_target_pairs={{0,3},{1,2},{2,1},{3,0},{4,7},{5,6},{6,5},{7,4},{8,11},{9,10},{10,... | collective-permute-start | bytes 786440 | tf_op jit(solution)/shard_map/ppermute | solution.py:498
  44.5 6.4 %collective-permute-done.16.refs_3_.refs_5_ = f32[32,8,256]{2,1,0:T(8,128)S(1)} collective-permute-done((f32[32,8,256]{2,1,0:T(8,128)S(1)}, f32[32,8,256]{2,1,0:T(8,128)S(1)}, u32[]{:S(2)}, u32[]{:S(2)}) %collective-permute-start.16) | collective-permute-done | bytes 262176 | tf_op jit(solution)/shard_map/ppermute | solution.py:498
  51.0 5.7 %collective-permute-done.15.refs_2_.refs_4_ = f32[32,8,256]{2,1,0:T(8,128)S(1)} collective-permute-done((f32[32,8,256]{2,1,0:T(8,128)S(1)}, f32[32,8,256]{2,1,0:T(8,128)S(1)}, u32[]{:S(2)}, u32[]{:S(2)}) %collective-permute-start.15) | collective-permute-done | bytes 262176 | tf_op jit(solution)/shard_map/ppermute | solution.py:497
  57.0 1.2 %collective-permute-start.19 = (f32[8,128]{1,0:T(8,128)S(1)}, f32[8,128]{1,0:T(8,128)S(1)}, u32[]{:S(2)}, u32[]{:S(2)}) collective-permute-start(f32[8,128]{1,0:T(8,128)S(1)} %correlation.1), channel_id=1, source_target_pairs={{0,6},{2,4},{4,2},{6,0},{1,7},{3,5},{5,3},{7,1},{8,14},{10,12},{12... | collective-permute-start | bytes 12296 | tf_op jit(solution)/shard_map/ppermute | solution.py:426
  58.9 1.2 %collective-permute-done.19 = f32[8,128]{1,0:T(8,128)S(1)} collective-permute-done((f32[8,128]{1,0:T(8,128)S(1)}, f32[8,128]{1,0:T(8,128)S(1)}, u32[]{:S(2)}, u32[]{:S(2)}) %collective-permute-start.19) | collective-permute-done | bytes 4128 | tf_op jit(solution)/shard_map/ppermute | solution.py:426
  60.1 1.7 %collective-permute-done.18 = f32[8,128]{1,0:T(8,128)S(1)} collective-permute-done((f32[8,128]{1,0:T(8,128)S(1)}, f32[8,128]{1,0:T(8,128)S(1)}, u32[]{:S(2)}, u32[]{:S(2)}) %collective-permute-start.18) | collective-permute-done | bytes 4128 | tf_op jit(solution)/shard_map/ppermute | solution.py:426
  61.8 2.5 %collective-permute-start.22 = (f32[8,128]{1,0:T(8,128)S(1)}, f32[8,128]{1,0:T(8,128)S(1)}, u32[]{:S(2)}, u32[]{:S(2)}) collective-permute-start(f32[8,128]{1,0:T(8,128)S(1)} %add_add_fusion.1), channel_id=1, source_target_pairs={{0,24},{8,16},{16,8},{24,0},{1,25},{9,17},{17,9},{25,1},{2,26},{10... | collective-permute-start | bytes 12296 | tf_op jit(solution)/shard_map/ppermute | solution.py:426
  64.4 2.5 %collective-permute-start.21 = (f32[8,128]{1,0:T(8,128)S(1)}, f32[8,128]{1,0:T(8,128)S(1)}, u32[]{:S(2)}, u32[]{:S(2)}) collective-permute-start(f32[8,128]{1,0:T(8,128)S(1)} %add_add_fusion.1), channel_id=1, source_target_pairs={{0,16},{8,24},{16,0},{24,8},{1,17},{9,25},{17,1},{25,9},{2,18},{10... | collective-permute-start | bytes 12296 | tf_op jit(solution)/shard_map/ppermute | solution.py:426
  67.3 1.6 %collective-permute-done.21 = f32[8,128]{1,0:T(8,128)S(1)} collective-permute-done((f32[8,128]{1,0:T(8,128)S(1)}, f32[8,128]{1,0:T(8,128)S(1)}, u32[]{:S(2)}, u32[]{:S(2)}) %collective-permute-start.21) | collective-permute-done | bytes 4128 | tf_op jit(solution)/shard_map/ppermute | solution.py:426
  68.9 1.6 %collective-permute-done.20 = f32[8,128]{1,0:T(8,128)S(1)} collective-permute-done((f32[8,128]{1,0:T(8,128)S(1)}, f32[8,128]{1,0:T(8,128)S(1)}, u32[]{:S(2)}, u32[]{:S(2)}) %collective-permute-start.20) | collective-permute-done | bytes 4128 | tf_op jit(solution)/shard_map/ppermute | solution.py:426
  70.5 1.7 %basis.1 = f32[2,32,8,256]{3,2,1,0:T(8,128)} custom-call(f32[8,128]{1,0:T(8,128)S(1)} %add_add_fusion.refs_0_, s32[4]{0:T(128)S(1)} %copy-done.2, f32[32,8,256]{2,1,0:T(8,128)S(1)} %get-tuple-element.33.refs_0_.refs_2_, f32[32,8,256]{2,1,0:T(8,128)S(1)} %collective-permute-done.14.refs_1_.refs_3_, f32[32,8,256]{2,1,0:T(8,128)S(1)} %collective-permute-done.15.refs_2_.refs_4_, ...), custom_call_target="tpu_custom_call" | custom-call | tf_op jit(solution)/shard_map/basis/pallas_call | solution.py:508
  (35 shorter events, 4.4 us)
Async XLA Ops:
  0.0 3.5 %collective-permute-start = (f32[2,32,8,256]{3,2,1,0:T(8,128)}, f32[2,32,8,256]{3,2,1,0:T(8,128)S(1)}, u32[]{:S(2)}, u32[]{:S(2)}) collective-permute-start(f32[2,32,8,256]{3,2,1,0:T(8,128)} %refs_0_.3), channel_id=1, source_target_pairs={{0,2},{2,0},{4,6},{6,4},{1,3},{3,1},{5,7},{7,5},{8,10},{10,8},{12,... | collective-permute-start | bytes 1572872 | tf_op jit(solution)/shard_map/ppermute | solution.py:394
  0.5 3.0 %collective-permute-start.1 = (f32[32,8,256]{2,1,0:T(8,128)}, f32[32,8,256]{2,1,0:T(8,128)S(1)}, u32[]{:S(2)}, u32[]{:S(2)}) collective-permute-start(f32[32,8,256]{2,1,0:T(8,128)} %refs_2_.3), channel_id=1, source_target_pairs={{0,2},{2,0},{4,6},{6,4},{1,3},{3,1},{5,7},{7,5},{8,10},{10,8},{12,... | collective-permute-start | bytes 786440 | tf_op jit(solution)/shard_map/ppermute | solution.py:394
  0.5 8.7 %collective-permute-start.2 = (f32[32,8,256]{2,1,0:T(8,128)}, f32[32,8,256]{2,1,0:T(8,128)S(1)}, u32[]{:S(2)}, u32[]{:S(2)}) collective-permute-start(f32[32,8,256]{2,1,0:T(8,128)} %refs_2_.3), channel_id=1, source_target_pairs={{0,1},{1,0},{2,4},{3,5},{4,2},{5,3},{6,7},{7,6},{8,9},{9,8},{10,12... | collective-permute-start | bytes 786440 | tf_op jit(solution)/shard_map/ppermute | solution.py:407
  5.5 8.0 %collective-permute-start.3 = (f32[2,14,8,256]{3,2,1,0:T(8,128)S(1)}, f32[2,14,8,256]{3,2,1,0:T(8,128)S(1)}, u32[]{:S(2)}, u32[]{:S(2)}) collective-permute-start(f32[2,14,8,256]{3,2,1,0:T(8,128)S(1)} %get-tuple-element.20), channel_id=1, source_target_pairs={{0,8},{2,10},{4,12},{6,14},{8,0},{10,2},{12,4},{14,6},{16,24},{18,... | collective-permute-start | bytes 688136 | tf_op jit(solution)/shard_map/ppermute | solution.py:389
  7.6 13.4 %collective-permute-start.5 = (f32[32,8,256]{2,1,0:T(8,128)S(1)}, f32[32,8,256]{2,1,0:T(8,128)S(1)}, u32[]{:S(2)}, u32[]{:S(2)}) collective-permute-start(f32[32,8,256]{2,1,0:T(8,128)S(1)} %get-tuple-element.22), channel_id=1, source_target_pairs={{0,4},{2,6},{4,0},{6,2},{8,12},{10,14},{12,8},{14,10},{16,20},{18,... | collective-permute-start | bytes 786440 | tf_op jit(solution)/shard_map/ppermute | solution.py:389
  13.6 7.5 %collective-permute-start.4 = (f32[32,8,256]{2,1,0:T(8,128)S(1)}, f32[32,8,256]{2,1,0:T(8,128)S(1)}, u32[]{:S(2)}, u32[]{:S(2)}) collective-permute-start(f32[32,8,256]{2,1,0:T(8,128)S(1)} %collective-permute-done.2.refs_4_), channel_id=1, source_target_pairs={{0,2},{2,0},{4,6},{6,4},{1,3},{3,1},{5,7},{7,5},{8,10},{10,8},{12,... | collective-permute-start | bytes 786440 | tf_op jit(solution)/shard_map/ppermute | solution.py:394
  13.6 7.5 %collective-permute-start.6 = (f32[2,14,8,256]{3,2,1,0:T(8,128)S(1)}, f32[2,14,8,256]{3,2,1,0:T(8,128)S(1)}, u32[]{:S(2)}, u32[]{:S(2)}) collective-permute-start(f32[2,14,8,256]{3,2,1,0:T(8,128)S(1)} %get-tuple-element.23), channel_id=1, source_target_pairs={{0,2},{2,0},{4,6},{6,4},{8,16},{10,18},{12,20},{14,22},{16,8},{18,... | collective-permute-start | bytes 688136 | tf_op jit(solution)/shard_map/ppermute | solution.py:389
  14.1 6.9 %collective-permute-start.7 = (f32[12,8,256]{2,1,0:T(8,128)S(1)}, f32[12,8,256]{2,1,0:T(8,128)S(1)}, u32[]{:S(2)}, u32[]{:S(2)}) collective-permute-start(f32[12,8,256]{2,1,0:T(8,128)S(1)} %get-tuple-element.24), channel_id=1, source_target_pairs={{0,12},{2,14},{4,8},{6,10},{8,4},{10,6},{12,0},{14,2},{16,28},{18,... | collective-permute-start | bytes 294920 | tf_op jit(solution)/shard_map/ppermute | solution.py:389
  17.8 3.2 %collective-permute-start.8 = (f32[12,8,256]{2,1,0:T(8,128)S(1)}, f32[12,8,256]{2,1,0:T(8,128)S(1)}, u32[]{:S(2)}, u32[]{:S(2)}) collective-permute-start(f32[12,8,256]{2,1,0:T(8,128)S(1)} %get-tuple-element.25), channel_id=1, source_target_pairs={{0,2},{2,0},{4,6},{6,4},{8,20},{10,22},{12,16},{14,18},{16,12},{18... | collective-permute-start | bytes 294920 | tf_op jit(solution)/shard_map/ppermute | solution.py:389
  26.1 11.1 %collective-permute-start.9 = (f32[32,8,256]{2,1,0:T(8,128)S(1)}, f32[32,8,256]{2,1,0:T(8,128)S(1)}, u32[]{:S(2)}, u32[]{:S(2)}) collective-permute-start(f32[32,8,256]{2,1,0:T(8,128)S(1)} %get-tuple-element.28), channel_id=1, source_target_pairs={{0,4},{2,6},{4,0},{6,2},{8,12},{10,14},{12,8},{14,10},{16,20},{18,... | collective-permute-start | bytes 786440 | tf_op jit(solution)/shard_map/ppermute | solution.py:389
  26.7 10.6 %collective-permute-start.10 = (f32[2,8,8,256]{3,2,1,0:T(8,128)S(1)}, f32[2,8,8,256]{3,2,1,0:T(8,128)S(1)}, u32[]{:S(2)}, u32[]{:S(2)}) collective-permute-start(f32[2,8,8,256]{3,2,1,0:T(8,128)S(1)} %get-tuple-element.29), channel_id=1, source_target_pairs={{0,8},{2,10},{4,12},{6,14},{8,0},{10,2},{12,4},{14,6},{16,24},{18,... | collective-permute-start | bytes 393224 | tf_op jit(solution)/shard_map/ppermute | solution.py:389
  32.0 5.3 %collective-permute-start.11 = (f32[2,8,8,256]{3,2,1,0:T(8,128)S(1)}, f32[2,8,8,256]{3,2,1,0:T(8,128)S(1)}, u32[]{:S(2)}, u32[]{:S(2)}) collective-permute-start(f32[2,8,8,256]{3,2,1,0:T(8,128)S(1)} %get-tuple-element.30), channel_id=1, source_target_pairs={{0,2},{2,0},{4,6},{6,4},{8,16},{10,18},{12,20},{14,22},{16,8},{18,... | collective-permute-start | bytes 393224 | tf_op jit(solution)/shard_map/ppermute | solution.py:389
  32.0 5.3 %collective-permute-start.12 = (f32[7,8,256]{2,1,0:T(8,128)S(1)}, f32[7,8,256]{2,1,0:T(8,128)S(1)}, u32[]{:S(2)}, u32[]{:S(2)}) collective-permute-start(f32[7,8,256]{2,1,0:T(8,128)S(1)} %get-tuple-element.31), channel_id=1, source_target_pairs={{0,12},{2,14},{4,8},{6,10},{8,4},{10,6},{12,0},{14,2},{16,28},{18,... | collective-permute-start | bytes 172040 | tf_op jit(solution)/shard_map/ppermute | solution.py:389
  34.5 2.7 %collective-permute-start.13 = (f32[7,8,256]{2,1,0:T(8,128)S(1)}, f32[7,8,256]{2,1,0:T(8,128)S(1)}, u32[]{:S(2)}, u32[]{:S(2)}) collective-permute-start(f32[7,8,256]{2,1,0:T(8,128)S(1)} %get-tuple-element.32), channel_id=1, source_target_pairs={{0,2},{2,0},{4,6},{6,4},{8,20},{10,22},{12,16},{14,18},{16,12},{18... | collective-permute-start | bytes 172040 | tf_op jit(solution)/shard_map/ppermute | solution.py:389
  42.3 8.6 %collective-permute-start.16 = (f32[32,8,256]{2,1,0:T(8,128)S(1)}, f32[32,8,256]{2,1,0:T(8,128)S(1)}, u32[]{:S(2)}, u32[]{:S(2)}) collective-permute-start(f32[32,8,256]{2,1,0:T(8,128)S(1)} %get-tuple-element.34), channel_id=1, source_target_pairs={{0,3},{1,2},{2,1},{3,0},{4,7},{5,6},{6,5},{7,4},{8,11},{9,10},{10,... | collective-permute-start | bytes 786440 | tf_op jit(solution)/shard_map/ppermute | solution.py:498
  43.3 7.7 %collective-permute-start.14 = (f32[32,8,256]{2,1,0:T(8,128)S(1)}, f32[32,8,256]{2,1,0:T(8,128)S(1)}, u32[]{:S(2)}, u32[]{:S(2)}) collective-permute-start(f32[32,8,256]{2,1,0:T(8,128)S(1)} %get-tuple-element.34), channel_id=1, source_target_pairs={{0,2},{2,0},{4,6},{6,4},{1,3},{3,1},{5,7},{7,5},{8,10},{10,8},{12,... | collective-permute-start | bytes 786440 | tf_op jit(solution)/shard_map/ppermute | solution.py:394
  44.0 12.6 %collective-permute-start.15 = (f32[32,8,256]{2,1,0:T(8,128)S(1)}, f32[32,8,256]{2,1,0:T(8,128)S(1)}, u32[]{:S(2)}, u32[]{:S(2)}) collective-permute-start(f32[32,8,256]{2,1,0:T(8,128)S(1)} %get-tuple-element.33.refs_0_.refs_2_), channel_id=1, source_target_pairs={{0,1},{1,0},{2,3},{3,2},{4,5},{5,4},{6,7},{7,6},{8,9},{9,8},{10,11... | collective-permute-start | bytes 786440 | tf_op jit(solution)/shard_map/ppermute | solution.py:497
  57.0 3.1 %collective-permute-start.19 = (f32[8,128]{1,0:T(8,128)S(1)}, f32[8,128]{1,0:T(8,128)S(1)}, u32[]{:S(2)}, u32[]{:S(2)}) collective-permute-start(f32[8,128]{1,0:T(8,128)S(1)} %correlation.1), channel_id=1, source_target_pairs={{0,6},{2,4},{4,2},{6,0},{1,7},{3,5},{5,3},{7,1},{8,14},{10,12},{12... | collective-permute-start | bytes 12296 | tf_op jit(solution)/shard_map/ppermute | solution.py:426
  58.2 3.6 %collective-permute-start.18 = (f32[8,128]{1,0:T(8,128)S(1)}, f32[8,128]{1,0:T(8,128)S(1)}, u32[]{:S(2)}, u32[]{:S(2)}) collective-permute-start(f32[8,128]{1,0:T(8,128)S(1)} %correlation.1), channel_id=1, source_target_pairs={{0,4},{2,6},{4,0},{6,2},{1,5},{3,7},{5,1},{7,3},{8,12},{10,14},{12... | collective-permute-start | bytes 12296 | tf_op jit(solution)/shard_map/ppermute | solution.py:426
  58.7 3.1 %collective-permute-start.17 = (f32[8,128]{1,0:T(8,128)S(1)}, f32[8,128]{1,0:T(8,128)S(1)}, u32[]{:S(2)}, u32[]{:S(2)}) collective-permute-start(f32[8,128]{1,0:T(8,128)S(1)} %correlation.1), channel_id=1, source_target_pairs={{0,2},{2,0},{4,6},{6,4},{1,3},{3,1},{5,7},{7,5},{8,10},{10,8},{12,... | collective-permute-start | bytes 12296 | tf_op jit(solution)/shard_map/ppermute | solution.py:426
  61.8 8.7 %copy-start.2 = (s32[4]{0:T(128)S(1)}, s32[4]{0:T(128)}, u32[]{:S(2)}) copy-start(s32[4]{0:T(128)} %refs_1_.1) | copy-start | bytes 52
  61.8 5.5 %collective-permute-start.22 = (f32[8,128]{1,0:T(8,128)S(1)}, f32[8,128]{1,0:T(8,128)S(1)}, u32[]{:S(2)}, u32[]{:S(2)}) collective-permute-start(f32[8,128]{1,0:T(8,128)S(1)} %add_add_fusion.1), channel_id=1, source_target_pairs={{0,24},{8,16},{16,8},{24,0},{1,25},{9,17},{17,9},{25,1},{2,26},{10... | collective-permute-start | bytes 12296 | tf_op jit(solution)/shard_map/ppermute | solution.py:426
  64.4 4.5 %collective-permute-start.21 = (f32[8,128]{1,0:T(8,128)S(1)}, f32[8,128]{1,0:T(8,128)S(1)}, u32[]{:S(2)}, u32[]{:S(2)}) collective-permute-start(f32[8,128]{1,0:T(8,128)S(1)} %add_add_fusion.1), channel_id=1, source_target_pairs={{0,16},{8,24},{16,0},{24,8},{1,17},{9,25},{17,1},{25,9},{2,18},{10... | collective-permute-start | bytes 12296 | tf_op jit(solution)/shard_map/ppermute | solution.py:426
  66.9 3.6 %collective-permute-start.20 = (f32[8,128]{1,0:T(8,128)S(1)}, f32[8,128]{1,0:T(8,128)S(1)}, u32[]{:S(2)}, u32[]{:S(2)}) collective-permute-start(f32[8,128]{1,0:T(8,128)S(1)} %add_add_fusion.1), channel_id=1, source_target_pairs={{0,8},{8,0},{16,24},{24,16},{1,9},{9,1},{17,25},{25,17},{2,10},{10... | collective-permute-start | bytes 12296 | tf_op jit(solution)/shard_map/ppermute | solution.py:426
  (2 other events, 2.0 us)

commit v5 on v4

--- a/solution.py
+++ b/solution.py
@@ -81,7 +81,8 @@
             put(window, start, rows_of(slot), halo, change)
     for phase in y_phases():
         rows = rows_of(halo_slot(chip, upward(chip, phase)))
-        put(window, HALO, rows, y_halos[phase], change)
+        if y_halos is not None:
+            put(window, HALO, rows, y_halos[phase], change)
         for x_phase in range(2):
             corner = corners[2 * phase + x_phase]
             start = halo_start(upward(along_x, x_phase), width, corner.shape[0])
@@ -172,6 +173,17 @@
     return core == jnp.where(upward(chip, phase), 1, 0)
 
 
+def load_kernel(orbitals, potential, orbitals_out, potential_out, arrived):
+    copies = [
+        pltpu.make_async_copy(orbitals, orbitals_out, arrived.at[0]),
+        pltpu.make_async_copy(potential, potential_out, arrived.at[1]),
+    ]
+    for copy in copies:
+        copy.start()
+    for copy in copies:
+        copy.wait()
+
+
 def pack_kernel(orbitals, received, potential, received_potential, *outs):
     core, chip, along_x = place()
     width = potential.shape[0]
@@ -191,7 +203,9 @@
 
             @pl.when(chosen)
             def _(t=t, phase=phase):
-                y_out[phase][...] = tiles[t][...]
+                y_out[phase][:width] = tiles[t][...]
+                half = width // 2
+                y_out[phase][width:] = local[t][pl.ds(core * half, half)]
                 for x_phase in range(2):
                     right = upward(along_x, x_phase)
                     out = d_out[2 * phase + x_phase]
@@ -199,41 +213,46 @@
                     out[HALO - 1 :] = local[t][near_planes(right, width, HALO - 3)]
 
 
-def fill_local(window, potential, received_potential, edge, passed, x_halos, corners):
+def fill_local(window, potential, received_potential, passed, y_halos, x_halos, corners):
     core, chip, _ = place()
+    width = potential.shape[0]
+    half = width // 2
+
+    def change(v):
+        return (v - 0.5) / 4.25
+
     fill(
         window,
         (potential, received_potential),
         [x.at[:, HALO:] for x in x_halos],
-        [edge] * len(y_phases()),
+        None,
         [c.at[HALO - 1 :] for c in corners],
-        lambda v: (v - 0.5) / 4.25,
+        change,
     )
     for phase in y_phases():
-        up = upward(chip, phase)
-
-        @pl.when(core != jnp.where(up, 1, 0))
-        def _(up=up):
-            put(window, HALO, rows_of(halo_slot(chip, up)), passed, lambda v: (v - 0.5) / 4.25)
+        rows = rows_of(halo_slot(chip, upward(chip, phase)))
+        put(window, HALO + core * half, rows, y_halos[phase].at[width:], change)
+        put(window, HALO + (1 - core) * half, rows, passed[phase], change)
 
 
 def first_kernel(*refs):
     count = len(y_phases())
-    orbitals, received, potential, received_potential, edge, passed = refs[:6]
-    y_halos, x_halos, corners = refs[6 : 6 + count], refs[6 + count : 8 + count], refs[8 + count : 8 + 3 * count]
-    own_out, other_out = refs[8 + 3 * count : 10 + 3 * count]
-    outs = refs[10 + 3 * count : 12 + 6 * count]
-    a, b, local = refs[12 + 6 * count :]
+    orbitals, received, potential, received_potential = refs[:4]
+    passed, halos = refs[4 : 4 + count], refs[4 + count : 6 + 4 * count]
+    y_halos, x_halos, corners = halos_of(halos)
+    own_out, other_out = refs[6 + 4 * count : 8 + 4 * count]
+    outs = refs[8 + 4 * count : 10 + 7 * count]
+    a, b, local = refs[10 + 7 * count :]
     core, chip, along_x = place()
     width, depth = potential.shape[0], potential.shape[2]
     fill(
         a,
         (orbitals.at[core], received.at[core]),
         [x.at[:, :HALO] for x in x_halos],
-        y_halos,
+        [y.at[:width] for y in y_halos],
         [c.at[: HALO - 1] for c in corners],
     )
-    fill_local(local, potential, received_potential, edge, passed, x_halos, corners)
+    fill_local(local, potential, received_potential, passed, *halos_of(halos))
     four_steps(a, b, local, z_matrix(depth))
     y_out, x_out, d_out = outs[:count], outs[count : count + 2], outs[count + 2 :]
     slots = own_slots(core, chip)
@@ -259,18 +278,23 @@
                 d_out[2 * phase + x_phase][:, :, lanes] = planes(slot, start, HALO - 1)
 
 
+def halos_of(refs):
+    count = len(y_phases())
+    return refs[:count], refs[count : count + 2], refs[count + 2 :]
+
+
 def second_kernel(*refs):
     count = len(y_phases())
-    orbitals, received, potential, received_potential, edge, passed, own, other = refs[:8]
-    halos = refs[8 : 10 + 3 * count]
-    y_halos, x_halos, corners = halos[:count], halos[count : count + 2], halos[count + 2 :]
-    p_x_halos = refs[10 + 3 * count : 12 + 3 * count]
-    p_corners = refs[12 + 3 * count : 12 + 5 * count]
-    keep, give, a, b, local = refs[12 + 5 * count :]
-    core, chip, along_x = place()
+    orbitals, received, potential, received_potential = refs[:4]
+    passed, local_halos = refs[4 : 4 + count], refs[4 + count : 6 + 4 * count]
+    own, other = refs[6 + 4 * count : 8 + 4 * count]
+    halos = refs[8 + 4 * count : 10 + 7 * count]
+    keep, give, a, b, local = refs[10 + 7 * count :]
+    core, chip, _ = place()
     width, depth = potential.shape[0], potential.shape[2]
+    y_halos, x_halos, corners = halos_of(halos)
     fill(a, (own, other), x_halos, y_halos, corners)
-    fill_local(local, potential, received_potential, edge, passed, p_x_halos, p_corners)
+    fill_local(local, potential, received_potential, passed, *halos_of(local_halos))
     four_steps(a, b, local, z_matrix(depth))
     start = (orbitals.at[core], received.at[core])
     outs = (keep, give)
@@ -394,19 +418,6 @@
     return lax.ppermute(value, "gy", [(y, y ^ 1) for y in range(count)])
 
 
-def face(value):
-    count, bands = lax.axis_size("gy"), lax.axis_size("band")
-    pairs = []
-    for y in range(count):
-        for band in range(bands):
-            to = partner(y, 1, count)
-            if to is not None:
-                pairs.append((y * bands + band, to * bands + band))
-            elif bands % 2 == 0:
-                pairs.append((y * bands + band, y * bands + (band ^ 1)))
-    return lax.ppermute(value, ("gy", "band"), pairs)
-
-
 def exchange(payloads):
     count = len(y_phases())
     halos = [meet(payloads[phase], y_phase=phase) for phase in y_phases()]
@@ -442,49 +453,58 @@
     window = (2, width + 2 * HALO, 8 * tile_count() + 2 * PAD, LANES)
     scratch = [pltpu.VMEM(window, jnp.float32)] * 3
 
-    edge = face(potential)
     received = swap(orbitals)
     received_potential = swap(potential)
     tile = (width, height, depth)
-
-    def payloads(in_x, in_corner):
+    orbitals, potential = pl.pallas_call(
+        load_kernel,
+        out_shape=[struct(*orbitals.shape), struct(*tile)],
+        in_specs=[pl.BlockSpec(memory_space=pl.ANY)] * 2,
+        out_specs=[VMEM] * 2,
+        scratch_shapes=[pltpu.SemaphoreType.DMA((2,))],
+        compiler_params=PARAMS,
+        name="load",
+    )(orbitals, potential)
+
+    def payloads(in_y, in_x, in_corner):
         return (
-            [struct(*tile)] * count
+            [struct(in_y, height, depth)] * count
             + [struct(2, in_x, height, depth)] * 2
             + [struct(in_corner, height, depth)] * (2 * count)
         )
 
     packed = pl.pallas_call(
         pack_kernel,
-        out_shape=payloads(2 * HALO - 2, 2 * HALO - 4),
+        out_shape=payloads(width + width // 2, 2 * HALO - 2, 2 * HALO - 4),
         in_specs=[VMEM] * 4,
         out_specs=[VMEM] * (2 + 3 * count),
         compiler_params=PARAMS,
         name="pack",
     )(orbitals, received, potential, received_potential)
     halos = exchange(packed)
-    edge, _ = lax.optimization_barrier((edge, halos[count]))
-    passed = swap(edge)
-    local = (potential, received_potential, edge, passed)
+    passed = []
+    for phase in y_phases():
+        half, *_ = lax.optimization_barrier((halos[phase][width:], *halos[count:]))
+        passed.append(swap(half))
+    local = (potential, received_potential, *passed, *halos)
     own, sibling, *packed = pl.pallas_call(
         first_kernel,
-        out_shape=[struct(*tile)] * 2 + payloads(HALO, HALO - 1),
-        in_specs=[VMEM] * (8 + 3 * count),
+        out_shape=[struct(*tile)] * 2 + payloads(width, HALO, HALO - 1),
+        in_specs=[VMEM] * (6 + 4 * count),
         out_specs=[VMEM] * (4 + 3 * count),
         scratch_shapes=scratch,
         compiler_params=PARAMS,
         name="first_round",
-    )(orbitals, received, *local, *halos)
-    second_halos = exchange(packed)
+    )(orbitals, received, *local)
     keep, give = pl.pallas_call(
         second_kernel,
         out_shape=[struct(*tile)] * 2,
-        in_specs=[VMEM] * (12 + 5 * count),
+        in_specs=[VMEM] * (10 + 7 * count),
         out_specs=[VMEM] * 2,
         scratch_shapes=scratch,
         compiler_params=PARAMS,
         name="second_round",
-    )(orbitals, received, *local, own, sibling, *second_halos, *halos[count:])
+    )(orbitals, received, *local, own, sibling, *exchange(packed))
 
     slots = [keep, swap(give)]
     for d in range(1, bands):

time: 72.4 us -> 69.8 us (0.964)
  starting transfers between devices: 29.1 us -> 25.5 us
  waiting for transfers between devices: 28.8 us -> 29.8 us
    ppermute x1 -> x0, starting transfers between devices: 2.94 us -> none  [face(): return lax.ppermute(value, ('gy', 'band'), pairs)]
    ppermute x10, starting transfers between devices: 16.3 us -> 14.6 us  [meet(): return lax.ppermute(value, ('gx', 'gy'), pairs)]
    ppermute x4, waiting for transfers between devices: 0.01 us -> 1.34 us  [swap(): return lax.ppermute(value, 'gy', [(y, y ^ 1) for y in range(count)])]
    ppermute x6, starting transfers between devices: 7.11 us -> 8.07 us  [of(): return lax.ppermute(value, axis, [(i, i ^ step) for i in range(count)])]
    pallas_call x2 -> x3, Pallas kernels: 5.15 us -> 5.2 us  [the longest x1 5.03 us: per_device(): pl.pallas_call(first_kernel, out_shape=[struct(*tile)] * 2 + payloads(wid...]
  transfers between devices with their start and end apart: 23 -> 22, of which waited for: 10 -> 9; matrix products, arithmetic and copies ran while one was open for 0% -> 0% of each run, Pallas kernels for 0% -> 0%
where the time goes in v5:
time: 69.8 us; the launch traced here: 69.7 us
  waiting for transfers between devices  29.8 us (43%)
  starting transfers between devices  25.5 us (37%)
  Pallas kernels  12.2 us (17%)
  local copies, waits for them, and re-layouts  2.01 us (3%)
    ppermute x10, starting transfers between devices, meet(): return lax.ppermute(value, ('gx', 'gy'), pairs)  14.6 us
    ppermute x10, waiting for transfers between devices, meet(): return lax.ppermute(value, ('gx', 'gy'), pairs)  10.4 us
    ppermute x6, starting transfers between devices, of(): return lax.ppermute(value, axis, [(i, i ^ step) for i in range(count)])  8.07 us
    ppermute x1, waiting for transfers between devices, per_device(): slots.append(lax.ppermute(give, ('gy', 'band'), crossed))  6.41 us
    ppermute x6, waiting for transfers between devices, of(): return lax.ppermute(value, axis, [(i, i ^ step) for i in range(count)])  5.91 us
    ppermute x1, waiting for transfers between devices, per_device(): slots.append(lax.ppermute(keep, ('gy', 'band'), same))  5.67 us
    pallas_call x1, Pallas kernels, per_device(): pl.pallas_call(first_kernel, out_shape=[struct(*tile)] * 2 + payloads(wid...  5.03 us
    pallas_call x1, Pallas kernels, per_device(): pl.pallas_call(second_kernel, out_shape=[struct(*tile)] * 2, in_specs=[VM...  5 us
  transfers between devices with their start and end apart: 22, of which 9 were waited for; matrix products, arithmetic and copies ran while one was open for 0% of the time, Pallas kernels for 0%

profile of v5, /device:TPU:0, one launch (start us, length us, event | category | flops | bytes accessed | tf_op | source)
XLA Modules:
  0.0 69.7 jit_solution(10169510213748871399)
XLA Ops:
  0.5 1.0 %copy-done = f32[2,32,8,256]{3,2,1,0:T(8,128)S(1)} copy-done((f32[2,32,8,256]{3,2,1,0:T(8,128)S(1)}, f32[2,32,8,256]{3,2,1,0:T(8,128)}, u32[]{:S(2)}) %copy-start) | copy-done | bytes 524312
  1.6 0.9 %copy-done.1 = f32[32,8,256]{2,1,0:T(8,128)S(1)} copy-done((f32[32,8,256]{2,1,0:T(8,128)S(1)}, f32[32,8,256]{2,1,0:T(8,128)}, u32[]{:S(2)}) %copy-start.1) | copy-done | bytes 262168
  2.7 3.0 %collective-permute-start.2 = (f32[48,8,256]{2,1,0:T(8,128)S(1)}, f32[48,8,256]{2,1,0:T(8,128)S(1)}, u32[]{:S(2)}, u32[]{:S(2)}) collective-permute-start(f32[48,8,256]{2,1,0:T(8,128)S(1)} %get-tuple-element.24), channel_id=1, source_target_pairs={{0,4},{2,6},{4,0},{6,2},{8,12},{10,14},{12,8},{14,10},{16,20},{18,... | collective-permute-start | bytes 1179656 | tf_op jit(solution)/shard_map/ppermute | solution.py:413
  5.7 1.6 %collective-permute-start.3 = (f32[2,14,8,256]{3,2,1,0:T(8,128)S(1)}, f32[2,14,8,256]{3,2,1,0:T(8,128)S(1)}, u32[]{:S(2)}, u32[]{:S(2)}) collective-permute-start(f32[2,14,8,256]{3,2,1,0:T(8,128)S(1)} %get-tuple-element.25), channel_id=1, source_target_pairs={{0,8},{2,10},{4,12},{6,14},{8,0},{10,2},{12,4},{14,6},{16,24},{18,... | collective-permute-start | bytes 688136 | tf_op jit(solution)/shard_map/ppermute | solution.py:413
  7.3 3.1 %collective-permute-start.5 = (f32[12,8,256]{2,1,0:T(8,128)S(1)}, f32[12,8,256]{2,1,0:T(8,128)S(1)}, u32[]{:S(2)}, u32[]{:S(2)}) collective-permute-start(f32[12,8,256]{2,1,0:T(8,128)S(1)} %get-tuple-element.27), channel_id=1, source_target_pairs={{0,12},{2,14},{4,8},{6,10},{8,4},{10,6},{12,0},{14,2},{16,28},{18,... | collective-permute-start | bytes 294920 | tf_op jit(solution)/shard_map/ppermute | solution.py:413
  10.4 6.7 %collective-permute-done.2.refs_5_ = f32[48,8,256]{2,1,0:T(8,128)S(1)} collective-permute-done((f32[48,8,256]{2,1,0:T(8,128)S(1)}, f32[48,8,256]{2,1,0:T(8,128)S(1)}, u32[]{:S(2)}, u32[]{:S(2)}) %collective-permute-start.2) | collective-permute-done | bytes 393248 | tf_op jit(solution)/shard_map/ppermute | solution.py:413
  17.3 1.3 %collective-permute-done.7.refs_4_ = f32[16,8,256]{2,1,0:T(8,128)S(1)} collective-permute-done((f32[16,8,256]{2,1,0:T(8,128)S(1)}, f32[16,8,256]{2,1,0:T(8,128)S(1)}, u32[]{:S(2)}, u32[]{:S(2)}) %collective-permute-start.7) | collective-permute-done | bytes 131104 | tf_op jit(solution)/shard_map/ppermute | solution.py:418
  18.6 5.0 %first_round.1 = (f32[32,8,256]{2,1,0:T(8,128)S(1)}, f32[32,8,256]{2,1,0:T(8,128)S(1)}, f32[32,8,256]{2,1,0:T(8,128)S(1)}, f32[2,8,8,256]{3,2,1,0:T(8,128)S(1)},...) custom-call(f32[2,32,8,256]{3,2,1,0:T(8,128)S(1)} %get-tuple-element.22.orbitals.refs_0_, ...), custom_call_target="tpu_custom_call" | custom-call | tf_op jit(solution)/shard_map/first_round/pallas_call | solution.py:490
  23.6 1.8 %collective-permute-start.8 = (f32[32,8,256]{2,1,0:T(8,128)S(1)}, f32[32,8,256]{2,1,0:T(8,128)S(1)}, u32[]{:S(2)}, u32[]{:S(2)}) collective-permute-start(f32[32,8,256]{2,1,0:T(8,128)S(1)} %get-tuple-element.32), channel_id=1, source_target_pairs={{0,4},{2,6},{4,0},{6,2},{8,12},{10,14},{12,8},{14,10},{16,20},{18,... | collective-permute-start | bytes 786440 | tf_op jit(solution)/shard_map/ppermute | solution.py:413
  25.4 3.6 %collective-permute-start.9 = (f32[2,8,8,256]{3,2,1,0:T(8,128)S(1)}, f32[2,8,8,256]{3,2,1,0:T(8,128)S(1)}, u32[]{:S(2)}, u32[]{:S(2)}) collective-permute-start(f32[2,8,8,256]{3,2,1,0:T(8,128)S(1)} %get-tuple-element.33), channel_id=1, source_target_pairs={{0,8},{2,10},{4,12},{6,14},{8,0},{10,2},{12,4},{14,6},{16,24},{18,... | collective-permute-start | bytes 393224 | tf_op jit(solution)/shard_map/ppermute | solution.py:413
  29.1 1.5 %collective-permute-start.11 = (f32[7,8,256]{2,1,0:T(8,128)S(1)}, f32[7,8,256]{2,1,0:T(8,128)S(1)}, u32[]{:S(2)}, u32[]{:S(2)}) collective-permute-start(f32[7,8,256]{2,1,0:T(8,128)S(1)} %get-tuple-element.35), channel_id=1, source_target_pairs={{0,12},{2,14},{4,8},{6,10},{8,4},{10,6},{12,0},{14,2},{16,28},{18,... | collective-permute-start | bytes 172040 | tf_op jit(solution)/shard_map/ppermute | solution.py:413
  30.6 3.7 %collective-permute-done.11.refs_15_ = f32[7,8,256]{2,1,0:T(8,128)S(1)} collective-permute-done((f32[7,8,256]{2,1,0:T(8,128)S(1)}, f32[7,8,256]{2,1,0:T(8,128)S(1)}, u32[]{:S(2)}, u32[]{:S(2)}) %collective-permute-start.11) | collective-permute-done | bytes 57376 | tf_op jit(solution)/shard_map/ppermute | solution.py:413
  34.3 5.0 %second_round.1 = (f32[32,8,256]{2,1,0:T(8,128)S(1)}, f32[32,8,256]{2,1,0:T(8,128)S(1)}) custom-call(f32[2,32,8,256]{3,2,1,0:T(8,128)S(1)} %get-tuple-element.22.orbitals.refs_0_, f32[2,32,8,256]{3,2,1,0:T(8,128)S(1)} %collective-permute-done.received.refs_1_, f32[32,8,256]{2,1,0:T(8,128)S(1)} %get-tuple-element.23.potential.refs_2_, ...), custom_call_target="tpu_custom_call" | custom-call | tf_op jit(solution)/shard_map/second_round/pallas_call | solution.py:499
  39.3 0.9 %collective-permute-start.15 = (f32[32,8,256]{2,1,0:T(8,128)S(1)}, f32[32,8,256]{2,1,0:T(8,128)S(1)}, u32[]{:S(2)}, u32[]{:S(2)}) collective-permute-start(f32[32,8,256]{2,1,0:T(8,128)S(1)} %get-tuple-element.38), channel_id=1, source_target_pairs={{0,3},{1,2},{2,1},{3,0},{4,7},{5,6},{6,5},{7,4},{8,11},{9,10},{10,... | collective-permute-start | bytes 786440 | tf_op jit(solution)/shard_map/ppermute | solution.py:518
  41.5 6.4 %collective-permute-done.15.refs_3_.refs_5_ = f32[32,8,256]{2,1,0:T(8,128)S(1)} collective-permute-done((f32[32,8,256]{2,1,0:T(8,128)S(1)}, f32[32,8,256]{2,1,0:T(8,128)S(1)}, u32[]{:S(2)}, u32[]{:S(2)}) %collective-permute-start.15) | collective-permute-done | bytes 262176 | tf_op jit(solution)/shard_map/ppermute | solution.py:518
  47.9 5.7 %collective-permute-done.14.refs_2_.refs_4_ = f32[32,8,256]{2,1,0:T(8,128)S(1)} collective-permute-done((f32[32,8,256]{2,1,0:T(8,128)S(1)}, f32[32,8,256]{2,1,0:T(8,128)S(1)}, u32[]{:S(2)}, u32[]{:S(2)}) %collective-permute-start.14) | collective-permute-done | bytes 262176 | tf_op jit(solution)/shard_map/ppermute | solution.py:517
  54.7 1.0 %collective-permute-start.17 = (f32[8,128]{1,0:T(8,128)S(1)}, f32[8,128]{1,0:T(8,128)S(1)}, u32[]{:S(2)}, u32[]{:S(2)}) collective-permute-start(f32[8,128]{1,0:T(8,128)S(1)} %correlation.1), channel_id=1, source_target_pairs={{0,4},{2,6},{4,0},{6,2},{1,5},{3,7},{5,1},{7,3},{8,12},{10,14},{12... | collective-permute-start | bytes 12296 | tf_op jit(solution)/shard_map/ppermute | solution.py:437
  55.9 1.2 %collective-permute-done.18 = f32[8,128]{1,0:T(8,128)S(1)} collective-permute-done((f32[8,128]{1,0:T(8,128)S(1)}, f32[8,128]{1,0:T(8,128)S(1)}, u32[]{:S(2)}, u32[]{:S(2)}) %collective-permute-start.18) | collective-permute-done | bytes 4128 | tf_op jit(solution)/shard_map/ppermute | solution.py:437
  57.1 1.2 %collective-permute-done.17 = f32[8,128]{1,0:T(8,128)S(1)} collective-permute-done((f32[8,128]{1,0:T(8,128)S(1)}, f32[8,128]{1,0:T(8,128)S(1)}, u32[]{:S(2)}, u32[]{:S(2)}) %collective-permute-start.17) | collective-permute-done | bytes 4128 | tf_op jit(solution)/shard_map/ppermute | solution.py:437
  58.3 3.4 %collective-permute-start.21 = (f32[8,128]{1,0:T(8,128)S(1)}, f32[8,128]{1,0:T(8,128)S(1)}, u32[]{:S(2)}, u32[]{:S(2)}) collective-permute-start(f32[8,128]{1,0:T(8,128)S(1)} %add_add_fusion.1), channel_id=1, source_target_pairs={{0,24},{8,16},{16,8},{24,0},{1,25},{9,17},{17,9},{25,1},{2,26},{10... | collective-permute-start | bytes 12296 | tf_op jit(solution)/shard_map/ppermute | solution.py:437
  61.7 2.6 %collective-permute-start.20 = (f32[8,128]{1,0:T(8,128)S(1)}, f32[8,128]{1,0:T(8,128)S(1)}, u32[]{:S(2)}, u32[]{:S(2)}) collective-permute-start(f32[8,128]{1,0:T(8,128)S(1)} %add_add_fusion.1), channel_id=1, source_target_pairs={{0,16},{8,24},{16,0},{24,8},{1,17},{9,25},{17,1},{25,9},{2,18},{10... | collective-permute-start | bytes 12296 | tf_op jit(solution)/shard_map/ppermute | solution.py:437
  64.5 1.8 %collective-permute-done.20 = f32[8,128]{1,0:T(8,128)S(1)} collective-permute-done((f32[8,128]{1,0:T(8,128)S(1)}, f32[8,128]{1,0:T(8,128)S(1)}, u32[]{:S(2)}, u32[]{:S(2)}) %collective-permute-start.20) | collective-permute-done | bytes 4128 | tf_op jit(solution)/shard_map/ppermute | solution.py:437
  66.2 1.7 %collective-permute-done.19 = f32[8,128]{1,0:T(8,128)S(1)} collective-permute-done((f32[8,128]{1,0:T(8,128)S(1)}, f32[8,128]{1,0:T(8,128)S(1)}, u32[]{:S(2)}, u32[]{:S(2)}) %collective-permute-start.19) | collective-permute-done | bytes 4128 | tf_op jit(solution)/shard_map/ppermute | solution.py:437
  68.0 1.7 %basis.1 = f32[2,32,8,256]{3,2,1,0:T(8,128)} custom-call(f32[8,128]{1,0:T(8,128)S(1)} %add_add_fusion.refs_0_, s32[4]{0:T(128)S(1)} %copy-done.2, f32[32,8,256]{2,1,0:T(8,128)S(1)} %get-tuple-element.37.refs_0_.refs_2_, f32[32,8,256]{2,1,0:T(8,128)S(1)} %collective-permute-done.13.refs_1_.refs_3_, f32[32,8,256]{2,1,0:T(8,128)S(1)} %collective-permute-done.14.refs_2_.refs_4_, ...), custom_call_target="tpu_custom_call" | custom-call | tf_op jit(solution)/shard_map/basis/pallas_call | solution.py:528
  (35 shorter events, 3.5 us)
Async XLA Ops:
  0.0 2.6 %collective-permute-start = (f32[2,32,8,256]{3,2,1,0:T(8,128)}, f32[2,32,8,256]{3,2,1,0:T(8,128)S(1)}, u32[]{:S(2)}, u32[]{:S(2)}) collective-permute-start(f32[2,32,8,256]{3,2,1,0:T(8,128)} %orbitals.1), channel_id=1, source_target_pairs={{0,2},{2,0},{4,6},{6,4},{1,3},{3,1},{5,7},{7,5},{8,10},{10,8},{12,... | collective-permute-start | bytes 1572872 | tf_op jit(solution)/shard_map/ppermute | solution.py:418
  0.5 2.1 %collective-permute-start.1 = (f32[32,8,256]{2,1,0:T(8,128)}, f32[32,8,256]{2,1,0:T(8,128)S(1)}, u32[]{:S(2)}, u32[]{:S(2)}) collective-permute-start(f32[32,8,256]{2,1,0:T(8,128)} %potential.1), channel_id=1, source_target_pairs={{0,2},{2,0},{4,6},{6,4},{1,3},{3,1},{5,7},{7,5},{8,10},{10,8},{12,... | collective-permute-start | bytes 786440 | tf_op jit(solution)/shard_map/ppermute | solution.py:418
  0.5 1.0 %copy-start = (f32[2,32,8,256]{3,2,1,0:T(8,128)S(1)}, f32[2,32,8,256]{3,2,1,0:T(8,128)}, u32[]{:S(2)}) copy-start(f32[2,32,8,256]{3,2,1,0:T(8,128)} %orbitals.1) | copy-start | bytes 1572868
  2.7 14.4 %collective-permute-start.2 = (f32[48,8,256]{2,1,0:T(8,128)S(1)}, f32[48,8,256]{2,1,0:T(8,128)S(1)}, u32[]{:S(2)}, u32[]{:S(2)}) collective-permute-start(f32[48,8,256]{2,1,0:T(8,128)S(1)} %get-tuple-element.24), channel_id=1, source_target_pairs={{0,4},{2,6},{4,0},{6,2},{8,12},{10,14},{12,8},{14,10},{16,20},{18,... | collective-permute-start | bytes 1179656 | tf_op jit(solution)/shard_map/ppermute | solution.py:413
  5.7 11.4 %collective-permute-start.3 = (f32[2,14,8,256]{3,2,1,0:T(8,128)S(1)}, f32[2,14,8,256]{3,2,1,0:T(8,128)S(1)}, u32[]{:S(2)}, u32[]{:S(2)}) collective-permute-start(f32[2,14,8,256]{3,2,1,0:T(8,128)S(1)} %get-tuple-element.25), channel_id=1, source_target_pairs={{0,8},{2,10},{4,12},{6,14},{8,0},{10,2},{12,4},{14,6},{16,24},{18,... | collective-permute-start | bytes 688136 | tf_op jit(solution)/shard_map/ppermute | solution.py:413
  7.3 9.9 %collective-permute-start.4 = (f32[2,14,8,256]{3,2,1,0:T(8,128)S(1)}, f32[2,14,8,256]{3,2,1,0:T(8,128)S(1)}, u32[]{:S(2)}, u32[]{:S(2)}) collective-permute-start(f32[2,14,8,256]{3,2,1,0:T(8,128)S(1)} %get-tuple-element.26), channel_id=1, source_target_pairs={{0,2},{2,0},{4,6},{6,4},{8,16},{10,18},{12,20},{14,22},{16,8},{18,... | collective-permute-start | bytes 688136 | tf_op jit(solution)/shard_map/ppermute | solution.py:413
  7.3 9.8 %collective-permute-start.5 = (f32[12,8,256]{2,1,0:T(8,128)S(1)}, f32[12,8,256]{2,1,0:T(8,128)S(1)}, u32[]{:S(2)}, u32[]{:S(2)}) collective-permute-start(f32[12,8,256]{2,1,0:T(8,128)S(1)} %get-tuple-element.27), channel_id=1, source_target_pairs={{0,12},{2,14},{4,8},{6,10},{8,4},{10,6},{12,0},{14,2},{16,28},{18,... | collective-permute-start | bytes 294920 | tf_op jit(solution)/shard_map/ppermute | solution.py:413
  10.4 6.7 %collective-permute-start.6 = (f32[12,8,256]{2,1,0:T(8,128)S(1)}, f32[12,8,256]{2,1,0:T(8,128)S(1)}, u32[]{:S(2)}, u32[]{:S(2)}) collective-permute-start(f32[12,8,256]{2,1,0:T(8,128)S(1)} %get-tuple-element.28), channel_id=1, source_target_pairs={{0,2},{2,0},{4,6},{6,4},{8,20},{10,22},{12,16},{14,18},{16,12},{18... | collective-permute-start | bytes 294920 | tf_op jit(solution)/shard_map/ppermute | solution.py:413
  17.2 1.4 %collective-permute-start.7 = (f32[16,8,256]{2,1,0:T(8,128)S(1)}, f32[16,8,256]{2,1,0:T(8,128)S(1)}, u32[]{:S(2)}, u32[]{:S(2)}) collective-permute-start(f32[16,8,256]{2,1,0:T(8,128)S(1)} %slice.4), channel_id=1, source_target_pairs={{0,2},{2,0},{4,6},{6,4},{1,3},{3,1},{5,7},{7,5},{8,10},{10,8},{12,... | collective-permute-start | bytes 393224 | tf_op jit(solution)/shard_map/ppermute | solution.py:418
  23.6 10.7 %collective-permute-start.8 = (f32[32,8,256]{2,1,0:T(8,128)S(1)}, f32[32,8,256]{2,1,0:T(8,128)S(1)}, u32[]{:S(2)}, u32[]{:S(2)}) collective-permute-start(f32[32,8,256]{2,1,0:T(8,128)S(1)} %get-tuple-element.32), channel_id=1, source_target_pairs={{0,4},{2,6},{4,0},{6,2},{8,12},{10,14},{12,8},{14,10},{16,20},{18,... | collective-permute-start | bytes 786440 | tf_op jit(solution)/shard_map/ppermute | solution.py:413
  25.4 8.9 %collective-permute-start.9 = (f32[2,8,8,256]{3,2,1,0:T(8,128)S(1)}, f32[2,8,8,256]{3,2,1,0:T(8,128)S(1)}, u32[]{:S(2)}, u32[]{:S(2)}) collective-permute-start(f32[2,8,8,256]{3,2,1,0:T(8,128)S(1)} %get-tuple-element.33), channel_id=1, source_target_pairs={{0,8},{2,10},{4,12},{6,14},{8,0},{10,2},{12,4},{14,6},{16,24},{18,... | collective-permute-start | bytes 393224 | tf_op jit(solution)/shard_map/ppermute | solution.py:413
  29.1 5.2 %collective-permute-start.10 = (f32[2,8,8,256]{3,2,1,0:T(8,128)S(1)}, f32[2,8,8,256]{3,2,1,0:T(8,128)S(1)}, u32[]{:S(2)}, u32[]{:S(2)}) collective-permute-start(f32[2,8,8,256]{3,2,1,0:T(8,128)S(1)} %get-tuple-element.34), channel_id=1, source_target_pairs={{0,2},{2,0},{4,6},{6,4},{8,16},{10,18},{12,20},{14,22},{16,8},{18,... | collective-permute-start | bytes 393224 | tf_op jit(solution)/shard_map/ppermute | solution.py:413
  29.1 5.2 %collective-permute-start.11 = (f32[7,8,256]{2,1,0:T(8,128)S(1)}, f32[7,8,256]{2,1,0:T(8,128)S(1)}, u32[]{:S(2)}, u32[]{:S(2)}) collective-permute-start(f32[7,8,256]{2,1,0:T(8,128)S(1)} %get-tuple-element.35), channel_id=1, source_target_pairs={{0,12},{2,14},{4,8},{6,10},{8,4},{10,6},{12,0},{14,2},{16,28},{18,... | collective-permute-start | bytes 172040 | tf_op jit(solution)/shard_map/ppermute | solution.py:413
  30.6 3.7 %collective-permute-start.12 = (f32[7,8,256]{2,1,0:T(8,128)S(1)}, f32[7,8,256]{2,1,0:T(8,128)S(1)}, u32[]{:S(2)}, u32[]{:S(2)}) collective-permute-start(f32[7,8,256]{2,1,0:T(8,128)S(1)} %get-tuple-element.36), channel_id=1, source_target_pairs={{0,2},{2,0},{4,6},{6,4},{8,20},{10,22},{12,16},{14,18},{16,12},{18... | collective-permute-start | bytes 172040 | tf_op jit(solution)/shard_map/ppermute | solution.py:413
  39.3 8.6 %collective-permute-start.15 = (f32[32,8,256]{2,1,0:T(8,128)S(1)}, f32[32,8,256]{2,1,0:T(8,128)S(1)}, u32[]{:S(2)}, u32[]{:S(2)}) collective-permute-start(f32[32,8,256]{2,1,0:T(8,128)S(1)} %get-tuple-element.38), channel_id=1, source_target_pairs={{0,3},{1,2},{2,1},{3,0},{4,7},{5,6},{6,5},{7,4},{8,11},{9,10},{10,... | collective-permute-start | bytes 786440 | tf_op jit(solution)/shard_map/ppermute | solution.py:518
  40.2 7.7 %collective-permute-start.13 = (f32[32,8,256]{2,1,0:T(8,128)S(1)}, f32[32,8,256]{2,1,0:T(8,128)S(1)}, u32[]{:S(2)}, u32[]{:S(2)}) collective-permute-start(f32[32,8,256]{2,1,0:T(8,128)S(1)} %get-tuple-element.38), channel_id=1, source_target_pairs={{0,2},{2,0},{4,6},{6,4},{1,3},{3,1},{5,7},{7,5},{8,10},{10,8},{12,... | collective-permute-start | bytes 786440 | tf_op jit(solution)/shard_map/ppermute | solution.py:418
  41.0 12.6 %collective-permute-start.14 = (f32[32,8,256]{2,1,0:T(8,128)S(1)}, f32[32,8,256]{2,1,0:T(8,128)S(1)}, u32[]{:S(2)}, u32[]{:S(2)}) collective-permute-start(f32[32,8,256]{2,1,0:T(8,128)S(1)} %get-tuple-element.37.refs_0_.refs_2_), channel_id=1, source_target_pairs={{0,1},{1,0},{2,3},{3,2},{4,5},{5,4},{6,7},{7,6},{8,9},{9,8},{10,11... | collective-permute-start | bytes 786440 | tf_op jit(solution)/shard_map/ppermute | solution.py:517
  54.0 3.1 %collective-permute-start.18 = (f32[8,128]{1,0:T(8,128)S(1)}, f32[8,128]{1,0:T(8,128)S(1)}, u32[]{:S(2)}, u32[]{:S(2)}) collective-permute-start(f32[8,128]{1,0:T(8,128)S(1)} %correlation.1), channel_id=1, source_target_pairs={{0,6},{2,4},{4,2},{6,0},{1,7},{3,5},{5,3},{7,1},{8,14},{10,12},{12... | collective-permute-start | bytes 12296 | tf_op jit(solution)/shard_map/ppermute | solution.py:437
  54.7 3.6 %collective-permute-start.17 = (f32[8,128]{1,0:T(8,128)S(1)}, f32[8,128]{1,0:T(8,128)S(1)}, u32[]{:S(2)}, u32[]{:S(2)}) collective-permute-start(f32[8,128]{1,0:T(8,128)S(1)} %correlation.1), channel_id=1, source_target_pairs={{0,4},{2,6},{4,0},{6,2},{1,5},{3,7},{5,1},{7,3},{8,12},{10,14},{12... | collective-permute-start | bytes 12296 | tf_op jit(solution)/shard_map/ppermute | solution.py:437
  55.7 2.6 %collective-permute-start.16 = (f32[8,128]{1,0:T(8,128)S(1)}, f32[8,128]{1,0:T(8,128)S(1)}, u32[]{:S(2)}, u32[]{:S(2)}) collective-permute-start(f32[8,128]{1,0:T(8,128)S(1)} %correlation.1), channel_id=1, source_target_pairs={{0,2},{2,0},{4,6},{6,4},{1,3},{3,1},{5,7},{7,5},{8,10},{10,8},{12,... | collective-permute-start | bytes 12296 | tf_op jit(solution)/shard_map/ppermute | solution.py:437
  58.3 9.7 %copy-start.2 = (s32[4]{0:T(128)S(1)}, s32[4]{0:T(128)}, u32[]{:S(2)}) copy-start(s32[4]{0:T(128)} %refs_1_.1) | copy-start | bytes 52
  58.3 6.1 %collective-permute-start.21 = (f32[8,128]{1,0:T(8,128)S(1)}, f32[8,128]{1,0:T(8,128)S(1)}, u32[]{:S(2)}, u32[]{:S(2)}) collective-permute-start(f32[8,128]{1,0:T(8,128)S(1)} %add_add_fusion.1), channel_id=1, source_target_pairs={{0,24},{8,16},{16,8},{24,0},{1,25},{9,17},{17,9},{25,1},{2,26},{10... | collective-permute-start | bytes 12296 | tf_op jit(solution)/shard_map/ppermute | solution.py:437
  61.7 4.5 %collective-permute-start.20 = (f32[8,128]{1,0:T(8,128)S(1)}, f32[8,128]{1,0:T(8,128)S(1)}, u32[]{:S(2)}, u32[]{:S(2)}) collective-permute-start(f32[8,128]{1,0:T(8,128)S(1)} %add_add_fusion.1), channel_id=1, source_target_pairs={{0,16},{8,24},{16,0},{24,8},{1,17},{9,25},{17,1},{25,9},{2,18},{10... | collective-permute-start | bytes 12296 | tf_op jit(solution)/shard_map/ppermute | solution.py:437
  64.3 3.6 %collective-permute-start.19 = (f32[8,128]{1,0:T(8,128)S(1)}, f32[8,128]{1,0:T(8,128)S(1)}, u32[]{:S(2)}, u32[]{:S(2)}) collective-permute-start(f32[8,128]{1,0:T(8,128)S(1)} %add_add_fusion.1), channel_id=1, source_target_pairs={{0,8},{8,0},{16,24},{24,16},{1,9},{9,1},{17,25},{25,17},{2,10},{10... | collective-permute-start | bytes 12296 | tf_op jit(solution)/shard_map/ppermute | solution.py:437
  (1 other events, 0.9 us)

commit v6 on v5

--- a/solution.py
+++ b/solution.py
@@ -289,7 +289,9 @@
     passed, local_halos = refs[4 : 4 + count], refs[4 + count : 6 + 4 * count]
     own, other = refs[6 + 4 * count : 8 + 4 * count]
     halos = refs[8 + 4 * count : 10 + 7 * count]
-    keep, give, a, b, local = refs[10 + 7 * count :]
+    keep, give = refs[10 + 7 * count : 12 + 7 * count]
+    early = refs[12 + 7 * count : -3]
+    a, b, local = refs[-3:]
     core, chip, _ = place()
     width, depth = potential.shape[0], potential.shape[2]
     y_halos, x_halos, corners = halos_of(halos)
@@ -303,6 +305,25 @@
             lanes = slice(half * LANES, (half + 1) * LANES)
             tile = a[half, HALO : HALO + width, rows_of(slot), :]
             outs[t][:, :, lanes] = 2.0 * tile - start[t][:, :, lanes]
+    half = width // 2
+    for d in range(1, lax.axis_size("band")):
+        upper, _ = halves_met(d)
+        for out, whole in zip(early[2 * d - 2 : 2 * d], outs):
+            out[...] = whole[pl.ds(upper * half, half)]
+
+
+def halves_met(d):
+    bands, band = lax.axis_size("band"), lax.axis_index("band")
+    to, source = lax.rem(band + d, bands), lax.rem(band + bands - d, bands)
+    return jnp.where(band < to, 1, 0), jnp.where(source < band, 1, 0)
+
+
+def late_kernel(keep, sibling, *outs):
+    half = keep.shape[0] // 2
+    for d, out in enumerate(outs, 1):
+        upper, _ = halves_met(d)
+        for t, whole in enumerate((keep, sibling)):
+            out[t] = whole[pl.ds((1 - upper) * half, half)]
 
 
 def slot_orbitals(bands):
@@ -315,27 +336,37 @@
     return names
 
 
-def correlation_kernel(bands, *refs):
-    slots, out = refs[:-1], refs[-1]
+def correlation_kernel(*refs):
+    bands = lax.axis_size("band")
+    own, early, out = refs[:2], refs[2:-1], refs[-1]
     names = slot_orbitals(bands)
     row = lax.broadcasted_iota(jnp.int32, (8, LANES), 0)
     column = lax.broadcasted_iota(jnp.int32, (8, LANES), 1)
-    count = len(slots)
-    pairs = [(i, j) for i in range(count) for j in range(i, count)]
-    width, height, depth = slots[0].shape
+    pairs = [(0, 0), (0, 1), (1, 1)] + [(i, 2 * d + j) for d in range(1, bands) for i in range(2) for j in range(2)]
+    width, height, depth = own[0].shape
+    half = width // 2
+
+    def summed_up(value):
+        total = jnp.sum(value, axis=0)
+        return sum(total[:, k * LANES : (k + 1) * LANES] for k in range(depth // LANES))
 
     def body(index, totals):
-        planes = [s[pl.ds(index * PLANES, PLANES)] for s in slots]
+        def planes(ref, upper):
+            return ref[pl.ds(upper * half + index * PLANES, PLANES)]
+
+        halves = [[planes(ref, upper) for ref in own] for upper in range(2)]
         found = []
         for (i, j), total in zip(pairs, totals):
-            product = jnp.sum(planes[i] * planes[j], axis=0)
-            for half in range(depth // LANES):
-                total = total + product[:, half * LANES : (half + 1) * LANES]
+            if j < 2:
+                total = total + summed_up(halves[0][i] * halves[0][j] + halves[1][i] * halves[1][j])
+            else:
+                _, upper = halves_met(j // 2)
+                total = total + summed_up(planes(own[i], upper) * planes(early[j - 2], 0))
             found.append(total)
         return tuple(found)
 
     zero = jnp.zeros((height, LANES), jnp.float32)
-    totals = lax.fori_loop(0, width // PLANES, body, (zero,) * len(pairs))
+    totals = lax.fori_loop(0, half // PLANES, body, (zero,) * len(pairs))
     result = jnp.zeros((8, LANES), jnp.float32)
     for (i, j), total in zip(pairs, totals):
         here = ((row == names[i]) & (column == names[j])) | ((row == names[j]) & (column == names[i]))
@@ -345,8 +376,17 @@
 
 def basis_kernel(bands, cells, *refs):
     correlation, order = refs[:2]
-    slots = refs[2 : 2 + 2 * bands]
-    out, mixing = refs[2 + 2 * bands :]
+    early, late = refs[4 : 2 + 2 * bands], refs[2 + 2 * bands : 1 + 3 * bands]
+    out, mixing = refs[1 + 3 * bands : 3 + 3 * bands]
+    joined = refs[3 + 3 * bands :]
+    slots = list(refs[2:4]) + list(joined)
+    for d in range(1, bands):
+        _, upper = halves_met(d)
+        for t in range(2):
+            whole = joined[2 * d - 2 + t]
+            half = whole.shape[0] // 2
+            whole[pl.ds(upper * half, half)] = early[2 * d - 2 + t][...]
+            whole[pl.ds((1 - upper) * half, half)] = late[d - 1][t]
     names = slot_orbitals(bands)
     count = 2 * bands
     band = lax.axis_index("band")
@@ -418,6 +458,15 @@
     return lax.ppermute(value, "gy", [(y, y ^ 1) for y in range(count)])
 
 
+def to_band(value, d, crossed=False):
+    bands = lax.axis_size("band")
+    pairs = []
+    for y in range(lax.axis_size("gy")):
+        for band in range(bands):
+            pairs.append((y * bands + band, (y ^ crossed) * bands + (band + d) % bands))
+    return lax.ppermute(value, ("gy", "band"), pairs)
+
+
 def exchange(payloads):
     count = len(y_phases())
     halos = [meet(payloads[phase], y_phase=phase) for phase in y_phases()]
@@ -496,44 +545,47 @@
         compiler_params=PARAMS,
         name="first_round",
     )(orbitals, received, *local)
-    keep, give = pl.pallas_call(
+    half = (width // 2, height, depth)
+    keep, give, *early = pl.pallas_call(
         second_kernel,
-        out_shape=[struct(*tile)] * 2,
+        out_shape=[struct(*tile)] * 2 + [struct(*half)] * (2 * bands - 2),
         in_specs=[VMEM] * (10 + 7 * count),
-        out_specs=[VMEM] * 2,
+        out_specs=[VMEM] * (2 * bands),
         scratch_shapes=scratch,
         compiler_params=PARAMS,
         name="second_round",
     )(orbitals, received, *local, own, sibling, *exchange(packed))
 
-    slots = [keep, swap(give)]
-    for d in range(1, bands):
-        same, crossed = [], []
-        for y in range(lax.axis_size("gy")):
-            for b in range(bands):
-                to = (b + d) % bands
-                same.append((y * bands + b, y * bands + to))
-                crossed.append((y * bands + b, (y ^ 1) * bands + to))
-        slots.append(lax.ppermute(keep, ("gy", "band"), same))
-        slots.append(lax.ppermute(give, ("gy", "band"), crossed))
+    early = [to_band(value, 1 + k // 2, crossed=k % 2 == 1) for k, value in enumerate(early)]
+    sibling = swap(give)
+    late = pl.pallas_call(
+        late_kernel,
+        out_shape=[struct(2, *half)] * (bands - 1),
+        in_specs=[VMEM] * 2,
+        out_specs=[VMEM] * (bands - 1),
+        compiler_params=PARAMS,
+        name="late",
+    )(keep, sibling)
+    late = [to_band(value, d) for d, value in enumerate(late, 1)]
     partial_value = pl.pallas_call(
-        functools.partial(correlation_kernel, bands),
+        correlation_kernel,
         out_shape=struct(8, LANES),
-        in_specs=[VMEM] * len(slots),
+        in_specs=[VMEM] * (2 * bands),
         out_specs=VMEM,
         compiler_params=PARAMS,
         name="correlation",
-    )(*slots)
-    correlation = summed(summed(partial_value, "gy"), "gx")
+    )(keep, sibling, *early)
+    correlation = summed(summed(summed(partial_value, "band"), "gy"), "gx")
     return pl.pallas_call(
         functools.partial(basis_kernel, bands, cells),
         out_shape=struct(*orbitals.shape),
-        in_specs=[SMEM, SMEM] + [VMEM] * len(slots),
+        in_specs=[SMEM, SMEM] + [VMEM] * (3 * bands - 1),
         out_specs=VMEM,
-        scratch_shapes=[pltpu.VMEM((2 * bands, 2 * bands, 8, LANES), jnp.float32)],
+        scratch_shapes=[pltpu.VMEM((2 * bands, 2 * bands, 8, LANES), jnp.float32)]
+        + [pltpu.VMEM(tile, jnp.float32)] * (2 * bands - 2),
         compiler_params=PARAMS,
         name="basis",
-    )(correlation, order, *slots)
+    )(correlation, order, keep, sibling, *early, *late)
 
 
 def solution(mesh):

time: 69.8 us -> 66.5 us (0.953)
  waiting for transfers between devices: 29.8 us -> 24 us
  starting transfers between devices: 25.5 us -> 28 us
    ppermute x2 -> x3, waiting for transfers between devices: 12.1 us -> 6.41 us  [to_band(): return lax.ppermute(value, ('gy', 'band'), pairs)]
    ppermute x2 -> x3, starting transfers between devices: 1.42 us -> 3.42 us  [to_band(): return lax.ppermute(value, ('gy', 'band'), pairs)]
    ppermute x6 -> x7, starting transfers between devices: 8.07 us -> 9.25 us  [of(): return lax.ppermute(value, axis, [(i, i ^ step) for i in range(count)])]
    ppermute x4, starting transfers between devices: 1.37 us -> 0.65 us  [swap(): return lax.ppermute(value, 'gy', [(y, y ^ 1) for y in range(count)])]
    ppermute x6 -> x7, waiting for transfers between devices: 5.91 us -> 5.79 us  [of(): return lax.ppermute(value, axis, [(i, i ^ step) for i in range(count)])]
    pallas_call x2 -> x3, Pallas kernels: 5.34 us -> 5.26 us  [the longest x1 5.02 us: per_device(): pl.pallas_call(second_kernel, out_shape=[struct(*tile)] * 2 + [struct(*ha...]
  transfers between devices with their start and end apart: 22 -> 24, of which waited for: 9 -> 9; matrix products, arithmetic and copies ran while one was open for 0% -> 0% of each run, Pallas kernels for 0% -> 0%
where the time goes in v6:
time: 66.5 us; the launch traced here: 66.3 us
  starting transfers between devices  28 us (42%)
  waiting for transfers between devices  24 us (36%)
  Pallas kernels  12.2 us (18%)
  local copies, waits for them, and re-layouts  2.01 us (3%)
    ppermute x10, starting transfers between devices, meet(): return lax.ppermute(value, ('gx', 'gy'), pairs)  14.6 us
    ppermute x10, waiting for transfers between devices, meet(): return lax.ppermute(value, ('gx', 'gy'), pairs)  10.4 us
    ppermute x7, starting transfers between devices, of(): return lax.ppermute(value, axis, [(i, i ^ step) for i in range(count)])  9.25 us
    ppermute x3, waiting for transfers between devices, to_band(): return lax.ppermute(value, ('gy', 'band'), pairs)  6.41 us
    ppermute x7, waiting for transfers between devices, of(): return lax.ppermute(value, axis, [(i, i ^ step) for i in range(count)])  5.79 us
    pallas_call x1, Pallas kernels, per_device(): pl.pallas_call(first_kernel, out_shape=[struct(*tile)] * 2 + payloads(wid...  5.03 us
    pallas_call x1, Pallas kernels, per_device(): pl.pallas_call(second_kernel, out_shape=[struct(*tile)] * 2 + [struct(*ha...  5.02 us
    ppermute x3, starting transfers between devices, to_band(): return lax.ppermute(value, ('gy', 'band'), pairs)  3.42 us
  transfers between devices with their start and end apart: 24, of which 9 were waited for; matrix products, arithmetic and copies ran while one was open for 0% of the time, Pallas kernels for 0%

profile of v6, /device:TPU:0, one launch (start us, length us, event | category | flops | bytes accessed | tf_op | source)
XLA Modules:
  0.0 66.3 jit_solution(1580053821891043167)
XLA Ops:
  0.5 1.0 %copy-done = f32[2,32,8,256]{3,2,1,0:T(8,128)S(1)} copy-done((f32[2,32,8,256]{3,2,1,0:T(8,128)S(1)}, f32[2,32,8,256]{3,2,1,0:T(8,128)}, u32[]{:S(2)}) %copy-start) | copy-done | bytes 524312
  2.7 3.0 %collective-permute-start.2 = (f32[48,8,256]{2,1,0:T(8,128)S(1)}, f32[48,8,256]{2,1,0:T(8,128)S(1)}, u32[]{:S(2)}, u32[]{:S(2)}) collective-permute-start(f32[48,8,256]{2,1,0:T(8,128)S(1)} %get-tuple-element.26), channel_id=1, source_target_pairs={{0,4},{2,6},{4,0},{6,2},{8,12},{10,14},{12,8},{14,10},{16,20},{18,... | collective-permute-start | bytes 1179656 | tf_op jit(solution)/shard_map/ppermute | solution.py:453
  5.7 1.6 %collective-permute-start.3 = (f32[2,14,8,256]{3,2,1,0:T(8,128)S(1)}, f32[2,14,8,256]{3,2,1,0:T(8,128)S(1)}, u32[]{:S(2)}, u32[]{:S(2)}) collective-permute-start(f32[2,14,8,256]{3,2,1,0:T(8,128)S(1)} %get-tuple-element.27), channel_id=1, source_target_pairs={{0,8},{2,10},{4,12},{6,14},{8,0},{10,2},{12,4},{14,6},{16,24},{18,... | collective-permute-start | bytes 688136 | tf_op jit(solution)/shard_map/ppermute | solution.py:453
  7.3 3.1 %collective-permute-start.5 = (f32[12,8,256]{2,1,0:T(8,128)S(1)}, f32[12,8,256]{2,1,0:T(8,128)S(1)}, u32[]{:S(2)}, u32[]{:S(2)}) collective-permute-start(f32[12,8,256]{2,1,0:T(8,128)S(1)} %get-tuple-element.29), channel_id=1, source_target_pairs={{0,12},{2,14},{4,8},{6,10},{8,4},{10,6},{12,0},{14,2},{16,28},{18,... | collective-permute-start | bytes 294920 | tf_op jit(solution)/shard_map/ppermute | solution.py:453
  10.4 6.7 %collective-permute-done.2.refs_5_ = f32[48,8,256]{2,1,0:T(8,128)S(1)} collective-permute-done((f32[48,8,256]{2,1,0:T(8,128)S(1)}, f32[48,8,256]{2,1,0:T(8,128)S(1)}, u32[]{:S(2)}, u32[]{:S(2)}) %collective-permute-start.2) | collective-permute-done | bytes 393248 | tf_op jit(solution)/shard_map/ppermute | solution.py:453
  17.3 1.3 %collective-permute-done.7.refs_4_ = f32[16,8,256]{2,1,0:T(8,128)S(1)} collective-permute-done((f32[16,8,256]{2,1,0:T(8,128)S(1)}, f32[16,8,256]{2,1,0:T(8,128)S(1)}, u32[]{:S(2)}, u32[]{:S(2)}) %collective-permute-start.7) | collective-permute-done | bytes 131104 | tf_op jit(solution)/shard_map/ppermute | solution.py:458
  18.6 5.0 %first_round.1 = (f32[32,8,256]{2,1,0:T(8,128)S(1)}, f32[32,8,256]{2,1,0:T(8,128)S(1)}, f32[32,8,256]{2,1,0:T(8,128)S(1)}, f32[2,8,8,256]{3,2,1,0:T(8,128)S(1)},...) custom-call(f32[2,32,8,256]{3,2,1,0:T(8,128)S(1)} %get-tuple-element.24.orbitals.refs_0_, ...), custom_call_target="tpu_custom_call" | custom-call | tf_op jit(solution)/shard_map/first_round/pallas_call | solution.py:539
  23.6 1.8 %collective-permute-start.8 = (f32[32,8,256]{2,1,0:T(8,128)S(1)}, f32[32,8,256]{2,1,0:T(8,128)S(1)}, u32[]{:S(2)}, u32[]{:S(2)}) collective-permute-start(f32[32,8,256]{2,1,0:T(8,128)S(1)} %get-tuple-element.34), channel_id=1, source_target_pairs={{0,4},{2,6},{4,0},{6,2},{8,12},{10,14},{12,8},{14,10},{16,20},{18,... | collective-permute-start | bytes 786440 | tf_op jit(solution)/shard_map/ppermute | solution.py:453
  25.4 3.6 %collective-permute-start.9 = (f32[2,8,8,256]{3,2,1,0:T(8,128)S(1)}, f32[2,8,8,256]{3,2,1,0:T(8,128)S(1)}, u32[]{:S(2)}, u32[]{:S(2)}) collective-permute-start(f32[2,8,8,256]{3,2,1,0:T(8,128)S(1)} %get-tuple-element.35), channel_id=1, source_target_pairs={{0,8},{2,10},{4,12},{6,14},{8,0},{10,2},{12,4},{14,6},{16,24},{18,... | collective-permute-start | bytes 393224 | tf_op jit(solution)/shard_map/ppermute | solution.py:453
  29.1 1.5 %collective-permute-start.11 = (f32[7,8,256]{2,1,0:T(8,128)S(1)}, f32[7,8,256]{2,1,0:T(8,128)S(1)}, u32[]{:S(2)}, u32[]{:S(2)}) collective-permute-start(f32[7,8,256]{2,1,0:T(8,128)S(1)} %get-tuple-element.37), channel_id=1, source_target_pairs={{0,12},{2,14},{4,8},{6,10},{8,4},{10,6},{12,0},{14,2},{16,28},{18,... | collective-permute-start | bytes 172040 | tf_op jit(solution)/shard_map/ppermute | solution.py:453
  30.6 3.7 %collective-permute-done.11.refs_15_ = f32[7,8,256]{2,1,0:T(8,128)S(1)} collective-permute-done((f32[7,8,256]{2,1,0:T(8,128)S(1)}, f32[7,8,256]{2,1,0:T(8,128)S(1)}, u32[]{:S(2)}, u32[]{:S(2)}) %collective-permute-start.11) | collective-permute-done | bytes 57376 | tf_op jit(solution)/shard_map/ppermute | solution.py:453
  34.3 5.0 %second_round.1 = (f32[32,8,256]{2,1,0:T(8,128)S(1)}, f32[32,8,256]{2,1,0:T(8,128)S(1)}, f32[16,8,256]{2,1,0:T(8,128)S(1)}, f32[16,8,256]{2,1,0:T(8,128)S(1)}) custom-call(f32[2,32,8,256]{3,2,1,0:T(8,128)S(1)} %get-tuple-element.24.orbitals.refs_0_, f32[2,32,8,256]{3,2,1,0:T(8,128)S(1)} %collective-permute-done.received.refs_1_, ...), custom_call_target="tpu_custom_call" | custom-call | tf_op jit(solution)/shard_map/second_round/pallas_call | solution.py:549
  39.4 1.6 %collective-permute-start.14 = (f32[16,8,256]{2,1,0:T(8,128)S(1)}, f32[16,8,256]{2,1,0:T(8,128)S(1)}, u32[]{:S(2)}, u32[]{:S(2)}) collective-permute-start(f32[16,8,256]{2,1,0:T(8,128)S(1)} %get-tuple-element.41), channel_id=1, source_target_pairs={{0,1},{1,0},{2,3},{3,2},{4,5},{5,4},{6,7},{7,6},{8,9},{9,8},{10,11... | collective-permute-start | bytes 393224 | tf_op jit(solution)/shard_map/ppermute | solution.py:467
  41.3 4.5 %collective-permute-done.14.refs_2_.refs_4_ = f32[16,8,256]{2,1,0:T(8,128)S(1)} collective-permute-done((f32[16,8,256]{2,1,0:T(8,128)S(1)}, f32[16,8,256]{2,1,0:T(8,128)S(1)}, u32[]{:S(2)}, u32[]{:S(2)}) %collective-permute-start.14) | collective-permute-done | bytes 131104 | tf_op jit(solution)/shard_map/ppermute | solution.py:467
  45.8 1.9 %collective-permute-done.15.refs_3_.refs_5_ = f32[16,8,256]{2,1,0:T(8,128)S(1)} collective-permute-done((f32[16,8,256]{2,1,0:T(8,128)S(1)}, f32[16,8,256]{2,1,0:T(8,128)S(1)}, u32[]{:S(2)}, u32[]{:S(2)}) %collective-permute-start.15) | collective-permute-done | bytes 131104 | tf_op jit(solution)/shard_map/ppermute | solution.py:467
  47.9 1.6 %collective-permute-start.16 = (f32[8,128]{1,0:T(8,128)S(1)}, f32[8,128]{1,0:T(8,128)S(1)}, u32[]{:S(2)}, u32[]{:S(2)}) collective-permute-start(f32[8,128]{1,0:T(8,128)S(1)} %correlation.1), channel_id=1, source_target_pairs={{0,1},{1,0},{2,3},{3,2},{4,5},{5,4},{6,7},{7,6},{8,9},{9,8},{10,11... | collective-permute-start | bytes 12296 | tf_op jit(solution)/shard_map/ppermute | solution.py:486
  49.5 2.1 %collective-permute-done.16 = f32[8,128]{1,0:T(8,128)S(1)} collective-permute-done((f32[8,128]{1,0:T(8,128)S(1)}, f32[8,128]{1,0:T(8,128)S(1)}, u32[]{:S(2)}, u32[]{:S(2)}) %collective-permute-start.16) | collective-permute-done | bytes 4128 | tf_op jit(solution)/shard_map/ppermute | solution.py:486
  51.6 1.0 %collective-permute-start.18 = (f32[8,128]{1,0:T(8,128)S(1)}, f32[8,128]{1,0:T(8,128)S(1)}, u32[]{:S(2)}, u32[]{:S(2)}) collective-permute-start(f32[8,128]{1,0:T(8,128)S(1)} %add.21), channel_id=1, source_target_pairs={{0,4},{2,6},{4,0},{6,2},{1,5},{3,7},{5,1},{7,3},{8,12},{10,14},{12... | collective-permute-start | bytes 12296 | tf_op jit(solution)/shard_map/ppermute | solution.py:486
  53.5 1.6 %collective-permute-start.23 = (f32[2,16,8,256]{3,2,1,0:T(8,128)S(1)}, f32[2,16,8,256]{3,2,1,0:T(8,128)S(1)}, u32[]{:S(2)}, u32[]{:S(2)}) collective-permute-start(f32[2,16,8,256]{3,2,1,0:T(8,128)S(1)} %late.1), channel_id=1, source_target_pairs={{0,1},{1,0},{2,3},{3,2},{4,5},{5,4},{6,7},{7,6},{8,9},{9,8},{10,11... | collective-permute-start | bytes 786440 | tf_op jit(solution)/shard_map/ppermute | solution.py:467
  55.3 3.1 %collective-permute-start.22 = (f32[8,128]{1,0:T(8,128)S(1)}, f32[8,128]{1,0:T(8,128)S(1)}, u32[]{:S(2)}, u32[]{:S(2)}) collective-permute-start(f32[8,128]{1,0:T(8,128)S(1)} %add_add_fusion.1), channel_id=1, source_target_pairs={{0,24},{8,16},{16,8},{24,0},{1,25},{9,17},{17,9},{25,1},{2,26},{10... | collective-permute-start | bytes 12296 | tf_op jit(solution)/shard_map/ppermute | solution.py:486
  58.4 2.6 %collective-permute-start.21 = (f32[8,128]{1,0:T(8,128)S(1)}, f32[8,128]{1,0:T(8,128)S(1)}, u32[]{:S(2)}, u32[]{:S(2)}) collective-permute-start(f32[8,128]{1,0:T(8,128)S(1)} %add_add_fusion.1), channel_id=1, source_target_pairs={{0,16},{8,24},{16,0},{24,8},{1,17},{9,25},{17,1},{25,9},{2,18},{10... | collective-permute-start | bytes 12296 | tf_op jit(solution)/shard_map/ppermute | solution.py:486
  61.1 1.8 %collective-permute-done.21 = f32[8,128]{1,0:T(8,128)S(1)} collective-permute-done((f32[8,128]{1,0:T(8,128)S(1)}, f32[8,128]{1,0:T(8,128)S(1)}, u32[]{:S(2)}, u32[]{:S(2)}) %collective-permute-start.21) | collective-permute-done | bytes 4128 | tf_op jit(solution)/shard_map/ppermute | solution.py:486
  62.9 1.7 %collective-permute-done.20 = f32[8,128]{1,0:T(8,128)S(1)} collective-permute-done((f32[8,128]{1,0:T(8,128)S(1)}, f32[8,128]{1,0:T(8,128)S(1)}, u32[]{:S(2)}, u32[]{:S(2)}) %collective-permute-start.20) | collective-permute-done | bytes 4128 | tf_op jit(solution)/shard_map/ppermute | solution.py:486
  64.6 1.7 %basis.1 = f32[2,32,8,256]{3,2,1,0:T(8,128)} custom-call(f32[8,128]{1,0:T(8,128)S(1)} %add_add_fusion.refs_0_, s32[4]{0:T(128)S(1)} %copy-done.2, f32[32,8,256]{2,1,0:T(8,128)S(1)} %get-tuple-element.39.refs_0_.keep.refs_2_, f32[32,8,256]{2,1,0:T(8,128)S(1)} %collective-permute-done.13.refs_1_.sibling.refs_3_, ...), custom_call_target="tpu_custom_call" | custom-call | tf_op jit(solution)/shard_map/basis/pallas_call | solution.py:579
  (41 shorter events, 3.5 us)
Async XLA Ops:
  0.0 2.6 %collective-permute-start = (f32[2,32,8,256]{3,2,1,0:T(8,128)}, f32[2,32,8,256]{3,2,1,0:T(8,128)S(1)}, u32[]{:S(2)}, u32[]{:S(2)}) collective-permute-start(f32[2,32,8,256]{3,2,1,0:T(8,128)} %orbitals.1), channel_id=1, source_target_pairs={{0,2},{2,0},{4,6},{6,4},{1,3},{3,1},{5,7},{7,5},{8,10},{10,8},{12,... | collective-permute-start | bytes 1572872 | tf_op jit(solution)/shard_map/ppermute | solution.py:458
  0.5 2.1 %collective-permute-start.1 = (f32[32,8,256]{2,1,0:T(8,128)}, f32[32,8,256]{2,1,0:T(8,128)S(1)}, u32[]{:S(2)}, u32[]{:S(2)}) collective-permute-start(f32[32,8,256]{2,1,0:T(8,128)} %potential.1), channel_id=1, source_target_pairs={{0,2},{2,0},{4,6},{6,4},{1,3},{3,1},{5,7},{7,5},{8,10},{10,8},{12,... | collective-permute-start | bytes 786440 | tf_op jit(solution)/shard_map/ppermute | solution.py:458
  2.7 14.4 %collective-permute-start.2 = (f32[48,8,256]{2,1,0:T(8,128)S(1)}, f32[48,8,256]{2,1,0:T(8,128)S(1)}, u32[]{:S(2)}, u32[]{:S(2)}) collective-permute-start(f32[48,8,256]{2,1,0:T(8,128)S(1)} %get-tuple-element.26), channel_id=1, source_target_pairs={{0,4},{2,6},{4,0},{6,2},{8,12},{10,14},{12,8},{14,10},{16,20},{18,... | collective-permute-start | bytes 1179656 | tf_op jit(solution)/shard_map/ppermute | solution.py:453
  5.7 11.4 %collective-permute-start.3 = (f32[2,14,8,256]{3,2,1,0:T(8,128)S(1)}, f32[2,14,8,256]{3,2,1,0:T(8,128)S(1)}, u32[]{:S(2)}, u32[]{:S(2)}) collective-permute-start(f32[2,14,8,256]{3,2,1,0:T(8,128)S(1)} %get-tuple-element.27), channel_id=1, source_target_pairs={{0,8},{2,10},{4,12},{6,14},{8,0},{10,2},{12,4},{14,6},{16,24},{18,... | collective-permute-start | bytes 688136 | tf_op jit(solution)/shard_map/ppermute | solution.py:453
  7.3 9.9 %collective-permute-start.4 = (f32[2,14,8,256]{3,2,1,0:T(8,128)S(1)}, f32[2,14,8,256]{3,2,1,0:T(8,128)S(1)}, u32[]{:S(2)}, u32[]{:S(2)}) collective-permute-start(f32[2,14,8,256]{3,2,1,0:T(8,128)S(1)} %get-tuple-element.28), channel_id=1, source_target_pairs={{0,2},{2,0},{4,6},{6,4},{8,16},{10,18},{12,20},{14,22},{16,8},{18,... | collective-permute-start | bytes 688136 | tf_op jit(solution)/shard_map/ppermute | solution.py:453
  7.3 9.8 %collective-permute-start.5 = (f32[12,8,256]{2,1,0:T(8,128)S(1)}, f32[12,8,256]{2,1,0:T(8,128)S(1)}, u32[]{:S(2)}, u32[]{:S(2)}) collective-permute-start(f32[12,8,256]{2,1,0:T(8,128)S(1)} %get-tuple-element.29), channel_id=1, source_target_pairs={{0,12},{2,14},{4,8},{6,10},{8,4},{10,6},{12,0},{14,2},{16,28},{18,... | collective-permute-start | bytes 294920 | tf_op jit(solution)/shard_map/ppermute | solution.py:453
  10.4 6.7 %collective-permute-start.6 = (f32[12,8,256]{2,1,0:T(8,128)S(1)}, f32[12,8,256]{2,1,0:T(8,128)S(1)}, u32[]{:S(2)}, u32[]{:S(2)}) collective-permute-start(f32[12,8,256]{2,1,0:T(8,128)S(1)} %get-tuple-element.30), channel_id=1, source_target_pairs={{0,2},{2,0},{4,6},{6,4},{8,20},{10,22},{12,16},{14,18},{16,12},{18... | collective-permute-start | bytes 294920 | tf_op jit(solution)/shard_map/ppermute | solution.py:453
  17.2 1.4 %collective-permute-start.7 = (f32[16,8,256]{2,1,0:T(8,128)S(1)}, f32[16,8,256]{2,1,0:T(8,128)S(1)}, u32[]{:S(2)}, u32[]{:S(2)}) collective-permute-start(f32[16,8,256]{2,1,0:T(8,128)S(1)} %slice.4), channel_id=1, source_target_pairs={{0,2},{2,0},{4,6},{6,4},{1,3},{3,1},{5,7},{7,5},{8,10},{10,8},{12,... | collective-permute-start | bytes 393224 | tf_op jit(solution)/shard_map/ppermute | solution.py:458
  23.6 10.7 %collective-permute-start.8 = (f32[32,8,256]{2,1,0:T(8,128)S(1)}, f32[32,8,256]{2,1,0:T(8,128)S(1)}, u32[]{:S(2)}, u32[]{:S(2)}) collective-permute-start(f32[32,8,256]{2,1,0:T(8,128)S(1)} %get-tuple-element.34), channel_id=1, source_target_pairs={{0,4},{2,6},{4,0},{6,2},{8,12},{10,14},{12,8},{14,10},{16,20},{18,... | collective-permute-start | bytes 786440 | tf_op jit(solution)/shard_map/ppermute | solution.py:453
  25.4 8.9 %collective-permute-start.9 = (f32[2,8,8,256]{3,2,1,0:T(8,128)S(1)}, f32[2,8,8,256]{3,2,1,0:T(8,128)S(1)}, u32[]{:S(2)}, u32[]{:S(2)}) collective-permute-start(f32[2,8,8,256]{3,2,1,0:T(8,128)S(1)} %get-tuple-element.35), channel_id=1, source_target_pairs={{0,8},{2,10},{4,12},{6,14},{8,0},{10,2},{12,4},{14,6},{16,24},{18,... | collective-permute-start | bytes 393224 | tf_op jit(solution)/shard_map/ppermute | solution.py:453
  29.1 5.2 %collective-permute-start.10 = (f32[2,8,8,256]{3,2,1,0:T(8,128)S(1)}, f32[2,8,8,256]{3,2,1,0:T(8,128)S(1)}, u32[]{:S(2)}, u32[]{:S(2)}) collective-permute-start(f32[2,8,8,256]{3,2,1,0:T(8,128)S(1)} %get-tuple-element.36), channel_id=1, source_target_pairs={{0,2},{2,0},{4,6},{6,4},{8,16},{10,18},{12,20},{14,22},{16,8},{18,... | collective-permute-start | bytes 393224 | tf_op jit(solution)/shard_map/ppermute | solution.py:453
  29.1 5.2 %collective-permute-start.11 = (f32[7,8,256]{2,1,0:T(8,128)S(1)}, f32[7,8,256]{2,1,0:T(8,128)S(1)}, u32[]{:S(2)}, u32[]{:S(2)}) collective-permute-start(f32[7,8,256]{2,1,0:T(8,128)S(1)} %get-tuple-element.37), channel_id=1, source_target_pairs={{0,12},{2,14},{4,8},{6,10},{8,4},{10,6},{12,0},{14,2},{16,28},{18,... | collective-permute-start | bytes 172040 | tf_op jit(solution)/shard_map/ppermute | solution.py:453
  30.6 3.7 %collective-permute-start.12 = (f32[7,8,256]{2,1,0:T(8,128)S(1)}, f32[7,8,256]{2,1,0:T(8,128)S(1)}, u32[]{:S(2)}, u32[]{:S(2)}) collective-permute-start(f32[7,8,256]{2,1,0:T(8,128)S(1)} %get-tuple-element.38), channel_id=1, source_target_pairs={{0,2},{2,0},{4,6},{6,4},{8,20},{10,22},{12,16},{14,18},{16,12},{18... | collective-permute-start | bytes 172040 | tf_op jit(solution)/shard_map/ppermute | solution.py:453
  39.3 8.3 %collective-permute-start.13 = (f32[32,8,256]{2,1,0:T(8,128)S(1)}, f32[32,8,256]{2,1,0:T(8,128)S(1)}, u32[]{:S(2)}, u32[]{:S(2)}) collective-permute-start(f32[32,8,256]{2,1,0:T(8,128)S(1)} %get-tuple-element.40), channel_id=1, source_target_pairs={{0,2},{2,0},{4,6},{6,4},{1,3},{3,1},{5,7},{7,5},{8,10},{10,8},{12,... | collective-permute-start | bytes 786440 | tf_op jit(solution)/shard_map/ppermute | solution.py:458
  39.4 6.4 %collective-permute-start.14 = (f32[16,8,256]{2,1,0:T(8,128)S(1)}, f32[16,8,256]{2,1,0:T(8,128)S(1)}, u32[]{:S(2)}, u32[]{:S(2)}) collective-permute-start(f32[16,8,256]{2,1,0:T(8,128)S(1)} %get-tuple-element.41), channel_id=1, source_target_pairs={{0,1},{1,0},{2,3},{3,2},{4,5},{5,4},{6,7},{7,6},{8,9},{9,8},{10,11... | collective-permute-start | bytes 393224 | tf_op jit(solution)/shard_map/ppermute | solution.py:467
  41.0 6.7 %collective-permute-start.15 = (f32[16,8,256]{2,1,0:T(8,128)S(1)}, f32[16,8,256]{2,1,0:T(8,128)S(1)}, u32[]{:S(2)}, u32[]{:S(2)}) collective-permute-start(f32[16,8,256]{2,1,0:T(8,128)S(1)} %get-tuple-element.42), channel_id=1, source_target_pairs={{0,3},{1,2},{2,1},{3,0},{4,7},{5,6},{6,5},{7,4},{8,11},{9,10},{10,... | collective-permute-start | bytes 393224 | tf_op jit(solution)/shard_map/ppermute | solution.py:467
  47.9 3.7 %collective-permute-start.16 = (f32[8,128]{1,0:T(8,128)S(1)}, f32[8,128]{1,0:T(8,128)S(1)}, u32[]{:S(2)}, u32[]{:S(2)}) collective-permute-start(f32[8,128]{1,0:T(8,128)S(1)} %correlation.1), channel_id=1, source_target_pairs={{0,1},{1,0},{2,3},{3,2},{4,5},{5,4},{6,7},{7,6},{8,9},{9,8},{10,11... | collective-permute-start | bytes 12296 | tf_op jit(solution)/shard_map/ppermute | solution.py:486
  51.6 3.4 %collective-permute-start.19 = (f32[8,128]{1,0:T(8,128)S(1)}, f32[8,128]{1,0:T(8,128)S(1)}, u32[]{:S(2)}, u32[]{:S(2)}) collective-permute-start(f32[8,128]{1,0:T(8,128)S(1)} %add.21), channel_id=1, source_target_pairs={{0,6},{2,4},{4,2},{6,0},{1,7},{3,5},{5,3},{7,1},{8,14},{10,12},{12... | collective-permute-start | bytes 12296 | tf_op jit(solution)/shard_map/ppermute | solution.py:486
  51.6 3.6 %collective-permute-start.18 = (f32[8,128]{1,0:T(8,128)S(1)}, f32[8,128]{1,0:T(8,128)S(1)}, u32[]{:S(2)}, u32[]{:S(2)}) collective-permute-start(f32[8,128]{1,0:T(8,128)S(1)} %add.21), channel_id=1, source_target_pairs={{0,4},{2,6},{4,0},{6,2},{1,5},{3,7},{5,1},{7,3},{8,12},{10,14},{12... | collective-permute-start | bytes 12296 | tf_op jit(solution)/shard_map/ppermute | solution.py:486
  52.6 2.6 %collective-permute-start.17 = (f32[8,128]{1,0:T(8,128)S(1)}, f32[8,128]{1,0:T(8,128)S(1)}, u32[]{:S(2)}, u32[]{:S(2)}) collective-permute-start(f32[8,128]{1,0:T(8,128)S(1)} %add.21), channel_id=1, source_target_pairs={{0,2},{2,0},{4,6},{6,4},{1,3},{3,1},{5,7},{7,5},{8,10},{10,8},{12,... | collective-permute-start | bytes 12296 | tf_op jit(solution)/shard_map/ppermute | solution.py:486
  53.5 11.1 %collective-permute-start.23 = (f32[2,16,8,256]{3,2,1,0:T(8,128)S(1)}, f32[2,16,8,256]{3,2,1,0:T(8,128)S(1)}, u32[]{:S(2)}, u32[]{:S(2)}) collective-permute-start(f32[2,16,8,256]{3,2,1,0:T(8,128)S(1)} %late.1), channel_id=1, source_target_pairs={{0,1},{1,0},{2,3},{3,2},{4,5},{5,4},{6,7},{7,6},{8,9},{9,8},{10,11... | collective-permute-start | bytes 786440 | tf_op jit(solution)/shard_map/ppermute | solution.py:467
  55.3 5.8 %collective-permute-start.22 = (f32[8,128]{1,0:T(8,128)S(1)}, f32[8,128]{1,0:T(8,128)S(1)}, u32[]{:S(2)}, u32[]{:S(2)}) collective-permute-start(f32[8,128]{1,0:T(8,128)S(1)} %add_add_fusion.1), channel_id=1, source_target_pairs={{0,24},{8,16},{16,8},{24,0},{1,25},{9,17},{17,9},{25,1},{2,26},{10... | collective-permute-start | bytes 12296 | tf_op jit(solution)/shard_map/ppermute | solution.py:486
  58.4 4.5 %collective-permute-start.21 = (f32[8,128]{1,0:T(8,128)S(1)}, f32[8,128]{1,0:T(8,128)S(1)}, u32[]{:S(2)}, u32[]{:S(2)}) collective-permute-start(f32[8,128]{1,0:T(8,128)S(1)} %add_add_fusion.1), channel_id=1, source_target_pairs={{0,16},{8,24},{16,0},{24,8},{1,17},{9,25},{17,1},{25,9},{2,18},{10... | collective-permute-start | bytes 12296 | tf_op jit(solution)/shard_map/ppermute | solution.py:486
  61.0 3.6 %collective-permute-start.20 = (f32[8,128]{1,0:T(8,128)S(1)}, f32[8,128]{1,0:T(8,128)S(1)}, u32[]{:S(2)}, u32[]{:S(2)}) collective-permute-start(f32[8,128]{1,0:T(8,128)S(1)} %add_add_fusion.1), channel_id=1, source_target_pairs={{0,8},{8,0},{16,24},{24,16},{1,9},{9,1},{17,25},{25,17},{2,10},{10... | collective-permute-start | bytes 12296 | tf_op jit(solution)/shard_map/ppermute | solution.py:486
  (3 other events, 11.3 us)

commit v7 on v6

--- a/solution.py
+++ b/solution.py
@@ -12,6 +12,7 @@
 PAD = 8
 LANES = 128
 PLANES = 4
+BY_PRODUCT, BY_ROLLS, UNROLL = 8, 4, 2
 NEAR = -(2.0 / 3.0) / 4.25
 FAR = (1.0 / 24.0) / 4.25
 VMEM = pl.BlockSpec(memory_space=pltpu.VMEM)
@@ -69,7 +70,32 @@
     return jnp.where(right, HALO + width, HALO - count)
 
 
-def fill(window, tiles, x_halos, y_halos, corners, change=lambda a: a):
+def corner_plane(right, width, distance):
+    return jnp.where(right, HALO + width + distance - 1, HALO - distance)
+
+
+def put_corner(window, corner, reach, right, up, rows, width, change=lambda a: a):
+    for k in range(1, reach // 2 + 1):
+        tile = corner[k - 1]
+        put(window, corner_plane(right, width, k), rows, tile[None], change)
+        if k != reach - k:
+            other = jnp.where(up, pltpu.roll(tile, k, 0), pltpu.roll(tile, 8 - k, 0))
+            put(window, corner_plane(right, width, reach - k), rows, other[None], change)
+
+
+def pack_corner(out, plane, reach, up):
+    for k in range(1, reach // 2 + 1):
+        tile = plane(k)
+        if k != reach - k:
+            other = plane(reach - k)
+            other = jnp.where(up, pltpu.roll(other, k, 0), pltpu.roll(other, 8 - k, 0))
+            row = lax.broadcasted_iota(jnp.int32, tile.shape, 0)
+            mine = jnp.where(up, row - k, 7 - k - row) >= 0
+            tile = jnp.where(mine, tile, other)
+        out[k - 1] = tile
+
+
+def fill(window, tiles, x_halos, y_halos, corners, reach, change=lambda a: a):
     core, chip, along_x = place()
     width = tiles[0].shape[0]
     slots = own_slots(core, chip)
@@ -80,13 +106,12 @@
             start = halo_start(upward(along_x, phase), width, halo.shape[0])
             put(window, start, rows_of(slot), halo, change)
     for phase in y_phases():
-        rows = rows_of(halo_slot(chip, upward(chip, phase)))
-        if y_halos is not None:
-            put(window, HALO, rows, y_halos[phase], change)
+        up = upward(chip, phase)
+        rows = rows_of(halo_slot(chip, up))
+        put(window, HALO, rows, y_halos[phase], change)
         for x_phase in range(2):
             corner = corners[2 * phase + x_phase]
-            start = halo_start(upward(along_x, x_phase), width, corner.shape[0])
-            put(window, start, rows, corner, change)
+            put_corner(window, corner, reach, upward(along_x, x_phase), up, rows, width, change)
 
 
 def near_planes(right, width, count):
@@ -101,32 +126,68 @@
     return jnp.where(gap == 1, -16.0, jnp.where(gap == 2, 1.0, 0.0)).astype(jnp.bfloat16)
 
 
-def stencil(source, target, local, x, along_z, first):
+def sides(source, half, x, count, body):
+    def at(dx, dy):
+        return source[half, pl.ds(x + dx, count), body.start + dy : body.stop + dy, :]
+
+    near = at(-1, 0) + at(1, 0) + at(0, -1) + at(0, 1)
+    far = at(-2, 0) + at(2, 0) + at(0, -2) + at(0, 2)
+    return near, far
+
+
+def z_by_product(values, along_z):
+    count, height, _ = values[0].shape
+    flat = [v.reshape(count * height, LANES) for v in values]
+    high = [v.astype(jnp.bfloat16) for v in flat]
+    low = [(v - h.astype(jnp.float32)).astype(jnp.bfloat16) for v, h in zip(flat, high)]
+    pieces = jnp.concatenate([jnp.concatenate(high, axis=1), jnp.concatenate(low, axis=1)], axis=0)
+    both = jnp.dot(pieces, along_z, preferred_element_type=jnp.float32)
+    total = both[: count * height] + both[count * height :]
+    return [total[:, h * LANES : (h + 1) * LANES].reshape(values[0].shape) for h in range(2)]
+
+
+def z_by_rolls(values):
+    lane = lax.broadcasted_iota(jnp.int32, values[0].shape, 2)
+    zero = jnp.zeros_like(values[0])
+    found = []
+    for distance in (1, 2):
+        back = [pltpu.roll(v, distance, 2) for v in values]
+        ahead = [pltpu.roll(v, LANES - distance, 2) for v in values]
+        first, last = lane < distance, lane >= LANES - distance
+        found.append(
+            [
+                jnp.where(first, zero, back[0]) + jnp.where(last, ahead[1], ahead[0]),
+                jnp.where(first, back[0], back[1]) + jnp.where(last, zero, ahead[1]),
+            ]
+        )
+    return found
+
+
+def stencil(source, target, local, x, by_product, by_rolls, along_z, first):
     height = source.shape[2] - 2 * PAD
     body = slice(PAD, PAD + height)
-    now = pl.ds(x, PLANES)
-    values = [source[half, now, body, :] for half in range(2)]
-    high = [v.astype(jnp.bfloat16) for v in values]
-    low = [(v - h.astype(jnp.float32)).astype(jnp.bfloat16) for v, h in zip(values, high)]
-
-    def joined(parts):
-        return jnp.concatenate([p.reshape(PLANES * height, LANES) for p in parts], axis=1)
-
-    z_sum = jnp.dot(joined(high), along_z, preferred_element_type=jnp.float32)
-    z_sum = z_sum + jnp.dot(joined(low), along_z, preferred_element_type=jnp.float32)
     scale = 1.0 if first else 2.0
-    for half in range(2):
-        near = source[half, pl.ds(x - 1, PLANES), body, :] + source[half, pl.ds(x + 1, PLANES), body, :]
-        near = near + source[half, now, PAD - 1 : PAD - 1 + height, :]
-        near = near + source[half, now, PAD + 1 : PAD + 1 + height, :]
-        far = source[half, pl.ds(x - 2, PLANES), body, :] + source[half, pl.ds(x + 2, PLANES), body, :]
-        far = far + source[half, now, PAD - 2 : PAD - 2 + height, :]
-        far = far + source[half, now, PAD + 2 : PAD + 2 + height, :]
-        far = far + z_sum[:, half * LANES : (half + 1) * LANES].reshape(PLANES, height, LANES)
-        result = local[half, now, body, :] * values[half] * scale
-        result = result + near * (NEAR * scale) + far * (FAR * scale)
-        if not first:
-            result = result - target[half, now, body, :]
+    results = []
+    for start, count, product in ((x, by_product, True), (x + by_product, by_rolls, False)):
+        if not count:
+            continue
+        now = pl.ds(start, count)
+        values = [source[half, now, body, :] for half in range(2)]
+        if product:
+            z_far = z_by_product(values, along_z)
+        else:
+            z_near, z_far = z_by_rolls(values)
+        for half in range(2):
+            near, far = sides(source, half, start, count, body)
+            far = far + z_far[half]
+            if not product:
+                near = near + z_near[half]
+            result = local[half, now, body, :] * values[half] * scale
+            result = result + near * (NEAR * scale) + far * (FAR * scale)
+            if not first:
+                result = result - target[half, now, body, :]
+            results.append((half, now, result))
+    for half, now, result in results:
         target[half, now, body, :] = result
 
 
@@ -141,13 +202,19 @@
     for step in range(STEPS):
         source, target = buffers[step % 2], buffers[(step + 1) % 2]
         low = 2 * (step + 1)
-        blocks = (extent - 2 * low) // PLANES
+        together = BY_PRODUCT + BY_ROLLS
+        blocks, rest = divmod(extent - 2 * low, together)
 
         def block(index, carry, source=source, target=target, low=low, step=step):
-            stencil(source, target, local, low + index * PLANES, along_z, step == 0)
+            x = low + index * together
+            stencil(source, target, local, x, BY_PRODUCT, BY_ROLLS, along_z, step == 0)
             return carry
 
-        lax.fori_loop(0, blocks, block, 0, unroll=2)
+        lax.fori_loop(0, blocks, block, 0, unroll=UNROLL)
+        if rest:
+            by_rolls = min(BY_ROLLS, rest // 3)
+            x = low + blocks * together
+            stencil(source, target, local, x, rest - by_rolls, by_rolls, along_z, step == 0)
         if step < STEPS - 1:
             outside_is_zero(target)
 
@@ -203,20 +270,22 @@
 
             @pl.when(chosen)
             def _(t=t, phase=phase):
-                y_out[phase][:width] = tiles[t][...]
-                half = width // 2
-                y_out[phase][width:] = local[t][pl.ds(core * half, half)]
+                y_out[phase][...] = tiles[t][...]
+                up = upward(chip, phase)
                 for x_phase in range(2):
                     right = upward(along_x, x_phase)
                     out = d_out[2 * phase + x_phase]
-                    out[: HALO - 1] = tiles[t][near_planes(right, width, HALO - 1)]
-                    out[HALO - 1 :] = local[t][near_planes(right, width, HALO - 3)]
-
-
-def fill_local(window, potential, received_potential, passed, y_halos, x_halos, corners):
+
+                    def plane(k, field, right=right):
+                        return field[jnp.where(right, width - k, k - 1)]
+
+                    pack_corner(out, functools.partial(plane, field=tiles[t]), HALO, up)
+                    rest = out.at[HALO // 2 :]
+                    pack_corner(rest, functools.partial(plane, field=local[t]), HALO - 2, up)
+
+
+def fill_local(window, potential, received_potential, edge, passed, x_halos, corners):
     core, chip, _ = place()
-    width = potential.shape[0]
-    half = width // 2
 
     def change(v):
         return (v - 0.5) / 4.25
@@ -225,34 +294,38 @@
         window,
         (potential, received_potential),
         [x.at[:, HALO:] for x in x_halos],
-        None,
-        [c.at[HALO - 1 :] for c in corners],
+        [edge] * len(y_phases()),
+        [c.at[HALO // 2 :] for c in corners],
+        HALO - 2,
         change,
     )
     for phase in y_phases():
-        rows = rows_of(halo_slot(chip, upward(chip, phase)))
-        put(window, HALO + core * half, rows, y_halos[phase].at[width:], change)
-        put(window, HALO + (1 - core) * half, rows, passed[phase], change)
+        up = upward(chip, phase)
+
+        @pl.when(core != jnp.where(up, 1, 0))
+        def _(up=up):
+            put(window, HALO, rows_of(halo_slot(chip, up)), passed, change)
 
 
 def first_kernel(*refs):
     count = len(y_phases())
-    orbitals, received, potential, received_potential = refs[:4]
-    passed, halos = refs[4 : 4 + count], refs[4 + count : 6 + 4 * count]
-    y_halos, x_halos, corners = halos_of(halos)
-    own_out, other_out = refs[6 + 4 * count : 8 + 4 * count]
-    outs = refs[8 + 4 * count : 10 + 7 * count]
-    a, b, local = refs[10 + 7 * count :]
+    orbitals, received, potential, received_potential, edge, passed = refs[:6]
+    halos = refs[6 : 8 + 3 * count]
+    own_out, other_out = refs[8 + 3 * count : 10 + 3 * count]
+    outs = refs[10 + 3 * count : 12 + 6 * count]
+    a, b, local = refs[12 + 6 * count :]
     core, chip, along_x = place()
     width, depth = potential.shape[0], potential.shape[2]
+    y_halos, x_halos, corners = halos_of(halos)
     fill(
         a,
         (orbitals.at[core], received.at[core]),
         [x.at[:, :HALO] for x in x_halos],
-        [y.at[:width] for y in y_halos],
-        [c.at[: HALO - 1] for c in corners],
+        y_halos,
+        [c.at[: HALO // 2] for c in corners],
+        HALO,
     )
-    fill_local(local, potential, received_potential, passed, *halos_of(halos))
+    fill_local(local, potential, received_potential, edge, passed, x_halos, corners)
     four_steps(a, b, local, z_matrix(depth))
     y_out, x_out, d_out = outs[:count], outs[count : count + 2], outs[count + 2 :]
     slots = own_slots(core, chip)
@@ -274,8 +347,13 @@
             slot = jnp.where(edge_is_own(core, chip, phase), *slots)
             y_out[phase][:, :, lanes] = planes(slot, 0, width)
             for x_phase in range(2):
-                start = ends(upward(along_x, x_phase), HALO - 1)
-                d_out[2 * phase + x_phase][:, :, lanes] = planes(slot, start, HALO - 1)
+                right = upward(along_x, x_phase)
+
+                def plane(k, right=right, slot=slot, planes=planes):
+                    return planes(slot, jnp.where(right, width - k, k - 1), 1)[0]
+
+                out = d_out[2 * phase + x_phase].at[:, :, lanes]
+                pack_corner(out, plane, HALO, upward(chip, phase))
 
 
 def halos_of(refs):
@@ -285,18 +363,19 @@
 
 def second_kernel(*refs):
     count = len(y_phases())
-    orbitals, received, potential, received_potential = refs[:4]
-    passed, local_halos = refs[4 : 4 + count], refs[4 + count : 6 + 4 * count]
-    own, other = refs[6 + 4 * count : 8 + 4 * count]
-    halos = refs[8 + 4 * count : 10 + 7 * count]
-    keep, give = refs[10 + 7 * count : 12 + 7 * count]
-    early = refs[12 + 7 * count : -3]
+    orbitals, received, potential, received_potential, edge, passed = refs[:6]
+    local_halos = refs[6 : 8 + 3 * count]
+    own, other = refs[8 + 3 * count : 10 + 3 * count]
+    halos = refs[10 + 3 * count : 12 + 6 * count]
+    keep, give = refs[12 + 6 * count : 14 + 6 * count]
+    early = refs[14 + 6 * count : -3]
     a, b, local = refs[-3:]
     core, chip, _ = place()
     width, depth = potential.shape[0], potential.shape[2]
     y_halos, x_halos, corners = halos_of(halos)
-    fill(a, (own, other), x_halos, y_halos, corners)
-    fill_local(local, potential, received_potential, passed, *halos_of(local_halos))
+    fill(a, (own, other), x_halos, y_halos, corners, HALO)
+    _, p_x_halos, p_corners = halos_of(local_halos)
+    fill_local(local, potential, received_potential, edge, passed, p_x_halos, p_corners)
     four_steps(a, b, local, z_matrix(depth))
     start = (orbitals.at[core], received.at[core])
     outs = (keep, give)
@@ -467,6 +546,19 @@
     return lax.ppermute(value, ("gy", "band"), pairs)
 
 
+def face(value):
+    count, bands = lax.axis_size("gy"), lax.axis_size("band")
+    pairs = []
+    for y in range(count):
+        for band in range(bands):
+            to = partner(y, 1, count)
+            if to is not None:
+                pairs.append((y * bands + band, to * bands + band))
+            elif bands % 2 == 0:
+                pairs.append((y * bands + band, y * bands + (band ^ 1)))
+    return lax.ppermute(value, ("gy", "band"), pairs)
+
+
 def exchange(payloads):
     count = len(y_phases())
     halos = [meet(payloads[phase], y_phase=phase) for phase in y_phases()]
@@ -504,6 +596,7 @@
 
     received = swap(orbitals)
     received_potential = swap(potential)
+    edge = face(potential)
     tile = (width, height, depth)
     orbitals, potential = pl.pallas_call(
         load_kernel,
@@ -515,31 +608,29 @@
         name="load",
     )(orbitals, potential)
 
-    def payloads(in_y, in_x, in_corner):
+    def payloads(in_x, in_corner):
         return (
-            [struct(in_y, height, depth)] * count
+            [struct(*tile)] * count
             + [struct(2, in_x, height, depth)] * 2
             + [struct(in_corner, height, depth)] * (2 * count)
         )
 
     packed = pl.pallas_call(
         pack_kernel,
-        out_shape=payloads(width + width // 2, 2 * HALO - 2, 2 * HALO - 4),
+        out_shape=payloads(2 * HALO - 2, HALO - 1),
         in_specs=[VMEM] * 4,
         out_specs=[VMEM] * (2 + 3 * count),
         compiler_params=PARAMS,
         name="pack",
     )(orbitals, received, potential, received_potential)
     halos = exchange(packed)
-    passed = []
-    for phase in y_phases():
-        half, *_ = lax.optimization_barrier((halos[phase][width:], *halos[count:]))
-        passed.append(swap(half))
-    local = (potential, received_potential, *passed, *halos)
+    edge, *_ = lax.optimization_barrier((edge, *halos))
+    passed = swap(edge)
+    local = (potential, received_potential, edge, passed, *halos)
     own, sibling, *packed = pl.pallas_call(
         first_kernel,
-        out_shape=[struct(*tile)] * 2 + payloads(width, HALO, HALO - 1),
-        in_specs=[VMEM] * (6 + 4 * count),
+        out_shape=[struct(*tile)] * 2 + payloads(HALO, HALO // 2),
+        in_specs=[VMEM] * (8 + 3 * count),
         out_specs=[VMEM] * (4 + 3 * count),
         scratch_shapes=scratch,
         compiler_params=PARAMS,
@@ -549,7 +640,7 @@
     keep, give, *early = pl.pallas_call(
         second_kernel,
         out_shape=[struct(*tile)] * 2 + [struct(*half)] * (2 * bands - 2),
-        in_specs=[VMEM] * (10 + 7 * count),
+        in_specs=[VMEM] * (12 + 6 * count),
         out_specs=[VMEM] * (2 * bands),
         scratch_shapes=scratch,
         compiler_params=PARAMS,

time: 66.5 us -> 60.2 us (0.905)
  Pallas kernels: 12.2 us -> 9.51 us
  waiting for transfers between devices: 24 us -> 21.4 us
  starting transfers between devices: 28 us -> 26.9 us
    ppermute x10, waiting for transfers between devices: 10.4 us -> 6.7 us  [meet(): return lax.ppermute(value, ('gx', 'gy'), pairs)]
    ppermute x0 -> x1, starting transfers between devices: none -> 2.94 us  [face(): return lax.ppermute(value, ('gy', 'band'), pairs)]
    ppermute x10, starting transfers between devices: 14.6 us -> 12.5 us  [meet(): return lax.ppermute(value, ('gx', 'gy'), pairs)]
    pallas_call x2, Pallas kernels: 5.13 us -> 3.78 us  [the longest x1 3.69 us: per_device(): pl.pallas_call(first_kernel, out_shape=[struct(*tile)] * 2 + payloads(HAL...]
    pallas_call x1, Pallas kernels: 5.02 us -> 3.69 us  [per_device(): pl.pallas_call(second_kernel, out_shape=[struct(*tile)] * 2 + [struct(*ha...]
    ppermute x7, starting transfers between devices: 9.25 us -> 7.93 us  [of(): return lax.ppermute(value, axis, [(i, i ^ step) for i in range(count)])]
    ppermute x7, waiting for transfers between devices: 5.79 us -> 6.79 us  [of(): return lax.ppermute(value, axis, [(i, i ^ step) for i in range(count)])]
  transfers between devices with their start and end apart: 24 -> 25, of which waited for: 9 -> 12; matrix products, arithmetic and copies ran while one was open for 0% -> 0% of each run, Pallas kernels for 0% -> 0%
where the time goes in v7:
time: 60.2 us; the launch traced here: 60 us
  starting transfers between devices  26.9 us (45%)
  waiting for transfers between devices  21.4 us (36%)
  Pallas kernels  9.51 us (16%)
  local copies, waits for them, and re-layouts  2 us (3%)
    ppermute x10, starting transfers between devices, meet(): return lax.ppermute(value, ('gx', 'gy'), pairs)  12.5 us
    ppermute x7, starting transfers between devices, of(): return lax.ppermute(value, axis, [(i, i ^ step) for i in range(count)])  7.93 us
    ppermute x7, waiting for transfers between devices, of(): return lax.ppermute(value, axis, [(i, i ^ step) for i in range(count)])  6.79 us
    ppermute x10, waiting for transfers between devices, meet(): return lax.ppermute(value, ('gx', 'gy'), pairs)  6.7 us
    ppermute x3, waiting for transfers between devices, to_band(): return lax.ppermute(value, ('gy', 'band'), pairs)  6.41 us
    pallas_call x1, Pallas kernels, per_device(): pl.pallas_call(first_kernel, out_shape=[struct(*tile)] * 2 + payloads(HAL...  3.69 us
    pallas_call x1, Pallas kernels, per_device(): pl.pallas_call(second_kernel, out_shape=[struct(*tile)] * 2 + [struct(*ha...  3.69 us
    ppermute x1, starting transfers between devices, face(): return lax.ppermute(value, ('gy', 'band'), pairs)  2.94 us
  transfers between devices with their start and end apart: 25, of which 12 were waited for; matrix products, arithmetic and copies ran while one was open for 0% of the time, Pallas kernels for 0%

profile of v7, /device:TPU:0, one launch (start us, length us, event | category | flops | bytes accessed | tf_op | source)
XLA Modules:
  0.0 60.0 jit_solution(4988625816859281780)
XLA Ops:
  0.5 2.9 %collective-permute-start.2 = (f32[32,8,256]{2,1,0:T(8,128)}, f32[32,8,256]{2,1,0:T(8,128)S(1)}, u32[]{:S(2)}, u32[]{:S(2)}) collective-permute-start(f32[32,8,256]{2,1,0:T(8,128)} %potential.1), channel_id=1, source_target_pairs={{0,1},{1,0},{2,4},{3,5},{4,2},{5,3},{6,7},{7,6},{8,9},{9,8},{10,12... | collective-permute-start | bytes 786440 | tf_op jit(solution)/shard_map/ppermute | solution.py:559
  3.5 1.0 %copy-done = f32[2,32,8,256]{3,2,1,0:T(8,128)S(1)} copy-done((f32[2,32,8,256]{3,2,1,0:T(8,128)S(1)}, f32[2,32,8,256]{3,2,1,0:T(8,128)}, u32[]{:S(2)}) %copy-start) | copy-done | bytes 524312
  4.5 0.9 %copy-done.1 = f32[32,8,256]{2,1,0:T(8,128)S(1)} copy-done((f32[32,8,256]{2,1,0:T(8,128)S(1)}, f32[32,8,256]{2,1,0:T(8,128)}, u32[]{:S(2)}) %copy-start.1) | copy-done | bytes 262168
  5.7 1.7 %collective-permute-start.4 = (f32[2,14,8,256]{3,2,1,0:T(8,128)S(1)}, f32[2,14,8,256]{3,2,1,0:T(8,128)S(1)}, u32[]{:S(2)}, u32[]{:S(2)}) collective-permute-start(f32[2,14,8,256]{3,2,1,0:T(8,128)S(1)} %get-tuple-element.27), channel_id=1, source_target_pairs={{0,8},{2,10},{4,12},{6,14},{8,0},{10,2},{12,4},{14,6},{16,24},{18,... | collective-permute-start | bytes 688136 | tf_op jit(solution)/shard_map/ppermute | solution.py:532
  8.0 3.9 %collective-permute-start.6 = (f32[7,8,256]{2,1,0:T(8,128)S(1)}, f32[7,8,256]{2,1,0:T(8,128)S(1)}, u32[]{:S(2)}, u32[]{:S(2)}) collective-permute-start(f32[7,8,256]{2,1,0:T(8,128)S(1)} %get-tuple-element.29), channel_id=1, source_target_pairs={{0,12},{2,14},{4,8},{6,10},{8,4},{10,6},{12,0},{14,2},{16,28},{18,... | collective-permute-start | bytes 172040 | tf_op jit(solution)/shard_map/ppermute | solution.py:532
  11.9 3.9 %collective-permute-done.6.refs_9_ = f32[7,8,256]{2,1,0:T(8,128)S(1)} collective-permute-done((f32[7,8,256]{2,1,0:T(8,128)S(1)}, f32[7,8,256]{2,1,0:T(8,128)S(1)}, u32[]{:S(2)}, u32[]{:S(2)}) %collective-permute-start.6) | collective-permute-done | bytes 57376 | tf_op jit(solution)/shard_map/ppermute | solution.py:532
  15.9 1.5 %collective-permute-done.8.refs_5_ = f32[32,8,256]{2,1,0:T(8,128)S(1)} collective-permute-done((f32[32,8,256]{2,1,0:T(8,128)S(1)}, f32[32,8,256]{2,1,0:T(8,128)S(1)}, u32[]{:S(2)}, u32[]{:S(2)}) %collective-permute-start.8) | collective-permute-done | bytes 262176 | tf_op jit(solution)/shard_map/ppermute | solution.py:537
  17.4 3.7 %first_round.1 = (f32[32,8,256]{2,1,0:T(8,128)S(1)}, f32[32,8,256]{2,1,0:T(8,128)S(1)}, f32[32,8,256]{2,1,0:T(8,128)S(1)}, f32[2,8,8,256]{3,2,1,0:T(8,128)S(1)},...) custom-call(f32[2,32,8,256]{3,2,1,0:T(8,128)S(1)} %get-tuple-element.24.orbitals.refs_0_, ...), custom_call_target="tpu_custom_call" | custom-call | tf_op jit(solution)/shard_map/first_round/pallas_call | solution.py:630
  21.1 1.1 %collective-permute-start.9 = (f32[32,8,256]{2,1,0:T(8,128)S(1)}, f32[32,8,256]{2,1,0:T(8,128)S(1)}, u32[]{:S(2)}, u32[]{:S(2)}) collective-permute-start(f32[32,8,256]{2,1,0:T(8,128)S(1)} %get-tuple-element.34), channel_id=1, source_target_pairs={{0,4},{2,6},{4,0},{6,2},{8,12},{10,14},{12,8},{14,10},{16,20},{18,... | collective-permute-start | bytes 786440 | tf_op jit(solution)/shard_map/ppermute | solution.py:532
  22.2 2.7 %collective-permute-start.10 = (f32[2,8,8,256]{3,2,1,0:T(8,128)S(1)}, f32[2,8,8,256]{3,2,1,0:T(8,128)S(1)}, u32[]{:S(2)}, u32[]{:S(2)}) collective-permute-start(f32[2,8,8,256]{3,2,1,0:T(8,128)S(1)} %get-tuple-element.35), channel_id=1, source_target_pairs={{0,8},{2,10},{4,12},{6,14},{8,0},{10,2},{12,4},{14,6},{16,24},{18,... | collective-permute-start | bytes 393224 | tf_op jit(solution)/shard_map/ppermute | solution.py:532
  25.0 2.4 %collective-permute-start.12 = (f32[4,8,256]{2,1,0:T(8,128)S(1)}, f32[4,8,256]{2,1,0:T(8,128)S(1)}, u32[]{:S(2)}, u32[]{:S(2)}) collective-permute-start(f32[4,8,256]{2,1,0:T(8,128)S(1)} %get-tuple-element.37), channel_id=1, source_target_pairs={{0,12},{2,14},{4,8},{6,10},{8,4},{10,6},{12,0},{14,2},{16,28},{18,... | collective-permute-start | bytes 98312 | tf_op jit(solution)/shard_map/ppermute | solution.py:532
  27.4 2.5 %collective-permute-done.12.refs_16_ = f32[4,8,256]{2,1,0:T(8,128)S(1)} collective-permute-done((f32[4,8,256]{2,1,0:T(8,128)S(1)}, f32[4,8,256]{2,1,0:T(8,128)S(1)}, u32[]{:S(2)}, u32[]{:S(2)}) %collective-permute-start.12) | collective-permute-done | bytes 32800 | tf_op jit(solution)/shard_map/ppermute | solution.py:532
  30.2 3.7 %second_round.1 = (f32[32,8,256]{2,1,0:T(8,128)S(1)}, f32[32,8,256]{2,1,0:T(8,128)S(1)}, f32[16,8,256]{2,1,0:T(8,128)S(1)}, f32[16,8,256]{2,1,0:T(8,128)S(1)}) custom-call(f32[2,32,8,256]{3,2,1,0:T(8,128)S(1)} %get-tuple-element.24.orbitals.refs_0_, f32[2,32,8,256]{3,2,1,0:T(8,128)S(1)} %collective-permute-done.received.refs_1_, ...), custom_call_target="tpu_custom_call" | custom-call | tf_op jit(solution)/shard_map/second_round/pallas_call | solution.py:640
  34.0 1.0 %collective-permute-start.15 = (f32[16,8,256]{2,1,0:T(8,128)S(1)}, f32[16,8,256]{2,1,0:T(8,128)S(1)}, u32[]{:S(2)}, u32[]{:S(2)}) collective-permute-start(f32[16,8,256]{2,1,0:T(8,128)S(1)} %get-tuple-element.41), channel_id=1, source_target_pairs={{0,1},{1,0},{2,3},{3,2},{4,5},{5,4},{6,7},{7,6},{8,9},{9,8},{10,11... | collective-permute-start | bytes 393224 | tf_op jit(solution)/shard_map/ppermute | solution.py:546
  35.8 4.5 %collective-permute-done.15.refs_2_.refs_4_ = f32[16,8,256]{2,1,0:T(8,128)S(1)} collective-permute-done((f32[16,8,256]{2,1,0:T(8,128)S(1)}, f32[16,8,256]{2,1,0:T(8,128)S(1)}, u32[]{:S(2)}, u32[]{:S(2)}) %collective-permute-start.15) | collective-permute-done | bytes 131104 | tf_op jit(solution)/shard_map/ppermute | solution.py:546
  40.3 1.9 %collective-permute-done.16.refs_3_.refs_5_ = f32[16,8,256]{2,1,0:T(8,128)S(1)} collective-permute-done((f32[16,8,256]{2,1,0:T(8,128)S(1)}, f32[16,8,256]{2,1,0:T(8,128)S(1)}, u32[]{:S(2)}, u32[]{:S(2)}) %collective-permute-start.16) | collective-permute-done | bytes 131104 | tf_op jit(solution)/shard_map/ppermute | solution.py:546
  42.5 1.0 %collective-permute-start.17 = (f32[8,128]{1,0:T(8,128)S(1)}, f32[8,128]{1,0:T(8,128)S(1)}, u32[]{:S(2)}, u32[]{:S(2)}) collective-permute-start(f32[8,128]{1,0:T(8,128)S(1)} %correlation.1), channel_id=1, source_target_pairs={{0,1},{1,0},{2,3},{3,2},{4,5},{5,4},{6,7},{7,6},{8,9},{9,8},{10,11... | collective-permute-start | bytes 12296 | tf_op jit(solution)/shard_map/ppermute | solution.py:578
  43.4 2.7 %collective-permute-done.17 = f32[8,128]{1,0:T(8,128)S(1)} collective-permute-done((f32[8,128]{1,0:T(8,128)S(1)}, f32[8,128]{1,0:T(8,128)S(1)}, u32[]{:S(2)}, u32[]{:S(2)}) %collective-permute-start.17) | collective-permute-done | bytes 4128 | tf_op jit(solution)/shard_map/ppermute | solution.py:578
  46.1 1.1 %collective-permute-start.19 = (f32[8,128]{1,0:T(8,128)S(1)}, f32[8,128]{1,0:T(8,128)S(1)}, u32[]{:S(2)}, u32[]{:S(2)}) collective-permute-start(f32[8,128]{1,0:T(8,128)S(1)} %add.21), channel_id=1, source_target_pairs={{0,4},{2,6},{4,0},{6,2},{1,5},{3,7},{5,1},{7,3},{8,12},{10,14},{12... | collective-permute-start | bytes 12296 | tf_op jit(solution)/shard_map/ppermute | solution.py:578
  48.0 1.0 %collective-permute-start.24 = (f32[2,16,8,256]{3,2,1,0:T(8,128)S(1)}, f32[2,16,8,256]{3,2,1,0:T(8,128)S(1)}, u32[]{:S(2)}, u32[]{:S(2)}) collective-permute-start(f32[2,16,8,256]{3,2,1,0:T(8,128)S(1)} %late.1), channel_id=1, source_target_pairs={{0,1},{1,0},{2,3},{3,2},{4,5},{5,4},{6,7},{7,6},{8,9},{9,8},{10,11... | collective-permute-start | bytes 786440 | tf_op jit(solution)/shard_map/ppermute | solution.py:546
  49.8 3.7 %collective-permute-start.23 = (f32[8,128]{1,0:T(8,128)S(1)}, f32[8,128]{1,0:T(8,128)S(1)}, u32[]{:S(2)}, u32[]{:S(2)}) collective-permute-start(f32[8,128]{1,0:T(8,128)S(1)} %add_add_fusion.1), channel_id=1, source_target_pairs={{0,24},{8,16},{16,8},{24,0},{1,25},{9,17},{17,9},{25,1},{2,26},{10... | collective-permute-start | bytes 12296 | tf_op jit(solution)/shard_map/ppermute | solution.py:578
  53.5 1.1 %collective-permute-start.22 = (f32[8,128]{1,0:T(8,128)S(1)}, f32[8,128]{1,0:T(8,128)S(1)}, u32[]{:S(2)}, u32[]{:S(2)}) collective-permute-start(f32[8,128]{1,0:T(8,128)S(1)} %add_add_fusion.1), channel_id=1, source_target_pairs={{0,16},{8,24},{16,0},{24,8},{1,17},{9,25},{17,1},{25,9},{2,18},{10... | collective-permute-start | bytes 12296 | tf_op jit(solution)/shard_map/ppermute | solution.py:578
  55.3 2.7 %collective-permute-done.22 = f32[8,128]{1,0:T(8,128)S(1)} collective-permute-done((f32[8,128]{1,0:T(8,128)S(1)}, f32[8,128]{1,0:T(8,128)S(1)}, u32[]{:S(2)}, u32[]{:S(2)}) %collective-permute-start.22) | collective-permute-done | bytes 4128 | tf_op jit(solution)/shard_map/ppermute | solution.py:578
  58.2 1.7 %basis.1 = f32[2,32,8,256]{3,2,1,0:T(8,128)} custom-call(f32[8,128]{1,0:T(8,128)S(1)} %add_add_fusion.refs_0_, s32[4]{0:T(128)S(1)} %copy-done.2, f32[32,8,256]{2,1,0:T(8,128)S(1)} %get-tuple-element.39.refs_0_.keep.refs_2_, f32[32,8,256]{2,1,0:T(8,128)S(1)} %collective-permute-done.14.refs_1_.sibling.refs_3_, ...), custom_call_target="tpu_custom_call" | custom-call | tf_op jit(solution)/shard_map/basis/pallas_call | solution.py:670
  (42 shorter events, 5.4 us)
Async XLA Ops:
  0.0 5.5 %collective-permute-start = (f32[2,32,8,256]{3,2,1,0:T(8,128)}, f32[2,32,8,256]{3,2,1,0:T(8,128)S(1)}, u32[]{:S(2)}, u32[]{:S(2)}) collective-permute-start(f32[2,32,8,256]{3,2,1,0:T(8,128)} %orbitals.1), channel_id=1, source_target_pairs={{0,2},{2,0},{4,6},{6,4},{1,3},{3,1},{5,7},{7,5},{8,10},{10,8},{12,... | collective-permute-start | bytes 1572872 | tf_op jit(solution)/shard_map/ppermute | solution.py:537
  0.5 5.1 %collective-permute-start.1 = (f32[32,8,256]{2,1,0:T(8,128)}, f32[32,8,256]{2,1,0:T(8,128)S(1)}, u32[]{:S(2)}, u32[]{:S(2)}) collective-permute-start(f32[32,8,256]{2,1,0:T(8,128)} %potential.1), channel_id=1, source_target_pairs={{0,2},{2,0},{4,6},{6,4},{1,3},{3,1},{5,7},{7,5},{8,10},{10,8},{12,... | collective-permute-start | bytes 786440 | tf_op jit(solution)/shard_map/ppermute | solution.py:537
  0.5 11.4 %collective-permute-start.2 = (f32[32,8,256]{2,1,0:T(8,128)}, f32[32,8,256]{2,1,0:T(8,128)S(1)}, u32[]{:S(2)}, u32[]{:S(2)}) collective-permute-start(f32[32,8,256]{2,1,0:T(8,128)} %potential.1), channel_id=1, source_target_pairs={{0,1},{1,0},{2,4},{3,5},{4,2},{5,3},{6,7},{7,6},{8,9},{9,8},{10,12... | collective-permute-start | bytes 786440 | tf_op jit(solution)/shard_map/ppermute | solution.py:559
  5.6 10.2 %collective-permute-start.3 = (f32[32,8,256]{2,1,0:T(8,128)S(1)}, f32[32,8,256]{2,1,0:T(8,128)S(1)}, u32[]{:S(2)}, u32[]{:S(2)}) collective-permute-start(f32[32,8,256]{2,1,0:T(8,128)S(1)} %get-tuple-element.26), channel_id=1, source_target_pairs={{0,4},{2,6},{4,0},{6,2},{8,12},{10,14},{12,8},{14,10},{16,20},{18,... | collective-permute-start | bytes 786440 | tf_op jit(solution)/shard_map/ppermute | solution.py:532
  5.7 10.0 %collective-permute-start.4 = (f32[2,14,8,256]{3,2,1,0:T(8,128)S(1)}, f32[2,14,8,256]{3,2,1,0:T(8,128)S(1)}, u32[]{:S(2)}, u32[]{:S(2)}) collective-permute-start(f32[2,14,8,256]{3,2,1,0:T(8,128)S(1)} %get-tuple-element.27), channel_id=1, source_target_pairs={{0,8},{2,10},{4,12},{6,14},{8,0},{10,2},{12,4},{14,6},{16,24},{18,... | collective-permute-start | bytes 688136 | tf_op jit(solution)/shard_map/ppermute | solution.py:532
  7.4 8.4 %collective-permute-start.5 = (f32[2,14,8,256]{3,2,1,0:T(8,128)S(1)}, f32[2,14,8,256]{3,2,1,0:T(8,128)S(1)}, u32[]{:S(2)}, u32[]{:S(2)}) collective-permute-start(f32[2,14,8,256]{3,2,1,0:T(8,128)S(1)} %get-tuple-element.28), channel_id=1, source_target_pairs={{0,2},{2,0},{4,6},{6,4},{8,16},{10,18},{12,20},{14,22},{16,8},{18,... | collective-permute-start | bytes 688136 | tf_op jit(solution)/shard_map/ppermute | solution.py:532
  8.0 7.8 %collective-permute-start.6 = (f32[7,8,256]{2,1,0:T(8,128)S(1)}, f32[7,8,256]{2,1,0:T(8,128)S(1)}, u32[]{:S(2)}, u32[]{:S(2)}) collective-permute-start(f32[7,8,256]{2,1,0:T(8,128)S(1)} %get-tuple-element.29), channel_id=1, source_target_pairs={{0,12},{2,14},{4,8},{6,10},{8,4},{10,6},{12,0},{14,2},{16,28},{18,... | collective-permute-start | bytes 172040 | tf_op jit(solution)/shard_map/ppermute | solution.py:532
  11.9 3.9 %collective-permute-start.7 = (f32[7,8,256]{2,1,0:T(8,128)S(1)}, f32[7,8,256]{2,1,0:T(8,128)S(1)}, u32[]{:S(2)}, u32[]{:S(2)}) collective-permute-start(f32[7,8,256]{2,1,0:T(8,128)S(1)} %get-tuple-element.30), channel_id=1, source_target_pairs={{0,2},{2,0},{4,6},{6,4},{8,20},{10,22},{12,16},{14,18},{16,12},{18... | collective-permute-start | bytes 172040 | tf_op jit(solution)/shard_map/ppermute | solution.py:532
  21.1 9.1 %collective-permute-start.9 = (f32[32,8,256]{2,1,0:T(8,128)S(1)}, f32[32,8,256]{2,1,0:T(8,128)S(1)}, u32[]{:S(2)}, u32[]{:S(2)}) collective-permute-start(f32[32,8,256]{2,1,0:T(8,128)S(1)} %get-tuple-element.34), channel_id=1, source_target_pairs={{0,4},{2,6},{4,0},{6,2},{8,12},{10,14},{12,8},{14,10},{16,20},{18,... | collective-permute-start | bytes 786440 | tf_op jit(solution)/shard_map/ppermute | solution.py:532
  22.2 7.6 %collective-permute-start.10 = (f32[2,8,8,256]{3,2,1,0:T(8,128)S(1)}, f32[2,8,8,256]{3,2,1,0:T(8,128)S(1)}, u32[]{:S(2)}, u32[]{:S(2)}) collective-permute-start(f32[2,8,8,256]{3,2,1,0:T(8,128)S(1)} %get-tuple-element.35), channel_id=1, source_target_pairs={{0,8},{2,10},{4,12},{6,14},{8,0},{10,2},{12,4},{14,6},{16,24},{18,... | collective-permute-start | bytes 393224 | tf_op jit(solution)/shard_map/ppermute | solution.py:532
  25.0 4.9 %collective-permute-start.11 = (f32[2,8,8,256]{3,2,1,0:T(8,128)S(1)}, f32[2,8,8,256]{3,2,1,0:T(8,128)S(1)}, u32[]{:S(2)}, u32[]{:S(2)}) collective-permute-start(f32[2,8,8,256]{3,2,1,0:T(8,128)S(1)} %get-tuple-element.36), channel_id=1, source_target_pairs={{0,2},{2,0},{4,6},{6,4},{8,16},{10,18},{12,20},{14,22},{16,8},{18,... | collective-permute-start | bytes 393224 | tf_op jit(solution)/shard_map/ppermute | solution.py:532
  25.0 4.9 %collective-permute-start.12 = (f32[4,8,256]{2,1,0:T(8,128)S(1)}, f32[4,8,256]{2,1,0:T(8,128)S(1)}, u32[]{:S(2)}, u32[]{:S(2)}) collective-permute-start(f32[4,8,256]{2,1,0:T(8,128)S(1)} %get-tuple-element.37), channel_id=1, source_target_pairs={{0,12},{2,14},{4,8},{6,10},{8,4},{10,6},{12,0},{14,2},{16,28},{18,... | collective-permute-start | bytes 98312 | tf_op jit(solution)/shard_map/ppermute | solution.py:532
  27.4 2.5 %collective-permute-start.13 = (f32[4,8,256]{2,1,0:T(8,128)S(1)}, f32[4,8,256]{2,1,0:T(8,128)S(1)}, u32[]{:S(2)}, u32[]{:S(2)}) collective-permute-start(f32[4,8,256]{2,1,0:T(8,128)S(1)} %get-tuple-element.38), channel_id=1, source_target_pairs={{0,2},{2,0},{4,6},{6,4},{8,20},{10,22},{12,16},{14,18},{16,12},{18... | collective-permute-start | bytes 98312 | tf_op jit(solution)/shard_map/ppermute | solution.py:532
  33.9 8.3 %collective-permute-start.14 = (f32[32,8,256]{2,1,0:T(8,128)S(1)}, f32[32,8,256]{2,1,0:T(8,128)S(1)}, u32[]{:S(2)}, u32[]{:S(2)}) collective-permute-start(f32[32,8,256]{2,1,0:T(8,128)S(1)} %get-tuple-element.40), channel_id=1, source_target_pairs={{0,2},{2,0},{4,6},{6,4},{1,3},{3,1},{5,7},{7,5},{8,10},{10,8},{12,... | collective-permute-start | bytes 786440 | tf_op jit(solution)/shard_map/ppermute | solution.py:537
  34.0 6.4 %collective-permute-start.15 = (f32[16,8,256]{2,1,0:T(8,128)S(1)}, f32[16,8,256]{2,1,0:T(8,128)S(1)}, u32[]{:S(2)}, u32[]{:S(2)}) collective-permute-start(f32[16,8,256]{2,1,0:T(8,128)S(1)} %get-tuple-element.41), channel_id=1, source_target_pairs={{0,1},{1,0},{2,3},{3,2},{4,5},{5,4},{6,7},{7,6},{8,9},{9,8},{10,11... | collective-permute-start | bytes 393224 | tf_op jit(solution)/shard_map/ppermute | solution.py:546
  34.9 7.3 %collective-permute-start.16 = (f32[16,8,256]{2,1,0:T(8,128)S(1)}, f32[16,8,256]{2,1,0:T(8,128)S(1)}, u32[]{:S(2)}, u32[]{:S(2)}) collective-permute-start(f32[16,8,256]{2,1,0:T(8,128)S(1)} %get-tuple-element.42), channel_id=1, source_target_pairs={{0,3},{1,2},{2,1},{3,0},{4,7},{5,6},{6,5},{7,4},{8,11},{9,10},{10,... | collective-permute-start | bytes 393224 | tf_op jit(solution)/shard_map/ppermute | solution.py:546
  42.5 3.7 %collective-permute-start.17 = (f32[8,128]{1,0:T(8,128)S(1)}, f32[8,128]{1,0:T(8,128)S(1)}, u32[]{:S(2)}, u32[]{:S(2)}) collective-permute-start(f32[8,128]{1,0:T(8,128)S(1)} %correlation.1), channel_id=1, source_target_pairs={{0,1},{1,0},{2,3},{3,2},{4,5},{5,4},{6,7},{7,6},{8,9},{9,8},{10,11... | collective-permute-start | bytes 12296 | tf_op jit(solution)/shard_map/ppermute | solution.py:578
  46.1 3.0 %collective-permute-start.20 = (f32[8,128]{1,0:T(8,128)S(1)}, f32[8,128]{1,0:T(8,128)S(1)}, u32[]{:S(2)}, u32[]{:S(2)}) collective-permute-start(f32[8,128]{1,0:T(8,128)S(1)} %add.21), channel_id=1, source_target_pairs={{0,6},{2,4},{4,2},{6,0},{1,7},{3,5},{5,3},{7,1},{8,14},{10,12},{12... | collective-permute-start | bytes 12296 | tf_op jit(solution)/shard_map/ppermute | solution.py:578
  46.1 3.6 %collective-permute-start.19 = (f32[8,128]{1,0:T(8,128)S(1)}, f32[8,128]{1,0:T(8,128)S(1)}, u32[]{:S(2)}, u32[]{:S(2)}) collective-permute-start(f32[8,128]{1,0:T(8,128)S(1)} %add.21), channel_id=1, source_target_pairs={{0,4},{2,6},{4,0},{6,2},{1,5},{3,7},{5,1},{7,3},{8,12},{10,14},{12... | collective-permute-start | bytes 12296 | tf_op jit(solution)/shard_map/ppermute | solution.py:578
  47.3 2.5 %collective-permute-start.18 = (f32[8,128]{1,0:T(8,128)S(1)}, f32[8,128]{1,0:T(8,128)S(1)}, u32[]{:S(2)}, u32[]{:S(2)}) collective-permute-start(f32[8,128]{1,0:T(8,128)S(1)} %add.21), channel_id=1, source_target_pairs={{0,2},{2,0},{4,6},{6,4},{1,3},{3,1},{5,7},{7,5},{8,10},{10,8},{12,... | collective-permute-start | bytes 12296 | tf_op jit(solution)/shard_map/ppermute | solution.py:578
  48.0 10.2 %collective-permute-start.24 = (f32[2,16,8,256]{3,2,1,0:T(8,128)S(1)}, f32[2,16,8,256]{3,2,1,0:T(8,128)S(1)}, u32[]{:S(2)}, u32[]{:S(2)}) collective-permute-start(f32[2,16,8,256]{3,2,1,0:T(8,128)S(1)} %late.1), channel_id=1, source_target_pairs={{0,1},{1,0},{2,3},{3,2},{4,5},{5,4},{6,7},{7,6},{8,9},{9,8},{10,11... | collective-permute-start | bytes 786440 | tf_op jit(solution)/shard_map/ppermute | solution.py:546
  49.8 5.5 %collective-permute-start.23 = (f32[8,128]{1,0:T(8,128)S(1)}, f32[8,128]{1,0:T(8,128)S(1)}, u32[]{:S(2)}, u32[]{:S(2)}) collective-permute-start(f32[8,128]{1,0:T(8,128)S(1)} %add_add_fusion.1), channel_id=1, source_target_pairs={{0,24},{8,16},{16,8},{24,0},{1,25},{9,17},{17,9},{25,1},{2,26},{10... | collective-permute-start | bytes 12296 | tf_op jit(solution)/shard_map/ppermute | solution.py:578
  53.5 4.5 %collective-permute-start.22 = (f32[8,128]{1,0:T(8,128)S(1)}, f32[8,128]{1,0:T(8,128)S(1)}, u32[]{:S(2)}, u32[]{:S(2)}) collective-permute-start(f32[8,128]{1,0:T(8,128)S(1)} %add_add_fusion.1), channel_id=1, source_target_pairs={{0,16},{8,24},{16,0},{24,8},{1,17},{9,25},{17,1},{25,9},{2,18},{10... | collective-permute-start | bytes 12296 | tf_op jit(solution)/shard_map/ppermute | solution.py:578
  54.6 3.6 %collective-permute-start.21 = (f32[8,128]{1,0:T(8,128)S(1)}, f32[8,128]{1,0:T(8,128)S(1)}, u32[]{:S(2)}, u32[]{:S(2)}) collective-permute-start(f32[8,128]{1,0:T(8,128)S(1)} %add_add_fusion.1), channel_id=1, source_target_pairs={{0,8},{8,0},{16,24},{24,16},{1,9},{9,1},{17,25},{25,17},{2,10},{10... | collective-permute-start | bytes 12296 | tf_op jit(solution)/shard_map/ppermute | solution.py:578
  (4 other events, 12.0 us)

commit v8 on v7

--- a/solution.py
+++ b/solution.py
@@ -12,12 +12,14 @@
 PAD = 8
 LANES = 128
 PLANES = 4
-BY_PRODUCT, BY_ROLLS, UNROLL = 8, 4, 2
+OWN_ROWS = slice(PAD + 8, PAD + 24)
+HALO_ROWS = (slice(PAD, PAD + 8), slice(PAD + 24, PAD + 32))
+TOGETHER = {8: (16, 8, 1), 16: (12, 6, 1), 32: (8, 2, 1)}
 NEAR = -(2.0 / 3.0) / 4.25
 FAR = (1.0 / 24.0) / 4.25
 VMEM = pl.BlockSpec(memory_space=pltpu.VMEM)
 SMEM = pl.BlockSpec(memory_space=pltpu.SMEM)
-PARAMS = pltpu.CompilerParams(vmem_limit_bytes=40 * 1024 * 1024)
+PARAMS = pltpu.CompilerParams(vmem_limit_bytes=16 * 1024 * 1024)
 
 
 def struct(*shape):
@@ -33,10 +35,6 @@
     return lax.axis_size("gy") == 4
 
 
-def tile_count():
-    return 3 if one_sided() else 4
-
-
 def y_phases():
     return range(1 if one_sided() else 2)
 
@@ -45,14 +43,12 @@
     return (position % 2) == phase
 
 
-def own_slots(core, chip):
-    first = chip if one_sided() else 1
-    return first + core, first + 1 - core
-
-
-def halo_slot(chip, up):
-    first = chip if one_sided() else 1
-    return jnp.where(up, first + 2, first - 1)
+def own_slots(core):
+    return 1 + core, 2 - core
+
+
+def halo_slot(up):
+    return jnp.where(up, 3, 0)
 
 
 def rows_of(slot):
@@ -95,20 +91,31 @@
         out[k - 1] = tile
 
 
-def fill(window, tiles, x_halos, y_halos, corners, reach, change=lambda a: a):
-    core, chip, along_x = place()
+def fill_own(window, tiles, x_halos, change=lambda a: a):
+    core, _, along_x = place()
     width = tiles[0].shape[0]
-    slots = own_slots(core, chip)
-    for index, slot in enumerate(slots):
+    for index, slot in enumerate(own_slots(core)):
         put(window, HALO, rows_of(slot), tiles[index], change)
+    fill_x(window, width, x_halos, change)
+
+
+def fill_x(window, width, x_halos, change=lambda a: a):
+    core, _, along_x = place()
+    for index, slot in enumerate(own_slots(core)):
         for phase in range(2):
             halo = x_halos[phase].at[index]
             start = halo_start(upward(along_x, phase), width, halo.shape[0])
             put(window, start, rows_of(slot), halo, change)
+
+
+def fill_y(window, y_halos, corners, reach, change=lambda a: a):
+    _, chip, along_x = place()
+    width = window.shape[1] - 2 * HALO
     for phase in y_phases():
         up = upward(chip, phase)
-        rows = rows_of(halo_slot(chip, up))
-        put(window, HALO, rows, y_halos[phase], change)
+        rows = rows_of(halo_slot(up))
+        if y_halos is not None:
+            put(window, HALO, rows, y_halos[phase], change)
         for x_phase in range(2):
             corner = corners[2 * phase + x_phase]
             put_corner(window, corner, reach, upward(along_x, x_phase), up, rows, width, change)
@@ -163,10 +170,8 @@
     return found
 
 
-def stencil(source, target, local, x, by_product, by_rolls, along_z, first):
-    height = source.shape[2] - 2 * PAD
-    body = slice(PAD, PAD + height)
-    scale = 1.0 if first else 2.0
+def stencil(source, previous, target, local, x, by_product, by_rolls, along_z, body):
+    scale = 1.0 if previous is None else 2.0
     results = []
     for start, count, product in ((x, by_product, True), (x + by_product, by_rolls, False)):
         if not count:
@@ -184,56 +189,85 @@
                 near = near + z_near[half]
             result = local[half, now, body, :] * values[half] * scale
             result = result + near * (NEAR * scale) + far * (FAR * scale)
-            if not first:
-                result = result - target[half, now, body, :]
+            if previous is not None:
+                result = result - previous[half, now, body, :]
             results.append((half, now, result))
     for half, now, result in results:
         target[half, now, body, :] = result
 
 
-def four_steps(a, b, local, along_z):
-    extent = a.shape[1]
-    height = a.shape[2] - 2 * PAD
-    for buffer in (a, b):
-        for rows in (slice(0, PAD), slice(PAD + height, PAD + height + PAD)):
-            buffer[:, :, rows, :] = jnp.zeros((2, extent, PAD, LANES), jnp.float32)
-    outside_is_zero(a)
-    buffers = (a, b)
+def four_steps(levels, local, depth, body, last):
+    along_z = z_matrix(depth)
+    extent = local.shape[1]
+    outside_is_zero(levels[0], body)
     for step in range(STEPS):
-        source, target = buffers[step % 2], buffers[(step + 1) % 2]
+        rows = last if step == STEPS - 1 else body
         low = 2 * (step + 1)
-        together = BY_PRODUCT + BY_ROLLS
+        by_product, by_rolls, unroll = TOGETHER[rows.stop - rows.start]
+        together = by_product + by_rolls
         blocks, rest = divmod(extent - 2 * low, together)
-
-        def block(index, carry, source=source, target=target, low=low, step=step):
-            x = low + index * together
-            stencil(source, target, local, x, BY_PRODUCT, BY_ROLLS, along_z, step == 0)
+        previous = levels[step - 1] if step else None
+
+        def do(x, by_product, by_rolls, rows=rows, step=step, previous=previous):
+            source, target = levels[step], levels[step + 1]
+            stencil(source, previous, target, local, x, by_product, by_rolls, along_z, rows)
+
+        def block(index, carry, do=do, low=low, by_product=by_product, by_rolls=by_rolls):
+            do(low + index * (by_product + by_rolls), by_product, by_rolls)
             return carry
 
-        lax.fori_loop(0, blocks, block, 0, unroll=UNROLL)
+        lax.fori_loop(0, blocks, block, 0, unroll=min(unroll, blocks))
         if rest:
-            by_rolls = min(BY_ROLLS, rest // 3)
-            x = low + blocks * together
-            stencil(source, target, local, x, rest - by_rolls, by_rolls, along_z, step == 0)
+            rolled = min(by_rolls, rest // 3)
+            do(low + blocks * together, rest - rolled, rolled)
         if step < STEPS - 1:
-            outside_is_zero(target)
-
-
-def outside_is_zero(window):
+            outside_is_zero(levels[step + 1], body)
+
+
+def outside_is_zero(window, body):
     _, chip, along_x = place()
     extent = window.shape[1]
 
-    def clear(where, planes, rows=slice(None)):
+    def clear(where, planes, rows):
         @pl.when(where)
         def _():
             region = window[:, planes, rows, :]
             window[:, planes, rows, :] = jnp.zeros_like(region)
 
-    clear(along_x == 0, slice(0, HALO))
-    clear(along_x == lax.axis_size("gx") - 1, slice(extent - HALO, extent))
+    clear(along_x == 0, slice(0, HALO), body)
+    clear(along_x == lax.axis_size("gx") - 1, slice(extent - HALO, extent), body)
     if not one_sided():
-        clear(chip == 0, slice(None), slice(PAD, PAD + 8))
-        clear(chip == lax.axis_size("gy") // 2 - 1, slice(None), slice(PAD + 24, PAD + 32))
+        clear(chip == 0, slice(None), HALO_ROWS[0])
+        clear(chip == lax.axis_size("gy") // 2 - 1, slice(None), HALO_ROWS[1])
+
+
+def first_part(levels, local, depth):
+    if not one_sided():
+        return
+    _, chip, _ = place()
+    for position in range(2):
+
+        @pl.when(chip == position)
+        def _(position=position):
+            for window in levels[:STEPS]:
+                region = window[:, :, HALO_ROWS[position], :]
+                window[:, :, HALO_ROWS[position], :] = jnp.zeros_like(region)
+
+    four_steps(levels, local, depth, OWN_ROWS, OWN_ROWS)
+
+
+def second_part(levels, local, depth):
+    if not one_sided():
+        four_steps(levels, local, depth, slice(PAD, PAD + 32), OWN_ROWS)
+        return
+    _, chip, _ = place()
+    for position in range(2):
+        inner = slice(PAD + 16, PAD + 24) if position == 0 else slice(PAD + 8, PAD + 16)
+        body = slice(PAD + 16, PAD + 32) if position == 0 else slice(PAD, PAD + 16)
+
+        @pl.when(chip == position)
+        def _(inner=inner, body=body):
+            four_steps(levels, local, depth, body, inner)
 
 
 def edge_is_own(core, chip, phase):
@@ -270,7 +304,9 @@
 
             @pl.when(chosen)
             def _(t=t, phase=phase):
-                y_out[phase][...] = tiles[t][...]
+                y_out[phase][:width] = tiles[t][...]
+                half = width // 2
+                y_out[phase][width:] = local[t][pl.ds(core * half, half)]
                 up = upward(chip, phase)
                 for x_phase in range(2):
                     right = upward(along_x, x_phase)
@@ -284,64 +320,55 @@
                     pack_corner(rest, functools.partial(plane, field=local[t]), HALO - 2, up)
 
 
-def fill_local(window, potential, received_potential, edge, passed, x_halos, corners):
-    core, chip, _ = place()
-
-    def change(v):
-        return (v - 0.5) / 4.25
-
-    fill(
-        window,
-        (potential, received_potential),
-        [x.at[:, HALO:] for x in x_halos],
-        [edge] * len(y_phases()),
-        [c.at[HALO // 2 :] for c in corners],
-        HALO - 2,
-        change,
-    )
+def halos_of(refs):
+    count = len(y_phases())
+    return refs[:count], refs[count : count + 2], refs[count + 2 :]
+
+
+def diagonal(potential):
+    return (potential - 0.5) / 4.25
+
+
+def first_own_kernel(orbitals, received, potential, received_potential, x_a, x_b, *outs):
+    levels, local = outs[:-1], outs[-1]
+    core, _, _ = place()
+    x_halos = (x_a, x_b)
+    tiles = (orbitals.at[core], received.at[core])
+    fill_own(levels[0], tiles, [x.at[:, :HALO] for x in x_halos])
+    tiles = (potential, received_potential)
+    fill_own(local, tiles, [x.at[:, HALO:] for x in x_halos], diagonal)
+    first_part(levels, local, potential.shape[2])
+
+
+def first_rest_kernel(*refs):
+    count = len(y_phases())
+    passed, y_halos = refs[6 : 6 + count], refs[6 + count : 6 + 2 * count]
+    corners, outs = refs[6 + 2 * count : 6 + 4 * count], refs[6 + 4 * count :]
+    levels, local = outs[: STEPS + 1], outs[STEPS + 1]
+    payloads = outs[STEPS + 2 :]
+    core, chip, along_x = place()
+    width, depth = local.shape[1] - 2 * HALO, 2 * LANES
+    fill_y(levels[0], [y.at[:width] for y in y_halos], [c.at[: HALO // 2] for c in corners], HALO)
+    fill_y(local, None, [c.at[HALO // 2 :] for c in corners], HALO - 2, diagonal)
+    half = width // 2
     for phase in y_phases():
-        up = upward(chip, phase)
-
-        @pl.when(core != jnp.where(up, 1, 0))
-        def _(up=up):
-            put(window, HALO, rows_of(halo_slot(chip, up)), passed, change)
-
-
-def first_kernel(*refs):
-    count = len(y_phases())
-    orbitals, received, potential, received_potential, edge, passed = refs[:6]
-    halos = refs[6 : 8 + 3 * count]
-    own_out, other_out = refs[8 + 3 * count : 10 + 3 * count]
-    outs = refs[10 + 3 * count : 12 + 6 * count]
-    a, b, local = refs[12 + 6 * count :]
-    core, chip, along_x = place()
-    width, depth = potential.shape[0], potential.shape[2]
-    y_halos, x_halos, corners = halos_of(halos)
-    fill(
-        a,
-        (orbitals.at[core], received.at[core]),
-        [x.at[:, :HALO] for x in x_halos],
-        y_halos,
-        [c.at[: HALO // 2] for c in corners],
-        HALO,
-    )
-    fill_local(local, potential, received_potential, edge, passed, x_halos, corners)
-    four_steps(a, b, local, z_matrix(depth))
-    y_out, x_out, d_out = outs[:count], outs[count : count + 2], outs[count + 2 :]
-    slots = own_slots(core, chip)
+        rows = rows_of(halo_slot(upward(chip, phase)))
+        put(local, HALO + core * half, rows, y_halos[phase].at[width:], diagonal)
+        put(local, HALO + (1 - core) * half, rows, passed[phase], diagonal)
+
+    second_part(levels, local, depth)
+    y_out, x_out, d_out = halos_of(payloads)
+    slots = own_slots(core)
+    result = levels[STEPS]
     for half in range(2):
         lanes = slice(half * LANES, (half + 1) * LANES)
 
         def planes(slot, start, size, half=half):
-            return a[half, pl.ds(HALO + start, size), rows_of(slot), :]
-
-        def ends(right, size):
-            return jnp.where(right, width - size, 0)
-
-        for t, out in enumerate((own_out, other_out)):
-            out[:, :, lanes] = planes(slots[t], 0, width)
+            return result[half, pl.ds(HALO + start, size), rows_of(slot), :]
+
+        for t in range(2):
             for x_phase in range(2):
-                start = ends(upward(along_x, x_phase), HALO)
+                start = jnp.where(upward(along_x, x_phase), width - HALO, 0)
                 x_out[x_phase][t, :, :, lanes] = planes(slots[t], start, HALO)
         for phase in y_phases():
             slot = jnp.where(edge_is_own(core, chip, phase), *slots)
@@ -356,33 +383,31 @@
                 pack_corner(out, plane, HALO, upward(chip, phase))
 
 
-def halos_of(refs):
+def second_own_kernel(before, local, x_a, x_b, *levels):
+    width = before.shape[1] - 2 * HALO
+    for half in range(2):
+        inside = (half, slice(HALO, HALO + width), OWN_ROWS)
+        levels[0][inside] = before[inside]
+    fill_x(levels[0], width, (x_a, x_b))
+    first_part(levels, local, LANES * 2)
+
+
+def second_rest_kernel(*refs):
     count = len(y_phases())
-    return refs[:count], refs[count : count + 2], refs[count + 2 :]
-
-
-def second_kernel(*refs):
-    count = len(y_phases())
-    orbitals, received, potential, received_potential, edge, passed = refs[:6]
-    local_halos = refs[6 : 8 + 3 * count]
-    own, other = refs[8 + 3 * count : 10 + 3 * count]
-    halos = refs[10 + 3 * count : 12 + 6 * count]
-    keep, give = refs[12 + 6 * count : 14 + 6 * count]
-    early = refs[14 + 6 * count : -3]
-    a, b, local = refs[-3:]
-    core, chip, _ = place()
-    width, depth = potential.shape[0], potential.shape[2]
-    y_halos, x_halos, corners = halos_of(halos)
-    fill(a, (own, other), x_halos, y_halos, corners, HALO)
-    _, p_x_halos, p_corners = halos_of(local_halos)
-    fill_local(local, potential, received_potential, edge, passed, p_x_halos, p_corners)
-    four_steps(a, b, local, z_matrix(depth))
+    local, orbitals, received = refs[STEPS + 1 : STEPS + 4]
+    refs = refs[STEPS + 4 :]
+    y_halos, corners = refs[:count], refs[count : 3 * count]
+    levels, outs = refs[3 * count : 3 * count + STEPS + 1], refs[3 * count + STEPS + 1 :]
+    outs, early = outs[:2], outs[2:]
+    core, _, _ = place()
+    width, depth = orbitals.shape[1], orbitals.shape[3]
+    fill_y(levels[0], y_halos, corners, HALO)
+    second_part(levels, local, depth)
     start = (orbitals.at[core], received.at[core])
-    outs = (keep, give)
-    for t, slot in enumerate(own_slots(core, chip)):
+    for t, slot in enumerate(own_slots(core)):
         for half in range(2):
             lanes = slice(half * LANES, (half + 1) * LANES)
-            tile = a[half, HALO : HALO + width, rows_of(slot), :]
+            tile = levels[STEPS][half, HALO : HALO + width, rows_of(slot), :]
             outs[t][:, :, lanes] = 2.0 * tile - start[t][:, :, lanes]
     half = width // 2
     for d in range(1, lax.axis_size("band")):
@@ -546,19 +571,6 @@
     return lax.ppermute(value, ("gy", "band"), pairs)
 
 
-def face(value):
-    count, bands = lax.axis_size("gy"), lax.axis_size("band")
-    pairs = []
-    for y in range(count):
-        for band in range(bands):
-            to = partner(y, 1, count)
-            if to is not None:
-                pairs.append((y * bands + band, to * bands + band))
-            elif bands % 2 == 0:
-                pairs.append((y * bands + band, y * bands + (band ^ 1)))
-    return lax.ppermute(value, ("gy", "band"), pairs)
-
-
 def exchange(payloads):
     count = len(y_phases())
     halos = [meet(payloads[phase], y_phase=phase) for phase in y_phases()]
@@ -591,12 +603,11 @@
     bands = lax.axis_size("band")
     cells = float(width * lax.axis_size("gx") * height * lax.axis_size("gy") * depth)
     count = len(y_phases())
-    window = (2, width + 2 * HALO, 8 * tile_count() + 2 * PAD, LANES)
-    scratch = [pltpu.VMEM(window, jnp.float32)] * 3
+    window = struct(2, width + 2 * HALO, 32 + 2 * PAD, LANES)
+    windows = STEPS + 1
 
     received = swap(orbitals)
     received_potential = swap(potential)
-    edge = face(potential)
     tile = (width, height, depth)
     orbitals, potential = pl.pallas_call(
         load_kernel,
@@ -608,44 +619,65 @@
         name="load",
     )(orbitals, potential)
 
-    def payloads(in_x, in_corner):
+    def payloads(in_y, in_x, in_corner):
         return (
-            [struct(*tile)] * count
+            [struct(in_y, height, depth)] * count
             + [struct(2, in_x, height, depth)] * 2
             + [struct(in_corner, height, depth)] * (2 * count)
         )
 
     packed = pl.pallas_call(
         pack_kernel,
-        out_shape=payloads(2 * HALO - 2, HALO - 1),
+        out_shape=payloads(width + width // 2, 2 * HALO - 2, HALO - 1),
         in_specs=[VMEM] * 4,
         out_specs=[VMEM] * (2 + 3 * count),
         compiler_params=PARAMS,
         name="pack",
     )(orbitals, received, potential, received_potential)
     halos = exchange(packed)
-    edge, *_ = lax.optimization_barrier((edge, *halos))
-    passed = swap(edge)
-    local = (potential, received_potential, edge, passed, *halos)
-    own, sibling, *packed = pl.pallas_call(
-        first_kernel,
-        out_shape=[struct(*tile)] * 2 + payloads(HALO, HALO // 2),
-        in_specs=[VMEM] * (8 + 3 * count),
-        out_specs=[VMEM] * (4 + 3 * count),
-        scratch_shapes=scratch,
-        compiler_params=PARAMS,
-        name="first_round",
-    )(orbitals, received, *local)
+    y_halos, x_halos, corners = halos_of(halos)
+    *levels, local = pl.pallas_call(
+        first_own_kernel,
+        out_shape=[window] * (windows + 1),
+        in_specs=[VMEM] * 6,
+        out_specs=[VMEM] * (windows + 1),
+        compiler_params=PARAMS,
+        name="first_own",
+    )(orbitals, received, potential, received_potential, *x_halos)
+    passed = []
+    for phase in y_phases():
+        half, *_ = lax.optimization_barrier((y_halos[phase][width:], *y_halos, *corners, *levels))
+        passed.append(swap(half))
+    outs = pl.pallas_call(
+        first_rest_kernel,
+        out_shape=[window] * (windows + 1) + payloads(width, HALO, HALO // 2),
+        in_specs=[VMEM] * (windows + 1 + 4 * count),
+        out_specs=[VMEM] * (windows + 3 + 3 * count),
+        input_output_aliases={k: k for k in range(windows + 1)},
+        compiler_params=PARAMS,
+        name="first_rest",
+    )(*levels, local, *passed, *y_halos, *corners)
+    levels, local, packed = outs[:windows], outs[windows], outs[windows + 1 :]
+    y_halos, x_halos, corners = halos_of(exchange(packed))
+    levels = pl.pallas_call(
+        second_own_kernel,
+        out_shape=[window] * windows,
+        in_specs=[VMEM] * 4,
+        out_specs=[VMEM] * windows,
+        compiler_params=PARAMS,
+        name="second_own",
+    )(levels[STEPS], local, *x_halos)
     half = (width // 2, height, depth)
-    keep, give, *early = pl.pallas_call(
-        second_kernel,
-        out_shape=[struct(*tile)] * 2 + [struct(*half)] * (2 * bands - 2),
-        in_specs=[VMEM] * (12 + 6 * count),
-        out_specs=[VMEM] * (2 * bands),
-        scratch_shapes=scratch,
-        compiler_params=PARAMS,
-        name="second_round",
-    )(orbitals, received, *local, own, sibling, *exchange(packed))
+    outs = pl.pallas_call(
+        second_rest_kernel,
+        out_shape=[window] * windows + [struct(*tile)] * 2 + [struct(*half)] * (2 * bands - 2),
+        in_specs=[VMEM] * (windows + 3 + 3 * count),
+        out_specs=[VMEM] * (windows + 2 * bands),
+        input_output_aliases={k: k for k in range(windows)},
+        compiler_params=PARAMS,
+        name="second_rest",
+    )(*levels, local, orbitals, received, *y_halos, *corners)
+    keep, give, *early = outs[windows:]
 
     early = [to_band(value, 1 + k // 2, crossed=k % 2 == 1) for k, value in enumerate(early)]
     sibling = swap(give)

time: 60.2 us -> 58.9 us (0.978)
  waiting for transfers between devices: 21.4 us -> 17.9 us
  Pallas kernels: 9.51 us -> 12.5 us
  starting transfers between devices: 26.9 us -> 26 us
    pallas_call x3 -> x5, Pallas kernels: 7.46 us -> 10.5 us  [the longest x1 2.8 us: per_device(): pl.pallas_call(first_own_kernel, out_shape=[window] * (windows + 1), in_s...]
    ppermute x1 -> x0, starting transfers between devices: 2.94 us -> none  [face(): return lax.ppermute(value, ('gy', 'band'), pairs)]
    ppermute x7, waiting for transfers between devices: 6.79 us -> 5.02 us  [of(): return lax.ppermute(value, axis, [(i, i ^ step) for i in range(count)])]
    ppermute x10, waiting for transfers between devices: 6.7 us -> 5.18 us  [meet(): return lax.ppermute(value, ('gx', 'gy'), pairs)]
    ppermute x10, starting transfers between devices: 12.5 us -> 14 us  [meet(): return lax.ppermute(value, ('gx', 'gy'), pairs)]
  transfers between devices with their start and end apart: 25 -> 24, of which waited for: 12 -> 9; matrix products, arithmetic and copies ran while one was open for 0% -> 0% of each run, Pallas kernels for 0% -> 10%
where the time goes in v8:
time: 58.9 us; the launch traced here: 58.7 us
  starting transfers between devices  26 us (44%)
  waiting for transfers between devices  17.9 us (30%)
  Pallas kernels  12.5 us (21%)
  local copies, waits for them, and re-layouts  2.01 us (3%)
    ppermute x10, starting transfers between devices, meet(): return lax.ppermute(value, ('gx', 'gy'), pairs)  14 us
    ppermute x7, starting transfers between devices, of(): return lax.ppermute(value, axis, [(i, i ^ step) for i in range(count)])  7.87 us
    ppermute x3, waiting for transfers between devices, to_band(): return lax.ppermute(value, ('gy', 'band'), pairs)  6.41 us
    ppermute x10, waiting for transfers between devices, meet(): return lax.ppermute(value, ('gx', 'gy'), pairs)  5.18 us
    ppermute x7, waiting for transfers between devices, of(): return lax.ppermute(value, axis, [(i, i ^ step) for i in range(count)])  5.02 us
    ppermute x3, starting transfers between devices, to_band(): return lax.ppermute(value, ('gy', 'band'), pairs)  3.42 us
    pallas_call x1, Pallas kernels, per_device(): pl.pallas_call(first_own_kernel, out_shape=[window] * (windows + 1), in_s...  2.8 us
    pallas_call x1, Pallas kernels, per_device(): pl.pallas_call(second_own_kernel, out_shape=[window] * windows, in_specs=...  2.7 us
  transfers between devices with their start and end apart: 24, of which 9 were waited for; matrix products, arithmetic and copies ran while one was open for 0% of the time, Pallas kernels for 10%

profile of v8, /device:TPU:0, one launch (start us, length us, event | category | flops | bytes accessed | tf_op | source)
XLA Modules:
  0.0 58.7 jit_solution(11040417725223917522)
XLA Ops:
  2.7 3.0 %collective-permute-start.4 = (f32[48,8,256]{2,1,0:T(8,128)S(1)}, f32[48,8,256]{2,1,0:T(8,128)S(1)}, u32[]{:S(2)}, u32[]{:S(2)}) collective-permute-start(f32[48,8,256]{2,1,0:T(8,128)S(1)} %get-tuple-element.45), channel_id=1, source_target_pairs={{0,4},{2,6},{4,0},{6,2},{8,12},{10,14},{12,8},{14,10},{16,20},{18,... | collective-permute-start | bytes 1179656 | tf_op jit(solution)/shard_map/ppermute | solution.py:557
  5.8 1.6 %collective-permute-start.2 = (f32[2,14,8,256]{3,2,1,0:T(8,128)S(1)}, f32[2,14,8,256]{3,2,1,0:T(8,128)S(1)}, u32[]{:S(2)}, u32[]{:S(2)}) collective-permute-start(f32[2,14,8,256]{3,2,1,0:T(8,128)S(1)} %get-tuple-element.37), channel_id=1, source_target_pairs={{0,8},{2,10},{4,12},{6,14},{8,0},{10,2},{12,4},{14,6},{16,24},{18,... | collective-permute-start | bytes 688136 | tf_op jit(solution)/shard_map/ppermute | solution.py:557
  7.3 3.1 %collective-permute-start.5 = (f32[7,8,256]{2,1,0:T(8,128)S(1)}, f32[7,8,256]{2,1,0:T(8,128)S(1)}, u32[]{:S(2)}, u32[]{:S(2)}) collective-permute-start(f32[7,8,256]{2,1,0:T(8,128)S(1)} %get-tuple-element.46), channel_id=1, source_target_pairs={{0,12},{2,14},{4,8},{6,10},{8,4},{10,6},{12,0},{14,2},{16,28},{18,... | collective-permute-start | bytes 172040 | tf_op jit(solution)/shard_map/ppermute | solution.py:557
  10.4 3.2 %collective-permute-done.2.x_a = f32[2,14,8,256]{3,2,1,0:T(8,128)S(1)} collective-permute-done((f32[2,14,8,256]{3,2,1,0:T(8,128)S(1)}, f32[2,14,8,256]{3,2,1,0:T(8,128)S(1)}, u32[]{:S(2)}, u32[]{:S(2)}) %collective-permute-start.2) | collective-permute-done | bytes 229408 | tf_op jit(solution)/shard_map/ppermute | solution.py:557
  13.6 2.8 %first_own.1 = (f32[2,48,48,128]{3,2,1,0:T(8,128)S(1)}, f32[2,48,48,128]{3,2,1,0:T(8,128)S(1)}, f32[2,48,48,128]{3,2,1,0:T(8,128)S(1)}, f32[2,48,48,128]{3,2,1,0...) custom-call(f32[2,32,8,256]{3,2,1,0:T(8,128)S(1)} %get-tuple-element.35.orbitals.refs_6_, ...), custom_call_target="tpu_custom_call" | custom-call | tf_op jit(solution)/shard_map/first_own/pallas_call | solution.py:639
  16.5 1.3 %collective-permute-done.7.refs_6_ = f32[16,8,256]{2,1,0:T(8,128)S(1)} collective-permute-done((f32[16,8,256]{2,1,0:T(8,128)S(1)}, f32[16,8,256]{2,1,0:T(8,128)S(1)}, u32[]{:S(2)}, u32[]{:S(2)}) %collective-permute-start.7) | collective-permute-done | bytes 131104 | tf_op jit(solution)/shard_map/ppermute | solution.py:562
  17.9 2.4 %first_rest.1 = (f32[2,48,48,128]{3,2,1,0:T(8,128)S(1)}, f32[2,48,48,128]{3,2,1,0:T(8,128)S(1)}, f32[2,48,48,128]{3,2,1,0:T(8,128)S(1)}, f32[2,48,48,128]{3,2,1,...) custom-call(f32[2,48,48,128]{3,2,1,0:T(8,128)S(1)} %get-tuple-elemen, ...), custom_call_target="tpu_custom_call", output_to_operand_aliasing={{0}: (0, {}), {1}: (1, {}), {2}: (2, {}), {3}: (3, {}), {4}... | custom-call | tf_op jit(solution)/shard_map/first_rest/pallas_call | solution.py:651
  20.3 1.7 %collective-permute-start.10 = (f32[32,8,256]{2,1,0:T(8,128)S(1)}, f32[32,8,256]{2,1,0:T(8,128)S(1)}, u32[]{:S(2)}, u32[]{:S(2)}) collective-permute-start(f32[32,8,256]{2,1,0:T(8,128)S(1)} %get-tuple-element.58), channel_id=1, source_target_pairs={{0,4},{2,6},{4,0},{6,2},{8,12},{10,14},{12,8},{14,10},{16,20},{18,... | collective-permute-start | bytes 786440 | tf_op jit(solution)/shard_map/ppermute | solution.py:557
  22.0 2.8 %collective-permute-start.8 = (f32[2,8,8,256]{3,2,1,0:T(8,128)S(1)}, f32[2,8,8,256]{3,2,1,0:T(8,128)S(1)}, u32[]{:S(2)}, u32[]{:S(2)}) collective-permute-start(f32[2,8,8,256]{3,2,1,0:T(8,128)S(1)} %get-tuple-element.51), channel_id=1, source_target_pairs={{0,8},{2,10},{4,12},{6,14},{8,0},{10,2},{12,4},{14,6},{16,24},{18,... | collective-permute-start | bytes 393224 | tf_op jit(solution)/shard_map/ppermute | solution.py:557
  24.8 1.9 %collective-permute-start.11 = (f32[4,8,256]{2,1,0:T(8,128)S(1)}, f32[4,8,256]{2,1,0:T(8,128)S(1)}, u32[]{:S(2)}, u32[]{:S(2)}) collective-permute-start(f32[4,8,256]{2,1,0:T(8,128)S(1)} %get-tuple-element.59), channel_id=1, source_target_pairs={{0,12},{2,14},{4,8},{6,10},{8,4},{10,6},{12,0},{14,2},{16,28},{18,... | collective-permute-start | bytes 98312 | tf_op jit(solution)/shard_map/ppermute | solution.py:557
  26.6 2.0 %collective-permute-done.8.x_a = f32[2,8,8,256]{3,2,1,0:T(8,128)S(1)} collective-permute-done((f32[2,8,8,256]{3,2,1,0:T(8,128)S(1)}, f32[2,8,8,256]{3,2,1,0:T(8,128)S(1)}, u32[]{:S(2)}, u32[]{:S(2)}) %collective-permute-start.8) | collective-permute-done | bytes 131104 | tf_op jit(solution)/shard_map/ppermute | solution.py:557
  28.6 2.7 %second_own.1 = (f32[2,48,48,128]{3,2,1,0:T(8,128)S(1)}, f32[2,48,48,128]{3,2,1,0:T(8,128)S(1)}, f32[2,48,48,128]{3,2,1,0:T(8,128)S(1)}, f32[2,48,48,128]{3,2,1,0:T(8,128)S(1)}, f32[2,48,48,128]{3,2,1,0:T(8,128)S(1)}) custom-call(f32[2,48,48,128]{3,2,1,0:T(8,128)S(1)} %get-tuple-element.49.before, f32[2,48,48,128]{3,2,1,0:T(8,128)S(1)} %get-tuple-element.50.local.refs_5_, ...), custom_call_target="tpu_custom_call" | custom-call | tf_op jit(solution)/shard_map/second_own/pallas_call | solution.py:662
  31.4 2.5 %second_rest.1 = (f32[2,48,48,128]{3,2,1,0:T(8,128)S(1)}, f32[2,48,48,128]{3,2,1,0:T(8,128)S(1)}, f32[2,48,48,128]{3,2,1,0:T(8,128)S(1)}, f32[2,48,48,128]{3,2,1...) custom-call(f32[2,48,48,128]{3,2,1,0:T(8,128)S(1)} %get-tuple-elemen, ...), custom_call_target="tpu_custom_call", output_to_operand_aliasing={{0}: (0, {}), {1}: (1, {}), {2}: (2, {}), {3}: (3, {}), {4}... | custom-call | tf_op jit(solution)/shard_map/second_rest/pallas_call | solution.py:671
  33.9 1.6 %collective-permute-start.14 = (f32[16,8,256]{2,1,0:T(8,128)S(1)}, f32[16,8,256]{2,1,0:T(8,128)S(1)}, u32[]{:S(2)}, u32[]{:S(2)}) collective-permute-start(f32[16,8,256]{2,1,0:T(8,128)S(1)} %get-tuple-element.63), channel_id=1, source_target_pairs={{0,1},{1,0},{2,3},{3,2},{4,5},{5,4},{6,7},{7,6},{8,9},{9,8},{10,11... | collective-permute-start | bytes 393224 | tf_op jit(solution)/shard_map/ppermute | solution.py:571
  35.8 4.5 %collective-permute-done.14.refs_2_.refs_4_ = f32[16,8,256]{2,1,0:T(8,128)S(1)} collective-permute-done((f32[16,8,256]{2,1,0:T(8,128)S(1)}, f32[16,8,256]{2,1,0:T(8,128)S(1)}, u32[]{:S(2)}, u32[]{:S(2)}) %collective-permute-start.14) | collective-permute-done | bytes 131104 | tf_op jit(solution)/shard_map/ppermute | solution.py:571
  40.3 1.9 %collective-permute-done.15.refs_3_.refs_5_ = f32[16,8,256]{2,1,0:T(8,128)S(1)} collective-permute-done((f32[16,8,256]{2,1,0:T(8,128)S(1)}, f32[16,8,256]{2,1,0:T(8,128)S(1)}, u32[]{:S(2)}, u32[]{:S(2)}) %collective-permute-start.15) | collective-permute-done | bytes 131104 | tf_op jit(solution)/shard_map/ppermute | solution.py:571
  42.4 1.6 %collective-permute-start.16 = (f32[8,128]{1,0:T(8,128)S(1)}, f32[8,128]{1,0:T(8,128)S(1)}, u32[]{:S(2)}, u32[]{:S(2)}) collective-permute-start(f32[8,128]{1,0:T(8,128)S(1)} %correlation.1), channel_id=1, source_target_pairs={{0,1},{1,0},{2,3},{3,2},{4,5},{5,4},{6,7},{7,6},{8,9},{9,8},{10,11... | collective-permute-start | bytes 12296 | tf_op jit(solution)/shard_map/ppermute | solution.py:590
  44.0 2.1 %collective-permute-done.16 = f32[8,128]{1,0:T(8,128)S(1)} collective-permute-done((f32[8,128]{1,0:T(8,128)S(1)}, f32[8,128]{1,0:T(8,128)S(1)}, u32[]{:S(2)}, u32[]{:S(2)}) %collective-permute-start.16) | collective-permute-done | bytes 4128 | tf_op jit(solution)/shard_map/ppermute | solution.py:590
  46.9 1.1 %collective-permute-start.17 = (f32[8,128]{1,0:T(8,128)S(1)}, f32[8,128]{1,0:T(8,128)S(1)}, u32[]{:S(2)}, u32[]{:S(2)}) collective-permute-start(f32[8,128]{1,0:T(8,128)S(1)} %add.21), channel_id=1, source_target_pairs={{0,2},{2,0},{4,6},{6,4},{1,3},{3,1},{5,7},{7,5},{8,10},{10,8},{12,... | collective-permute-start | bytes 12296 | tf_op jit(solution)/shard_map/ppermute | solution.py:590
  48.0 1.6 %collective-permute-start.23 = (f32[2,16,8,256]{3,2,1,0:T(8,128)S(1)}, f32[2,16,8,256]{3,2,1,0:T(8,128)S(1)}, u32[]{:S(2)}, u32[]{:S(2)}) collective-permute-start(f32[2,16,8,256]{3,2,1,0:T(8,128)S(1)} %late.1), channel_id=1, source_target_pairs={{0,1},{1,0},{2,3},{3,2},{4,5},{5,4},{6,7},{7,6},{8,9},{9,8},{10,11... | collective-permute-start | bytes 786440 | tf_op jit(solution)/shard_map/ppermute | solution.py:571
  49.8 2.6 %collective-permute-start.22 = (f32[8,128]{1,0:T(8,128)S(1)}, f32[8,128]{1,0:T(8,128)S(1)}, u32[]{:S(2)}, u32[]{:S(2)}) collective-permute-start(f32[8,128]{1,0:T(8,128)S(1)} %add_add_fusion.1), channel_id=1, source_target_pairs={{0,24},{8,16},{16,8},{24,0},{1,25},{9,17},{17,9},{25,1},{2,26},{10... | collective-permute-start | bytes 12296 | tf_op jit(solution)/shard_map/ppermute | solution.py:590
  53.1 1.1 %collective-permute-start.20 = (f32[8,128]{1,0:T(8,128)S(1)}, f32[8,128]{1,0:T(8,128)S(1)}, u32[]{:S(2)}, u32[]{:S(2)}) collective-permute-start(f32[8,128]{1,0:T(8,128)S(1)} %add_add_fusion.1), channel_id=1, source_target_pairs={{0,8},{8,0},{16,24},{24,16},{1,9},{9,1},{17,25},{25,17},{2,10},{10... | collective-permute-start | bytes 12296 | tf_op jit(solution)/shard_map/ppermute | solution.py:590
  55.2 1.7 %collective-permute-done.21 = f32[8,128]{1,0:T(8,128)S(1)} collective-permute-done((f32[8,128]{1,0:T(8,128)S(1)}, f32[8,128]{1,0:T(8,128)S(1)}, u32[]{:S(2)}, u32[]{:S(2)}) %collective-permute-start.21) | collective-permute-done | bytes 4128 | tf_op jit(solution)/shard_map/ppermute | solution.py:590
  56.9 1.7 %basis.1 = f32[2,32,8,256]{3,2,1,0:T(8,128)} custom-call(f32[8,128]{1,0:T(8,128)S(1)} %add_add_fusion.refs_0_, s32[4]{0:T(128)S(1)} %copy-done.2, f32[32,8,256]{2,1,0:T(8,128)S(1)} %get-tuple-element.61.refs_0_.keep.refs_2_, f32[32,8,256]{2,1,0:T(8,128)S(1)} %collective-permute-done.13.refs_1_.sibling.refs_3_, ...), custom_call_target="tpu_custom_call" | custom-call | tf_op jit(solution)/shard_map/basis/pallas_call | solution.py:702
  (43 shorter events, 6.1 us)
Async XLA Ops:
  0.0 2.6 %collective-permute-start = (f32[2,32,8,256]{3,2,1,0:T(8,128)}, f32[2,32,8,256]{3,2,1,0:T(8,128)S(1)}, u32[]{:S(2)}, u32[]{:S(2)}) collective-permute-start(f32[2,32,8,256]{3,2,1,0:T(8,128)} %orbitals.1), channel_id=1, source_target_pairs={{0,2},{2,0},{4,6},{6,4},{1,3},{3,1},{5,7},{7,5},{8,10},{10,8},{12,... | collective-permute-start | bytes 1572872 | tf_op jit(solution)/shard_map/ppermute | solution.py:562
  0.5 2.1 %collective-permute-start.1 = (f32[32,8,256]{2,1,0:T(8,128)}, f32[32,8,256]{2,1,0:T(8,128)S(1)}, u32[]{:S(2)}, u32[]{:S(2)}) collective-permute-start(f32[32,8,256]{2,1,0:T(8,128)} %potential.1), channel_id=1, source_target_pairs={{0,2},{2,0},{4,6},{6,4},{1,3},{3,1},{5,7},{7,5},{8,10},{10,8},{12,... | collective-permute-start | bytes 786440 | tf_op jit(solution)/shard_map/ppermute | solution.py:562
  2.7 13.7 %collective-permute-start.4 = (f32[48,8,256]{2,1,0:T(8,128)S(1)}, f32[48,8,256]{2,1,0:T(8,128)S(1)}, u32[]{:S(2)}, u32[]{:S(2)}) collective-permute-start(f32[48,8,256]{2,1,0:T(8,128)S(1)} %get-tuple-element.45), channel_id=1, source_target_pairs={{0,4},{2,6},{4,0},{6,2},{8,12},{10,14},{12,8},{14,10},{16,20},{18,... | collective-permute-start | bytes 1179656 | tf_op jit(solution)/shard_map/ppermute | solution.py:557
  5.8 7.8 %collective-permute-start.2 = (f32[2,14,8,256]{3,2,1,0:T(8,128)S(1)}, f32[2,14,8,256]{3,2,1,0:T(8,128)S(1)}, u32[]{:S(2)}, u32[]{:S(2)}) collective-permute-start(f32[2,14,8,256]{3,2,1,0:T(8,128)S(1)} %get-tuple-element.37), channel_id=1, source_target_pairs={{0,8},{2,10},{4,12},{6,14},{8,0},{10,2},{12,4},{14,6},{16,24},{18,... | collective-permute-start | bytes 688136 | tf_op jit(solution)/shard_map/ppermute | solution.py:557
  7.3 6.3 %collective-permute-start.3 = (f32[2,14,8,256]{3,2,1,0:T(8,128)S(1)}, f32[2,14,8,256]{3,2,1,0:T(8,128)S(1)}, u32[]{:S(2)}, u32[]{:S(2)}) collective-permute-start(f32[2,14,8,256]{3,2,1,0:T(8,128)S(1)} %get-tuple-element.38), channel_id=1, source_target_pairs={{0,2},{2,0},{4,6},{6,4},{8,16},{10,18},{12,20},{14,22},{16,8},{18,... | collective-permute-start | bytes 688136 | tf_op jit(solution)/shard_map/ppermute | solution.py:557
  7.3 9.1 %collective-permute-start.5 = (f32[7,8,256]{2,1,0:T(8,128)S(1)}, f32[7,8,256]{2,1,0:T(8,128)S(1)}, u32[]{:S(2)}, u32[]{:S(2)}) collective-permute-start(f32[7,8,256]{2,1,0:T(8,128)S(1)} %get-tuple-element.46), channel_id=1, source_target_pairs={{0,12},{2,14},{4,8},{6,10},{8,4},{10,6},{12,0},{14,2},{16,28},{18,... | collective-permute-start | bytes 172040 | tf_op jit(solution)/shard_map/ppermute | solution.py:557
  10.4 6.0 %collective-permute-start.6 = (f32[7,8,256]{2,1,0:T(8,128)S(1)}, f32[7,8,256]{2,1,0:T(8,128)S(1)}, u32[]{:S(2)}, u32[]{:S(2)}) collective-permute-start(f32[7,8,256]{2,1,0:T(8,128)S(1)} %get-tuple-element.47), channel_id=1, source_target_pairs={{0,2},{2,0},{4,6},{6,4},{8,20},{10,22},{12,16},{14,18},{16,12},{18... | collective-permute-start | bytes 172040 | tf_op jit(solution)/shard_map/ppermute | solution.py:557
  16.5 1.4 %collective-permute-start.7 = (f32[16,8,256]{2,1,0:T(8,128)S(1)}, f32[16,8,256]{2,1,0:T(8,128)S(1)}, u32[]{:S(2)}, u32[]{:S(2)}) collective-permute-start(f32[16,8,256]{2,1,0:T(8,128)S(1)} %slice.4), channel_id=1, source_target_pairs={{0,2},{2,0},{4,6},{6,4},{1,3},{3,1},{5,7},{7,5},{8,10},{10,8},{12,... | collective-permute-start | bytes 393224 | tf_op jit(solution)/shard_map/ppermute | solution.py:562
  20.3 11.0 %collective-permute-start.10 = (f32[32,8,256]{2,1,0:T(8,128)S(1)}, f32[32,8,256]{2,1,0:T(8,128)S(1)}, u32[]{:S(2)}, u32[]{:S(2)}) collective-permute-start(f32[32,8,256]{2,1,0:T(8,128)S(1)} %get-tuple-element.58), channel_id=1, source_target_pairs={{0,4},{2,6},{4,0},{6,2},{8,12},{10,14},{12,8},{14,10},{16,20},{18,... | collective-permute-start | bytes 786440 | tf_op jit(solution)/shard_map/ppermute | solution.py:557
  22.0 6.7 %collective-permute-start.8 = (f32[2,8,8,256]{3,2,1,0:T(8,128)S(1)}, f32[2,8,8,256]{3,2,1,0:T(8,128)S(1)}, u32[]{:S(2)}, u32[]{:S(2)}) collective-permute-start(f32[2,8,8,256]{3,2,1,0:T(8,128)S(1)} %get-tuple-element.51), channel_id=1, source_target_pairs={{0,8},{2,10},{4,12},{6,14},{8,0},{10,2},{12,4},{14,6},{16,24},{18,... | collective-permute-start | bytes 393224 | tf_op jit(solution)/shard_map/ppermute | solution.py:557
  24.8 3.9 %collective-permute-start.9 = (f32[2,8,8,256]{3,2,1,0:T(8,128)S(1)}, f32[2,8,8,256]{3,2,1,0:T(8,128)S(1)}, u32[]{:S(2)}, u32[]{:S(2)}) collective-permute-start(f32[2,8,8,256]{3,2,1,0:T(8,128)S(1)} %get-tuple-element.52), channel_id=1, source_target_pairs={{0,2},{2,0},{4,6},{6,4},{8,16},{10,18},{12,20},{14,22},{16,8},{18,... | collective-permute-start | bytes 393224 | tf_op jit(solution)/shard_map/ppermute | solution.py:557
  24.8 6.6 %collective-permute-start.11 = (f32[4,8,256]{2,1,0:T(8,128)S(1)}, f32[4,8,256]{2,1,0:T(8,128)S(1)}, u32[]{:S(2)}, u32[]{:S(2)}) collective-permute-start(f32[4,8,256]{2,1,0:T(8,128)S(1)} %get-tuple-element.59), channel_id=1, source_target_pairs={{0,12},{2,14},{4,8},{6,10},{8,4},{10,6},{12,0},{14,2},{16,28},{18,... | collective-permute-start | bytes 98312 | tf_op jit(solution)/shard_map/ppermute | solution.py:557
  26.6 4.7 %collective-permute-start.12 = (f32[4,8,256]{2,1,0:T(8,128)S(1)}, f32[4,8,256]{2,1,0:T(8,128)S(1)}, u32[]{:S(2)}, u32[]{:S(2)}) collective-permute-start(f32[4,8,256]{2,1,0:T(8,128)S(1)} %get-tuple-element.60), channel_id=1, source_target_pairs={{0,2},{2,0},{4,6},{6,4},{8,20},{10,22},{12,16},{14,18},{16,12},{18... | collective-permute-start | bytes 98312 | tf_op jit(solution)/shard_map/ppermute | solution.py:557
  33.9 8.3 %collective-permute-start.13 = (f32[32,8,256]{2,1,0:T(8,128)S(1)}, f32[32,8,256]{2,1,0:T(8,128)S(1)}, u32[]{:S(2)}, u32[]{:S(2)}) collective-permute-start(f32[32,8,256]{2,1,0:T(8,128)S(1)} %get-tuple-element.62), channel_id=1, source_target_pairs={{0,2},{2,0},{4,6},{6,4},{1,3},{3,1},{5,7},{7,5},{8,10},{10,8},{12,... | collective-permute-start | bytes 786440 | tf_op jit(solution)/shard_map/ppermute | solution.py:562
  33.9 6.4 %collective-permute-start.14 = (f32[16,8,256]{2,1,0:T(8,128)S(1)}, f32[16,8,256]{2,1,0:T(8,128)S(1)}, u32[]{:S(2)}, u32[]{:S(2)}) collective-permute-start(f32[16,8,256]{2,1,0:T(8,128)S(1)} %get-tuple-element.63), channel_id=1, source_target_pairs={{0,1},{1,0},{2,3},{3,2},{4,5},{5,4},{6,7},{7,6},{8,9},{9,8},{10,11... | collective-permute-start | bytes 393224 | tf_op jit(solution)/shard_map/ppermute | solution.py:571
  35.5 6.7 %collective-permute-start.15 = (f32[16,8,256]{2,1,0:T(8,128)S(1)}, f32[16,8,256]{2,1,0:T(8,128)S(1)}, u32[]{:S(2)}, u32[]{:S(2)}) collective-permute-start(f32[16,8,256]{2,1,0:T(8,128)S(1)} %get-tuple-element.64), channel_id=1, source_target_pairs={{0,3},{1,2},{2,1},{3,0},{4,7},{5,6},{6,5},{7,4},{8,11},{9,10},{10,... | collective-permute-start | bytes 393224 | tf_op jit(solution)/shard_map/ppermute | solution.py:571
  42.4 3.7 %collective-permute-start.16 = (f32[8,128]{1,0:T(8,128)S(1)}, f32[8,128]{1,0:T(8,128)S(1)}, u32[]{:S(2)}, u32[]{:S(2)}) collective-permute-start(f32[8,128]{1,0:T(8,128)S(1)} %correlation.1), channel_id=1, source_target_pairs={{0,1},{1,0},{2,3},{3,2},{4,5},{5,4},{6,7},{7,6},{8,9},{9,8},{10,11... | collective-permute-start | bytes 12296 | tf_op jit(solution)/shard_map/ppermute | solution.py:590
  46.1 3.4 %collective-permute-start.19 = (f32[8,128]{1,0:T(8,128)S(1)}, f32[8,128]{1,0:T(8,128)S(1)}, u32[]{:S(2)}, u32[]{:S(2)}) collective-permute-start(f32[8,128]{1,0:T(8,128)S(1)} %add.21), channel_id=1, source_target_pairs={{0,6},{2,4},{4,2},{6,0},{1,7},{3,5},{5,3},{7,1},{8,14},{10,12},{12... | collective-permute-start | bytes 12296 | tf_op jit(solution)/shard_map/ppermute | solution.py:590
  46.1 3.6 %collective-permute-start.18 = (f32[8,128]{1,0:T(8,128)S(1)}, f32[8,128]{1,0:T(8,128)S(1)}, u32[]{:S(2)}, u32[]{:S(2)}) collective-permute-start(f32[8,128]{1,0:T(8,128)S(1)} %add.21), channel_id=1, source_target_pairs={{0,4},{2,6},{4,0},{6,2},{1,5},{3,7},{5,1},{7,3},{8,12},{10,14},{12... | collective-permute-start | bytes 12296 | tf_op jit(solution)/shard_map/ppermute | solution.py:590
  46.9 2.9 %collective-permute-start.17 = (f32[8,128]{1,0:T(8,128)S(1)}, f32[8,128]{1,0:T(8,128)S(1)}, u32[]{:S(2)}, u32[]{:S(2)}) collective-permute-start(f32[8,128]{1,0:T(8,128)S(1)} %add.21), channel_id=1, source_target_pairs={{0,2},{2,0},{4,6},{6,4},{1,3},{3,1},{5,7},{7,5},{8,10},{10,8},{12,... | collective-permute-start | bytes 12296 | tf_op jit(solution)/shard_map/ppermute | solution.py:590
  48.0 8.9 %collective-permute-start.23 = (f32[2,16,8,256]{3,2,1,0:T(8,128)S(1)}, f32[2,16,8,256]{3,2,1,0:T(8,128)S(1)}, u32[]{:S(2)}, u32[]{:S(2)}) collective-permute-start(f32[2,16,8,256]{3,2,1,0:T(8,128)S(1)} %late.1), channel_id=1, source_target_pairs={{0,1},{1,0},{2,3},{3,2},{4,5},{5,4},{6,7},{7,6},{8,9},{9,8},{10,11... | collective-permute-start | bytes 786440 | tf_op jit(solution)/shard_map/ppermute | solution.py:571
  49.8 5.5 %collective-permute-start.22 = (f32[8,128]{1,0:T(8,128)S(1)}, f32[8,128]{1,0:T(8,128)S(1)}, u32[]{:S(2)}, u32[]{:S(2)}) collective-permute-start(f32[8,128]{1,0:T(8,128)S(1)} %add_add_fusion.1), channel_id=1, source_target_pairs={{0,24},{8,16},{16,8},{24,0},{1,25},{9,17},{17,9},{25,1},{2,26},{10... | collective-permute-start | bytes 12296 | tf_op jit(solution)/shard_map/ppermute | solution.py:590
  52.4 4.5 %collective-permute-start.21 = (f32[8,128]{1,0:T(8,128)S(1)}, f32[8,128]{1,0:T(8,128)S(1)}, u32[]{:S(2)}, u32[]{:S(2)}) collective-permute-start(f32[8,128]{1,0:T(8,128)S(1)} %add_add_fusion.1), channel_id=1, source_target_pairs={{0,16},{8,24},{16,0},{24,8},{1,17},{9,25},{17,1},{25,9},{2,18},{10... | collective-permute-start | bytes 12296 | tf_op jit(solution)/shard_map/ppermute | solution.py:590
  53.1 3.8 %collective-permute-start.20 = (f32[8,128]{1,0:T(8,128)S(1)}, f32[8,128]{1,0:T(8,128)S(1)}, u32[]{:S(2)}, u32[]{:S(2)}) collective-permute-start(f32[8,128]{1,0:T(8,128)S(1)} %add_add_fusion.1), channel_id=1, source_target_pairs={{0,8},{8,0},{16,24},{24,16},{1,9},{9,1},{17,25},{25,17},{2,10},{10... | collective-permute-start | bytes 12296 | tf_op jit(solution)/shard_map/ppermute | solution.py:590
  (3 other events, 27.6 us)

commit v9 on v8

--- a/solution.py
+++ b/solution.py
@@ -14,7 +14,7 @@
 PLANES = 4
 OWN_ROWS = slice(PAD + 8, PAD + 24)
 HALO_ROWS = (slice(PAD, PAD + 8), slice(PAD + 24, PAD + 32))
-TOGETHER = {8: (16, 8, 1), 16: (12, 6, 1), 32: (8, 2, 1)}
+TOGETHER = {8: (32, 0, 1), 16: (8, 4, 2), 32: (8, 2, 1)}
 NEAR = -(2.0 / 3.0) / 4.25
 FAR = (1.0 / 24.0) / 4.25
 VMEM = pl.BlockSpec(memory_space=pltpu.VMEM)
@@ -288,9 +288,8 @@
 def pack_kernel(orbitals, received, potential, received_potential, *outs):
     core, chip, along_x = place()
     width = potential.shape[0]
-    y_out = outs[: len(y_phases())]
-    x_out = outs[len(y_phases()) : len(y_phases()) + 2]
-    d_out = outs[len(y_phases()) + 2 :]
+    p_out, outs = outs[: len(y_phases())], outs[len(y_phases()) :]
+    y_out, x_out, d_out = halos_of(outs)
     tiles = (orbitals.at[core], received.at[core])
     local = (potential, received_potential)
     for x_phase in range(2):
@@ -304,9 +303,9 @@
 
             @pl.when(chosen)
             def _(t=t, phase=phase):
-                y_out[phase][:width] = tiles[t][...]
+                y_out[phase][...] = tiles[t][...]
                 half = width // 2
-                y_out[phase][width:] = local[t][pl.ds(core * half, half)]
+                p_out[phase][...] = local[t][pl.ds(core * half, half)]
                 up = upward(chip, phase)
                 for x_phase in range(2):
                     right = upward(along_x, x_phase)
@@ -342,18 +341,19 @@
 
 def first_rest_kernel(*refs):
     count = len(y_phases())
-    passed, y_halos = refs[6 : 6 + count], refs[6 + count : 6 + 2 * count]
-    corners, outs = refs[6 + 2 * count : 6 + 4 * count], refs[6 + 4 * count :]
+    came, passed = refs[6 : 6 + count], refs[6 + count : 6 + 2 * count]
+    y_halos, corners = refs[6 + 2 * count : 6 + 3 * count], refs[6 + 3 * count : 6 + 5 * count]
+    outs = refs[6 + 5 * count :]
     levels, local = outs[: STEPS + 1], outs[STEPS + 1]
     payloads = outs[STEPS + 2 :]
     core, chip, along_x = place()
     width, depth = local.shape[1] - 2 * HALO, 2 * LANES
-    fill_y(levels[0], [y.at[:width] for y in y_halos], [c.at[: HALO // 2] for c in corners], HALO)
+    fill_y(levels[0], y_halos, [c.at[: HALO // 2] for c in corners], HALO)
     fill_y(local, None, [c.at[HALO // 2 :] for c in corners], HALO - 2, diagonal)
     half = width // 2
     for phase in y_phases():
         rows = rows_of(halo_slot(upward(chip, phase)))
-        put(local, HALO + core * half, rows, y_halos[phase].at[width:], diagonal)
+        put(local, HALO + core * half, rows, came[phase], diagonal)
         put(local, HALO + (1 - core) * half, rows, passed[phase], diagonal)
 
     second_part(levels, local, depth)
@@ -619,23 +619,25 @@
         name="load",
     )(orbitals, potential)
 
-    def payloads(in_y, in_x, in_corner):
+    def payloads(in_x, in_corner):
         return (
-            [struct(in_y, height, depth)] * count
+            [struct(*tile)] * count
             + [struct(2, in_x, height, depth)] * 2
             + [struct(in_corner, height, depth)] * (2 * count)
         )
 
-    packed = pl.pallas_call(
+    *packed, = pl.pallas_call(
         pack_kernel,
-        out_shape=payloads(width + width // 2, 2 * HALO - 2, HALO - 1),
+        out_shape=[struct(width // 2, height, depth)] * count + payloads(2 * HALO - 2, HALO - 1),
         in_specs=[VMEM] * 4,
-        out_specs=[VMEM] * (2 + 3 * count),
+        out_specs=[VMEM] * (2 + 4 * count),
         compiler_params=PARAMS,
         name="pack",
     )(orbitals, received, potential, received_potential)
-    halos = exchange(packed)
-    y_halos, x_halos, corners = halos_of(halos)
+    came = [meet(packed[phase], y_phase=phase) for phase in y_phases()]
+    packed[-1], came = lax.optimization_barrier((packed[-1], came))
+    y_halos, x_halos, corners = halos_of(exchange(packed[count:]))
+    passed = [swap(value) for value in came]
     *levels, local = pl.pallas_call(
         first_own_kernel,
         out_shape=[window] * (windows + 1),
@@ -644,19 +646,15 @@
         compiler_params=PARAMS,
         name="first_own",
     )(orbitals, received, potential, received_potential, *x_halos)
-    passed = []
-    for phase in y_phases():
-        half, *_ = lax.optimization_barrier((y_halos[phase][width:], *y_halos, *corners, *levels))
-        passed.append(swap(half))
     outs = pl.pallas_call(
         first_rest_kernel,
-        out_shape=[window] * (windows + 1) + payloads(width, HALO, HALO // 2),
-        in_specs=[VMEM] * (windows + 1 + 4 * count),
+        out_shape=[window] * (windows + 1) + payloads(HALO, HALO // 2),
+        in_specs=[VMEM] * (windows + 1 + 5 * count),
         out_specs=[VMEM] * (windows + 3 + 3 * count),
         input_output_aliases={k: k for k in range(windows + 1)},
         compiler_params=PARAMS,
         name="first_rest",
-    )(*levels, local, *passed, *y_halos, *corners)
+    )(*levels, local, *came, *passed, *y_halos, *corners)
     levels, local, packed = outs[:windows], outs[windows], outs[windows + 1 :]
     y_halos, x_halos, corners = halos_of(exchange(packed))
     levels = pl.pallas_call(

time: 58.9 us -> 57.1 us (0.969)
  starting transfers between devices: 26 us -> 24.6 us
  Pallas kernels: 12.5 us -> 11.7 us
  waiting for transfers between devices: 17.9 us -> 18.5 us
    ppermute x10 -> x11, starting transfers between devices: 14 us -> 12.6 us  [meet(): return lax.ppermute(value, ('gx', 'gy'), pairs)]
    ppermute x4, waiting for transfers between devices: 1.34 us -> 0.01 us  [swap(): return lax.ppermute(value, 'gy', [(y, y ^ 1) for y in range(count)])]
    ppermute x10 -> x11, waiting for transfers between devices: 5.18 us -> 6.45 us  [meet(): return lax.ppermute(value, ('gx', 'gy'), pairs)]
  transfers between devices with their start and end apart: 24 -> 25, of which waited for: 9 -> 10; matrix products, arithmetic and copies ran while one was open for 0% -> 0% of each run, Pallas kernels for 10% -> 9%
where the time goes in v9:
time: 57.1 us; the launch traced here: 56.9 us
  starting transfers between devices  24.6 us (43%)
  waiting for transfers between devices  18.5 us (32%)
  Pallas kernels  11.7 us (20%)
  local copies, waits for them, and re-layouts  2 us (4%)
    ppermute x11, starting transfers between devices, meet(): return lax.ppermute(value, ('gx', 'gy'), pairs)  12.6 us
    ppermute x7, starting transfers between devices, of(): return lax.ppermute(value, axis, [(i, i ^ step) for i in range(count)])  7.96 us
    ppermute x11, waiting for transfers between devices, meet(): return lax.ppermute(value, ('gx', 'gy'), pairs)  6.45 us
    ppermute x3, waiting for transfers between devices, to_band(): return lax.ppermute(value, ('gy', 'band'), pairs)  6.41 us
    ppermute x7, waiting for transfers between devices, of(): return lax.ppermute(value, axis, [(i, i ^ step) for i in range(count)])  5.6 us
    ppermute x3, starting transfers between devices, to_band(): return lax.ppermute(value, ('gy', 'band'), pairs)  3.42 us
    pallas_call x1, Pallas kernels, per_device(): pl.pallas_call(first_own_kernel, out_shape=[window] * (windows + 1), in_s...  2.51 us
    pallas_call x1, Pallas kernels, per_device(): pl.pallas_call(second_own_kernel, out_shape=[window] * windows, in_specs=...  2.41 us
  transfers between devices with their start and end apart: 25, of which 10 were waited for; matrix products, arithmetic and copies ran while one was open for 0% of the time, Pallas kernels for 9%

profile of v9, /device:TPU:0, one launch (start us, length us, event | category | flops | bytes accessed | tf_op | source)
XLA Modules:
  0.0 56.9 jit_solution(7773153340137045770)
XLA Ops:
  0.5 1.0 %copy-done = f32[2,32,8,256]{3,2,1,0:T(8,128)S(1)} copy-done((f32[2,32,8,256]{3,2,1,0:T(8,128)S(1)}, f32[2,32,8,256]{3,2,1,0:T(8,128)}, u32[]{:S(2)}) %copy-start) | copy-done | bytes 524312
  1.6 0.9 %copy-done.1 = f32[32,8,256]{2,1,0:T(8,128)S(1)} copy-done((f32[32,8,256]{2,1,0:T(8,128)S(1)}, f32[32,8,256]{2,1,0:T(8,128)}, u32[]{:S(2)}) %copy-start.1) | copy-done | bytes 262168
  2.7 3.1 %collective-permute-start.2 = (f32[2,14,8,256]{3,2,1,0:T(8,128)S(1)}, f32[2,14,8,256]{3,2,1,0:T(8,128)S(1)}, u32[]{:S(2)}, u32[]{:S(2)}) collective-permute-start(f32[2,14,8,256]{3,2,1,0:T(8,128)S(1)} %get-tuple-element.39), channel_id=1, source_target_pairs={{0,8},{2,10},{4,12},{6,14},{8,0},{10,2},{12,4},{14,6},{16,24},{18,... | collective-permute-start | bytes 688136 | tf_op jit(solution)/shard_map/ppermute | solution.py:557
  5.8 1.5 %collective-permute-start.4 = (f32[16,8,256]{2,1,0:T(8,128)S(1)}, f32[16,8,256]{2,1,0:T(8,128)S(1)}, u32[]{:S(2)}, u32[]{:S(2)}) collective-permute-start(f32[16,8,256]{2,1,0:T(8,128)S(1)} %get-tuple-element.48), channel_id=1, source_target_pairs={{0,4},{2,6},{4,0},{6,2},{8,12},{10,14},{12,8},{14,10},{16,20},{18,... | collective-permute-start | bytes 393224 | tf_op jit(solution)/shard_map/ppermute | solution.py:557
  7.8 4.4 %collective-permute-done.4.refs_6_ = f32[16,8,256]{2,1,0:T(8,128)S(1)} collective-permute-done((f32[16,8,256]{2,1,0:T(8,128)S(1)}, f32[16,8,256]{2,1,0:T(8,128)S(1)}, u32[]{:S(2)}, u32[]{:S(2)}) %collective-permute-start.4) | collective-permute-done | bytes 131104 | tf_op jit(solution)/shard_map/ppermute | solution.py:557
  12.2 1.4 %collective-permute-start.7 = (f32[7,8,256]{2,1,0:T(8,128)S(1)}, f32[7,8,256]{2,1,0:T(8,128)S(1)}, u32[]{:S(2)}, u32[]{:S(2)}) collective-permute-start(f32[7,8,256]{2,1,0:T(8,128)S(1)} %get-tuple-element.51), channel_id=1, source_target_pairs={{0,12},{2,14},{4,8},{6,10},{8,4},{10,6},{12,0},{14,2},{16,28},{18,... | collective-permute-start | bytes 172040 | tf_op jit(solution)/shard_map/ppermute | solution.py:557
  13.9 2.5 %first_own.1 = (f32[2,48,48,128]{3,2,1,0:T(8,128)S(1)}, f32[2,48,48,128]{3,2,1,0:T(8,128)S(1)}, f32[2,48,48,128]{3,2,1,0:T(8,128)S(1)}, f32[2,48,48,128]{3,2,1,0...) custom-call(f32[2,32,8,256]{3,2,1,0:T(8,128)S(1)} %get-tuple-element.37.orbitals.refs_6_, ...), custom_call_target="tpu_custom_call" | custom-call | tf_op jit(solution)/shard_map/first_own/pallas_call | solution.py:641
  16.4 1.2 %collective-permute-done.7.refs_9_ = f32[7,8,256]{2,1,0:T(8,128)S(1)} collective-permute-done((f32[7,8,256]{2,1,0:T(8,128)S(1)}, f32[7,8,256]{2,1,0:T(8,128)S(1)}, u32[]{:S(2)}, u32[]{:S(2)}) %collective-permute-start.7) | collective-permute-done | bytes 57376 | tf_op jit(solution)/shard_map/ppermute | solution.py:557
  17.8 2.2 %first_rest.1 = (f32[2,48,48,128]{3,2,1,0:T(8,128)S(1)}, f32[2,48,48,128]{3,2,1,0:T(8,128)S(1)}, f32[2,48,48,128]{3,2,1,0:T(8,128)S(1)}, f32[2,48,48,128]{3,2,1,...) custom-call(f32[2,48,48,128]{3,2,1,0:T(8,128)S(1)} %get-tuple-elemen, ...), custom_call_target="tpu_custom_call", output_to_operand_aliasing={{0}: (0, {}), {1}: (1, {}), {2}: (2, {}), {3}: (3, {}), {4}... | custom-call | tf_op jit(solution)/shard_map/first_rest/pallas_call | solution.py:649
  20.0 1.6 %collective-permute-start.11 = (f32[32,8,256]{2,1,0:T(8,128)S(1)}, f32[32,8,256]{2,1,0:T(8,128)S(1)}, u32[]{:S(2)}, u32[]{:S(2)}) collective-permute-start(f32[32,8,256]{2,1,0:T(8,128)S(1)} %get-tuple-element.62), channel_id=1, source_target_pairs={{0,4},{2,6},{4,0},{6,2},{8,12},{10,14},{12,8},{14,10},{16,20},{18,... | collective-permute-start | bytes 786440 | tf_op jit(solution)/shard_map/ppermute | solution.py:557
  21.6 1.6 %collective-permute-start.9 = (f32[2,8,8,256]{3,2,1,0:T(8,128)S(1)}, f32[2,8,8,256]{3,2,1,0:T(8,128)S(1)}, u32[]{:S(2)}, u32[]{:S(2)}) collective-permute-start(f32[2,8,8,256]{3,2,1,0:T(8,128)S(1)} %get-tuple-element.55), channel_id=1, source_target_pairs={{0,8},{2,10},{4,12},{6,14},{8,0},{10,2},{12,4},{14,6},{16,24},{18,... | collective-permute-start | bytes 393224 | tf_op jit(solution)/shard_map/ppermute | solution.py:557
  23.2 2.7 %collective-permute-start.12 = (f32[4,8,256]{2,1,0:T(8,128)S(1)}, f32[4,8,256]{2,1,0:T(8,128)S(1)}, u32[]{:S(2)}, u32[]{:S(2)}) collective-permute-start(f32[4,8,256]{2,1,0:T(8,128)S(1)} %get-tuple-element.63), channel_id=1, source_target_pairs={{0,12},{2,14},{4,8},{6,10},{8,4},{10,6},{12,0},{14,2},{16,28},{18,... | collective-permute-start | bytes 98312 | tf_op jit(solution)/shard_map/ppermute | solution.py:557
  26.6 2.4 %second_own.1 = (f32[2,48,48,128]{3,2,1,0:T(8,128)S(1)}, f32[2,48,48,128]{3,2,1,0:T(8,128)S(1)}, f32[2,48,48,128]{3,2,1,0:T(8,128)S(1)}, f32[2,48,48,128]{3,2,1,0:T(8,128)S(1)}, f32[2,48,48,128]{3,2,1,0:T(8,128)S(1)}) custom-call(f32[2,48,48,128]{3,2,1,0:T(8,128)S(1)} %get-tuple-element.53.before, f32[2,48,48,128]{3,2,1,0:T(8,128)S(1)} %get-tuple-element.54.local.refs_5_, ...), custom_call_target="tpu_custom_call" | custom-call | tf_op jit(solution)/shard_map/second_own/pallas_call | solution.py:660
  29.0 2.4 %second_rest.1 = (f32[2,48,48,128]{3,2,1,0:T(8,128)S(1)}, f32[2,48,48,128]{3,2,1,0:T(8,128)S(1)}, f32[2,48,48,128]{3,2,1,0:T(8,128)S(1)}, f32[2,48,48,128]{3,2,1...) custom-call(f32[2,48,48,128]{3,2,1,0:T(8,128)S(1)} %get-tuple-elemen, ...), custom_call_target="tpu_custom_call", output_to_operand_aliasing={{0}: (0, {}), {1}: (1, {}), {2}: (2, {}), {3}: (3, {}), {4}... | custom-call | tf_op jit(solution)/shard_map/second_rest/pallas_call | solution.py:669
  31.5 1.6 %collective-permute-start.15 = (f32[16,8,256]{2,1,0:T(8,128)S(1)}, f32[16,8,256]{2,1,0:T(8,128)S(1)}, u32[]{:S(2)}, u32[]{:S(2)}) collective-permute-start(f32[16,8,256]{2,1,0:T(8,128)S(1)} %get-tuple-element.67), channel_id=1, source_target_pairs={{0,1},{1,0},{2,3},{3,2},{4,5},{5,4},{6,7},{7,6},{8,9},{9,8},{10,11... | collective-permute-start | bytes 393224 | tf_op jit(solution)/shard_map/ppermute | solution.py:571
  33.4 4.5 %collective-permute-done.15.refs_2_.refs_4_ = f32[16,8,256]{2,1,0:T(8,128)S(1)} collective-permute-done((f32[16,8,256]{2,1,0:T(8,128)S(1)}, f32[16,8,256]{2,1,0:T(8,128)S(1)}, u32[]{:S(2)}, u32[]{:S(2)}) %collective-permute-start.15) | collective-permute-done | bytes 131104 | tf_op jit(solution)/shard_map/ppermute | solution.py:571
  37.9 1.9 %collective-permute-done.16.refs_3_.refs_5_ = f32[16,8,256]{2,1,0:T(8,128)S(1)} collective-permute-done((f32[16,8,256]{2,1,0:T(8,128)S(1)}, f32[16,8,256]{2,1,0:T(8,128)S(1)}, u32[]{:S(2)}, u32[]{:S(2)}) %collective-permute-start.16) | collective-permute-done | bytes 131104 | tf_op jit(solution)/shard_map/ppermute | solution.py:571
  40.0 1.6 %collective-permute-start.17 = (f32[8,128]{1,0:T(8,128)S(1)}, f32[8,128]{1,0:T(8,128)S(1)}, u32[]{:S(2)}, u32[]{:S(2)}) collective-permute-start(f32[8,128]{1,0:T(8,128)S(1)} %correlation.1), channel_id=1, source_target_pairs={{0,1},{1,0},{2,3},{3,2},{4,5},{5,4},{6,7},{7,6},{8,9},{9,8},{10,11... | collective-permute-start | bytes 12296 | tf_op jit(solution)/shard_map/ppermute | solution.py:590
  41.6 2.1 %collective-permute-done.17 = f32[8,128]{1,0:T(8,128)S(1)} collective-permute-done((f32[8,128]{1,0:T(8,128)S(1)}, f32[8,128]{1,0:T(8,128)S(1)}, u32[]{:S(2)}, u32[]{:S(2)}) %collective-permute-start.17) | collective-permute-done | bytes 4128 | tf_op jit(solution)/shard_map/ppermute | solution.py:590
  44.5 1.1 %collective-permute-start.18 = (f32[8,128]{1,0:T(8,128)S(1)}, f32[8,128]{1,0:T(8,128)S(1)}, u32[]{:S(2)}, u32[]{:S(2)}) collective-permute-start(f32[8,128]{1,0:T(8,128)S(1)} %add.21), channel_id=1, source_target_pairs={{0,2},{2,0},{4,6},{6,4},{1,3},{3,1},{5,7},{7,5},{8,10},{10,8},{12,... | collective-permute-start | bytes 12296 | tf_op jit(solution)/shard_map/ppermute | solution.py:590
  45.6 1.6 %collective-permute-start.24 = (f32[2,16,8,256]{3,2,1,0:T(8,128)S(1)}, f32[2,16,8,256]{3,2,1,0:T(8,128)S(1)}, u32[]{:S(2)}, u32[]{:S(2)}) collective-permute-start(f32[2,16,8,256]{3,2,1,0:T(8,128)S(1)} %late.1), channel_id=1, source_target_pairs={{0,1},{1,0},{2,3},{3,2},{4,5},{5,4},{6,7},{7,6},{8,9},{9,8},{10,11... | collective-permute-start | bytes 786440 | tf_op jit(solution)/shard_map/ppermute | solution.py:571
  47.4 3.3 %collective-permute-start.23 = (f32[8,128]{1,0:T(8,128)S(1)}, f32[8,128]{1,0:T(8,128)S(1)}, u32[]{:S(2)}, u32[]{:S(2)}) collective-permute-start(f32[8,128]{1,0:T(8,128)S(1)} %add_add_fusion.1), channel_id=1, source_target_pairs={{0,24},{8,16},{16,8},{24,0},{1,25},{9,17},{17,9},{25,1},{2,26},{10... | collective-permute-start | bytes 12296 | tf_op jit(solution)/shard_map/ppermute | solution.py:590
  52.8 2.3 %collective-permute-done.22 = f32[8,128]{1,0:T(8,128)S(1)} collective-permute-done((f32[8,128]{1,0:T(8,128)S(1)}, f32[8,128]{1,0:T(8,128)S(1)}, u32[]{:S(2)}, u32[]{:S(2)}) %collective-permute-start.22) | collective-permute-done | bytes 4128 | tf_op jit(solution)/shard_map/ppermute | solution.py:590
  55.2 1.7 %basis.1 = f32[2,32,8,256]{3,2,1,0:T(8,128)} custom-call(f32[8,128]{1,0:T(8,128)S(1)} %add_add_fusion.refs_0_, s32[4]{0:T(128)S(1)} %copy-done.2, f32[32,8,256]{2,1,0:T(8,128)S(1)} %get-tuple-element.65.refs_0_.keep.refs_2_, f32[32,8,256]{2,1,0:T(8,128)S(1)} %collective-permute-done.14.refs_1_.sibling.refs_3_, ...), custom_call_target="tpu_custom_call" | custom-call | tf_op jit(solution)/shard_map/basis/pallas_call | solution.py:700
  (44 shorter events, 6.1 us)
Async XLA Ops:
  0.0 2.6 %collective-permute-start = (f32[2,32,8,256]{3,2,1,0:T(8,128)}, f32[2,32,8,256]{3,2,1,0:T(8,128)S(1)}, u32[]{:S(2)}, u32[]{:S(2)}) collective-permute-start(f32[2,32,8,256]{3,2,1,0:T(8,128)} %orbitals.1), channel_id=1, source_target_pairs={{0,2},{2,0},{4,6},{6,4},{1,3},{3,1},{5,7},{7,5},{8,10},{10,8},{12,... | collective-permute-start | bytes 1572872 | tf_op jit(solution)/shard_map/ppermute | solution.py:562
  2.7 10.9 %collective-permute-start.2 = (f32[2,14,8,256]{3,2,1,0:T(8,128)S(1)}, f32[2,14,8,256]{3,2,1,0:T(8,128)S(1)}, u32[]{:S(2)}, u32[]{:S(2)}) collective-permute-start(f32[2,14,8,256]{3,2,1,0:T(8,128)S(1)} %get-tuple-element.39), channel_id=1, source_target_pairs={{0,8},{2,10},{4,12},{6,14},{8,0},{10,2},{12,4},{14,6},{16,24},{18,... | collective-permute-start | bytes 688136 | tf_op jit(solution)/shard_map/ppermute | solution.py:557
  5.8 6.4 %collective-permute-start.4 = (f32[16,8,256]{2,1,0:T(8,128)S(1)}, f32[16,8,256]{2,1,0:T(8,128)S(1)}, u32[]{:S(2)}, u32[]{:S(2)}) collective-permute-start(f32[16,8,256]{2,1,0:T(8,128)S(1)} %get-tuple-element.48), channel_id=1, source_target_pairs={{0,4},{2,6},{4,0},{6,2},{8,12},{10,14},{12,8},{14,10},{16,20},{18,... | collective-permute-start | bytes 393224 | tf_op jit(solution)/shard_map/ppermute | solution.py:557
  7.3 10.5 %collective-permute-start.6 = (f32[32,8,256]{2,1,0:T(8,128)S(1)}, f32[32,8,256]{2,1,0:T(8,128)S(1)}, u32[]{:S(2)}, u32[]{:S(2)}) collective-permute-start(f32[32,8,256]{2,1,0:T(8,128)S(1)} %get-tuple-element.50), channel_id=1, source_target_pairs={{0,4},{2,6},{4,0},{6,2},{8,12},{10,14},{12,8},{14,10},{16,20},{18,... | collective-permute-start | bytes 786440 | tf_op jit(solution)/shard_map/ppermute | solution.py:557
  7.8 6.0 %collective-permute-start.3 = (f32[2,14,8,256]{3,2,1,0:T(8,128)S(1)}, f32[2,14,8,256]{3,2,1,0:T(8,128)S(1)}, u32[]{:S(2)}, u32[]{:S(2)}) collective-permute-start(f32[2,14,8,256]{3,2,1,0:T(8,128)S(1)} %get-tuple-element.40), channel_id=1, source_target_pairs={{0,2},{2,0},{4,6},{6,4},{8,16},{10,18},{12,20},{14,22},{16,8},{18,... | collective-permute-start | bytes 688136 | tf_op jit(solution)/shard_map/ppermute | solution.py:557
  12.2 5.6 %collective-permute-start.5 = (f32[16,8,256]{2,1,0:T(8,128)S(1)}, f32[16,8,256]{2,1,0:T(8,128)S(1)}, u32[]{:S(2)}, u32[]{:S(2)}) collective-permute-start(f32[16,8,256]{2,1,0:T(8,128)S(1)} %collective-permute-done.4.refs_6_), channel_id=1, source_target_pairs={{0,2},{2,0},{4,6},{6,4},{1,3},{3,1},{5,7},{7,5},{8,10},{10,8},{12,... | collective-permute-start | bytes 393224 | tf_op jit(solution)/shard_map/ppermute | solution.py:562
  12.2 5.3 %collective-permute-start.7 = (f32[7,8,256]{2,1,0:T(8,128)S(1)}, f32[7,8,256]{2,1,0:T(8,128)S(1)}, u32[]{:S(2)}, u32[]{:S(2)}) collective-permute-start(f32[7,8,256]{2,1,0:T(8,128)S(1)} %get-tuple-element.51), channel_id=1, source_target_pairs={{0,12},{2,14},{4,8},{6,10},{8,4},{10,6},{12,0},{14,2},{16,28},{18,... | collective-permute-start | bytes 172040 | tf_op jit(solution)/shard_map/ppermute | solution.py:557
  13.6 3.9 %collective-permute-start.8 = (f32[7,8,256]{2,1,0:T(8,128)S(1)}, f32[7,8,256]{2,1,0:T(8,128)S(1)}, u32[]{:S(2)}, u32[]{:S(2)}) collective-permute-start(f32[7,8,256]{2,1,0:T(8,128)S(1)} %get-tuple-element.52), channel_id=1, source_target_pairs={{0,2},{2,0},{4,6},{6,4},{8,20},{10,22},{12,16},{14,18},{16,12},{18... | collective-permute-start | bytes 172040 | tf_op jit(solution)/shard_map/ppermute | solution.py:557
  20.0 9.0 %collective-permute-start.11 = (f32[32,8,256]{2,1,0:T(8,128)S(1)}, f32[32,8,256]{2,1,0:T(8,128)S(1)}, u32[]{:S(2)}, u32[]{:S(2)}) collective-permute-start(f32[32,8,256]{2,1,0:T(8,128)S(1)} %get-tuple-element.62), channel_id=1, source_target_pairs={{0,4},{2,6},{4,0},{6,2},{8,12},{10,14},{12,8},{14,10},{16,20},{18,... | collective-permute-start | bytes 786440 | tf_op jit(solution)/shard_map/ppermute | solution.py:557
  21.6 5.0 %collective-permute-start.9 = (f32[2,8,8,256]{3,2,1,0:T(8,128)S(1)}, f32[2,8,8,256]{3,2,1,0:T(8,128)S(1)}, u32[]{:S(2)}, u32[]{:S(2)}) collective-permute-start(f32[2,8,8,256]{3,2,1,0:T(8,128)S(1)} %get-tuple-element.55), channel_id=1, source_target_pairs={{0,8},{2,10},{4,12},{6,14},{8,0},{10,2},{12,4},{14,6},{16,24},{18,... | collective-permute-start | bytes 393224 | tf_op jit(solution)/shard_map/ppermute | solution.py:557
  23.2 3.3 %collective-permute-start.10 = (f32[2,8,8,256]{3,2,1,0:T(8,128)S(1)}, f32[2,8,8,256]{3,2,1,0:T(8,128)S(1)}, u32[]{:S(2)}, u32[]{:S(2)}) collective-permute-start(f32[2,8,8,256]{3,2,1,0:T(8,128)S(1)} %get-tuple-element.56), channel_id=1, source_target_pairs={{0,2},{2,0},{4,6},{6,4},{8,16},{10,18},{12,20},{14,22},{16,8},{18,... | collective-permute-start | bytes 393224 | tf_op jit(solution)/shard_map/ppermute | solution.py:557
  23.2 5.7 %collective-permute-start.12 = (f32[4,8,256]{2,1,0:T(8,128)S(1)}, f32[4,8,256]{2,1,0:T(8,128)S(1)}, u32[]{:S(2)}, u32[]{:S(2)}) collective-permute-start(f32[4,8,256]{2,1,0:T(8,128)S(1)} %get-tuple-element.63), channel_id=1, source_target_pairs={{0,12},{2,14},{4,8},{6,10},{8,4},{10,6},{12,0},{14,2},{16,28},{18,... | collective-permute-start | bytes 98312 | tf_op jit(solution)/shard_map/ppermute | solution.py:557
  25.9 3.1 %collective-permute-start.13 = (f32[4,8,256]{2,1,0:T(8,128)S(1)}, f32[4,8,256]{2,1,0:T(8,128)S(1)}, u32[]{:S(2)}, u32[]{:S(2)}) collective-permute-start(f32[4,8,256]{2,1,0:T(8,128)S(1)} %get-tuple-element.64), channel_id=1, source_target_pairs={{0,2},{2,0},{4,6},{6,4},{8,20},{10,22},{12,16},{14,18},{16,12},{18... | collective-permute-start | bytes 98312 | tf_op jit(solution)/shard_map/ppermute | solution.py:557
  31.4 8.3 %collective-permute-start.14 = (f32[32,8,256]{2,1,0:T(8,128)S(1)}, f32[32,8,256]{2,1,0:T(8,128)S(1)}, u32[]{:S(2)}, u32[]{:S(2)}) collective-permute-start(f32[32,8,256]{2,1,0:T(8,128)S(1)} %get-tuple-element.66), channel_id=1, source_target_pairs={{0,2},{2,0},{4,6},{6,4},{1,3},{3,1},{5,7},{7,5},{8,10},{10,8},{12,... | collective-permute-start | bytes 786440 | tf_op jit(solution)/shard_map/ppermute | solution.py:562
  31.5 6.4 %collective-permute-start.15 = (f32[16,8,256]{2,1,0:T(8,128)S(1)}, f32[16,8,256]{2,1,0:T(8,128)S(1)}, u32[]{:S(2)}, u32[]{:S(2)}) collective-permute-start(f32[16,8,256]{2,1,0:T(8,128)S(1)} %get-tuple-element.67), channel_id=1, source_target_pairs={{0,1},{1,0},{2,3},{3,2},{4,5},{5,4},{6,7},{7,6},{8,9},{9,8},{10,11... | collective-permute-start | bytes 393224 | tf_op jit(solution)/shard_map/ppermute | solution.py:571
  33.1 6.7 %collective-permute-start.16 = (f32[16,8,256]{2,1,0:T(8,128)S(1)}, f32[16,8,256]{2,1,0:T(8,128)S(1)}, u32[]{:S(2)}, u32[]{:S(2)}) collective-permute-start(f32[16,8,256]{2,1,0:T(8,128)S(1)} %get-tuple-element.68), channel_id=1, source_target_pairs={{0,3},{1,2},{2,1},{3,0},{4,7},{5,6},{6,5},{7,4},{8,11},{9,10},{10,... | collective-permute-start | bytes 393224 | tf_op jit(solution)/shard_map/ppermute | solution.py:571
  40.0 3.7 %collective-permute-start.17 = (f32[8,128]{1,0:T(8,128)S(1)}, f32[8,128]{1,0:T(8,128)S(1)}, u32[]{:S(2)}, u32[]{:S(2)}) collective-permute-start(f32[8,128]{1,0:T(8,128)S(1)} %correlation.1), channel_id=1, source_target_pairs={{0,1},{1,0},{2,3},{3,2},{4,5},{5,4},{6,7},{7,6},{8,9},{9,8},{10,11... | collective-permute-start | bytes 12296 | tf_op jit(solution)/shard_map/ppermute | solution.py:590
  43.7 3.4 %collective-permute-start.20 = (f32[8,128]{1,0:T(8,128)S(1)}, f32[8,128]{1,0:T(8,128)S(1)}, u32[]{:S(2)}, u32[]{:S(2)}) collective-permute-start(f32[8,128]{1,0:T(8,128)S(1)} %add.21), channel_id=1, source_target_pairs={{0,6},{2,4},{4,2},{6,0},{1,7},{3,5},{5,3},{7,1},{8,14},{10,12},{12... | collective-permute-start | bytes 12296 | tf_op jit(solution)/shard_map/ppermute | solution.py:590
  43.7 3.6 %collective-permute-start.19 = (f32[8,128]{1,0:T(8,128)S(1)}, f32[8,128]{1,0:T(8,128)S(1)}, u32[]{:S(2)}, u32[]{:S(2)}) collective-permute-start(f32[8,128]{1,0:T(8,128)S(1)} %add.21), channel_id=1, source_target_pairs={{0,4},{2,6},{4,0},{6,2},{1,5},{3,7},{5,1},{7,3},{8,12},{10,14},{12... | collective-permute-start | bytes 12296 | tf_op jit(solution)/shard_map/ppermute | solution.py:590
  44.5 2.9 %collective-permute-start.18 = (f32[8,128]{1,0:T(8,128)S(1)}, f32[8,128]{1,0:T(8,128)S(1)}, u32[]{:S(2)}, u32[]{:S(2)}) collective-permute-start(f32[8,128]{1,0:T(8,128)S(1)} %add.21), channel_id=1, source_target_pairs={{0,2},{2,0},{4,6},{6,4},{1,3},{3,1},{5,7},{7,5},{8,10},{10,8},{12,... | collective-permute-start | bytes 12296 | tf_op jit(solution)/shard_map/ppermute | solution.py:590
  45.6 9.6 %collective-permute-start.24 = (f32[2,16,8,256]{3,2,1,0:T(8,128)S(1)}, f32[2,16,8,256]{3,2,1,0:T(8,128)S(1)}, u32[]{:S(2)}, u32[]{:S(2)}) collective-permute-start(f32[2,16,8,256]{3,2,1,0:T(8,128)S(1)} %late.1), channel_id=1, source_target_pairs={{0,1},{1,0},{2,3},{3,2},{4,5},{5,4},{6,7},{7,6},{8,9},{9,8},{10,11... | collective-permute-start | bytes 786440 | tf_op jit(solution)/shard_map/ppermute | solution.py:571
  47.4 5.5 %collective-permute-start.23 = (f32[8,128]{1,0:T(8,128)S(1)}, f32[8,128]{1,0:T(8,128)S(1)}, u32[]{:S(2)}, u32[]{:S(2)}) collective-permute-start(f32[8,128]{1,0:T(8,128)S(1)} %add_add_fusion.1), channel_id=1, source_target_pairs={{0,24},{8,16},{16,8},{24,0},{1,25},{9,17},{17,9},{25,1},{2,26},{10... | collective-permute-start | bytes 12296 | tf_op jit(solution)/shard_map/ppermute | solution.py:590
  50.7 4.5 %collective-permute-start.22 = (f32[8,128]{1,0:T(8,128)S(1)}, f32[8,128]{1,0:T(8,128)S(1)}, u32[]{:S(2)}, u32[]{:S(2)}) collective-permute-start(f32[8,128]{1,0:T(8,128)S(1)} %add_add_fusion.1), channel_id=1, source_target_pairs={{0,16},{8,24},{16,0},{24,8},{1,17},{9,25},{17,1},{25,9},{2,18},{10... | collective-permute-start | bytes 12296 | tf_op jit(solution)/shard_map/ppermute | solution.py:590
  51.4 3.8 %collective-permute-start.21 = (f32[8,128]{1,0:T(8,128)S(1)}, f32[8,128]{1,0:T(8,128)S(1)}, u32[]{:S(2)}, u32[]{:S(2)}) collective-permute-start(f32[8,128]{1,0:T(8,128)S(1)} %add_add_fusion.1), channel_id=1, source_target_pairs={{0,8},{8,0},{16,24},{24,16},{1,9},{9,1},{17,25},{25,17},{2,10},{10... | collective-permute-start | bytes 12296 | tf_op jit(solution)/shard_map/ppermute | solution.py:590
  (4 other events, 30.3 us)

commit v10 on v9

--- a/solution.py
+++ b/solution.py
@@ -8,6 +8,7 @@
 from jax.sharding import PartitionSpec as P
 
 STEPS = 4
+SPLIT = 8
 HALO = 2 * STEPS
 PAD = 8
 LANES = 128
@@ -274,23 +275,13 @@
     return core == jnp.where(upward(chip, phase), 1, 0)
 
 
-def load_kernel(orbitals, potential, orbitals_out, potential_out, arrived):
-    copies = [
-        pltpu.make_async_copy(orbitals, orbitals_out, arrived.at[0]),
-        pltpu.make_async_copy(potential, potential_out, arrived.at[1]),
-    ]
-    for copy in copies:
-        copy.start()
-    for copy in copies:
-        copy.wait()
-
-
-def pack_kernel(orbitals, received, potential, received_potential, *outs):
+def pack_kernel(fields, received, received_potential, *outs):
+    potential = fields.at[fields.shape[0] - 1]
     core, chip, along_x = place()
     width = potential.shape[0]
     p_out, outs = outs[: len(y_phases())], outs[len(y_phases()) :]
     y_out, x_out, d_out = halos_of(outs)
-    tiles = (orbitals.at[core], received.at[core])
+    tiles = (fields.at[core], received.at[core])
     local = (potential, received_potential)
     for x_phase in range(2):
         right = upward(along_x, x_phase)
@@ -303,9 +294,10 @@
 
             @pl.when(chosen)
             def _(t=t, phase=phase):
-                y_out[phase][...] = tiles[t][...]
-                half = width // 2
-                p_out[phase][...] = local[t][pl.ds(core * half, half)]
+                half, split = width // 2, width // SPLIT
+                p_out[phase][:half] = local[t][pl.ds(core * half, half)]
+                p_out[phase][half:] = tiles[t][:split]
+                y_out[phase][...] = tiles[t][split:]
                 up = upward(chip, phase)
                 for x_phase in range(2):
                     right = upward(along_x, x_phase)
@@ -328,11 +320,12 @@
     return (potential - 0.5) / 4.25
 
 
-def first_own_kernel(orbitals, received, potential, received_potential, x_a, x_b, *outs):
+def first_own_kernel(fields, received, received_potential, x_a, x_b, *outs):
+    potential = fields.at[fields.shape[0] - 1]
     levels, local = outs[:-1], outs[-1]
     core, _, _ = place()
     x_halos = (x_a, x_b)
-    tiles = (orbitals.at[core], received.at[core])
+    tiles = (fields.at[core], received.at[core])
     fill_own(levels[0], tiles, [x.at[:, :HALO] for x in x_halos])
     tiles = (potential, received_potential)
     fill_own(local, tiles, [x.at[:, HALO:] for x in x_halos], diagonal)
@@ -348,12 +341,16 @@
     payloads = outs[STEPS + 2 :]
     core, chip, along_x = place()
     width, depth = local.shape[1] - 2 * HALO, 2 * LANES
-    fill_y(levels[0], y_halos, [c.at[: HALO // 2] for c in corners], HALO)
-    fill_y(local, None, [c.at[HALO // 2 :] for c in corners], HALO - 2, diagonal)
-    half = width // 2
+    half, split = width // 2, width // SPLIT
+    fill_y(levels[0], None, [c.at[: HALO // 2] for c in corners], HALO)
     for phase in y_phases():
         rows = rows_of(halo_slot(upward(chip, phase)))
-        put(local, HALO + core * half, rows, came[phase], diagonal)
+        put(levels[0], HALO, rows, came[phase].at[half:])
+        put(levels[0], HALO + split, rows, y_halos[phase])
+    fill_y(local, None, [c.at[HALO // 2 :] for c in corners], HALO - 2, diagonal)
+    for phase in y_phases():
+        rows = rows_of(halo_slot(upward(chip, phase)))
+        put(local, HALO + core * half, rows, came[phase].at[:half], diagonal)
         put(local, HALO + (1 - core) * half, rows, passed[phase], diagonal)
 
     second_part(levels, local, depth)
@@ -394,16 +391,16 @@
 
 def second_rest_kernel(*refs):
     count = len(y_phases())
-    local, orbitals, received = refs[STEPS + 1 : STEPS + 4]
+    local, fields, received = refs[STEPS + 1 : STEPS + 4]
     refs = refs[STEPS + 4 :]
     y_halos, corners = refs[:count], refs[count : 3 * count]
     levels, outs = refs[3 * count : 3 * count + STEPS + 1], refs[3 * count + STEPS + 1 :]
     outs, early = outs[:2], outs[2:]
     core, _, _ = place()
-    width, depth = orbitals.shape[1], orbitals.shape[3]
+    width, depth = fields.shape[1], fields.shape[3]
     fill_y(levels[0], y_halos, corners, HALO)
     second_part(levels, local, depth)
-    start = (orbitals.at[core], received.at[core])
+    start = (fields.at[core], received.at[core])
     for t, slot in enumerate(own_slots(core)):
         for half in range(2):
             lanes = slice(half * LANES, (half + 1) * LANES)
@@ -609,46 +606,39 @@
     received = swap(orbitals)
     received_potential = swap(potential)
     tile = (width, height, depth)
-    orbitals, potential = pl.pallas_call(
-        load_kernel,
-        out_shape=[struct(*orbitals.shape), struct(*tile)],
-        in_specs=[pl.BlockSpec(memory_space=pl.ANY)] * 2,
-        out_specs=[VMEM] * 2,
-        scratch_shapes=[pltpu.SemaphoreType.DMA((2,))],
-        compiler_params=PARAMS,
-        name="load",
-    )(orbitals, potential)
-
-    def payloads(in_x, in_corner):
+    fields = lax.concatenate([orbitals, potential[None]], 0)
+
+    def payloads(in_y, in_x, in_corner):
         return (
-            [struct(*tile)] * count
+            [struct(in_y, height, depth)] * count
             + [struct(2, in_x, height, depth)] * 2
             + [struct(in_corner, height, depth)] * (2 * count)
         )
 
     *packed, = pl.pallas_call(
         pack_kernel,
-        out_shape=[struct(width // 2, height, depth)] * count + payloads(2 * HALO - 2, HALO - 1),
-        in_specs=[VMEM] * 4,
+        out_shape=[struct(width // 2 + width // SPLIT, height, depth)] * count
+        + payloads(width - width // SPLIT, 2 * HALO - 2, HALO - 1),
+        in_specs=[VMEM] * 3,
         out_specs=[VMEM] * (2 + 4 * count),
         compiler_params=PARAMS,
         name="pack",
-    )(orbitals, received, potential, received_potential)
+    )(fields, received, received_potential)
     came = [meet(packed[phase], y_phase=phase) for phase in y_phases()]
     packed[-1], came = lax.optimization_barrier((packed[-1], came))
     y_halos, x_halos, corners = halos_of(exchange(packed[count:]))
-    passed = [swap(value) for value in came]
+    passed = [swap(value[: width // 2]) for value in came]
     *levels, local = pl.pallas_call(
         first_own_kernel,
         out_shape=[window] * (windows + 1),
-        in_specs=[VMEM] * 6,
+        in_specs=[VMEM] * 5,
         out_specs=[VMEM] * (windows + 1),
         compiler_params=PARAMS,
         name="first_own",
-    )(orbitals, received, potential, received_potential, *x_halos)
+    )(fields, received, received_potential, *x_halos)
     outs = pl.pallas_call(
         first_rest_kernel,
-        out_shape=[window] * (windows + 1) + payloads(HALO, HALO // 2),
+        out_shape=[window] * (windows + 1) + payloads(width, HALO, HALO // 2),
         in_specs=[VMEM] * (windows + 1 + 5 * count),
         out_specs=[VMEM] * (windows + 3 + 3 * count),
         input_output_aliases={k: k for k in range(windows + 1)},
@@ -674,7 +664,7 @@
         input_output_aliases={k: k for k in range(windows)},
         compiler_params=PARAMS,
         name="second_rest",
-    )(*levels, local, orbitals, received, *y_halos, *corners)
+    )(*levels, local, fields, received, *y_halos, *corners)
     keep, give, *early = outs[windows:]
 
     early = [to_band(value, 1 + k // 2, crossed=k % 2 == 1) for k, value in enumerate(early)]

time: 57.1 us -> 56.8 us (level)
  starting transfers between devices: 24.6 us -> 27.7 us
  waiting for transfers between devices: 18.5 us -> 16 us
  local copies, waits for them, and re-layouts: 2 us -> 0.02 us
  other arithmetic: 0.01 us -> 1.19 us
    ppermute x11, waiting for transfers between devices: 6.45 us -> 3.3 us  [meet(): return lax.ppermute(value, ('gx', 'gy'), pairs)]
    ppermute x11, starting transfers between devices: 12.6 us -> 15.7 us  [meet(): return lax.ppermute(value, ('gx', 'gy'), pairs)]
    unnamed x6 -> x2, local copies, waits for them, and re-layouts: 2 us -> 0.01 us
    concatenate x0 -> x1, other arithmetic: none -> 1.17 us  [per_device(): fields = lax.concatenate([orbitals, potential[None]], 0)]
    ppermute x4, waiting for transfers between devices: 0.01 us -> 0.89 us  [swap(): return lax.ppermute(value, 'gy', [(y, y ^ 1) for y in range(count)])]
  transfers between devices with their start and end apart: 25 -> 25, of which waited for: 10 -> 11; matrix products, arithmetic and copies ran while one was open for 0% -> 2% of each run, Pallas kernels for 9% -> 9%
where the time goes in v10:
time: 56.8 us; the launch traced here: 56.6 us
  starting transfers between devices  27.7 us (49%)
  waiting for transfers between devices  16 us (28%)
  Pallas kernels  11.6 us (20%)
  other arithmetic  1.19 us (2%)
    ppermute x11, starting transfers between devices, meet(): return lax.ppermute(value, ('gx', 'gy'), pairs)  15.7 us
    ppermute x7, starting transfers between devices, of(): return lax.ppermute(value, axis, [(i, i ^ step) for i in range(count)])  7.87 us
    ppermute x3, waiting for transfers between devices, to_band(): return lax.ppermute(value, ('gy', 'band'), pairs)  6.41 us
    ppermute x7, waiting for transfers between devices, of(): return lax.ppermute(value, axis, [(i, i ^ step) for i in range(count)])  5.44 us
    ppermute x3, starting transfers between devices, to_band(): return lax.ppermute(value, ('gy', 'band'), pairs)  3.42 us
    ppermute x11, waiting for transfers between devices, meet(): return lax.ppermute(value, ('gx', 'gy'), pairs)  3.3 us
    pallas_call x1, Pallas kernels, per_device(): pl.pallas_call(first_own_kernel, out_shape=[window] * (windows + 1), in_s...  2.51 us
    pallas_call x1, Pallas kernels, per_device(): pl.pallas_call(second_own_kernel, out_shape=[window] * windows, in_specs=...  2.42 us
  transfers between devices with their start and end apart: 25, of which 11 were waited for; matrix products, arithmetic and copies ran while one was open for 2% of the time, Pallas kernels for 9%

profile of v10, /device:TPU:0, one launch (start us, length us, event | category | flops | bytes accessed | tf_op | source)
XLA Modules:
  0.0 56.6 jit_solution(16895930627057468956)
XLA Ops:
  0.5 1.2 %pad_maximum_fusion.fields.refs_6_ = f32[3,32,8,256]{3,2,1,0:T(8,128)S(1)} fusion(f32[1,32,8,256]{3,2,1,0:T(8,128)} %bitcast.1, f32[2,32,8,256]{3,2,1,0:T(8,128)} %param.3), kind=kLoop, calls=%fused_computation | loop fusion | flops 196608 | bytes 1572864 | tf_op jit(solution)/shard_map/concatenate | solution.py:609
  2.7 3.0 %collective-permute-start.4 = (f32[20,8,256]{2,1,0:T(8,128)S(1)}, f32[20,8,256]{2,1,0:T(8,128)S(1)}, u32[]{:S(2)}, u32[]{:S(2)}) collective-permute-start(f32[20,8,256]{2,1,0:T(8,128)S(1)} %get-tuple-element.44), channel_id=1, source_target_pairs={{0,4},{2,6},{4,0},{6,2},{8,12},{10,14},{12,8},{14,10},{16,20},{18,... | collective-permute-start | bytes 491528 | tf_op jit(solution)/shard_map/ppermute | solution.py:554
  5.6 1.6 %collective-permute-start.2 = (f32[2,14,8,256]{3,2,1,0:T(8,128)S(1)}, f32[2,14,8,256]{3,2,1,0:T(8,128)S(1)}, u32[]{:S(2)}, u32[]{:S(2)}) collective-permute-start(f32[2,14,8,256]{3,2,1,0:T(8,128)S(1)} %get-tuple-element.35), channel_id=1, source_target_pairs={{0,8},{2,10},{4,12},{6,14},{8,0},{10,2},{12,4},{14,6},{16,24},{18,... | collective-permute-start | bytes 688136 | tf_op jit(solution)/shard_map/ppermute | solution.py:554
  7.7 2.5 %collective-permute-done.4.refs_6_ = f32[20,8,256]{2,1,0:T(8,128)S(1)} collective-permute-done((f32[20,8,256]{2,1,0:T(8,128)S(1)}, f32[20,8,256]{2,1,0:T(8,128)S(1)}, u32[]{:S(2)}, u32[]{:S(2)}) %collective-permute-start.4) | collective-permute-done | bytes 163872 | tf_op jit(solution)/shard_map/ppermute | solution.py:554
  10.3 3.4 %collective-permute-start.7 = (f32[7,8,256]{2,1,0:T(8,128)S(1)}, f32[7,8,256]{2,1,0:T(8,128)S(1)}, u32[]{:S(2)}, u32[]{:S(2)}) collective-permute-start(f32[7,8,256]{2,1,0:T(8,128)S(1)} %get-tuple-element.47), channel_id=1, source_target_pairs={{0,12},{2,14},{4,8},{6,10},{8,4},{10,6},{12,0},{14,2},{16,28},{18,... | collective-permute-start | bytes 172040 | tf_op jit(solution)/shard_map/ppermute | solution.py:554
  13.8 2.5 %first_own.1 = (f32[2,48,48,128]{3,2,1,0:T(8,128)S(1)}, f32[2,48,48,128]{3,2,1,0:T(8,128)S(1)}, f32[2,48,48,128]{3,2,1,0:T(8,128)S(1)}, f32[2,48,48,128]{3,2,1,0...) custom-call(f32[3,32,8,256]{3,2,1,0:T(8,128)S(1)} %pad_maximum_fusion.fields.refs_6_, ...), custom_call_target="tpu_custom_call" | custom-call | tf_op jit(solution)/shard_map/first_own/pallas_call | solution.py:631
  16.4 2.2 %first_rest.1 = (f32[2,48,48,128]{3,2,1,0:T(8,128)S(1)}, f32[2,48,48,128]{3,2,1,0:T(8,128)S(1)}, f32[2,48,48,128]{3,2,1,0:T(8,128)S(1)}, f32[2,48,48,128]{3,2,1,...) custom-call(f32[2,48,48,128]{3,2,1,0:T(8,128)S(1)} %get-tuple-elemen, ...), custom_call_target="tpu_custom_call", output_to_operand_aliasing={{0}: (0, {}), {1}: (1, {}), {2}: (2, {}), {3}: (3, {}), {4}... | custom-call | tf_op jit(solution)/shard_map/first_rest/pallas_call | solution.py:639
  18.7 1.6 %collective-permute-start.11 = (f32[32,8,256]{2,1,0:T(8,128)S(1)}, f32[32,8,256]{2,1,0:T(8,128)S(1)}, u32[]{:S(2)}, u32[]{:S(2)}) collective-permute-start(f32[32,8,256]{2,1,0:T(8,128)S(1)} %get-tuple-element.58), channel_id=1, source_target_pairs={{0,4},{2,6},{4,0},{6,2},{8,12},{10,14},{12,8},{14,10},{16,20},{18,... | collective-permute-start | bytes 786440 | tf_op jit(solution)/shard_map/ppermute | solution.py:554
  20.3 2.9 %collective-permute-start.9 = (f32[2,8,8,256]{3,2,1,0:T(8,128)S(1)}, f32[2,8,8,256]{3,2,1,0:T(8,128)S(1)}, u32[]{:S(2)}, u32[]{:S(2)}) collective-permute-start(f32[2,8,8,256]{3,2,1,0:T(8,128)S(1)} %get-tuple-element.51), channel_id=1, source_target_pairs={{0,8},{2,10},{4,12},{6,14},{8,0},{10,2},{12,4},{14,6},{16,24},{18,... | collective-permute-start | bytes 393224 | tf_op jit(solution)/shard_map/ppermute | solution.py:554
  23.3 2.5 %collective-permute-start.12 = (f32[4,8,256]{2,1,0:T(8,128)S(1)}, f32[4,8,256]{2,1,0:T(8,128)S(1)}, u32[]{:S(2)}, u32[]{:S(2)}) collective-permute-start(f32[4,8,256]{2,1,0:T(8,128)S(1)} %get-tuple-element.59), channel_id=1, source_target_pairs={{0,12},{2,14},{4,8},{6,10},{8,4},{10,6},{12,0},{14,2},{16,28},{18,... | collective-permute-start | bytes 98312 | tf_op jit(solution)/shard_map/ppermute | solution.py:554
  26.5 2.4 %second_own.1 = (f32[2,48,48,128]{3,2,1,0:T(8,128)S(1)}, f32[2,48,48,128]{3,2,1,0:T(8,128)S(1)}, f32[2,48,48,128]{3,2,1,0:T(8,128)S(1)}, f32[2,48,48,128]{3,2,1,0:T(8,128)S(1)}, f32[2,48,48,128]{3,2,1,0:T(8,128)S(1)}) custom-call(f32[2,48,48,128]{3,2,1,0:T(8,128)S(1)} %get-tuple-element.49.before, f32[2,48,48,128]{3,2,1,0:T(8,128)S(1)} %get-tuple-element.50.local.refs_5_, ...), custom_call_target="tpu_custom_call" | custom-call | tf_op jit(solution)/shard_map/second_own/pallas_call | solution.py:650
  29.0 2.4 %second_rest.1 = (f32[2,48,48,128]{3,2,1,0:T(8,128)S(1)}, f32[2,48,48,128]{3,2,1,0:T(8,128)S(1)}, f32[2,48,48,128]{3,2,1,0:T(8,128)S(1)}, f32[2,48,48,128]{3,2,1...) custom-call(f32[2,48,48,128]{3,2,1,0:T(8,128)S(1)} %get-tuple-elemen, ...), custom_call_target="tpu_custom_call", output_to_operand_aliasing={{0}: (0, {}), {1}: (1, {}), {2}: (2, {}), {3}: (3, {}), {4}... | custom-call | tf_op jit(solution)/shard_map/second_rest/pallas_call | solution.py:659
  31.5 1.6 %collective-permute-start.15 = (f32[16,8,256]{2,1,0:T(8,128)S(1)}, f32[16,8,256]{2,1,0:T(8,128)S(1)}, u32[]{:S(2)}, u32[]{:S(2)}) collective-permute-start(f32[16,8,256]{2,1,0:T(8,128)S(1)} %get-tuple-element.63), channel_id=1, source_target_pairs={{0,1},{1,0},{2,3},{3,2},{4,5},{5,4},{6,7},{7,6},{8,9},{9,8},{10,11... | collective-permute-start | bytes 393224 | tf_op jit(solution)/shard_map/ppermute | solution.py:568
  33.3 4.5 %collective-permute-done.15.refs_2_.refs_4_ = f32[16,8,256]{2,1,0:T(8,128)S(1)} collective-permute-done((f32[16,8,256]{2,1,0:T(8,128)S(1)}, f32[16,8,256]{2,1,0:T(8,128)S(1)}, u32[]{:S(2)}, u32[]{:S(2)}) %collective-permute-start.15) | collective-permute-done | bytes 131104 | tf_op jit(solution)/shard_map/ppermute | solution.py:568
  37.8 1.9 %collective-permute-done.16.refs_3_.refs_5_ = f32[16,8,256]{2,1,0:T(8,128)S(1)} collective-permute-done((f32[16,8,256]{2,1,0:T(8,128)S(1)}, f32[16,8,256]{2,1,0:T(8,128)S(1)}, u32[]{:S(2)}, u32[]{:S(2)}) %collective-permute-start.16) | collective-permute-done | bytes 131104 | tf_op jit(solution)/shard_map/ppermute | solution.py:568
  40.0 1.6 %collective-permute-start.17 = (f32[8,128]{1,0:T(8,128)S(1)}, f32[8,128]{1,0:T(8,128)S(1)}, u32[]{:S(2)}, u32[]{:S(2)}) collective-permute-start(f32[8,128]{1,0:T(8,128)S(1)} %correlation.1), channel_id=1, source_target_pairs={{0,1},{1,0},{2,3},{3,2},{4,5},{5,4},{6,7},{7,6},{8,9},{9,8},{10,11... | collective-permute-start | bytes 12296 | tf_op jit(solution)/shard_map/ppermute | solution.py:587
  41.5 2.1 %collective-permute-done.17 = f32[8,128]{1,0:T(8,128)S(1)} collective-permute-done((f32[8,128]{1,0:T(8,128)S(1)}, f32[8,128]{1,0:T(8,128)S(1)}, u32[]{:S(2)}, u32[]{:S(2)}) %collective-permute-start.17) | collective-permute-done | bytes 4128 | tf_op jit(solution)/shard_map/ppermute | solution.py:587
  44.4 1.1 %collective-permute-start.18 = (f32[8,128]{1,0:T(8,128)S(1)}, f32[8,128]{1,0:T(8,128)S(1)}, u32[]{:S(2)}, u32[]{:S(2)}) collective-permute-start(f32[8,128]{1,0:T(8,128)S(1)} %add.21), channel_id=1, source_target_pairs={{0,2},{2,0},{4,6},{6,4},{1,3},{3,1},{5,7},{7,5},{8,10},{10,8},{12,... | collective-permute-start | bytes 12296 | tf_op jit(solution)/shard_map/ppermute | solution.py:587
  45.6 1.6 %collective-permute-start.24 = (f32[2,16,8,256]{3,2,1,0:T(8,128)S(1)}, f32[2,16,8,256]{3,2,1,0:T(8,128)S(1)}, u32[]{:S(2)}, u32[]{:S(2)}) collective-permute-start(f32[2,16,8,256]{3,2,1,0:T(8,128)S(1)} %late.1), channel_id=1, source_target_pairs={{0,1},{1,0},{2,3},{3,2},{4,5},{5,4},{6,7},{7,6},{8,9},{9,8},{10,11... | collective-permute-start | bytes 786440 | tf_op jit(solution)/shard_map/ppermute | solution.py:568
  47.3 2.5 %collective-permute-start.23 = (f32[8,128]{1,0:T(8,128)S(1)}, f32[8,128]{1,0:T(8,128)S(1)}, u32[]{:S(2)}, u32[]{:S(2)}) collective-permute-start(f32[8,128]{1,0:T(8,128)S(1)} %add_add_fusion.1), channel_id=1, source_target_pairs={{0,24},{8,16},{16,8},{24,0},{1,25},{9,17},{17,9},{25,1},{2,26},{10... | collective-permute-start | bytes 12296 | tf_op jit(solution)/shard_map/ppermute | solution.py:587
  49.8 1.5 %collective-permute-start.22 = (f32[8,128]{1,0:T(8,128)S(1)}, f32[8,128]{1,0:T(8,128)S(1)}, u32[]{:S(2)}, u32[]{:S(2)}) collective-permute-start(f32[8,128]{1,0:T(8,128)S(1)} %add_add_fusion.1), channel_id=1, source_target_pairs={{0,16},{8,24},{16,0},{24,8},{1,17},{9,25},{17,1},{25,9},{2,18},{10... | collective-permute-start | bytes 12296 | tf_op jit(solution)/shard_map/ppermute | solution.py:587
  51.8 1.0 %collective-permute-done.23 = f32[8,128]{1,0:T(8,128)S(1)} collective-permute-done((f32[8,128]{1,0:T(8,128)S(1)}, f32[8,128]{1,0:T(8,128)S(1)}, u32[]{:S(2)}, u32[]{:S(2)}) %collective-permute-start.23) | collective-permute-done | bytes 4128 | tf_op jit(solution)/shard_map/ppermute | solution.py:587
  52.8 1.5 %collective-permute-done.22 = f32[8,128]{1,0:T(8,128)S(1)} collective-permute-done((f32[8,128]{1,0:T(8,128)S(1)}, f32[8,128]{1,0:T(8,128)S(1)}, u32[]{:S(2)}, u32[]{:S(2)}) %collective-permute-start.22) | collective-permute-done | bytes 4128 | tf_op jit(solution)/shard_map/ppermute | solution.py:587
  54.9 1.7 %basis.1 = f32[2,32,8,256]{3,2,1,0:T(8,128)} custom-call(f32[8,128]{1,0:T(8,128)S(1)} %add_add_fusion.refs_0_, s32[4]{0:T(128)S(1)} %copy-done, f32[32,8,256]{2,1,0:T(8,128)S(1)} %get-tuple-element.61.refs_0_.keep.refs_2_, f32[32,8,256]{2,1,0:T(8,128)S(1)} %collective-permute-done.14.refs_1_.sibling.refs_3_, ...), custom_call_target="tpu_custom_call" | custom-call | tf_op jit(solution)/shard_map/basis/pallas_call | solution.py:690
  (41 shorter events, 5.8 us)
Async XLA Ops:
  0.0 2.6 %collective-permute-start = (f32[2,32,8,256]{3,2,1,0:T(8,128)}, f32[2,32,8,256]{3,2,1,0:T(8,128)S(1)}, u32[]{:S(2)}, u32[]{:S(2)}) collective-permute-start(f32[2,32,8,256]{3,2,1,0:T(8,128)} %param.3), channel_id=1, source_target_pairs={{0,2},{2,0},{4,6},{6,4},{1,3},{3,1},{5,7},{7,5},{8,10},{10,8},{12,... | collective-permute-start | bytes 1572872 | tf_op jit(solution)/shard_map/ppermute | solution.py:559
  2.7 7.5 %collective-permute-start.4 = (f32[20,8,256]{2,1,0:T(8,128)S(1)}, f32[20,8,256]{2,1,0:T(8,128)S(1)}, u32[]{:S(2)}, u32[]{:S(2)}) collective-permute-start(f32[20,8,256]{2,1,0:T(8,128)S(1)} %get-tuple-element.44), channel_id=1, source_target_pairs={{0,4},{2,6},{4,0},{6,2},{8,12},{10,14},{12,8},{14,10},{16,20},{18,... | collective-permute-start | bytes 491528 | tf_op jit(solution)/shard_map/ppermute | solution.py:554
  5.6 8.0 %collective-permute-start.2 = (f32[2,14,8,256]{3,2,1,0:T(8,128)S(1)}, f32[2,14,8,256]{3,2,1,0:T(8,128)S(1)}, u32[]{:S(2)}, u32[]{:S(2)}) collective-permute-start(f32[2,14,8,256]{3,2,1,0:T(8,128)S(1)} %get-tuple-element.35), channel_id=1, source_target_pairs={{0,8},{2,10},{4,12},{6,14},{8,0},{10,2},{12,4},{14,6},{16,24},{18,... | collective-permute-start | bytes 688136 | tf_op jit(solution)/shard_map/ppermute | solution.py:554
  7.2 6.6 %collective-permute-start.3 = (f32[2,14,8,256]{3,2,1,0:T(8,128)S(1)}, f32[2,14,8,256]{3,2,1,0:T(8,128)S(1)}, u32[]{:S(2)}, u32[]{:S(2)}) collective-permute-start(f32[2,14,8,256]{3,2,1,0:T(8,128)S(1)} %get-tuple-element.36), channel_id=1, source_target_pairs={{0,2},{2,0},{4,6},{6,4},{8,16},{10,18},{12,20},{14,22},{16,8},{18,... | collective-permute-start | bytes 688136 | tf_op jit(solution)/shard_map/ppermute | solution.py:554
  7.2 9.2 %collective-permute-start.6 = (f32[28,8,256]{2,1,0:T(8,128)S(1)}, f32[28,8,256]{2,1,0:T(8,128)S(1)}, u32[]{:S(2)}, u32[]{:S(2)}) collective-permute-start(f32[28,8,256]{2,1,0:T(8,128)S(1)} %get-tuple-element.46), channel_id=1, source_target_pairs={{0,4},{2,6},{4,0},{6,2},{8,12},{10,14},{12,8},{14,10},{16,20},{18,... | collective-permute-start | bytes 688136 | tf_op jit(solution)/shard_map/ppermute | solution.py:554
  10.2 6.2 %collective-permute-start.5 = (f32[16,8,256]{2,1,0:T(8,128)S(1)}, f32[16,8,256]{2,1,0:T(8,128)S(1)}, u32[]{:S(2)}, u32[]{:S(2)}) collective-permute-start(f32[16,8,256]{2,1,0:T(8,128)S(1)} %slice.3), channel_id=1, source_target_pairs={{0,2},{2,0},{4,6},{6,4},{1,3},{3,1},{5,7},{7,5},{8,10},{10,8},{12,... | collective-permute-start | bytes 393224 | tf_op jit(solution)/shard_map/ppermute | solution.py:559
  10.3 6.1 %collective-permute-start.7 = (f32[7,8,256]{2,1,0:T(8,128)S(1)}, f32[7,8,256]{2,1,0:T(8,128)S(1)}, u32[]{:S(2)}, u32[]{:S(2)}) collective-permute-start(f32[7,8,256]{2,1,0:T(8,128)S(1)} %get-tuple-element.47), channel_id=1, source_target_pairs={{0,12},{2,14},{4,8},{6,10},{8,4},{10,6},{12,0},{14,2},{16,28},{18,... | collective-permute-start | bytes 172040 | tf_op jit(solution)/shard_map/ppermute | solution.py:554
  13.6 2.7 %collective-permute-start.8 = (f32[7,8,256]{2,1,0:T(8,128)S(1)}, f32[7,8,256]{2,1,0:T(8,128)S(1)}, u32[]{:S(2)}, u32[]{:S(2)}) collective-permute-start(f32[7,8,256]{2,1,0:T(8,128)S(1)} %get-tuple-element.48), channel_id=1, source_target_pairs={{0,2},{2,0},{4,6},{6,4},{8,20},{10,22},{12,16},{14,18},{16,12},{18... | collective-permute-start | bytes 172040 | tf_op jit(solution)/shard_map/ppermute | solution.py:554
  18.7 10.3 %collective-permute-start.11 = (f32[32,8,256]{2,1,0:T(8,128)S(1)}, f32[32,8,256]{2,1,0:T(8,128)S(1)}, u32[]{:S(2)}, u32[]{:S(2)}) collective-permute-start(f32[32,8,256]{2,1,0:T(8,128)S(1)} %get-tuple-element.58), channel_id=1, source_target_pairs={{0,4},{2,6},{4,0},{6,2},{8,12},{10,14},{12,8},{14,10},{16,20},{18,... | collective-permute-start | bytes 786440 | tf_op jit(solution)/shard_map/ppermute | solution.py:554
  20.3 6.2 %collective-permute-start.9 = (f32[2,8,8,256]{3,2,1,0:T(8,128)S(1)}, f32[2,8,8,256]{3,2,1,0:T(8,128)S(1)}, u32[]{:S(2)}, u32[]{:S(2)}) collective-permute-start(f32[2,8,8,256]{3,2,1,0:T(8,128)S(1)} %get-tuple-element.51), channel_id=1, source_target_pairs={{0,8},{2,10},{4,12},{6,14},{8,0},{10,2},{12,4},{14,6},{16,24},{18,... | collective-permute-start | bytes 393224 | tf_op jit(solution)/shard_map/ppermute | solution.py:554
  23.3 3.3 %collective-permute-start.10 = (f32[2,8,8,256]{3,2,1,0:T(8,128)S(1)}, f32[2,8,8,256]{3,2,1,0:T(8,128)S(1)}, u32[]{:S(2)}, u32[]{:S(2)}) collective-permute-start(f32[2,8,8,256]{3,2,1,0:T(8,128)S(1)} %get-tuple-element.52), channel_id=1, source_target_pairs={{0,2},{2,0},{4,6},{6,4},{8,16},{10,18},{12,20},{14,22},{16,8},{18,... | collective-permute-start | bytes 393224 | tf_op jit(solution)/shard_map/ppermute | solution.py:554
  23.3 5.7 %collective-permute-start.12 = (f32[4,8,256]{2,1,0:T(8,128)S(1)}, f32[4,8,256]{2,1,0:T(8,128)S(1)}, u32[]{:S(2)}, u32[]{:S(2)}) collective-permute-start(f32[4,8,256]{2,1,0:T(8,128)S(1)} %get-tuple-element.59), channel_id=1, source_target_pairs={{0,12},{2,14},{4,8},{6,10},{8,4},{10,6},{12,0},{14,2},{16,28},{18,... | collective-permute-start | bytes 98312 | tf_op jit(solution)/shard_map/ppermute | solution.py:554
  25.8 3.2 %collective-permute-start.13 = (f32[4,8,256]{2,1,0:T(8,128)S(1)}, f32[4,8,256]{2,1,0:T(8,128)S(1)}, u32[]{:S(2)}, u32[]{:S(2)}) collective-permute-start(f32[4,8,256]{2,1,0:T(8,128)S(1)} %get-tuple-element.60), channel_id=1, source_target_pairs={{0,2},{2,0},{4,6},{6,4},{8,20},{10,22},{12,16},{14,18},{16,12},{18... | collective-permute-start | bytes 98312 | tf_op jit(solution)/shard_map/ppermute | solution.py:554
  31.4 8.3 %collective-permute-start.14 = (f32[32,8,256]{2,1,0:T(8,128)S(1)}, f32[32,8,256]{2,1,0:T(8,128)S(1)}, u32[]{:S(2)}, u32[]{:S(2)}) collective-permute-start(f32[32,8,256]{2,1,0:T(8,128)S(1)} %get-tuple-element.62), channel_id=1, source_target_pairs={{0,2},{2,0},{4,6},{6,4},{1,3},{3,1},{5,7},{7,5},{8,10},{10,8},{12,... | collective-permute-start | bytes 786440 | tf_op jit(solution)/shard_map/ppermute | solution.py:559
  31.5 6.4 %collective-permute-start.15 = (f32[16,8,256]{2,1,0:T(8,128)S(1)}, f32[16,8,256]{2,1,0:T(8,128)S(1)}, u32[]{:S(2)}, u32[]{:S(2)}) collective-permute-start(f32[16,8,256]{2,1,0:T(8,128)S(1)} %get-tuple-element.63), channel_id=1, source_target_pairs={{0,1},{1,0},{2,3},{3,2},{4,5},{5,4},{6,7},{7,6},{8,9},{9,8},{10,11... | collective-permute-start | bytes 393224 | tf_op jit(solution)/shard_map/ppermute | solution.py:568
  33.0 6.7 %collective-permute-start.16 = (f32[16,8,256]{2,1,0:T(8,128)S(1)}, f32[16,8,256]{2,1,0:T(8,128)S(1)}, u32[]{:S(2)}, u32[]{:S(2)}) collective-permute-start(f32[16,8,256]{2,1,0:T(8,128)S(1)} %get-tuple-element.64), channel_id=1, source_target_pairs={{0,3},{1,2},{2,1},{3,0},{4,7},{5,6},{6,5},{7,4},{8,11},{9,10},{10,... | collective-permute-start | bytes 393224 | tf_op jit(solution)/shard_map/ppermute | solution.py:568
  40.0 3.7 %collective-permute-start.17 = (f32[8,128]{1,0:T(8,128)S(1)}, f32[8,128]{1,0:T(8,128)S(1)}, u32[]{:S(2)}, u32[]{:S(2)}) collective-permute-start(f32[8,128]{1,0:T(8,128)S(1)} %correlation.1), channel_id=1, source_target_pairs={{0,1},{1,0},{2,3},{3,2},{4,5},{5,4},{6,7},{7,6},{8,9},{9,8},{10,11... | collective-permute-start | bytes 12296 | tf_op jit(solution)/shard_map/ppermute | solution.py:587
  43.7 3.4 %collective-permute-start.20 = (f32[8,128]{1,0:T(8,128)S(1)}, f32[8,128]{1,0:T(8,128)S(1)}, u32[]{:S(2)}, u32[]{:S(2)}) collective-permute-start(f32[8,128]{1,0:T(8,128)S(1)} %add.21), channel_id=1, source_target_pairs={{0,6},{2,4},{4,2},{6,0},{1,7},{3,5},{5,3},{7,1},{8,14},{10,12},{12... | collective-permute-start | bytes 12296 | tf_op jit(solution)/shard_map/ppermute | solution.py:587
  43.7 3.6 %collective-permute-start.19 = (f32[8,128]{1,0:T(8,128)S(1)}, f32[8,128]{1,0:T(8,128)S(1)}, u32[]{:S(2)}, u32[]{:S(2)}) collective-permute-start(f32[8,128]{1,0:T(8,128)S(1)} %add.21), channel_id=1, source_target_pairs={{0,4},{2,6},{4,0},{6,2},{1,5},{3,7},{5,1},{7,3},{8,12},{10,14},{12... | collective-permute-start | bytes 12296 | tf_op jit(solution)/shard_map/ppermute | solution.py:587
  44.4 2.9 %collective-permute-start.18 = (f32[8,128]{1,0:T(8,128)S(1)}, f32[8,128]{1,0:T(8,128)S(1)}, u32[]{:S(2)}, u32[]{:S(2)}) collective-permute-start(f32[8,128]{1,0:T(8,128)S(1)} %add.21), channel_id=1, source_target_pairs={{0,2},{2,0},{4,6},{6,4},{1,3},{3,1},{5,7},{7,5},{8,10},{10,8},{12,... | collective-permute-start | bytes 12296 | tf_op jit(solution)/shard_map/ppermute | solution.py:587
  45.6 9.4 %collective-permute-start.24 = (f32[2,16,8,256]{3,2,1,0:T(8,128)S(1)}, f32[2,16,8,256]{3,2,1,0:T(8,128)S(1)}, u32[]{:S(2)}, u32[]{:S(2)}) collective-permute-start(f32[2,16,8,256]{3,2,1,0:T(8,128)S(1)} %late.1), channel_id=1, source_target_pairs={{0,1},{1,0},{2,3},{3,2},{4,5},{5,4},{6,7},{7,6},{8,9},{9,8},{10,11... | collective-permute-start | bytes 786440 | tf_op jit(solution)/shard_map/ppermute | solution.py:568
  47.3 5.5 %collective-permute-start.23 = (f32[8,128]{1,0:T(8,128)S(1)}, f32[8,128]{1,0:T(8,128)S(1)}, u32[]{:S(2)}, u32[]{:S(2)}) collective-permute-start(f32[8,128]{1,0:T(8,128)S(1)} %add_add_fusion.1), channel_id=1, source_target_pairs={{0,24},{8,16},{16,8},{24,0},{1,25},{9,17},{17,9},{25,1},{2,26},{10... | collective-permute-start | bytes 12296 | tf_op jit(solution)/shard_map/ppermute | solution.py:587
  49.8 4.5 %collective-permute-start.22 = (f32[8,128]{1,0:T(8,128)S(1)}, f32[8,128]{1,0:T(8,128)S(1)}, u32[]{:S(2)}, u32[]{:S(2)}) collective-permute-start(f32[8,128]{1,0:T(8,128)S(1)} %add_add_fusion.1), channel_id=1, source_target_pairs={{0,16},{8,24},{16,0},{24,8},{1,17},{9,25},{17,1},{25,9},{2,18},{10... | collective-permute-start | bytes 12296 | tf_op jit(solution)/shard_map/ppermute | solution.py:587
  51.3 3.6 %collective-permute-start.21 = (f32[8,128]{1,0:T(8,128)S(1)}, f32[8,128]{1,0:T(8,128)S(1)}, u32[]{:S(2)}, u32[]{:S(2)}) collective-permute-start(f32[8,128]{1,0:T(8,128)S(1)} %add_add_fusion.1), channel_id=1, source_target_pairs={{0,8},{8,0},{16,24},{24,16},{1,9},{9,1},{17,25},{25,17},{2,10},{10... | collective-permute-start | bytes 12296 | tf_op jit(solution)/shard_map/ppermute | solution.py:587
  (2 other events, 28.1 us)
